TPU v7x, 32 devices: a whole 2x2x4 slice. The times are simulated.
32 devices in a mesh: section: 8 (over z, core), expert: 4 (over y, x).
Axes of the slice: x: 2, y: 2, z: 4, core: 2. Of those that a mesh axis runs over, the one named last changes fastest.
Arguments:
- fwd_prev: bfloat16 [8, 512, 2048], P('section', 'expert'), may hold values from -24 to 24
- bwd_prev: bfloat16 [8, 512, 2048], P('section', 'expert'), may hold values from -6 to 6
- bwd_saved: bfloat16 [8, 512, 2048], P('section', 'expert'), may hold values from -24 to 24
- fwd_routes: int32 [8, 512, 2], P('section', 'expert'), may hold values from 0 to 3, all different within a row; in each aligned block of 128 rows (0 to 127, 128 to 255, ..., all dimensions but the last counted through in order) at most 96 rows name the same one
- fwd_gates: float32 [8, 512, 2], P('section', 'expert'), may hold values from 0.2 to 1
- bwd_routes: int32 [8, 512, 2], P('section', 'expert'), may hold values from 0 to 3, all different within a row; in each aligned block of 128 rows (0 to 127, 128 to 255, ..., all dimensions but the last counted through in order) at most 96 rows name the same one
- bwd_gates: float32 [8, 512, 2], P('section', 'expert'), may hold values from 0.2 to 1
- norm_gain: float32 [8, 2048], P('section'), may hold values from 0.25 to 1.75
- w_in: bfloat16 [8, 4, 2048, 1536], P('section', 'expert'), may hold values from -0.125 to 0.125
- w_out: bfloat16 [8, 4, 768, 2048], P('section', 'expert'), may hold values from -0.21875 to 0.21875
Outputs:
- fwd_out: bfloat16 [8, 512, 2048], P('section', 'expert')
- bwd_out: bfloat16 [8, 512, 2048], P('section', 'expert')
Inputs may be any that keep to these rules, and one draw needn't show every extreme that they name: `fwd_routes`: each row names 2 different experts; within the 128 rows of one device in one section no expert is named by more than 96 rows. `bwd_routes`: each row names 2 different experts; within the 128 rows of one device in one section no expert is named by more than 96 rows.
All inputs are finite; a program needn't handle non-finite values.
Results may differ from a plain program's by a relative error of at most 0.006.
Values may be sent and summed in bfloat16 or wider, within the bound.
No kernel may reach another device: no remote copies, remote signals or barrier semaphores. Data moves between devices by JAX's collectives and lax.ppermute only.
A program may use at most 64 MiB of HBM per device.

v0:
```python
import jax
import jax.numpy as jnp
from jax import lax
from jax.sharding import PartitionSpec as P

EPS = 1e-06


def passed_along(value, axis, steps):
    count = lax.axis_size(axis)
    pairs = [(source, (source + steps) % count) for source in range(count)]
    return lax.ppermute(value, axis, pairs)


def pair_places(routes, expert_count, capacity):
    flat_routes = routes.reshape(-1)
    onehot = (flat_routes[:, None] == jnp.arange(expert_count, dtype=jnp.int32)[None, :]).astype(
        jnp.int32
    )
    earlier = jnp.cumsum(onehot, axis=0) - onehot
    slot_index = jnp.sum(earlier * onehot, axis=1)
    return flat_routes * capacity + slot_index


def normalize(values, gain_row):
    wide = values.astype(jnp.float32)
    inv_rms = lax.rsqrt(jnp.mean(wide * wide, axis=-1, keepdims=True) + EPS)
    return (wide, inv_rms, (wide * inv_rms * gain_row).astype(jnp.bfloat16))


def place_rows(values, places, slot_total):
    owner_index = (
        jnp.full((slot_total,), values.shape[0], jnp.int32)
        .at[places]
        .set(jnp.arange(values.shape[0], dtype=jnp.int32))
    )
    padded = jnp.concatenate([values, jnp.zeros((1, values.shape[1]), values.dtype)], axis=0)
    return jnp.take(padded, owner_index, axis=0)


def expert_forward(in_rows, weight_in, weight_out, hidden_units):
    projected = jnp.dot(in_rows, weight_in, preferred_element_type=jnp.float32)
    hidden = (jax.nn.silu(projected[:, :hidden_units]) * projected[:, hidden_units:]).astype(
        jnp.bfloat16
    )
    return jnp.dot(hidden, weight_out, preferred_element_type=jnp.float32).astype(jnp.bfloat16)


def expert_backward(in_rows, grad_rows, weight_in, weight_out, hidden_units):
    projected = jnp.dot(in_rows, weight_in, preferred_element_type=jnp.float32)
    gate_pre = projected[:, :hidden_units]
    up_pre = projected[:, hidden_units:]
    d_hidden = lax.dot_general(
        grad_rows, weight_out, (((1,), (1,)), ((), ())), preferred_element_type=jnp.float32
    )
    sigmoid_gate = 1.0 / (1.0 + jnp.exp(-gate_pre))
    d_gate = (d_hidden * up_pre * sigmoid_gate * (1.0 + gate_pre * (1.0 - sigmoid_gate))).astype(
        jnp.bfloat16
    )
    d_up = (d_hidden * gate_pre * sigmoid_gate).astype(jnp.bfloat16)
    d_both = jnp.concatenate([d_gate, d_up], axis=1)
    return lax.dot_general(
        d_both, weight_in, (((1,), (1,)), ((), ())), preferred_element_type=jnp.float32
    ).astype(jnp.bfloat16)


def per_device(
    fwd_prev,
    bwd_prev,
    bwd_saved,
    fwd_routes,
    fwd_gates,
    bwd_routes,
    bwd_gates,
    norm_gain,
    w_in,
    w_out,
):
    expert_count = lax.axis_size("expert")
    tok_rows = fwd_prev.shape[1]
    features = fwd_prev.shape[2]
    top_count = fwd_routes.shape[2]
    hidden_units = w_in.shape[3] // 2
    capacity = 3 * tok_rows * top_count // (2 * expert_count)
    slot_total = expert_count * capacity
    gain_row = norm_gain[0]
    weight_in = w_in[0, 0]
    weight_out = w_out[0, 0]
    layer_in = passed_along(fwd_prev[0], "section", 1)
    grad_in = passed_along(bwd_prev[0], "section", -1)
    layer_wide, inv_fwd, normed_fwd = normalize(layer_in, gain_row)
    f_place = pair_places(fwd_routes[0], expert_count, capacity)
    f_rows = place_rows(jnp.repeat(normed_fwd, top_count, axis=0), f_place, slot_total).reshape(
        expert_count, capacity, features
    )
    saved_wide, inv_bwd, normed_bwd = normalize(bwd_saved[0], gain_row)
    b_place = pair_places(bwd_routes[0], expert_count, capacity)
    b_rows = place_rows(jnp.repeat(normed_bwd, top_count, axis=0), b_place, slot_total).reshape(
        expert_count, capacity, features
    )
    grad_pair = (
        (bwd_gates[0][:, :, None] * grad_in.astype(jnp.float32)[:, None, :])
        .astype(jnp.bfloat16)
        .reshape(tok_rows * top_count, features)
    )
    g_rows = place_rows(grad_pair, b_place, slot_total).reshape(expert_count, capacity, features)
    slot_rows = lax.all_to_all(f_rows, "expert", split_axis=0, concat_axis=0, tiled=True)
    flat_rows = slot_rows.reshape(-1, features)
    out_rows = lax.all_to_all(
        expert_forward(flat_rows, weight_in, weight_out, hidden_units).reshape(slot_rows.shape),
        "expert",
        split_axis=0,
        concat_axis=0,
        tiled=True,
    )
    slot_rows = lax.all_to_all(b_rows, "expert", split_axis=0, concat_axis=0, tiled=True)
    flat_rows = slot_rows.reshape(-1, features)
    flat_grads = lax.all_to_all(g_rows, "expert", split_axis=0, concat_axis=0, tiled=True).reshape(
        -1, features
    )
    d_rows = lax.all_to_all(
        expert_backward(flat_rows, flat_grads, weight_in, weight_out, hidden_units).reshape(
            slot_rows.shape
        ),
        "expert",
        split_axis=0,
        concat_axis=0,
        tiled=True,
    )
    picked = (
        jnp.take(out_rows.reshape(slot_total, features), f_place, axis=0)
        .reshape(tok_rows, top_count, features)
        .astype(jnp.float32)
    )
    fwd_block = (layer_wide + jnp.sum(fwd_gates[0][:, :, None] * picked, axis=1)).astype(
        jnp.bfloat16
    )
    d_picked = (
        jnp.take(d_rows.reshape(slot_total, features), b_place, axis=0)
        .reshape(tok_rows, top_count, features)
        .astype(jnp.float32)
    )
    d_normed = jnp.sum(d_picked, axis=1)
    scaled = d_normed * gain_row
    cubed = inv_bwd * inv_bwd * inv_bwd
    d_input = inv_bwd * scaled - cubed / features * saved_wide * jnp.sum(
        scaled * saved_wide, axis=-1, keepdims=True
    )
    bwd_block = (grad_in.astype(jnp.float32) + d_input).astype(jnp.bfloat16)
    return (fwd_block[None], bwd_block[None])


def solution(mesh):
    in_specs = (
        P("section", "expert", None),
        P("section", "expert", None),
        P("section", "expert", None),
        P("section", "expert", None),
        P("section", "expert", None),
        P("section", "expert", None),
        P("section", "expert", None),
        P("section", None),
        P("section", "expert", None, None),
        P("section", "expert", None, None),
    )
    out_specs = (P("section", "expert", None), P("section", "expert", None))
    return jax.shard_map(
        per_device, mesh=mesh, in_specs=in_specs, out_specs=out_specs, check_vma=False
    )
```

profile of v0, /device:TPU:0, one launch (start us, length us, event | category | flops | bytes accessed | tf_op | source)
XLA Modules:
  0.0 229.5 jit_solution(7323711447612865964)
XLA Ops:
  0.6 4.5 %collective-permute-start.1 = (bf16[128,2048]{1,0:T(8,128)(2,1)}, bf16[128,2048]{1,0:T(8,128)(2,1)}, u32[]{:S(2)}, u32[]{:S(2)}) collective-permute-start(bf16[128,2048]{1,0:T(8,128)(2,1)} %bitcast.103), channel_id=1, source_target_pairs={{0,28},{4,0},{8,4},{12,8},{16,12},{20,16},{24,20},{28,24},{1,29},{... | collective-permute-start | bytes 1572872 | tf_op jit(solution)/shard_map/ppermute | solution.py:12
  5.2 0.7 broadcast_multiply_fusion
  5.9 0.8 copy.23
  6.7 0.1 eq.62
  6.8 0.1 eq.58
  6.9 1.2 fusion.27
  8.2 1.2 fusion.29
  9.4 1.6 broadcast_in_dim.41
  11.0 2.3 reshape.189
  13.3 0.1 copy.27
  13.4 0.1 mul.197
  13.6 1.2 reduce-window.16
  15.2 0.1 copy.28
  15.3 0.1 mul.191
  15.4 2.3 %concatenate.14 = bf16[257,2048]{1,0:T(8,128)(2,1)} pad(bf16[256,2048]{1,0:T(8,128)(2,1)} %reshape.189, bf16[]{:T(256)} %constant.28.clone.1), padding=0_1x0_0 | pad | bytes 2101250 | tf_op jit(solution)/shard_map/concatenate | solution.py:37
  17.8 1.4 scatter_custom_fusion.1
  19.2 6.4 %gather_fusion.3 = bf16[384,2048]{1,0:T(8,128)(2,1)} fusion(bf16[257,2048]{1,0:T(8,128)(2,1)} %concatenate.14, s32[1024]{0:T(1024)S(1)} %pad_clamp_fusion.1), kind=kCustom, calls=%fused_computation.3.clone | custom fusion | bytes 3147264 | tf_op jit(solution)/shard_map/jit(_take)/gather | solution.py:38
  25.7 3.4 %mul.193 = f32[128,2,2048]{2,1,0:T(2,128)} broadcast(bf16[128,2048]{1,0:T(8,128)(2,1)} %collective-permute-done.1), dimensions={0,2} | broadcast | bytes 2621440 | tf_op jit(solution)/shard_map/mul | solution.py:102
  29.1 3.7 %mul.194 = f32[256,2048]{1,0:T(8,128)} reshape(f32[128,2,2048]{2,1,0:T(2,128)} %mul.193) | data formatting | bytes 4194304 | tf_op jit(solution)/shard_map/mul | solution.py:102
  32.8 1.8 multiply_convert_fusion
  34.5 1.1 concatenate.13
  35.6 6.4 %gather_fusion.2 = bf16[384,2048]{1,0:T(8,128)(2,1)} fusion(bf16[257,2048]{1,0:T(8,128)(2,1)} %concatenate.13, s32[1024]{0:T(1024)S(1)} %pad_clamp_fusion.1), kind=kCustom, calls=%fused_computation.2.clone | custom fusion | bytes 3147264 | tf_op jit(solution)/shard_map/jit(_take)/gather | solution.py:38
  42.0 3.8 %broadcast_select_fusion = (bf16[384,2048]{1,0:T(8,128)(2,1)}, bf16[384,2048]{1,0:T(8,128)(2,1)}) fusion(bf16[384,2048]{1,0:T(8,128)(2,1)} %gather_fusion.3, pred[384]{0:T(512)(128)(4,1)S(1)} %compare_and_fusion.1, bf16[384,2048]{1,0:T(8,128)(2,1)} %gather_fusion.2), kind=kLoop, calls=%fused_computation.28 | loop fusion | flops 1572864 | bytes 6291840 | tf_op jit(solution)/shard_map/jit(_take)/select_n | solution.py:38
  45.9 4.5 %all-to-all-start.3 = ((bf16[4,96,2048]{2,1,0:T(8,128)(2,1)}), bf16[4,96,2048]{2,1,0:T(8,128)(2,1)}, u32[]{:S(2)}, u32[]{:S(2)}) async-start(bf16[4,96,2048]{2,1,0:T(8,128)(2,1)} %bitcast.88), calls=%async_computation.3 | async-start | bytes 3145728 | tf_op jit(solution)/shard_map/all_to_all | solution.py:116
  50.4 0.1 copy.18
  50.6 0.1 eq.54
  50.7 1.2 reduce-window.14
  52.0 0.1 copy.20
  52.3 15.2 %all-to-all-done.3 = bf16[4,96,2048]{2,1,0:T(8,128)(2,1)} async-done(((bf16[4,96,2048]{2,1,0:T(8,128)(2,1)}), bf16[4,96,2048]{2,1,0:T(8,128)(2,1)}, u32[]{:S(2)}, u32[]{:S(2)}) %all-to-all-start.3) | async-done | bytes 1572896 | tf_op jit(solution)/shard_map/all_to_all | solution.py:116
  67.6 4.3 %all-to-all-start.2 = ((bf16[4,96,2048]{2,1,0:T(8,128)(2,1)}), bf16[4,96,2048]{2,1,0:T(8,128)(2,1)}, u32[]{:S(2)}, u32[]{:S(2)}) async-start(bf16[4,96,2048]{2,1,0:T(8,128)(2,1)} %bitcast.87), calls=%async_computation.2 | async-start | bytes 3145728 | tf_op jit(solution)/shard_map/all_to_all | solution.py:118
  71.9 0.1 eq.50
  72.1 0.1 copy.22
  72.2 0.1 mul.183
  72.4 1.6 scatter_custom_fusion
  73.9 7.3 %fusion.2 = f32[384,1536]{1,0:T(8,128)} fusion(bf16[384,2048]{1,0:T(8,128)(2,1)} %bitcast.24, bf16[1,1,2048,1536]{3,2,1,0:T(8,128)(2,1)} %param.22), kind=kOutput, calls=%fused_computation.9 | convolution fusion | flops 2415919104 | bytes 10223616 | tf_op jit(solution)/shard_map/dot_general | solution.py:50
  81.2 9.5 %all-to-all-done.2 = bf16[4,96,2048]{2,1,0:T(8,128)(2,1)} async-done(((bf16[4,96,2048]{2,1,0:T(8,128)(2,1)}), bf16[4,96,2048]{2,1,0:T(8,128)(2,1)}, u32[]{:S(2)}, u32[]{:S(2)}) %all-to-all-start.2) | async-done | bytes 1572896 | tf_op jit(solution)/shard_map/all_to_all | solution.py:118
  90.7 3.8 %fusion.18 = (bf16[384,768]{1,0:T(8,128)(2,1)S(1)}, bf16[384,768]{1,0:T(8,128)(2,1)S(1)}) fusion(f32[384,1536]{1,0:T(8,128)} %fusion.2, bf16[384,2048]{1,0:T(8,128)(2,1)} %bitcast.21, bf16[1,1,768,2048]{3,2,1,0:T(8,128)(2,1)S(1)} %copy-done), kind=kOutput, calls=%fused_computation.34 | convolution fusion | flops 1211793408 | bytes 8257536 | tf_op jit(solution)/shard_map/dot_general | solution.py:53
  94.5 8.1 %fusion.13 = bf16[384,2048]{1,0:T(8,128)(2,1)} fusion(bf16[1,1,2048,1536]{3,2,1,0:T(8,128)(2,1)} %param.22, bf16[384,768]{1,0:T(8,128)(2,1)S(1)} %get-tuple-element.9, bf16[384,768]{1,0:T(8,128)(2,1)S(1)} %get-tuple-element.8), kind=kOutput, calls=%fused_computation.18 | convolution fusion | flops 2419064832 | bytes 9043968 | tf_op jit(solution)/shard_map/dot_general | solution.py:62
  102.5 4.3 %all-to-all-start.4 = ((bf16[4,96,2048]{2,1,0:T(8,128)(2,1)}), bf16[4,96,2048]{2,1,0:T(8,128)(2,1)}, u32[]{:S(2)}, u32[]{:S(2)}) async-start(bf16[4,96,2048]{2,1,0:T(8,128)(2,1)} %bitcast.90), calls=%async_computation.4 | async-start | bytes 3145728 | tf_op jit(solution)/shard_map/all_to_all | solution.py:121
  107.0 1.2 fusion.23
  108.2 17.5 %all-to-all-done.4 = bf16[4,96,2048]{2,1,0:T(8,128)(2,1)} async-done(((bf16[4,96,2048]{2,1,0:T(8,128)(2,1)}), bf16[4,96,2048]{2,1,0:T(8,128)(2,1)}, u32[]{:S(2)}, u32[]{:S(2)}) %all-to-all-start.4) | async-done | bytes 1572896 | tf_op jit(solution)/shard_map/all_to_all | solution.py:121
  125.7 5.0 %gather_fusion.4 = bf16[256,2048]{1,0:T(8,128)(2,1)} fusion(bf16[384,2048]{1,0:T(8,128)(2,1)} %bitcast.26, s32[1024]{0:T(1024)S(1)} %pad_clamp_fusion), kind=kCustom, calls=%fused_computation.4.clone | custom fusion | bytes 2098176 | tf_op jit(solution)/shard_map/jit(_take)/gather | solution.py:139
  130.6 2.8 %select_convert_fusion = f32[256,2048]{1,0:T(8,128)} fusion(bf16[256,2048]{1,0:T(8,128)(2,1)} %gather_fusion.4, pred[256]{0:T(512)(128)(4,1)S(1)} %get-tuple-element.4), kind=kLoop, calls=%fused_computation.54 | loop fusion | flops 1048576 | bytes 3145984 | tf_op jit(solution)/shard_map/convert_element_type | solution.py:141
  133.4 3.5 %reshape.196 = f32[128,2,2048]{2,1,0:T(2,128)} reshape(f32[256,2048]{1,0:T(8,128)} %select_convert_fusion) | data formatting | bytes 4194304 | tf_op jit(solution)/shard_map/convert_element_type | solution.py:141
  136.9 5.2 %reduce_sum.74 = f32[128,2048]{1,0:T(8,128)} reduce(f32[128,2,2048]{2,1,0:T(2,128)} %reshape.196, f32[]{:T(128)} %constant.17.clone.1), dimensions={1}, to_apply=%region_11.14 | reduce | flops 262144 | bytes 3145732 | tf_op jit(solution)/shard_map/reduce_sum | solution.py:143
  142.0 1.7 fusion.34
  143.7 0.1 copy-done.2
  143.9 2.5 %fusion.37 = (bf16[1,128,2048]{2,1,0:T(8,128)(2,1)}, bf16[128,2048]{1,0:T(8,128)(2,1)S(1)}) fusion(f32[128,2048]{1,0:T(8,128)S(1)} %copy-done.1, bf16[1,128,2048]{2,1,0:T(8,128)(2,1)S(1)} %copy-done.2, f32[128]{0:T(128)S(1)} %fusion.34, f32[128]{0:T(128)S(1)} %get-tuple-element.12, f32[128]{0:T(128)S(1)} %get-tuple-element.13, f32[2048]{0:T(1024)S(1)} %bitcast.95, ...), kind=kLoop, calls=%fused_computation.57 | loop fusion | flops 3407872 | bytes 3680256 | tf_op jit(solution)/shard_map/broadcast_in_dim | solution.py:150
  146.3 1.7 broadcast_in_dim.39
  148.0 2.3 reshape.180
  150.2 2.4 %concatenate.12 = bf16[257,2048]{1,0:T(8,128)(2,1)} pad(bf16[256,2048]{1,0:T(8,128)(2,1)} %reshape.180, bf16[]{:T(256)} %constant.28.clone.1), padding=0_1x0_0 | pad | bytes 2101250 | tf_op jit(solution)/shard_map/concatenate | solution.py:37
  152.6 6.4 %gather_fusion = bf16[384,2048]{1,0:T(8,128)(2,1)} fusion(bf16[257,2048]{1,0:T(8,128)(2,1)} %concatenate.12, s32[1024]{0:T(1024)S(1)} %pad_clamp_fusion.3), kind=kCustom, calls=%fused_computation.clone | custom fusion | bytes 3147264 | tf_op jit(solution)/shard_map/jit(_take)/gather | solution.py:38
  159.0 1.6 broadcast_select_fusion.2
  160.6 21.7 %all_to_all.25 = bf16[4,96,2048]{2,1,0:T(8,128)(2,1)S(1)} all-to-all(bf16[4,96,2048]{2,1,0:T(8,128)(2,1)S(1)} %bitcast.89), channel_id=1, replica_groups=mesh['section'=8,'expert'=4] {'expert'}, dimensions={0} | all-to-all | bytes 3145728 | tf_op jit(solution)/shard_map/all_to_all | solution.py:107
  182.3 4.7 %fusion.4 = f32[384,1536]{1,0:T(8,128)S(1)} fusion(bf16[384,2048]{1,0:T(8,128)(2,1)S(1)} %bitcast.92, bf16[1,1,2048,1536]{3,2,1,0:T(8,128)(2,1)} %param.22), kind=kOutput, calls=%fused_computation.11 | convolution fusion | flops 2415919104 | bytes 10223616 | tf_op jit(solution)/shard_map/dot_general | solution.py:42
  187.0 2.6 %fusion.10 = bf16[384,2048]{1,0:T(8,128)(2,1)} fusion(bf16[1,1,768,2048]{3,2,1,0:T(8,128)(2,1)S(1)} %copy-done, f32[384,1536]{1,0:T(8,128)S(1)} %fusion.4), kind=kOutput, calls=%fused_computation.17 | convolution fusion | flops 1210515456 | bytes 7077888 | tf_op jit(solution)/shard_map/dot_general | solution.py:46
  189.7 4.5 %all-to-all-start.1 = ((bf16[4,96,2048]{2,1,0:T(8,128)(2,1)}), bf16[4,96,2048]{2,1,0:T(8,128)(2,1)}, u32[]{:S(2)}, u32[]{:S(2)}) async-start(bf16[4,96,2048]{2,1,0:T(8,128)(2,1)} %bitcast.91), calls=%async_computation.1 | async-start | bytes 3145728 | tf_op jit(solution)/shard_map/all_to_all | solution.py:109
  194.1 0.1 copy.17
  194.3 17.2 %all-to-all-done.1 = bf16[4,96,2048]{2,1,0:T(8,128)(2,1)} async-done(((bf16[4,96,2048]{2,1,0:T(8,128)(2,1)}), bf16[4,96,2048]{2,1,0:T(8,128)(2,1)}, u32[]{:S(2)}, u32[]{:S(2)}) %all-to-all-start.1) | async-done | bytes 1572896 | tf_op jit(solution)/shard_map/all_to_all | solution.py:109
  211.5 5.0 %gather_fusion.1 = bf16[256,2048]{1,0:T(8,128)(2,1)} fusion(bf16[384,2048]{1,0:T(8,128)(2,1)} %bitcast.12, s32[1024]{0:T(1024)S(1)} %pad_clamp_fusion.2), kind=kCustom, calls=%fused_computation.1.clone | custom fusion | bytes 2098176 | tf_op jit(solution)/shard_map/jit(_take)/gather | solution.py:131
  216.5 2.8 %select_convert_fusion.1 = f32[256,2048]{1,0:T(8,128)} fusion(bf16[256,2048]{1,0:T(8,128)(2,1)} %gather_fusion.1, pred[256]{0:T(512)(128)(4,1)S(1)} %get-tuple-element.6), kind=kLoop, calls=%fused_computation.55 | loop fusion | flops 1048576 | bytes 3145984 | tf_op jit(solution)/shard_map/convert_element_type | solution.py:133
  219.3 3.5 %reshape.194 = f32[128,2,2048]{2,1,0:T(2,128)} reshape(f32[256,2048]{1,0:T(8,128)} %select_convert_fusion.1) | data formatting | bytes 4194304 | tf_op jit(solution)/shard_map/convert_element_type | solution.py:133
  222.7 4.8 %multiply_reduce_fusion = f32[128,2048]{1,0:T(8,128)S(1)} fusion(f32[128,2,2048]{2,1,0:T(2,128)} %reshape.194, f32[128,2]{1,0:T(8,128)S(1)} %copy.17), kind=kLoop, calls=%fused_computation.20 | loop fusion | flops 786432 | bytes 3146752 | tf_op jit(solution)/shard_map/reduce_sum | solution.py:135
  227.5 2.0 fusion.38
  (48 shorter events, 0.9 us)
Async XLA Ops:
  0.6 90.1 %copy-start = (bf16[1,1,768,2048]{3,2,1,0:T(8,128)(2,1)S(1)}, bf16[1,1,768,2048]{3,2,1,0:T(8,128)(2,1)}, u32[]{:S(2)}) copy-start(bf16[1,1,768,2048]{3,2,1,0:T(8,128)(2,1)} %param.23) | copy-start | bytes 9437188
  0.6 25.0 %collective-permute-start.1 = (bf16[128,2048]{1,0:T(8,128)(2,1)}, bf16[128,2048]{1,0:T(8,128)(2,1)}, u32[]{:S(2)}, u32[]{:S(2)}) collective-permute-start(bf16[128,2048]{1,0:T(8,128)(2,1)} %bitcast.103), channel_id=1, source_target_pairs={{0,28},{4,0},{8,4},{12,8},{16,12},{20,16},{24,20},{28,24},{1,29},{... | collective-permute-start | bytes 1572872 | tf_op jit(solution)/shard_map/ppermute | solution.py:12
  9.4 5.8 %copy-start.5 = (f32[1,128,2]{1,2,0:T(2,128)S(1)}, f32[1,128,2]{1,2,0:T(2,128)}, u32[]{:S(2)}) copy-start(f32[1,128,2]{1,2,0:T(2,128)} %param.20) | copy-start | bytes 3076
  45.9 4.6 %copy-start.4 = (s32[1,128,2]{1,2,0:T(2,128)S(1)}, s32[1,128,2]{1,2,0:T(2,128)}, u32[]{:S(2)}) copy-start(s32[1,128,2]{1,2,0:T(2,128)} %param.17) | copy-start | bytes 3076
  45.9 21.7 %all-to-all-start.3 = ((bf16[4,96,2048]{2,1,0:T(8,128)(2,1)}), bf16[4,96,2048]{2,1,0:T(8,128)(2,1)}, u32[]{:S(2)}, u32[]{:S(2)}) async-start(bf16[4,96,2048]{2,1,0:T(8,128)(2,1)} %bitcast.88), calls=%async_computation.3 | async-start | bytes 3145728 | tf_op jit(solution)/shard_map/all_to_all | solution.py:116
  50.4 56.6 %collective-permute-start = (bf16[128,2048]{1,0:T(8,128)(2,1)}, bf16[128,2048]{1,0:T(8,128)(2,1)}, u32[]{:S(2)}, u32[]{:S(2)}) collective-permute-start(bf16[128,2048]{1,0:T(8,128)(2,1)} %bitcast.104), channel_id=1, source_target_pairs={{0,4},{4,8},{8,12},{12,16},{16,20},{20,24},{24,28},{28,0},{1,5},{5... | collective-permute-start | bytes 1572872 | tf_op jit(solution)/shard_map/ppermute | solution.py:12
  67.6 23.1 %all-to-all-start.2 = ((bf16[4,96,2048]{2,1,0:T(8,128)(2,1)}), bf16[4,96,2048]{2,1,0:T(8,128)(2,1)}, u32[]{:S(2)}, u32[]{:S(2)}) async-start(bf16[4,96,2048]{2,1,0:T(8,128)(2,1)} %bitcast.87), calls=%async_computation.2 | async-start | bytes 3145728 | tf_op jit(solution)/shard_map/all_to_all | solution.py:118
  102.5 23.1 %all-to-all-start.4 = ((bf16[4,96,2048]{2,1,0:T(8,128)(2,1)}), bf16[4,96,2048]{2,1,0:T(8,128)(2,1)}, u32[]{:S(2)}, u32[]{:S(2)}) async-start(bf16[4,96,2048]{2,1,0:T(8,128)(2,1)} %bitcast.90), calls=%async_computation.4 | async-start | bytes 3145728 | tf_op jit(solution)/shard_map/all_to_all | solution.py:121
  136.8 5.2 %copy-start.3 = (f32[1,2048]{1,0:T(1,128)S(1)}, f32[1,2048]{1,0:T(1,128)}, u32[]{:S(2)}) copy-start(f32[1,2048]{1,0:T(1,128)} %param.21) | copy-start | bytes 24580
  142.0 1.7 copy-start.1
  142.0 1.8 copy-start.2
  189.7 4.5 %copy-start.6 = (f32[1,128,2]{1,2,0:T(2,128)S(1)}, f32[1,128,2]{1,2,0:T(2,128)}, u32[]{:S(2)}) copy-start(f32[1,128,2]{1,2,0:T(2,128)} %param.18) | copy-start | bytes 3076
  189.7 21.9 %all-to-all-start.1 = ((bf16[4,96,2048]{2,1,0:T(8,128)(2,1)}), bf16[4,96,2048]{2,1,0:T(8,128)(2,1)}, u32[]{:S(2)}, u32[]{:S(2)}) async-start(bf16[4,96,2048]{2,1,0:T(8,128)(2,1)} %bitcast.91), calls=%async_computation.1 | async-start | bytes 3145728 | tf_op jit(solution)/shard_map/all_to_all | solution.py:109
where the time goes:
time: 231 us; the launch traced here: 230 us
  local copies, waits for them, and re-layouts  62.7 us (27%)
  waiting for transfers between devices  59.4 us (26%)
  other arithmetic  36.1 us (16%)
  matrix products  26.4 us (11%)
  starting transfers between devices  22.2 us (10%)
  blocking collectives  21.7 us (9%)
    all_to_all x1, blocking collectives, per_device(): lax.all_to_all(f_rows, 'expert', split_axis=0, concat_axis=0, tiled=True)  21.7 us
    gather x3, local copies, waits for them, and re-layouts, place_rows(): return jnp.take(padded, owner_index, axis=0)  19.3 us
    all_to_all x1, waiting for transfers between devices, per_device(): lax.all_to_all(expert_backward(flat_rows, flat_grads, weight_in, weight_o...  17.5 us
    all_to_all x1, waiting for transfers between devices, per_device(): lax.all_to_all(expert_forward(flat_rows, weight_in, weight_out, hidden_un...  17.2 us
    all_to_all x1, waiting for transfers between devices, per_device(): lax.all_to_all(b_rows, 'expert', split_axis=0, concat_axis=0, tiled=True)  15.2 us
    all_to_all x1, waiting for transfers between devices, per_device(): lax.all_to_all(g_rows, 'expert', split_axis=0, concat_axis=0, tiled=True)  9.49 us
    dot_general x1, matrix products, expert_backward(): lax.dot_general(d_both, weight_in, (((1,), (1,)), ((), ())), preferred_el...  8.08 us
    dot_general x1, matrix products, expert_backward(): projected = jnp.dot(in_rows, weight_in, preferred_element_type=jnp.float32)  7.26 us
  transfers between devices with their start and end apart: 6, of which 4 were waited for; matrix products, arithmetic and copies ran while one was open for 20% of the time, Pallas kernels for 0%

commit v1 on v0

v1 whole, which is shorter than its diff:
```python
import functools

import jax
import jax.numpy as jnp
from jax import lax
from jax.experimental import pallas as pl
from jax.experimental.pallas import tpu as pltpu
from jax.sharding import PartitionSpec as P

EPS = 1e-06
VMEM_LIMIT = 48 * 1024 * 1024


def passed_along(value, axis, steps):
    count = lax.axis_size(axis)
    pairs = [(source, (source + steps) % count) for source in range(count)]
    return lax.ppermute(value, axis, pairs)


def swapped(value, axis, offset):
    count = lax.axis_size(axis)
    pairs = [(source, source ^ offset) for source in range(count)]
    return lax.ppermute(value, axis, pairs)


def exchanged(blocks, axis):
    return [blocks[0]] + [swapped(blocks[d], axis, d) for d in range(1, len(blocks))]


def slot_table(routes, expert_count):
    top_count, tok_rows = routes.shape
    experts = max(8, expert_count)
    wanted = lax.broadcasted_iota(jnp.int32, (experts, tok_rows), 0)
    member = routes[0:1, :] == wanted
    for k in range(1, top_count):
        member = jnp.logical_or(member, routes[k : k + 1, :] == wanted)
    before = lax.broadcasted_iota(jnp.int32, (tok_rows, tok_rows), 0) < lax.broadcasted_iota(
        jnp.int32, (tok_rows, tok_rows), 1
    )
    slots = jnp.dot(
        member.astype(jnp.bfloat16),
        before.astype(jnp.bfloat16),
        preferred_element_type=jnp.float32,
    )
    return jnp.where(member, slots, -1.0)


def placement(slots, expert, capacity):
    tok_rows = slots.shape[1]
    row = lax.broadcasted_iota(jnp.int32, (capacity, tok_rows), 0).astype(jnp.float32)
    return slots[expert : expert + 1, :] == row


def gate_row(routes, gates, expert):
    total = jnp.zeros((1, routes.shape[1]), jnp.float32)
    for k in range(routes.shape[0]):
        total = total + jnp.where(routes[k : k + 1, :] == expert, gates[k : k + 1, :], 0.0)
    return total


def halves(weights):
    high = weights.astype(jnp.bfloat16)
    low = (weights - high.astype(jnp.float32)).astype(jnp.bfloat16)
    return high, low


def normed_kernel(values_ref, routes_ref, gain_ref, *out_refs):
    expert_count = len(out_refs)
    capacity = out_refs[0].shape[0]
    wide = values_ref[...].astype(jnp.float32)
    inv_rms = lax.rsqrt(jnp.mean(wide * wide, axis=-1, keepdims=True) + EPS)
    normed = (wide * inv_rms * gain_ref[...]).astype(jnp.bfloat16)
    slots = slot_table(routes_ref[...], expert_count)
    for e in range(expert_count):
        place = placement(slots, e, capacity).astype(jnp.bfloat16)
        out_refs[e][...] = jnp.dot(place, normed, preferred_element_type=jnp.float32).astype(
            jnp.bfloat16
        )


def grads_kernel(grads_ref, routes_ref, gates_ref, *out_refs):
    expert_count = len(out_refs)
    capacity = out_refs[0].shape[0]
    grads = grads_ref[...]
    routes = routes_ref[...]
    slots = slot_table(routes, expert_count)
    for e in range(expert_count):
        place = placement(slots, e, capacity)
        high, low = halves(jnp.where(place, gate_row(routes, gates_ref[...], e), 0.0))
        out_refs[e][...] = (
            jnp.dot(high, grads, preferred_element_type=jnp.float32)
            + jnp.dot(low, grads, preferred_element_type=jnp.float32)
        ).astype(jnp.bfloat16)


def rows_dot(weights, rows):
    return lax.dot_general(
        weights, rows, (((0,), (0,)), ((), ())), preferred_element_type=jnp.float32
    )


def fwd_end_kernel(layer_ref, routes_ref, gates_ref, *refs):
    row_refs, out_ref = refs[:-1], refs[-1]
    expert_count = len(row_refs)
    capacity = row_refs[0].shape[0]
    routes = routes_ref[...]
    slots = slot_table(routes, expert_count)
    total = layer_ref[...].astype(jnp.float32)
    for e in range(expert_count):
        place = placement(slots, e, capacity)
        high, low = halves(jnp.where(place, gate_row(routes, gates_ref[...], e), 0.0))
        rows = row_refs[e][...]
        total = total + (rows_dot(high, rows) + rows_dot(low, rows))
    out_ref[...] = total.astype(jnp.bfloat16)


def bwd_end_kernel(grads_ref, saved_ref, gain_ref, routes_ref, *refs):
    row_refs, out_ref = refs[:-1], refs[-1]
    expert_count = len(row_refs)
    capacity = row_refs[0].shape[0]
    features = saved_ref.shape[1]
    slots = slot_table(routes_ref[...], expert_count)
    d_normed = None
    for e in range(expert_count):
        place = placement(slots, e, capacity).astype(jnp.bfloat16)
        part = rows_dot(place, row_refs[e][...])
        d_normed = part if d_normed is None else d_normed + part
    wide = saved_ref[...].astype(jnp.float32)
    inv_rms = lax.rsqrt(jnp.mean(wide * wide, axis=-1, keepdims=True) + EPS)
    scaled = d_normed * gain_ref[...]
    cubed = inv_rms * inv_rms * inv_rms
    inner = jnp.sum(scaled * wide, axis=-1, keepdims=True)
    out_ref[...] = (
        grads_ref[...].astype(jnp.float32) + inv_rms * scaled - cubed / features * wide * inner
    ).astype(jnp.bfloat16)


def local_call(kernel, out_shapes, flops, moved):
    return pl.pallas_call(
        kernel,
        out_shape=out_shapes,
        compiler_params=pltpu.CompilerParams(vmem_limit_bytes=VMEM_LIMIT),
        cost_estimate=pl.CostEstimate(flops=flops, bytes_accessed=moved, transcendentals=0),
    )


def expert_forward(in_rows, weight_in, weight_out, hidden_units):
    projected = jnp.dot(in_rows, weight_in, preferred_element_type=jnp.float32)
    hidden = (jax.nn.silu(projected[:, :hidden_units]) * projected[:, hidden_units:]).astype(
        jnp.bfloat16
    )
    return jnp.dot(hidden, weight_out, preferred_element_type=jnp.float32).astype(jnp.bfloat16)


def expert_backward(in_rows, grad_rows, weight_in, weight_out, hidden_units):
    projected = jnp.dot(in_rows, weight_in, preferred_element_type=jnp.float32)
    gate_pre = projected[:, :hidden_units]
    up_pre = projected[:, hidden_units:]
    d_hidden = lax.dot_general(
        grad_rows, weight_out, (((1,), (1,)), ((), ())), preferred_element_type=jnp.float32
    )
    sigmoid_gate = 1.0 / (1.0 + jnp.exp(-gate_pre))
    d_gate = (d_hidden * up_pre * sigmoid_gate * (1.0 + gate_pre * (1.0 - sigmoid_gate))).astype(
        jnp.bfloat16
    )
    d_up = (d_hidden * gate_pre * sigmoid_gate).astype(jnp.bfloat16)
    d_both = jnp.concatenate([d_gate, d_up], axis=1)
    return lax.dot_general(
        d_both, weight_in, (((1,), (1,)), ((), ())), preferred_element_type=jnp.float32
    ).astype(jnp.bfloat16)


def per_device(
    fwd_prev,
    bwd_prev,
    bwd_saved,
    fwd_routes,
    fwd_gates,
    bwd_routes,
    bwd_gates,
    norm_gain,
    w_in,
    w_out,
):
    expert_count = lax.axis_size("expert")
    tok_rows = fwd_prev.shape[1]
    features = fwd_prev.shape[2]
    top_count = fwd_routes.shape[2]
    hidden_units = w_in.shape[3] // 2
    capacity = 3 * tok_rows * top_count // (2 * expert_count)
    gain_row = norm_gain
    weight_in = w_in[0, 0]
    weight_out = w_out[0, 0]
    me = lax.axis_index("expert")
    f_routes = (fwd_routes[0] ^ me).T
    b_routes = (bwd_routes[0] ^ me).T
    f_gates = fwd_gates[0].T
    b_gates = bwd_gates[0].T
    saved = bwd_saved[0]
    layer_in = passed_along(fwd_prev[0], "section", 1)
    grad_in = passed_along(bwd_prev[0], "section", -1)

    block = jax.ShapeDtypeStruct((capacity, features), jnp.bfloat16)
    whole = jax.ShapeDtypeStruct((tok_rows, features), jnp.bfloat16)
    one_dot = 2 * expert_count * capacity * tok_rows * features
    moved = 2 * features * (tok_rows + expert_count * capacity)
    normed_call = local_call(normed_kernel, [block] * expert_count, one_dot, moved)
    grads_call = local_call(grads_kernel, [block] * expert_count, 2 * one_dot, moved)
    fwd_end = local_call(fwd_end_kernel, whole, 2 * one_dot, moved)
    bwd_end = local_call(bwd_end_kernel, whole, one_dot, moved)

    b_rows = exchanged(normed_call(saved, b_routes, gain_row), "expert")
    f_rows = exchanged(normed_call(layer_in, f_routes, gain_row), "expert")
    g_rows = exchanged(grads_call(grad_in, b_routes, b_gates), "expert")

    def cut(rows):
        return [rows[d * capacity : (d + 1) * capacity] for d in range(expert_count)]

    f_done = expert_forward(jnp.concatenate(f_rows), weight_in, weight_out, hidden_units)
    f_back = exchanged(cut(f_done), "expert")
    b_done = expert_backward(
        jnp.concatenate(b_rows), jnp.concatenate(g_rows), weight_in, weight_out, hidden_units
    )
    b_back = exchanged(cut(b_done), "expert")
    fwd_block = fwd_end(layer_in, f_routes, f_gates, *f_back)
    bwd_block = bwd_end(grad_in, saved, gain_row, b_routes, *b_back)
    return (fwd_block[None], bwd_block[None])


def solution(mesh):
    in_specs = (
        P("section", "expert", None),
        P("section", "expert", None),
        P("section", "expert", None),
        P("section", "expert", None),
        P("section", "expert", None),
        P("section", "expert", None),
        P("section", "expert", None),
        P("section", None),
        P("section", "expert", None, None),
        P("section", "expert", None, None),
    )
    out_specs = (P("section", "expert", None), P("section", "expert", None))
    return jax.shard_map(
        per_device, mesh=mesh, in_specs=in_specs, out_specs=out_specs, check_vma=False
    )
```

time: 231 us -> 98.1 us (0.42)
  local copies, waits for them, and re-layouts: 62.7 us -> 2.74 us
  other arithmetic: 36.1 us -> 1.36 us
  blocking collectives: 21.7 us -> 0 us
  waiting for transfers between devices: 59.4 us -> 39 us
  matrix products: 26.4 us -> 17 us
  Pallas kernels: 0 us -> 8.86 us
  starting transfers between devices: 22.2 us -> 26.6 us
    all_to_all x4 -> x0, waiting for transfers between devices: 59.4 us -> none  [the longest x1 17.5 us: per_device(): lax.all_to_all(expert_backward(flat_rows, flat_grads, weight_in, weight_o...]
    ppermute x0 -> x15, waiting for transfers between devices: none -> 38.8 us  [swapped(): return lax.ppermute(value, axis, pairs)]
    gather x5 -> x0, local copies, waits for them, and re-layouts: 29.2 us -> none  [the longest x3 19.3 us: place_rows(): return jnp.take(padded, owner_index, axis=0)]
    ppermute x0 -> x15, starting transfers between devices: none -> 22.1 us  [swapped(): return lax.ppermute(value, axis, pairs)]
    all_to_all x1 -> x0, blocking collectives: 21.7 us -> none  [per_device(): lax.all_to_all(f_rows, 'expert', split_axis=0, concat_axis=0, tiled=True)]
    all_to_all x4 -> x0, starting transfers between devices: 17.6 us -> none  [the longest x1 4.48 us: per_device(): lax.all_to_all(b_rows, 'expert', split_axis=0, concat_axis=0, tiled=True)]
    reduce_sum x7 -> x0, other arithmetic: 14.2 us -> none  [the longest x1 5.17 us: per_device(): d_normed = jnp.sum(d_picked, axis=1)]
    pallas_call x0 -> x5, Pallas kernels: none -> 8.86 us  [the longest x1 2.97 us: per_device(): bwd_block = bwd_end(grad_in, saved, gain_row, b_routes, *b_back)]
  transfers between devices with their start and end apart: 6 -> 17, of which waited for: 4 -> 9; matrix products, arithmetic and copies ran while one was open for 20% -> 19% of each run, Pallas kernels for 0% -> 7%
where the time goes in v1:
time: 98.1 us; the launch traced here: 96.4 us
  waiting for transfers between devices  39 us (40%)
  starting transfers between devices  26.6 us (27%)
  matrix products  17 us (17%)
  Pallas kernels  8.86 us (9%)
  local copies, waits for them, and re-layouts  2.74 us (3%)
  other arithmetic  1.36 us (1%)
    ppermute x15, waiting for transfers between devices, swapped(): return lax.ppermute(value, axis, pairs)  38.8 us
    ppermute x15, starting transfers between devices, swapped(): return lax.ppermute(value, axis, pairs)  22.1 us
    dot_general x1, matrix products, expert_backward(): projected = jnp.dot(in_rows, weight_in, preferred_element_type=jnp.float32)  6.82 us
    ppermute x2, starting transfers between devices, passed_along(): return lax.ppermute(value, axis, pairs)  4.54 us
    dot_general x1, matrix products, expert_backward(): lax.dot_general(grad_rows, weight_out, (((1,), (1,)), ((), ())), preferre...  3.45 us
    pallas_call x1, Pallas kernels, per_device(): bwd_block = bwd_end(grad_in, saved, gain_row, b_routes, *b_back)  2.97 us
    dot_general x1, matrix products, expert_forward(): projected = jnp.dot(in_rows, weight_in, preferred_element_type=jnp.float32)  2.64 us
    dot_general x1, matrix products, expert_backward(): lax.dot_general(d_both, weight_in, (((1,), (1,)), ((), ())), preferred_el...  2.62 us
  transfers between devices with their start and end apart: 17, of which 9 were waited for; matrix products, arithmetic and copies ran while one was open for 19% of the time, Pallas kernels for 7%

profile of v1, /device:TPU:0, one launch (start us, length us, event | category | flops | bytes accessed | tf_op | source)
XLA Modules:
  0.0 96.4 jit_solution(17460806697380654483)
XLA Ops:
  0.6 0.0 copy-start
  0.6 4.5 %collective-permute-start.7 = (bf16[128,2048]{1,0:T(8,128)(2,1)}, bf16[128,2048]{1,0:T(8,128)(2,1)}, u32[]{:S(2)}, u32[]{:S(2)}) collective-permute-start(bf16[128,2048]{1,0:T(8,128)(2,1)} %bitcast.47), channel_id=1, source_target_pairs={{0,28},{4,0},{8,4},{12,8},{16,12},{20,16},{24,20},{28,24},{1,29},{... | collective-permute-start | bytes 1572872 | tf_op jit(solution)/shard_map/ppermute | solution.py:17
  5.2 0.7 xor_bitcast_fusion.routes_ref
  5.9 0.0 copy-start.1
  5.9 1.0 %copy-done.1 = bf16[1,128,2048]{2,1,0:T(8,128)(2,1)S(1)} copy-done((bf16[1,128,2048]{2,1,0:T(8,128)(2,1)S(1)}, bf16[1,128,2048]{2,1,0:T(8,128)(2,1)}, u32[]{:S(2)}) %copy-start.1) | copy-done | bytes 524312
  6.9 0.0 copy-start.3
  6.9 0.7 copy-done.3
  7.6 0.8 shard_map.116
  8.4 1.6 %collective-permute-start.11 = (bf16[96,2048]{1,0:T(8,128)(2,1)S(1)}, bf16[96,2048]{1,0:T(8,128)(2,1)S(1)}, u32[]{:S(2)}, u32[]{:S(2)}) collective-permute-start(bf16[96,2048]{1,0:T(8,128)(2,1)S(1)} %get-tuple-element.23), channel_id=1, source_target_pairs={{0,1},{1,0},{2,3},{3,2},{4,5},{5,4},{6,7},{7,6},{8,9},{9,8},{10,11... | collective-permute-start | bytes 1179656 | tf_op jit(solution)/shard_map/ppermute | solution.py:23
  9.9 1.5 %collective-permute-start.12 = (bf16[96,2048]{1,0:T(8,128)(2,1)S(1)}, bf16[96,2048]{1,0:T(8,128)(2,1)S(1)}, u32[]{:S(2)}, u32[]{:S(2)}) collective-permute-start(bf16[96,2048]{1,0:T(8,128)(2,1)S(1)} %get-tuple-element.24), channel_id=1, source_target_pairs={{0,2},{1,3},{2,0},{3,1},{4,6},{5,7},{6,4},{7,5},{8,10},{9,11},{10,... | collective-permute-start | bytes 1179656 | tf_op jit(solution)/shard_map/ppermute | solution.py:23
  11.4 0.5 collective-permute-start.13
  11.9 0.0 collective-permute-start
  11.9 0.7 xor_bitcast_fusion.1.routes_ref
  12.6 0.2 collective-permute-done.7.grads_ref
  12.8 0.7 copy-done.6
  13.5 2.1 %shard_map.115 = (bf16[96,2048]{1,0:T(8,128)(2,1)S(1)}, bf16[96,2048]{1,0:T(8,128)(2,1)S(1)}, bf16[96,2048]{1,0:T(8,128)(2,1)S(1)}, bf16[96,2048]{1,0:T(8,128)(2,1)S(1)}) custom-call(bf16[128,2048]{1,0:T(8,128)(2,1)} %collective-permute-done.7.grads_ref, s32[2,128]{1,0:T(2,128)S(1)} %xor_bitcast_fusion.routes_ref, f32[2,128]{1,0:T(2,128)S(1)} %bitcast.40), custom_call_target="tpu_custom_call" | custom-call | flops 402653184 | bytes 2097152 | tf_op jit(solution)/shard_map/pallas_call | solution.py:214
  15.7 2.5 %collective-permute-start.10 = (bf16[96,2048]{1,0:T(8,128)(2,1)S(1)}, bf16[96,2048]{1,0:T(8,128)(2,1)S(1)}, u32[]{:S(2)}, u32[]{:S(2)}) collective-permute-start(bf16[96,2048]{1,0:T(8,128)(2,1)S(1)} %get-tuple-element.21), channel_id=1, source_target_pairs={{0,3},{1,2},{2,1},{3,0},{4,7},{5,6},{6,5},{7,4},{8,11},{9,10},{10,... | collective-permute-start | bytes 1179656 | tf_op jit(solution)/shard_map/ppermute | solution.py:23
  18.2 2.3 %collective-permute-done.11 = bf16[96,2048]{1,0:T(8,128)(2,1)S(1)} collective-permute-done((bf16[96,2048]{1,0:T(8,128)(2,1)S(1)}, bf16[96,2048]{1,0:T(8,128)(2,1)S(1)}, u32[]{:S(2)}, u32[]{:S(2)}) %collective-permute-start.11) | collective-permute-done | bytes 393248 | tf_op jit(solution)/shard_map/ppermute | solution.py:23
  20.5 1.5 %collective-permute-start.8 = (bf16[96,2048]{1,0:T(8,128)(2,1)S(1)}, bf16[96,2048]{1,0:T(8,128)(2,1)S(1)}, u32[]{:S(2)}, u32[]{:S(2)}) collective-permute-start(bf16[96,2048]{1,0:T(8,128)(2,1)S(1)} %get-tuple-element.19), channel_id=1, source_target_pairs={{0,1},{1,0},{2,3},{3,2},{4,5},{5,4},{6,7},{7,6},{8,9},{9,8},{10,11... | collective-permute-start | bytes 1179656 | tf_op jit(solution)/shard_map/ppermute | solution.py:23
  22.0 13.8 %collective-permute-done.12 = bf16[96,2048]{1,0:T(8,128)(2,1)S(1)} collective-permute-done((bf16[96,2048]{1,0:T(8,128)(2,1)S(1)}, bf16[96,2048]{1,0:T(8,128)(2,1)S(1)}, u32[]{:S(2)}, u32[]{:S(2)}) %collective-permute-start.12) | collective-permute-done | bytes 393248 | tf_op jit(solution)/shard_map/ppermute | solution.py:23
  35.8 3.0 %collective-permute-start.9 = (bf16[96,2048]{1,0:T(8,128)(2,1)S(1)}, bf16[96,2048]{1,0:T(8,128)(2,1)S(1)}, u32[]{:S(2)}, u32[]{:S(2)}) collective-permute-start(bf16[96,2048]{1,0:T(8,128)(2,1)S(1)} %get-tuple-element.20), channel_id=1, source_target_pairs={{0,2},{1,3},{2,0},{3,1},{4,6},{5,7},{6,4},{7,5},{8,10},{9,11},{10,... | collective-permute-start | bytes 1179656 | tf_op jit(solution)/shard_map/ppermute | solution.py:23
  38.7 0.0 collective-permute-done.13
  38.7 6.8 %fusion.2 = f32[384,1536]{1,0:T(8,128)} fusion(bf16[1,1,2048,1536]{3,2,1,0:T(8,128)(2,1)} %param.18, bf16[96,2048]{1,0:T(8,128)(2,1)S(1)} %collective-permute-done.13, bf16[96,2048]{1,0:T(8,128)(2,1)S(1)} %collective-permute-done.12, bf16[96,2048]{1,0:T(8,128)(2,1)S(1)} %collective-permute-done.11, bf16[96,2048]{1,0:T(8,128)(2,1)S(1)} %get-tuple-element.22), kind=kOutput, calls=%fused_computation.2 | convolution fusion | flops 2422210560 | bytes 10223616 | tf_op jit(solution)/shard_map/dot_general | solution.py:156
  45.6 0.0 collective-permute-done.values_ref.layer_ref
  45.6 0.0 copy-done.4
  45.6 0.8 shard_map.113
  46.3 0.1 collective-permute-start.1
  46.4 0.1 collective-permute-start.2
  46.5 0.0 collective-permute-done.10
  46.5 3.4 %collective-permute-start.3 = (bf16[96,2048]{1,0:T(8,128)(2,1)S(1)}, bf16[96,2048]{1,0:T(8,128)(2,1)S(1)}, u32[]{:S(2)}, u32[]{:S(2)}) collective-permute-start(bf16[96,2048]{1,0:T(8,128)(2,1)S(1)} %get-tuple-element.17), channel_id=1, source_target_pairs={{0,3},{1,2},{2,1},{3,0},{4,7},{5,6},{6,5},{7,4},{8,11},{9,10},{10,... | collective-permute-start | bytes 1179656 | tf_op jit(solution)/shard_map/ppermute | solution.py:23
  49.9 0.0 collective-permute-done.8
  49.9 2.5 %collective-permute-done.9 = bf16[96,2048]{1,0:T(8,128)(2,1)S(1)} collective-permute-done((bf16[96,2048]{1,0:T(8,128)(2,1)S(1)}, bf16[96,2048]{1,0:T(8,128)(2,1)S(1)}, u32[]{:S(2)}, u32[]{:S(2)}) %collective-permute-start.9) | collective-permute-done | bytes 393248 | tf_op jit(solution)/shard_map/ppermute | solution.py:23
  52.4 0.0 copy-done
  52.4 3.4 %fusion.39 = (bf16[384,768]{1,0:T(8,128)(2,1)S(1)}, bf16[384,768]{1,0:T(8,128)(2,1)S(1)}) fusion(f32[384,1536]{1,0:T(8,128)} %fusion.2, bf16[1,1,768,2048]{3,2,1,0:T(8,128)(2,1)S(1)} %copy-done, bf16[96,2048]{1,0:T(8,128)(2,1)S(1)} %collective-permute-done.10, bf16[96,2048]{1,0:T(8,128)(2,1)S(1)} %collective-permute-done.9, ...), kind=kOutput, calls=%fused_computation.36 | convolution fusion | flops 1218084864 | bytes 8257536 | tf_op jit(solution)/shard_map/dot_general | solution.py:159
  55.9 0.0 slice-done
  55.9 0.0 slice-done.1
  55.9 0.0 slice-start.3
  55.9 2.6 %fusion.13 = bf16[384,2048]{1,0:T(8,128)(2,1)S(1)} fusion(bf16[1,1,2048,1536]{3,2,1,0:T(8,128)(2,1)S(1)} %bitcast.44, bf16[384,768]{1,0:T(8,128)(2,1)S(1)} %get-tuple-element.27, bf16[384,768]{1,0:T(8,128)(2,1)S(1)} %get-tuple-element.26), kind=kOutput, calls=%fused_computation.11 | convolution fusion | flops 2419064832 | bytes 9043968 | tf_op jit(solution)/shard_map/dot_general | solution.py:168
  58.5 0.1 fusion.51
  58.7 0.1 collective-permute-start.14
  58.8 2.5 %collective-permute-start.15 = (bf16[96,2048]{1,0:T(8,128)(2,1)S(1)}, bf16[96,2048]{1,0:T(8,128)(2,1)S(1)}, u32[]{:S(2)}, u32[]{:S(2)}) collective-permute-start(bf16[96,2048]{1,0:T(8,128)(2,1)S(1)} %get-tuple-element.29), channel_id=1, source_target_pairs={{0,2},{1,3},{2,0},{3,1},{4,6},{5,7},{6,4},{7,5},{8,10},{9,11},{10,... | collective-permute-start | bytes 1179656 | tf_op jit(solution)/shard_map/ppermute | solution.py:23
  61.3 0.0 collective-permute-done.1
  61.3 1.4 %collective-permute-start.16 = (bf16[96,2048]{1,0:T(8,128)(2,1)S(1)}, bf16[96,2048]{1,0:T(8,128)(2,1)S(1)}, u32[]{:S(2)}, u32[]{:S(2)}) collective-permute-start(bf16[96,2048]{1,0:T(8,128)(2,1)S(1)} %get-tuple-element.28), channel_id=1, source_target_pairs={{0,3},{1,2},{2,1},{3,0},{4,7},{5,6},{6,5},{7,4},{8,11},{9,10},{10,... | collective-permute-start | bytes 1179656 | tf_op jit(solution)/shard_map/ppermute | solution.py:23
  62.7 6.6 %collective-permute-done.2 = bf16[96,2048]{1,0:T(8,128)(2,1)S(1)} collective-permute-done((bf16[96,2048]{1,0:T(8,128)(2,1)S(1)}, bf16[96,2048]{1,0:T(8,128)(2,1)S(1)}, u32[]{:S(2)}, u32[]{:S(2)}) %collective-permute-start.2) | collective-permute-done | bytes 393248 | tf_op jit(solution)/shard_map/ppermute | solution.py:23
  69.3 0.0 collective-permute-done.3
  69.3 0.0 slice-done.2
  69.3 0.0 slice-done.3
  69.3 2.6 %fusion.4 = f32[384,1536]{1,0:T(8,128)S(1)} fusion(bf16[1,1,2048,1536]{3,2,1,0:T(8,128)(2,1)S(1)} %bitcast.46, bf16[96,2048]{1,0:T(8,128)(2,1)S(1)} %collective-permute-done.3, bf16[96,2048]{1,0:T(8,128)(2,1)S(1)} %collective-permute-done.2, bf16[96,2048]{1,0:T(8,128)(2,1)S(1)} %collective-permute-done.1, bf16[96,2048]{1,0:T(8,128)(2,1)S(1)} %get-tuple-element.14), kind=kOutput, calls=%fused_computation.4 | convolution fusion | flops 2422210560 | bytes 10223616 | tf_op jit(solution)/shard_map/dot_general | solution.py:148
  71.9 1.5 %fusion.10 = bf16[384,2048]{1,0:T(8,128)(2,1)S(1)} fusion(bf16[1,1,768,2048]{3,2,1,0:T(8,128)(2,1)S(1)} %copy-done, f32[384,1536]{1,0:T(8,128)S(1)} %fusion.4), kind=kOutput, calls=%fused_computation.10 | convolution fusion | flops 1210515456 | bytes 7077888 | tf_op jit(solution)/shard_map/dot_general | solution.py:152
  73.4 0.0 copy-start.2
  73.4 0.2 fusion.52
  73.5 0.1 collective-permute-start.4
  73.6 2.6 %collective-permute-start.5 = (bf16[96,2048]{1,0:T(8,128)(2,1)S(1)}, bf16[96,2048]{1,0:T(8,128)(2,1)S(1)}, u32[]{:S(2)}, u32[]{:S(2)}) collective-permute-start(bf16[96,2048]{1,0:T(8,128)(2,1)S(1)} %get-tuple-element.33), channel_id=1, source_target_pairs={{0,2},{1,3},{2,0},{3,1},{4,6},{5,7},{6,4},{7,5},{8,10},{9,11},{10,... | collective-permute-start | bytes 1179656 | tf_op jit(solution)/shard_map/ppermute | solution.py:23
  76.2 0.0 collective-permute-done.14.refs_1_
  76.2 1.4 %collective-permute-start.6 = (bf16[96,2048]{1,0:T(8,128)(2,1)S(1)}, bf16[96,2048]{1,0:T(8,128)(2,1)S(1)}, u32[]{:S(2)}, u32[]{:S(2)}) collective-permute-start(bf16[96,2048]{1,0:T(8,128)(2,1)S(1)} %get-tuple-element.32), channel_id=1, source_target_pairs={{0,3},{1,2},{2,1},{3,0},{4,7},{5,6},{6,5},{7,4},{8,11},{9,10},{10,... | collective-permute-start | bytes 1179656 | tf_op jit(solution)/shard_map/ppermute | solution.py:23
  77.6 7.2 %collective-permute-done.15.refs_2_ = bf16[96,2048]{1,0:T(8,128)(2,1)S(1)} collective-permute-done((bf16[96,2048]{1,0:T(8,128)(2,1)S(1)}, bf16[96,2048]{1,0:T(8,128)(2,1)S(1)}, u32[]{:S(2)}, u32[]{:S(2)}) %collective-permute-start.15) | collective-permute-done | bytes 393248 | tf_op jit(solution)/shard_map/ppermute | solution.py:23
  84.8 0.0 collective-permute-done.16.refs_3_
  84.8 0.0 copy-done.2
  84.8 3.0 %shard_map.117 = bf16[128,2048]{1,0:T(8,128)(2,1)} custom-call(bf16[128,2048]{1,0:T(8,128)(2,1)} %collective-permute-done.7.grads_ref, bf16[128,2048]{1,0:T(8,128)(2,1)S(1)} %bitcast.38, f32[1,2048]{1,0:T(1,128)S(1)} %copy-done.4, s32[2,128]{1,0:T(2,128)S(1)} %xor_bitcast_fusion.routes_ref, bf16[96,2048]{1,0:T(8,128)(2,1)S(1)} %get-tuple-element.31.refs_0_, ...), custom_call_target="tpu_custom_call" | custom-call | flops 201326592 | bytes 2097152 | tf_op jit(solution)/shard_map/pallas_call | solution.py:226
  87.8 0.9 collective-permute-done.4.refs_1_
  88.7 4.5 %collective-permute-done.5.refs_2_ = bf16[96,2048]{1,0:T(8,128)(2,1)S(1)} collective-permute-done((bf16[96,2048]{1,0:T(8,128)(2,1)S(1)}, bf16[96,2048]{1,0:T(8,128)(2,1)S(1)}, u32[]{:S(2)}, u32[]{:S(2)}) %collective-permute-start.5) | collective-permute-done | bytes 393248 | tf_op jit(solution)/shard_map/ppermute | solution.py:23
  93.2 1.0 collective-permute-done.6.refs_3_
  94.2 0.0 copy-done.5
  94.2 2.2 %shard_map.114 = bf16[128,2048]{1,0:T(8,128)(2,1)} custom-call(bf16[128,2048]{1,0:T(8,128)(2,1)S(1)} %collective-permute-done.values_ref.layer_ref, s32[2,128]{1,0:T(2,128)S(1)} %xor_bitcast_fusion.1.routes_ref, f32[2,128]{1,0:T(2,128)S(1)} %bitcast.39, bf16[96,2048]{1,0:T(8,128)(2,1)S(1)} %get-tuple-element.35.refs_0_, ...), custom_call_target="tpu_custom_call" | custom-call | flops 402653184 | bytes 2097152 | tf_op jit(solution)/shard_map/pallas_call | solution.py:225
  (8 shorter events, 0.0 us)
Async XLA Ops:
  0.6 51.8 %copy-start = (bf16[1,1,768,2048]{3,2,1,0:T(8,128)(2,1)S(1)}, bf16[1,1,768,2048]{3,2,1,0:T(8,128)(2,1)}, u32[]{:S(2)}) copy-start(bf16[1,1,768,2048]{3,2,1,0:T(8,128)(2,1)} %param.19) | copy-start | bytes 9437188
  0.6 12.2 %collective-permute-start.7 = (bf16[128,2048]{1,0:T(8,128)(2,1)}, bf16[128,2048]{1,0:T(8,128)(2,1)}, u32[]{:S(2)}, u32[]{:S(2)}) collective-permute-start(bf16[128,2048]{1,0:T(8,128)(2,1)} %bitcast.47), channel_id=1, source_target_pairs={{0,28},{4,0},{8,4},{12,8},{16,12},{20,16},{24,20},{28,24},{1,29},{... | collective-permute-start | bytes 1572872 | tf_op jit(solution)/shard_map/ppermute | solution.py:17
  5.9 1.0 %copy-start.1 = (bf16[1,128,2048]{2,1,0:T(8,128)(2,1)S(1)}, bf16[1,128,2048]{2,1,0:T(8,128)(2,1)}, u32[]{:S(2)}) copy-start(bf16[1,128,2048]{2,1,0:T(8,128)(2,1)} %param.12) | copy-start | bytes 1572868
  6.9 0.7 copy-start.3
  8.4 12.1 %collective-permute-start.11 = (bf16[96,2048]{1,0:T(8,128)(2,1)S(1)}, bf16[96,2048]{1,0:T(8,128)(2,1)S(1)}, u32[]{:S(2)}, u32[]{:S(2)}) collective-permute-start(bf16[96,2048]{1,0:T(8,128)(2,1)S(1)} %get-tuple-element.23), channel_id=1, source_target_pairs={{0,1},{1,0},{2,3},{3,2},{4,5},{5,4},{6,7},{7,6},{8,9},{9,8},{10,11... | collective-permute-start | bytes 1179656 | tf_op jit(solution)/shard_map/ppermute | solution.py:23
  9.9 25.8 %collective-permute-start.12 = (bf16[96,2048]{1,0:T(8,128)(2,1)S(1)}, bf16[96,2048]{1,0:T(8,128)(2,1)S(1)}, u32[]{:S(2)}, u32[]{:S(2)}) collective-permute-start(bf16[96,2048]{1,0:T(8,128)(2,1)S(1)} %get-tuple-element.24), channel_id=1, source_target_pairs={{0,2},{1,3},{2,0},{3,1},{4,6},{5,7},{6,4},{7,5},{8,10},{9,11},{10,... | collective-permute-start | bytes 1179656 | tf_op jit(solution)/shard_map/ppermute | solution.py:23
  11.4 27.3 %collective-permute-start.13 = (bf16[96,2048]{1,0:T(8,128)(2,1)S(1)}, bf16[96,2048]{1,0:T(8,128)(2,1)S(1)}, u32[]{:S(2)}, u32[]{:S(2)}) collective-permute-start(bf16[96,2048]{1,0:T(8,128)(2,1)S(1)} %get-tuple-element.25), channel_id=1, source_target_pairs={{0,3},{1,2},{2,1},{3,0},{4,7},{5,6},{6,5},{7,4},{8,11},{9,10},{10,... | collective-permute-start | bytes 1179656 | tf_op jit(solution)/shard_map/ppermute | solution.py:23
  11.9 33.6 %collective-permute-start = (bf16[128,2048]{1,0:T(8,128)(2,1)}, bf16[128,2048]{1,0:T(8,128)(2,1)S(1)}, u32[]{:S(2)}, u32[]{:S(2)}) collective-permute-start(bf16[128,2048]{1,0:T(8,128)(2,1)} %bitcast.48), channel_id=1, source_target_pairs={{0,4},{4,8},{8,12},{12,16},{16,20},{20,24},{24,28},{28,0},{1,5},{5... | collective-permute-start | bytes 1572872 | tf_op jit(solution)/shard_map/ppermute | solution.py:17
  12.8 0.7 copy-start.6
  15.7 30.8 %collective-permute-start.10 = (bf16[96,2048]{1,0:T(8,128)(2,1)S(1)}, bf16[96,2048]{1,0:T(8,128)(2,1)S(1)}, u32[]{:S(2)}, u32[]{:S(2)}) collective-permute-start(bf16[96,2048]{1,0:T(8,128)(2,1)S(1)} %get-tuple-element.21), channel_id=1, source_target_pairs={{0,3},{1,2},{2,1},{3,0},{4,7},{5,6},{6,5},{7,4},{8,11},{9,10},{10,... | collective-permute-start | bytes 1179656 | tf_op jit(solution)/shard_map/ppermute | solution.py:23
  20.5 29.4 %collective-permute-start.8 = (bf16[96,2048]{1,0:T(8,128)(2,1)S(1)}, bf16[96,2048]{1,0:T(8,128)(2,1)S(1)}, u32[]{:S(2)}, u32[]{:S(2)}) collective-permute-start(bf16[96,2048]{1,0:T(8,128)(2,1)S(1)} %get-tuple-element.19), channel_id=1, source_target_pairs={{0,1},{1,0},{2,3},{3,2},{4,5},{5,4},{6,7},{7,6},{8,9},{9,8},{10,11... | collective-permute-start | bytes 1179656 | tf_op jit(solution)/shard_map/ppermute | solution.py:23
  35.8 16.6 %collective-permute-start.9 = (bf16[96,2048]{1,0:T(8,128)(2,1)S(1)}, bf16[96,2048]{1,0:T(8,128)(2,1)S(1)}, u32[]{:S(2)}, u32[]{:S(2)}) collective-permute-start(bf16[96,2048]{1,0:T(8,128)(2,1)S(1)} %get-tuple-element.20), channel_id=1, source_target_pairs={{0,2},{1,3},{2,0},{3,1},{4,6},{5,7},{6,4},{7,5},{8,10},{9,11},{10,... | collective-permute-start | bytes 1179656 | tf_op jit(solution)/shard_map/ppermute | solution.py:23
  38.7 6.8 %copy-start.4 = (f32[1,2048]{1,0:T(1,128)S(1)}, f32[1,2048]{1,0:T(1,128)}, u32[]{:S(2)}) copy-start(f32[1,2048]{1,0:T(1,128)} %gain_ref.5) | copy-start | bytes 24580
  45.6 10.3 %slice-start = ((s8[6291456]{0:T(1024)(128)(4,1)}), s8[4194304]{0:T(1024)(128)(4,1)S(1)}, s32[]{:S(2)}) async-start(s8[6291456]{0:T(1024)(128)(4,1)} %bitcast.43), calls=%async_computation | async-start | bytes 8388608
  46.3 15.0 %collective-permute-start.1 = (bf16[96,2048]{1,0:T(8,128)(2,1)S(1)}, bf16[96,2048]{1,0:T(8,128)(2,1)S(1)}, u32[]{:S(2)}, u32[]{:S(2)}) collective-permute-start(bf16[96,2048]{1,0:T(8,128)(2,1)S(1)} %get-tuple-element.15), channel_id=1, source_target_pairs={{0,1},{1,0},{2,3},{3,2},{4,5},{5,4},{6,7},{7,6},{8,9},{9,8},{10,11... | collective-permute-start | bytes 1179656 | tf_op jit(solution)/shard_map/ppermute | solution.py:23
  46.4 22.8 %collective-permute-start.2 = (bf16[96,2048]{1,0:T(8,128)(2,1)S(1)}, bf16[96,2048]{1,0:T(8,128)(2,1)S(1)}, u32[]{:S(2)}, u32[]{:S(2)}) collective-permute-start(bf16[96,2048]{1,0:T(8,128)(2,1)S(1)} %get-tuple-element.16), channel_id=1, source_target_pairs={{0,2},{1,3},{2,0},{3,1},{4,6},{5,7},{6,4},{7,5},{8,10},{9,11},{10,... | collective-permute-start | bytes 1179656 | tf_op jit(solution)/shard_map/ppermute | solution.py:23
  46.5 22.7 %collective-permute-start.3 = (bf16[96,2048]{1,0:T(8,128)(2,1)S(1)}, bf16[96,2048]{1,0:T(8,128)(2,1)S(1)}, u32[]{:S(2)}, u32[]{:S(2)}) collective-permute-start(bf16[96,2048]{1,0:T(8,128)(2,1)S(1)} %get-tuple-element.17), channel_id=1, source_target_pairs={{0,3},{1,2},{2,1},{3,0},{4,7},{5,6},{6,5},{7,4},{8,11},{9,10},{10,... | collective-permute-start | bytes 1179656 | tf_op jit(solution)/shard_map/ppermute | solution.py:23
  52.4 3.5 %slice-start.1 = ((s8[6291456]{0:T(1024)(128)(4,1)}), s8[2097152]{0:T(1024)(128)(4,1)S(1)}, s32[]{:S(2)}) async-start(s8[6291456]{0:T(1024)(128)(4,1)} %bitcast.43), calls=%async_computation.1 | async-start | bytes 4194304
  52.4 16.9 %slice-start.2 = ((s8[6291456]{0:T(1024)(128)(4,1)}), s8[4194304]{0:T(1024)(128)(4,1)S(1)}, s32[]{:S(2)}) async-start(s8[6291456]{0:T(1024)(128)(4,1)} %bitcast.45), calls=%async_computation.2 | async-start | bytes 8388608
  55.9 13.4 %slice-start.3 = ((s8[6291456]{0:T(1024)(128)(4,1)}), s8[2097152]{0:T(1024)(128)(4,1)S(1)}, s32[]{:S(2)}) async-start(s8[6291456]{0:T(1024)(128)(4,1)} %bitcast.45), calls=%async_computation.3 | async-start | bytes 4194304
  58.7 17.5 %collective-permute-start.14 = (bf16[96,2048]{1,0:T(8,128)(2,1)S(1)}, bf16[96,2048]{1,0:T(8,128)(2,1)S(1)}, u32[]{:S(2)}, u32[]{:S(2)}) collective-permute-start(bf16[96,2048]{1,0:T(8,128)(2,1)S(1)} %get-tuple-element.30), channel_id=1, source_target_pairs={{0,1},{1,0},{2,3},{3,2},{4,5},{5,4},{6,7},{7,6},{8,9},{9,8},{10,11... | collective-permute-start | bytes 1179656 | tf_op jit(solution)/shard_map/ppermute | solution.py:23
  58.8 26.0 %collective-permute-start.15 = (bf16[96,2048]{1,0:T(8,128)(2,1)S(1)}, bf16[96,2048]{1,0:T(8,128)(2,1)S(1)}, u32[]{:S(2)}, u32[]{:S(2)}) collective-permute-start(bf16[96,2048]{1,0:T(8,128)(2,1)S(1)} %get-tuple-element.29), channel_id=1, source_target_pairs={{0,2},{1,3},{2,0},{3,1},{4,6},{5,7},{6,4},{7,5},{8,10},{9,11},{10,... | collective-permute-start | bytes 1179656 | tf_op jit(solution)/shard_map/ppermute | solution.py:23
  61.3 23.5 %collective-permute-start.16 = (bf16[96,2048]{1,0:T(8,128)(2,1)S(1)}, bf16[96,2048]{1,0:T(8,128)(2,1)S(1)}, u32[]{:S(2)}, u32[]{:S(2)}) collective-permute-start(bf16[96,2048]{1,0:T(8,128)(2,1)S(1)} %get-tuple-element.28), channel_id=1, source_target_pairs={{0,3},{1,2},{2,1},{3,0},{4,7},{5,6},{6,5},{7,4},{8,11},{9,10},{10,... | collective-permute-start | bytes 1179656 | tf_op jit(solution)/shard_map/ppermute | solution.py:23
  73.4 11.4 %copy-start.2 = (bf16[1,128,2048]{2,1,0:T(8,128)(2,1)S(1)}, bf16[1,128,2048]{2,1,0:T(8,128)(2,1)}, u32[]{:S(2)}) copy-start(bf16[1,128,2048]{2,1,0:T(8,128)(2,1)} %param.12) | copy-start | bytes 1572868
  73.5 15.1 %collective-permute-start.4 = (bf16[96,2048]{1,0:T(8,128)(2,1)S(1)}, bf16[96,2048]{1,0:T(8,128)(2,1)S(1)}, u32[]{:S(2)}, u32[]{:S(2)}) collective-permute-start(bf16[96,2048]{1,0:T(8,128)(2,1)S(1)} %get-tuple-element.34), channel_id=1, source_target_pairs={{0,1},{1,0},{2,3},{3,2},{4,5},{5,4},{6,7},{7,6},{8,9},{9,8},{10,11... | collective-permute-start | bytes 1179656 | tf_op jit(solution)/shard_map/ppermute | solution.py:23
  73.6 19.6 %collective-permute-start.5 = (bf16[96,2048]{1,0:T(8,128)(2,1)S(1)}, bf16[96,2048]{1,0:T(8,128)(2,1)S(1)}, u32[]{:S(2)}, u32[]{:S(2)}) collective-permute-start(bf16[96,2048]{1,0:T(8,128)(2,1)S(1)} %get-tuple-element.33), channel_id=1, source_target_pairs={{0,2},{1,3},{2,0},{3,1},{4,6},{5,7},{6,4},{7,5},{8,10},{9,11},{10,... | collective-permute-start | bytes 1179656 | tf_op jit(solution)/shard_map/ppermute | solution.py:23
  76.2 18.0 %collective-permute-start.6 = (bf16[96,2048]{1,0:T(8,128)(2,1)S(1)}, bf16[96,2048]{1,0:T(8,128)(2,1)S(1)}, u32[]{:S(2)}, u32[]{:S(2)}) collective-permute-start(bf16[96,2048]{1,0:T(8,128)(2,1)S(1)} %get-tuple-element.32), channel_id=1, source_target_pairs={{0,3},{1,2},{2,1},{3,0},{4,7},{5,6},{6,5},{7,4},{8,11},{9,10},{10,... | collective-permute-start | bytes 1179656 | tf_op jit(solution)/shard_map/ppermute | solution.py:23
  84.8 9.4 %copy-start.5 = (f32[1,128,2]{1,2,0:T(2,128)S(1)}, f32[1,128,2]{1,2,0:T(2,128)}, u32[]{:S(2)}) copy-start(f32[1,128,2]{1,2,0:T(2,128)} %param.14) | copy-start | bytes 3076

commit v2 on v1

--- a/solution.py
+++ b/solution.py
@@ -8,7 +8,7 @@
 from jax.sharding import PartitionSpec as P
 
 EPS = 1e-06
-VMEM_LIMIT = 48 * 1024 * 1024
+VMEM_LIMIT = 32 * 1024 * 1024
 
 
 def passed_along(value, axis, steps):
@@ -62,35 +62,6 @@
     high = weights.astype(jnp.bfloat16)
     low = (weights - high.astype(jnp.float32)).astype(jnp.bfloat16)
     return high, low
-
-
-def normed_kernel(values_ref, routes_ref, gain_ref, *out_refs):
-    expert_count = len(out_refs)
-    capacity = out_refs[0].shape[0]
-    wide = values_ref[...].astype(jnp.float32)
-    inv_rms = lax.rsqrt(jnp.mean(wide * wide, axis=-1, keepdims=True) + EPS)
-    normed = (wide * inv_rms * gain_ref[...]).astype(jnp.bfloat16)
-    slots = slot_table(routes_ref[...], expert_count)
-    for e in range(expert_count):
-        place = placement(slots, e, capacity).astype(jnp.bfloat16)
-        out_refs[e][...] = jnp.dot(place, normed, preferred_element_type=jnp.float32).astype(
-            jnp.bfloat16
-        )
-
-
-def grads_kernel(grads_ref, routes_ref, gates_ref, *out_refs):
-    expert_count = len(out_refs)
-    capacity = out_refs[0].shape[0]
-    grads = grads_ref[...]
-    routes = routes_ref[...]
-    slots = slot_table(routes, expert_count)
-    for e in range(expert_count):
-        place = placement(slots, e, capacity)
-        high, low = halves(jnp.where(place, gate_row(routes, gates_ref[...], e), 0.0))
-        out_refs[e][...] = (
-            jnp.dot(high, grads, preferred_element_type=jnp.float32)
-            + jnp.dot(low, grads, preferred_element_type=jnp.float32)
-        ).astype(jnp.bfloat16)
 
 
 def rows_dot(weights, rows):
@@ -135,39 +106,146 @@
     ).astype(jnp.bfloat16)
 
 
-def local_call(kernel, out_shapes, flops, moved):
+def tiles(size, step):
+    return [(start, min(step, size - start)) for start in range(0, size, step)]
+
+
+def named_here(table_ref, source, first, top_count, expert):
+    rows = table_ref[source]
+    routes = rows[first : first + top_count]
+    gates = rows[first + top_count : first + 2 * top_count]
+    member = routes == expert
+    tok_rows = routes.shape[1]
+    held = jnp.sum(member.astype(jnp.float32), axis=0, keepdims=True)
+    gate = jnp.sum(jnp.where(member, gates, 0.0), axis=0, keepdims=True)
+    before = lax.broadcasted_iota(jnp.int32, (tok_rows, tok_rows), 0) < lax.broadcasted_iota(
+        jnp.int32, (tok_rows, tok_rows), 1
+    )
+    slots = jnp.dot(
+        jnp.broadcast_to(held, (8, tok_rows)).astype(jnp.bfloat16),
+        before.astype(jnp.bfloat16),
+        preferred_element_type=jnp.float32,
+    )[0:1]
+    return jnp.where(held > 0.0, slots, -1.0), gate
+
+
+def placed_normed(values_ref, table_ref, gain_ref, rows_ref, me, first, top_count):
+    expert_count, _, tok_rows = table_ref.shape
+    capacity = rows_ref.shape[0] // expert_count
+    for d in range(expert_count):
+        source = me ^ d
+        slots, _ = named_here(table_ref, source, first, top_count, me.astype(jnp.float32))
+        wide = values_ref[pl.ds(pl.multiple_of(source * tok_rows, tok_rows), tok_rows), :].astype(
+            jnp.float32
+        )
+        inv_rms = lax.rsqrt(jnp.mean(wide * wide, axis=-1, keepdims=True) + EPS)
+        normed = (wide * inv_rms * gain_ref[...]).astype(jnp.bfloat16)
+        place = placement(slots, 0, capacity).astype(jnp.bfloat16)
+        rows_ref[d * capacity : (d + 1) * capacity, :] = jnp.dot(
+            place, normed, preferred_element_type=jnp.float32
+        ).astype(jnp.bfloat16)
+
+
+def placed_grads(grads_ref, table_ref, rows_ref, me, first, top_count):
+    expert_count, _, tok_rows = table_ref.shape
+    capacity = rows_ref.shape[0] // expert_count
+    for d in range(expert_count):
+        source = me ^ d
+        slots, gate = named_here(table_ref, source, first, top_count, me.astype(jnp.float32))
+        grads = grads_ref[pl.ds(pl.multiple_of(source * tok_rows, tok_rows), tok_rows), :]
+        high, low = halves(jnp.where(placement(slots, 0, capacity), gate, 0.0))
+        rows_ref[d * capacity : (d + 1) * capacity, :] = (
+            jnp.dot(high, grads, preferred_element_type=jnp.float32)
+            + jnp.dot(low, grads, preferred_element_type=jnp.float32)
+        ).astype(jnp.bfloat16)
+
+
+def expert_fwd_kernel(
+    top_count, me_ref, values_ref, table_ref, gain_ref, weight_in, weight_out, *refs
+):
+    out_refs = refs[:-2]
+    rows_ref, hidden_ref = refs[-2:]
+    capacity = out_refs[0].shape[0]
+    hidden_units, features = weight_out.shape
+    placed_normed(values_ref, table_ref, gain_ref, rows_ref, me_ref[0], 0, top_count)
+    for start, size in tiles(hidden_units, 256):
+        gate = jnp.dot(
+            rows_ref[...], weight_in[:, start : start + size], preferred_element_type=jnp.float32
+        )
+        up = jnp.dot(
+            rows_ref[...],
+            weight_in[:, hidden_units + start : hidden_units + start + size],
+            preferred_element_type=jnp.float32,
+        )
+        hidden_ref[:, start : start + size] = (gate / (1.0 + jnp.exp(-gate)) * up).astype(
+            jnp.bfloat16
+        )
+    for start, size in tiles(features, 512):
+        out = jnp.dot(
+            hidden_ref[...], weight_out[:, start : start + size], preferred_element_type=jnp.float32
+        )
+        for d in range(len(out_refs)):
+            out_refs[d][:, start : start + size] = out[d * capacity : (d + 1) * capacity].astype(
+                jnp.bfloat16
+            )
+
+
+def expert_bwd_kernel(
+    top_count, me_ref, values_ref, grad_in_ref, table_ref, gain_ref, weight_in, weight_out, *refs
+):
+    out_refs = refs[:-3]
+    rows_ref, grads_ref, both_ref = refs[-3:]
+    capacity = out_refs[0].shape[0]
+    hidden_units, features = weight_out.shape
+    first = 2 * top_count
+    placed_normed(values_ref, table_ref, gain_ref, rows_ref, me_ref[0], first, top_count)
+    placed_grads(grad_in_ref, table_ref, grads_ref, me_ref[0], first, top_count)
+    for start, size in tiles(hidden_units, 256):
+        gate = jnp.dot(
+            rows_ref[...], weight_in[:, start : start + size], preferred_element_type=jnp.float32
+        )
+        up = jnp.dot(
+            rows_ref[...],
+            weight_in[:, hidden_units + start : hidden_units + start + size],
+            preferred_element_type=jnp.float32,
+        )
+        d_hidden = lax.dot_general(
+            grads_ref[...],
+            weight_out[start : start + size, :],
+            (((1,), (1,)), ((), ())),
+            preferred_element_type=jnp.float32,
+        )
+        sig = 1.0 / (1.0 + jnp.exp(-gate))
+        both_ref[:, start : start + size] = (
+            d_hidden * up * sig * (1.0 + gate * (1.0 - sig))
+        ).astype(jnp.bfloat16)
+        both_ref[:, hidden_units + start : hidden_units + start + size] = (
+            d_hidden * gate * sig
+        ).astype(jnp.bfloat16)
+    for start, size in tiles(features, 512):
+        out = lax.dot_general(
+            both_ref[...],
+            weight_in[start : start + size, :],
+            (((1,), (1,)), ((), ())),
+            preferred_element_type=jnp.float32,
+        )
+        for d in range(len(out_refs)):
+            out_refs[d][:, start : start + size] = out[d * capacity : (d + 1) * capacity].astype(
+                jnp.bfloat16
+            )
+
+
+def local_call(kernel, out_shapes, inputs, flops, moved, scratch=(), scalars=0):
+    specs = [pl.BlockSpec(memory_space=pltpu.SMEM)] * scalars
+    specs += [pl.BlockSpec(memory_space=pltpu.VMEM)] * (len(inputs) - scalars)
     return pl.pallas_call(
         kernel,
         out_shape=out_shapes,
+        in_specs=specs,
+        scratch_shapes=list(scratch),
         compiler_params=pltpu.CompilerParams(vmem_limit_bytes=VMEM_LIMIT),
         cost_estimate=pl.CostEstimate(flops=flops, bytes_accessed=moved, transcendentals=0),
-    )
-
-
-def expert_forward(in_rows, weight_in, weight_out, hidden_units):
-    projected = jnp.dot(in_rows, weight_in, preferred_element_type=jnp.float32)
-    hidden = (jax.nn.silu(projected[:, :hidden_units]) * projected[:, hidden_units:]).astype(
-        jnp.bfloat16
-    )
-    return jnp.dot(hidden, weight_out, preferred_element_type=jnp.float32).astype(jnp.bfloat16)
-
-
-def expert_backward(in_rows, grad_rows, weight_in, weight_out, hidden_units):
-    projected = jnp.dot(in_rows, weight_in, preferred_element_type=jnp.float32)
-    gate_pre = projected[:, :hidden_units]
-    up_pre = projected[:, hidden_units:]
-    d_hidden = lax.dot_general(
-        grad_rows, weight_out, (((1,), (1,)), ((), ())), preferred_element_type=jnp.float32
-    )
-    sigmoid_gate = 1.0 / (1.0 + jnp.exp(-gate_pre))
-    d_gate = (d_hidden * up_pre * sigmoid_gate * (1.0 + gate_pre * (1.0 - sigmoid_gate))).astype(
-        jnp.bfloat16
-    )
-    d_up = (d_hidden * gate_pre * sigmoid_gate).astype(jnp.bfloat16)
-    d_both = jnp.concatenate([d_gate, d_up], axis=1)
-    return lax.dot_general(
-        d_both, weight_in, (((1,), (1,)), ((), ())), preferred_element_type=jnp.float32
-    ).astype(jnp.bfloat16)
+    )(*inputs)
 
 
 def per_device(
@@ -192,38 +270,69 @@
     weight_in = w_in[0, 0]
     weight_out = w_out[0, 0]
     me = lax.axis_index("expert")
-    f_routes = (fwd_routes[0] ^ me).T
-    b_routes = (bwd_routes[0] ^ me).T
+    f_routes = fwd_routes[0].T
+    b_routes = bwd_routes[0].T
     f_gates = fwd_gates[0].T
     b_gates = bwd_gates[0].T
     saved = bwd_saved[0]
+
+    def gathered(value):
+        return lax.all_gather(value, "expert", axis=0, tiled=True)
+
+    table = lax.all_gather(
+        jnp.concatenate(
+            [f_routes.astype(jnp.float32), f_gates, b_routes.astype(jnp.float32), b_gates]
+        ),
+        "expert",
+        axis=0,
+    )
+    all_saved = gathered(saved)
     layer_in = passed_along(fwd_prev[0], "section", 1)
     grad_in = passed_along(bwd_prev[0], "section", -1)
+    all_layer = gathered(layer_in)
+    all_grads = gathered(grad_in)
 
     block = jax.ShapeDtypeStruct((capacity, features), jnp.bfloat16)
     whole = jax.ShapeDtypeStruct((tok_rows, features), jnp.bfloat16)
-    one_dot = 2 * expert_count * capacity * tok_rows * features
-    moved = 2 * features * (tok_rows + expert_count * capacity)
-    normed_call = local_call(normed_kernel, [block] * expert_count, one_dot, moved)
-    grads_call = local_call(grads_kernel, [block] * expert_count, 2 * one_dot, moved)
-    fwd_end = local_call(fwd_end_kernel, whole, 2 * one_dot, moved)
-    bwd_end = local_call(bwd_end_kernel, whole, one_dot, moved)
-
-    b_rows = exchanged(normed_call(saved, b_routes, gain_row), "expert")
-    f_rows = exchanged(normed_call(layer_in, f_routes, gain_row), "expert")
-    g_rows = exchanged(grads_call(grad_in, b_routes, b_gates), "expert")
-
-    def cut(rows):
-        return [rows[d * capacity : (d + 1) * capacity] for d in range(expert_count)]
-
-    f_done = expert_forward(jnp.concatenate(f_rows), weight_in, weight_out, hidden_units)
-    f_back = exchanged(cut(f_done), "expert")
-    b_done = expert_backward(
-        jnp.concatenate(b_rows), jnp.concatenate(g_rows), weight_in, weight_out, hidden_units
-    )
-    b_back = exchanged(cut(b_done), "expert")
-    fwd_block = fwd_end(layer_in, f_routes, f_gates, *f_back)
-    bwd_block = bwd_end(grad_in, saved, gain_row, b_routes, *b_back)
+    blocks = [block] * expert_count
+    slot_total = expert_count * capacity
+    one_dot = 2 * slot_total * tok_rows * features
+    moved = 2 * features * (tok_rows + slot_total)
+    expert_flops = 2 * slot_total * features * hidden_units
+    expert_moved = 2 * features * (3 * hidden_units + 3 * slot_total)
+    rows_scratch = pltpu.VMEM((slot_total, features), jnp.bfloat16)
+    here = me.astype(jnp.int32).reshape(1)
+
+    f_done = local_call(
+        functools.partial(expert_fwd_kernel, top_count),
+        blocks,
+        (here, all_layer, table, gain_row, weight_in, weight_out),
+        3 * expert_flops,
+        expert_moved,
+        scratch=(rows_scratch, pltpu.VMEM((slot_total, hidden_units), jnp.bfloat16)),
+        scalars=1,
+    )
+    f_back = exchanged(f_done, "expert")
+    b_done = local_call(
+        functools.partial(expert_bwd_kernel, top_count),
+        blocks,
+        (here, all_saved, all_grads, table, gain_row, weight_in, weight_out),
+        5 * expert_flops,
+        expert_moved,
+        scratch=(
+            rows_scratch,
+            rows_scratch,
+            pltpu.VMEM((slot_total, 2 * hidden_units), jnp.bfloat16),
+        ),
+        scalars=1,
+    )
+    b_back = exchanged(b_done, "expert")
+    fwd_block = local_call(
+        fwd_end_kernel, whole, (layer_in, f_routes ^ me, f_gates, *f_back), 2 * one_dot, moved
+    )
+    bwd_block = local_call(
+        bwd_end_kernel, whole, (grad_in, saved, gain_row, b_routes ^ me, *b_back), one_dot, moved
+    )
     return (fwd_block[None], bwd_block[None])
 
 

time: 98.1 us -> 186 us (1.90)
  waiting for transfers between devices: 39 us -> 118 us
  starting transfers between devices: 26.6 us -> 7.79 us
  matrix products: 17 us -> 0 us
  local copies, waits for them, and re-layouts: 2.74 us -> 16.4 us
  between operations: 0.81 us -> 13.8 us
  Pallas kernels: 8.86 us -> 19.1 us
  blocking collectives: 0 us -> 8.65 us
    all_gather x0 -> x3, waiting for transfers between devices: none -> 83.9 us  [gathered(): return lax.all_gather(value, 'expert', axis=0, tiled=True)]
    ppermute x15 -> x6, waiting for transfers between devices: 38.8 us -> 14.7 us  [swapped(): return lax.ppermute(value, axis, pairs)]
    ppermute x2, waiting for transfers between devices: 0.22 us -> 18.1 us  [passed_along(): return lax.ppermute(value, axis, pairs)]
    dot_general x5 -> x0, matrix products: 17 us -> none  [the longest x1 6.82 us: expert_backward(): projected = jnp.dot(in_rows, weight_in, preferred_element_type=jnp.float32)]
    ppermute x15 -> x6, starting transfers between devices: 22.1 us -> 7.11 us  [swapped(): return lax.ppermute(value, axis, pairs)]
    unnamed x22 -> x30, local copies, waits for them, and re-layouts: 2.46 us -> 16.4 us
    pallas_call x5 -> x4, Pallas kernels: 8.86 us -> 19.1 us  [local_call(): pl.pallas_call(kernel, out_shape=out_shapes, in_specs=specs, scratch_shap...]
    all_gather x0 -> x1, blocking collectives: none -> 8.65 us  [per_device(): lax.all_gather(jnp.concatenate([f_routes.astype(jnp.float32), f_gates, b_...]
  transfers between devices with their start and end apart: 17 -> 11, of which waited for: 9 -> 7; matrix products, arithmetic and copies ran while one was open for 19% -> 1% of each run, Pallas kernels for 7% -> 9%
where the time goes in v2:
time: 186 us
  waiting for transfers between devices  118 us (63%)
  Pallas kernels  19.1 us (10%)
  local copies, waits for them, and re-layouts  16.4 us (9%)
  between operations  13.8 us (7%)
  blocking collectives  8.65 us (5%)
  starting transfers between devices  7.79 us (4%)
  other arithmetic  2.22 us (1%)
    all_gather x3, waiting for transfers between devices, gathered(): return lax.all_gather(value, 'expert', axis=0, tiled=True)  83.9 us
    pallas_call x4, Pallas kernels, local_call(): pl.pallas_call(kernel, out_shape=out_shapes, in_specs=specs, scratch_shap...  19.1 us
    ppermute x2, waiting for transfers between devices, passed_along(): return lax.ppermute(value, axis, pairs)  18.1 us
    unnamed x30, local copies, waits for them, and re-layouts  16.4 us
    ppermute x6, waiting for transfers between devices, swapped(): return lax.ppermute(value, axis, pairs)  14.7 us
    all_gather x1, blocking collectives, per_device(): lax.all_gather(jnp.concatenate([f_routes.astype(jnp.float32), f_gates, b_...  8.65 us
    ppermute x6, starting transfers between devices, swapped(): return lax.ppermute(value, axis, pairs)  7.11 us
  transfers between devices with their start and end apart: 11, of which 7 were waited for; matrix products, arithmetic and copies ran while one was open for 1% of the time, Pallas kernels for 9%

profile of v2, /device:TPU:0, one launch (start us, length us, event | category | flops | bytes accessed | tf_op | source)
XLA Modules:
  0.0 185.5 jit_solution(15326323483127945210)
XLA Ops:
  7.2 0.0 all-gather.6.cloned.1.call-start
  7.2 0.5 collective-permute-start
  7.7 11.1 %collective-permute-done.layer_ref = bf16[128,2048]{1,0:T(8,128)(2,1)S(1)} collective-permute-done((bf16[128,2048]{1,0:T(8,128)(2,1)}, bf16[128,2048]{1,0:T(8,128)(2,1)S(1)}, u32[]{:S(2)}, u32[]{:S(2)}) %collective-permute-start) | collective-permute-done | bytes 524320 | tf_op jit(solution)/shard_map/ppermute | solution.py:17
  18.8 0.0 copy-start.1
  18.8 0.8 copy-done.1
  19.6 0.0 all-gather.6.cloned.1.call-update
  19.6 0.0 all-gather.10.cloned.1.call-start
  19.7 0.7 all-gather.10.cloned.1.call-update
  20.4 0.0 all-gather.8.cloned.1.call-start
  20.4 0.1 collective-permute-start.4
  20.5 7.0 %collective-permute-done.4.grads_ref = bf16[128,2048]{1,0:T(8,128)(2,1)S(1)} collective-permute-done((bf16[128,2048]{1,0:T(8,128)(2,1)}, bf16[128,2048]{1,0:T(8,128)(2,1)S(1)}, u32[]{:S(2)}, u32[]{:S(2)}) %collective-permute-start.4) | collective-permute-done | bytes 524320 | tf_op jit(solution)/shard_map/ppermute | solution.py:17
  27.5 0.0 copy-start.3
  27.5 0.8 copy-done.3
  28.3 0.0 all-gather.8.cloned.1.call-update
  28.4 0.8 xor_bitcast_fusion
  29.1 0.8 convert_bitcast_fusion.1
  29.9 0.7 pad_maximum_fusion
  30.6 8.7 %all-gather = f32[32,128]{1,0:T(8,128)S(1)} all-gather(f32[8,128]{1,0:T(8,128)S(1)} %pad_maximum_fusion), channel_id=2, replica_groups=mesh['section'=8,'expert'=4] {'expert'}, dimensions={0}, use_global_device_ids=true | all-gather | bytes 20480 | tf_op jit(solution)/shard_map/all_gather | solution.py:282
  39.2 15.9 %all-gather.6.cloned.1.call-done.values_ref = bf16[512,2048]{1,0:T(8,128)(2,1)} async-done(((bf16[128,2048]{1,0:T(8,128)(2,1)}), bf16[512,2048]{1,0:T(8,128)(2,1)}) %all-gather.6.cloned.1.call-update) | async-done | bytes 2097168 | tf_op jit(solution)/shard_map/all_gather | solution.py:280
  55.2 0.0 copy-start.5
  55.2 0.7 copy-done.5
  55.9 0.0 copy-start.8
  55.9 2.8 %copy-done.8 = bf16[1,1,2048,1536]{3,2,1,0:T(8,128)(2,1)S(1)} copy-done((bf16[1,1,2048,1536]{3,2,1,0:T(8,128)(2,1)S(1)}, bf16[1,1,2048,1536]{3,2,1,0:T(8,128)(2,1)}, u32[]{:S(2)}) %copy-start.8) | copy-done | bytes 6291480
  58.6 0.0 copy-start.10
  58.6 1.9 %copy-done.10 = bf16[1,1,768,2048]{3,2,1,0:T(8,128)(2,1)S(1)} copy-done((bf16[1,1,768,2048]{3,2,1,0:T(8,128)(2,1)S(1)}, bf16[1,1,768,2048]{3,2,1,0:T(8,128)(2,1)}, u32[]{:S(2)}) %copy-start.10) | copy-done | bytes 3145752
  60.5 0.0 copy-start.13
  60.5 1.6 copy-done.13
  62.1 0.0 copy-start.6
  62.1 5.0 %shard_map.113 = (bf16[96,2048]{1,0:T(8,128)(2,1)S(1)}, bf16[96,2048]{1,0:T(8,128)(2,1)S(1)}, bf16[96,2048]{1,0:T(8,128)(2,1)S(1)}, bf16[96,2048]{1,0:T(8,128)(2,1)S(1)}) custom-call(s32[1]{0:T(128)} %bitcast.5.me_ref, bf16[512,2048]{1,0:T(8,128)(2,1)S(1)} %copy-done.13, f32[4,8,128]{2,1,0:T(8,128)S(1)} %bitcast.33, f32[1,2048]{1,0:T(1,128)S(1)} %copy-done.5, ...), custom_call_target="tpu_custom_call" | custom-call | flops 3623878656 | bytes 14155776 | tf_op jit(solution)/shard_map/pallas_call | solution.py:241
  67.2 1.5 collective-permute-start.1
  68.7 0.6 collective-permute-start.2
  69.3 1.5 collective-permute-start.3
  70.7 31.5 %all-gather.10.cloned.1.call-done = bf16[1,512,2048]{2,1,0:T(8,128)(2,1)} async-done(((bf16[1,128,2048]{2,1,0:T(8,128)(2,1)}), bf16[1,512,2048]{2,1,0:T(8,128)(2,1)}) %all-gather.10.cloned.1.call-update) | async-done | bytes 2097168 | tf_op jit(solution)/shard_map/all_gather | solution.py:280
  102.2 36.6 %all-gather.8.cloned.1.call-done.grad_in_ref = bf16[512,2048]{1,0:T(8,128)(2,1)} async-done(((bf16[128,2048]{1,0:T(8,128)(2,1)}), bf16[512,2048]{1,0:T(8,128)(2,1)}) %all-gather.8.cloned.1.call-update) | async-done | bytes 2097168 | tf_op jit(solution)/shard_map/all_gather | solution.py:280
  138.7 0.0 copy-done.6
  138.8 0.0 copy-start.9
  138.8 2.8 %copy-done.9 = bf16[1,1,2048,1536]{3,2,1,0:T(8,128)(2,1)S(1)} copy-done((bf16[1,1,2048,1536]{3,2,1,0:T(8,128)(2,1)S(1)}, bf16[1,1,2048,1536]{3,2,1,0:T(8,128)(2,1)}, u32[]{:S(2)}) %copy-start.9) | copy-done | bytes 6291480
  141.5 0.0 copy-start.11
  141.5 1.9 %copy-done.11 = bf16[1,1,768,2048]{3,2,1,0:T(8,128)(2,1)S(1)} copy-done((bf16[1,1,768,2048]{3,2,1,0:T(8,128)(2,1)S(1)}, bf16[1,1,768,2048]{3,2,1,0:T(8,128)(2,1)}, u32[]{:S(2)}) %copy-start.11) | copy-done | bytes 3145752
  143.4 0.0 copy-start.12
  143.4 1.6 copy-done.12
  145.0 0.0 copy-start.14
  145.0 1.6 copy-done.14
  146.6 0.0 copy-start.2
  146.6 0.0 copy-start.7
  146.6 9.9 %shard_map.115 = (bf16[96,2048]{1,0:T(8,128)(2,1)S(1)}, bf16[96,2048]{1,0:T(8,128)(2,1)S(1)}, bf16[96,2048]{1,0:T(8,128)(2,1)S(1)}, bf16[96,2048]{1,0:T(8,128)(2,1)S(1)}) custom-call(s32[1]{0:T(128)} %bitcast.5.me_ref, bf16[512,2048]{1,0:T(8,128)(2,1)S(1)} %bitcast.41, bf16[512,2048]{1,0:T(8,128)(2,1)S(1)} %copy-done.14, f32[4,8,128]{2,1,0:T(8,128)S(1)} %bitcast.34, ...), custom_call_target="tpu_custom_call" | custom-call | flops 6039797760 | bytes 14155776 | tf_op jit(solution)/shard_map/pallas_call | solution.py:241
  156.5 0.0 copy-start
  156.5 0.0 copy-start.4
  156.5 1.5 collective-permute-start.5
  158.1 0.6 collective-permute-start.6
  158.6 0.0 collective-permute-done.1.refs_1_
  158.6 1.5 collective-permute-start.7
  160.1 0.0 collective-permute-done.2.refs_2_
  160.1 0.0 collective-permute-done.3.refs_3_
  160.1 0.0 copy-done.2
  160.1 0.0 copy-done.7
  160.1 2.2 %shard_map.114 = bf16[128,2048]{1,0:T(8,128)(2,1)} custom-call(bf16[128,2048]{1,0:T(8,128)(2,1)S(1)} %copy-done.2, s32[2,128]{1,0:T(2,128)S(1)} %get-tuple-element.21.routes_ref, f32[2,128]{1,0:T(2,128)S(1)} %bitcast.36, bf16[96,2048]{1,0:T(8,128)(2,1)S(1)} %get-tuple-element.10.refs_0_, bf16[96,2048]{1,0:T(8,128)(2,1)S(1)} %collective-permute-done.1.refs_1_, ...), custom_call_target="tpu_custom_call" | custom-call | flops 402653184 | bytes 2097152 | tf_op jit(solution)/shard_map/pallas_call | solution.py:241
  162.3 6.3 %collective-permute-done.5.refs_1_ = bf16[96,2048]{1,0:T(8,128)(2,1)S(1)} collective-permute-done((bf16[96,2048]{1,0:T(8,128)(2,1)S(1)}, bf16[96,2048]{1,0:T(8,128)(2,1)S(1)}, u32[]{:S(2)}, u32[]{:S(2)}) %collective-permute-start.5) | collective-permute-done | bytes 393248 | tf_op jit(solution)/shard_map/ppermute | solution.py:23
  168.6 8.5 %collective-permute-done.6.refs_2_ = bf16[96,2048]{1,0:T(8,128)(2,1)S(1)} collective-permute-done((bf16[96,2048]{1,0:T(8,128)(2,1)S(1)}, bf16[96,2048]{1,0:T(8,128)(2,1)S(1)}, u32[]{:S(2)}, u32[]{:S(2)}) %collective-permute-start.6) | collective-permute-done | bytes 393248 | tf_op jit(solution)/shard_map/ppermute | solution.py:23
  177.1 0.0 collective-permute-done.7.refs_3_
  177.1 0.0 copy-done
  177.1 0.0 copy-done.4
  177.1 1.9 %shard_map.116 = bf16[128,2048]{1,0:T(8,128)(2,1)} custom-call(bf16[128,2048]{1,0:T(8,128)(2,1)S(1)} %copy-done.4, bf16[128,2048]{1,0:T(8,128)(2,1)S(1)} %bitcast.32, f32[1,2048]{1,0:T(1,128)S(1)} %copy-done.6, s32[2,128]{1,0:T(2,128)S(1)} %get-tuple-element.18.routes_ref, bf16[96,2048]{1,0:T(8,128)(2,1)S(1)} %get-tuple-element.14.refs_0_, ...), custom_call_target="tpu_custom_call" | custom-call | flops 201326592 | bytes 2097152 | tf_op jit(solution)/shard_map/pallas_call | solution.py:241
Async XLA Ops:
  7.2 48.0 %all-gather.6.cloned.1.call-start = ((), (), s32[]{:S(2)}) async-start(), calls=%async_computation | async-start | bytes 2621440 | tf_op jit(solution)/shard_map/all_gather | solution.py:280
  7.2 11.6 %collective-permute-start = (bf16[128,2048]{1,0:T(8,128)(2,1)}, bf16[128,2048]{1,0:T(8,128)(2,1)S(1)}, u32[]{:S(2)}, u32[]{:S(2)}) collective-permute-start(bf16[128,2048]{1,0:T(8,128)(2,1)} %bitcast.45), channel_id=1, source_target_pairs={{0,4},{4,8},{8,12},{12,16},{16,20},{20,24},{24,28},{28,0},{1,5},{5... | collective-permute-start | bytes 1572872 | tf_op jit(solution)/shard_map/ppermute | solution.py:17
  18.8 0.8 copy-start.1
  19.6 82.5 %all-gather.10.cloned.1.call-start = ((), (), s32[]{:S(2)}) async-start(), calls=%async_computation.2 | async-start | bytes 2621440 | tf_op jit(solution)/shard_map/all_gather | solution.py:280
  20.4 118.3 %all-gather.8.cloned.1.call-start = ((), (), s32[]{:S(2)}) async-start(), calls=%async_computation.1 | async-start | bytes 2621440 | tf_op jit(solution)/shard_map/all_gather | solution.py:280
  20.4 7.1 %collective-permute-start.4 = (bf16[128,2048]{1,0:T(8,128)(2,1)}, bf16[128,2048]{1,0:T(8,128)(2,1)S(1)}, u32[]{:S(2)}, u32[]{:S(2)}) collective-permute-start(bf16[128,2048]{1,0:T(8,128)(2,1)} %bitcast.46), channel_id=1, source_target_pairs={{0,28},{4,0},{8,4},{12,8},{16,12},{20,16},{24,20},{28,24},{1,29},{... | collective-permute-start | bytes 1572872 | tf_op jit(solution)/shard_map/ppermute | solution.py:17
  27.5 0.8 copy-start.3
  55.2 0.7 copy-start.5
  55.9 2.8 %copy-start.8 = (bf16[1,1,2048,1536]{3,2,1,0:T(8,128)(2,1)S(1)}, bf16[1,1,2048,1536]{3,2,1,0:T(8,128)(2,1)}, u32[]{:S(2)}) copy-start(bf16[1,1,2048,1536]{3,2,1,0:T(8,128)(2,1)} %param.18) | copy-start | bytes 18874372
  58.6 1.9 %copy-start.10 = (bf16[1,1,768,2048]{3,2,1,0:T(8,128)(2,1)S(1)}, bf16[1,1,768,2048]{3,2,1,0:T(8,128)(2,1)}, u32[]{:S(2)}) copy-start(bf16[1,1,768,2048]{3,2,1,0:T(8,128)(2,1)} %param.19) | copy-start | bytes 9437188
  60.5 1.6 copy-start.13
  62.1 76.6 %copy-start.6 = (f32[1,2048]{1,0:T(1,128)S(1)}, f32[1,2048]{1,0:T(1,128)}, u32[]{:S(2)}) copy-start(f32[1,2048]{1,0:T(1,128)} %gain_ref.5) | copy-start | bytes 24580
  67.2 91.5 %collective-permute-start.1 = (bf16[96,2048]{1,0:T(8,128)(2,1)S(1)}, bf16[96,2048]{1,0:T(8,128)(2,1)S(1)}, u32[]{:S(2)}, u32[]{:S(2)}) collective-permute-start(bf16[96,2048]{1,0:T(8,128)(2,1)S(1)} %get-tuple-element.11), channel_id=1, source_target_pairs={{0,1},{1,0},{2,3},{3,2},{4,5},{5,4},{6,7},{7,6},{8,9},{9,8},{10,11... | collective-permute-start | bytes 1179656 | tf_op jit(solution)/shard_map/ppermute | solution.py:23
  68.7 91.4 %collective-permute-start.2 = (bf16[96,2048]{1,0:T(8,128)(2,1)S(1)}, bf16[96,2048]{1,0:T(8,128)(2,1)S(1)}, u32[]{:S(2)}, u32[]{:S(2)}) collective-permute-start(bf16[96,2048]{1,0:T(8,128)(2,1)S(1)} %get-tuple-element.12), channel_id=1, source_target_pairs={{0,2},{1,3},{2,0},{3,1},{4,6},{5,7},{6,4},{7,5},{8,10},{9,11},{10,... | collective-permute-start | bytes 1179656 | tf_op jit(solution)/shard_map/ppermute | solution.py:23
  69.3 90.8 %collective-permute-start.3 = (bf16[96,2048]{1,0:T(8,128)(2,1)S(1)}, bf16[96,2048]{1,0:T(8,128)(2,1)S(1)}, u32[]{:S(2)}, u32[]{:S(2)}) collective-permute-start(bf16[96,2048]{1,0:T(8,128)(2,1)S(1)} %get-tuple-element.13), channel_id=1, source_target_pairs={{0,3},{1,2},{2,1},{3,0},{4,7},{5,6},{6,5},{7,4},{8,11},{9,10},{10,... | collective-permute-start | bytes 1179656 | tf_op jit(solution)/shard_map/ppermute | solution.py:23
  138.8 2.8 %copy-start.9 = (bf16[1,1,2048,1536]{3,2,1,0:T(8,128)(2,1)S(1)}, bf16[1,1,2048,1536]{3,2,1,0:T(8,128)(2,1)}, u32[]{:S(2)}) copy-start(bf16[1,1,2048,1536]{3,2,1,0:T(8,128)(2,1)} %param.18) | copy-start | bytes 18874372
  141.5 1.9 %copy-start.11 = (bf16[1,1,768,2048]{3,2,1,0:T(8,128)(2,1)S(1)}, bf16[1,1,768,2048]{3,2,1,0:T(8,128)(2,1)}, u32[]{:S(2)}) copy-start(bf16[1,1,768,2048]{3,2,1,0:T(8,128)(2,1)} %param.19) | copy-start | bytes 9437188
  143.4 1.6 copy-start.12
  145.0 1.6 copy-start.14
  146.6 13.5 %copy-start.2 = (bf16[128,2048]{1,0:T(8,128)(2,1)S(1)}, bf16[128,2048]{1,0:T(8,128)(2,1)}, u32[]{:S(2)}) copy-start(bf16[128,2048]{1,0:T(8,128)(2,1)} %copy-done.1) | copy-start | bytes 1572868
  146.6 13.5 %copy-start.7 = (f32[1,128,2]{1,2,0:T(2,128)S(1)}, f32[1,128,2]{1,2,0:T(2,128)}, u32[]{:S(2)}) copy-start(f32[1,128,2]{1,2,0:T(2,128)} %param.14) | copy-start | bytes 3076
  156.5 20.6 %copy-start = (bf16[1,128,2048]{2,1,0:T(8,128)(2,1)S(1)}, bf16[1,128,2048]{2,1,0:T(8,128)(2,1)}, u32[]{:S(2)}) copy-start(bf16[1,128,2048]{2,1,0:T(8,128)(2,1)} %param.12) | copy-start | bytes 1572868
  156.5 20.6 %copy-start.4 = (bf16[128,2048]{1,0:T(8,128)(2,1)S(1)}, bf16[128,2048]{1,0:T(8,128)(2,1)}, u32[]{:S(2)}) copy-start(bf16[128,2048]{1,0:T(8,128)(2,1)} %copy-done.3) | copy-start | bytes 1572868
  156.5 12.1 %collective-permute-start.5 = (bf16[96,2048]{1,0:T(8,128)(2,1)S(1)}, bf16[96,2048]{1,0:T(8,128)(2,1)S(1)}, u32[]{:S(2)}, u32[]{:S(2)}) collective-permute-start(bf16[96,2048]{1,0:T(8,128)(2,1)S(1)} %get-tuple-element.15), channel_id=1, source_target_pairs={{0,1},{1,0},{2,3},{3,2},{4,5},{5,4},{6,7},{7,6},{8,9},{9,8},{10,11... | collective-permute-start | bytes 1179656 | tf_op jit(solution)/shard_map/ppermute | solution.py:23
  158.1 19.0 %collective-permute-start.6 = (bf16[96,2048]{1,0:T(8,128)(2,1)S(1)}, bf16[96,2048]{1,0:T(8,128)(2,1)S(1)}, u32[]{:S(2)}, u32[]{:S(2)}) collective-permute-start(bf16[96,2048]{1,0:T(8,128)(2,1)S(1)} %get-tuple-element.16), channel_id=1, source_target_pairs={{0,2},{1,3},{2,0},{3,1},{4,6},{5,7},{6,4},{7,5},{8,10},{9,11},{10,... | collective-permute-start | bytes 1179656 | tf_op jit(solution)/shard_map/ppermute | solution.py:23
  158.6 18.4 %collective-permute-start.7 = (bf16[96,2048]{1,0:T(8,128)(2,1)S(1)}, bf16[96,2048]{1,0:T(8,128)(2,1)S(1)}, u32[]{:S(2)}, u32[]{:S(2)}) collective-permute-start(bf16[96,2048]{1,0:T(8,128)(2,1)S(1)} %get-tuple-element.17), channel_id=1, source_target_pairs={{0,3},{1,2},{2,1},{3,0},{4,7},{5,6},{6,5},{7,4},{8,11},{9,10},{10,... | collective-permute-start | bytes 1179656 | tf_op jit(solution)/shard_map/ppermute | solution.py:23
Sparse Core Ops, SparseCore 0:
  19.8 35.3 all-gather.5
  57.0 45.1 all-gather.9
  104.0 34.6 all-gather.7

commit v3 on v1

--- a/solution.py
+++ b/solution.py
@@ -8,7 +8,7 @@
 from jax.sharding import PartitionSpec as P
 
 EPS = 1e-06
-VMEM_LIMIT = 48 * 1024 * 1024
+VMEM_LIMIT = 32 * 1024 * 1024
 
 
 def passed_along(value, axis, steps):
@@ -135,39 +135,118 @@
     ).astype(jnp.bfloat16)
 
 
-def local_call(kernel, out_shapes, flops, moved):
+def joined(refs):
+    rows = [ref[...] for ref in refs]
+    if rows[0].shape[0] % 16 == 0:
+        return jnp.concatenate(rows, axis=0)
+    return jnp.concatenate([r.astype(jnp.float32) for r in rows], axis=0).astype(jnp.bfloat16)
+
+
+def tiles(size, step):
+    return [(start, min(step, size - start)) for start in range(0, size, step)]
+
+
+def expert_fwd_kernel(*refs):
+    expert_count = (len(refs) - 4) // 2
+    row_refs = refs[:expert_count]
+    weight_in, weight_out = refs[expert_count : expert_count + 2]
+    out_refs = refs[expert_count + 2 : 2 * expert_count + 2]
+    rows_ref, hidden_ref = refs[-2:]
+    capacity = row_refs[0].shape[0]
+    hidden_units, features = weight_out.shape
+    rows_ref[...] = joined(row_refs)
+    for start, size in tiles(hidden_units, 256):
+        gate = jnp.dot(
+            rows_ref[...], weight_in[:, start : start + size], preferred_element_type=jnp.float32
+        )
+        up = jnp.dot(
+            rows_ref[...],
+            weight_in[:, hidden_units + start : hidden_units + start + size],
+            preferred_element_type=jnp.float32,
+        )
+        hidden_ref[:, start : start + size] = (gate / (1.0 + jnp.exp(-gate)) * up).astype(
+            jnp.bfloat16
+        )
+    for start, size in tiles(features, 512):
+        out = jnp.dot(
+            hidden_ref[...], weight_out[:, start : start + size], preferred_element_type=jnp.float32
+        )
+        for d in range(expert_count):
+            out_refs[d][:, start : start + size] = out[d * capacity : (d + 1) * capacity].astype(
+                jnp.bfloat16
+            )
+
+
+def expert_again_kernel(*refs):
+    expert_count = len(refs) - 4
+    row_refs = refs[:expert_count]
+    weight_in, gate_ref, up_ref, rows_ref = refs[expert_count:]
+    hidden_units = gate_ref.shape[1]
+    rows_ref[...] = joined(row_refs)
+    for start, size in tiles(hidden_units, 256):
+        gate_ref[:, start : start + size] = jnp.dot(
+            rows_ref[...], weight_in[:, start : start + size], preferred_element_type=jnp.float32
+        )
+        up_ref[:, start : start + size] = jnp.dot(
+            rows_ref[...],
+            weight_in[:, hidden_units + start : hidden_units + start + size],
+            preferred_element_type=jnp.float32,
+        )
+
+
+def expert_bwd_kernel(*refs):
+    expert_count = (len(refs) - 6) // 2
+    grad_refs = refs[:expert_count]
+    gate_ref, up_ref, weight_in, weight_out = refs[expert_count : expert_count + 4]
+    out_refs = refs[expert_count + 4 : 2 * expert_count + 4]
+    grads_ref, both_ref = refs[-2:]
+    capacity = grad_refs[0].shape[0]
+    hidden_units, features = weight_out.shape
+    grads_ref[...] = joined(grad_refs)
+    for start, size in tiles(hidden_units, 256):
+        gate = gate_ref[:, start : start + size]
+        up = up_ref[:, start : start + size]
+        d_hidden = lax.dot_general(
+            grads_ref[...],
+            weight_out[start : start + size, :],
+            (((1,), (1,)), ((), ())),
+            preferred_element_type=jnp.float32,
+        )
+        sig = 1.0 / (1.0 + jnp.exp(-gate))
+        both_ref[:, start : start + size] = (
+            d_hidden * up * sig * (1.0 + gate * (1.0 - sig))
+        ).astype(jnp.bfloat16)
+        both_ref[:, hidden_units + start : hidden_units + start + size] = (
+            d_hidden * gate * sig
+        ).astype(jnp.bfloat16)
+    for start, size in tiles(features, 512):
+        out = lax.dot_general(
+            both_ref[...],
+            weight_in[start : start + size, :],
+            (((1,), (1,)), ((), ())),
+            preferred_element_type=jnp.float32,
+        )
+        for d in range(expert_count):
+            out_refs[d][:, start : start + size] = out[d * capacity : (d + 1) * capacity].astype(
+                jnp.bfloat16
+            )
+
+
+def local_call(kernel, out_shapes, inputs, flops, moved, scratch=(), after=()):
+    in_specs = [pl.BlockSpec(memory_space=pltpu.VMEM)] * len(inputs)
+    held = len(inputs)
+
+    def body(*refs):
+        kernel(*refs[:held], *refs[held + len(after) :])
+
     return pl.pallas_call(
-        kernel,
+        body if after else kernel,
         out_shape=out_shapes,
+        in_specs=in_specs + [pl.BlockSpec(memory_space=pl.ANY)] * len(after),
+        scratch_shapes=list(scratch),
         compiler_params=pltpu.CompilerParams(vmem_limit_bytes=VMEM_LIMIT),
         cost_estimate=pl.CostEstimate(flops=flops, bytes_accessed=moved, transcendentals=0),
-    )
-
-
-def expert_forward(in_rows, weight_in, weight_out, hidden_units):
-    projected = jnp.dot(in_rows, weight_in, preferred_element_type=jnp.float32)
-    hidden = (jax.nn.silu(projected[:, :hidden_units]) * projected[:, hidden_units:]).astype(
-        jnp.bfloat16
-    )
-    return jnp.dot(hidden, weight_out, preferred_element_type=jnp.float32).astype(jnp.bfloat16)
-
-
-def expert_backward(in_rows, grad_rows, weight_in, weight_out, hidden_units):
-    projected = jnp.dot(in_rows, weight_in, preferred_element_type=jnp.float32)
-    gate_pre = projected[:, :hidden_units]
-    up_pre = projected[:, hidden_units:]
-    d_hidden = lax.dot_general(
-        grad_rows, weight_out, (((1,), (1,)), ((), ())), preferred_element_type=jnp.float32
-    )
-    sigmoid_gate = 1.0 / (1.0 + jnp.exp(-gate_pre))
-    d_gate = (d_hidden * up_pre * sigmoid_gate * (1.0 + gate_pre * (1.0 - sigmoid_gate))).astype(
-        jnp.bfloat16
-    )
-    d_up = (d_hidden * gate_pre * sigmoid_gate).astype(jnp.bfloat16)
-    d_both = jnp.concatenate([d_gate, d_up], axis=1)
-    return lax.dot_general(
-        d_both, weight_in, (((1,), (1,)), ((), ())), preferred_element_type=jnp.float32
-    ).astype(jnp.bfloat16)
+    )(*inputs, *after)
 
 
 def per_device(
@@ -204,26 +283,67 @@
     whole = jax.ShapeDtypeStruct((tok_rows, features), jnp.bfloat16)
     one_dot = 2 * expert_count * capacity * tok_rows * features
     moved = 2 * features * (tok_rows + expert_count * capacity)
-    normed_call = local_call(normed_kernel, [block] * expert_count, one_dot, moved)
-    grads_call = local_call(grads_kernel, [block] * expert_count, 2 * one_dot, moved)
-    fwd_end = local_call(fwd_end_kernel, whole, 2 * one_dot, moved)
-    bwd_end = local_call(bwd_end_kernel, whole, one_dot, moved)
-
-    b_rows = exchanged(normed_call(saved, b_routes, gain_row), "expert")
-    f_rows = exchanged(normed_call(layer_in, f_routes, gain_row), "expert")
-    g_rows = exchanged(grads_call(grad_in, b_routes, b_gates), "expert")
-
-    def cut(rows):
-        return [rows[d * capacity : (d + 1) * capacity] for d in range(expert_count)]
-
-    f_done = expert_forward(jnp.concatenate(f_rows), weight_in, weight_out, hidden_units)
-    f_back = exchanged(cut(f_done), "expert")
-    b_done = expert_backward(
-        jnp.concatenate(b_rows), jnp.concatenate(g_rows), weight_in, weight_out, hidden_units
-    )
-    b_back = exchanged(cut(b_done), "expert")
-    fwd_block = fwd_end(layer_in, f_routes, f_gates, *f_back)
-    bwd_block = bwd_end(grad_in, saved, gain_row, b_routes, *b_back)
+    slot_total = expert_count * capacity
+    blocks = [block] * expert_count
+    expert_flops = 2 * slot_total * features * hidden_units
+    expert_moved = 2 * features * (3 * hidden_units + 3 * slot_total)
+    rows_scratch = pltpu.VMEM((slot_total, features), jnp.bfloat16)
+
+    b_sent = local_call(normed_kernel, blocks, (saved, b_routes, gain_row), one_dot, moved)
+    b_rows = exchanged(b_sent, "expert")
+    f_sent = local_call(
+        normed_kernel, blocks, (layer_in, f_routes, gain_row), one_dot, moved, after=(b_sent[0],)
+    )
+    f_rows = exchanged(f_sent, "expert")
+    g_sent = local_call(
+        grads_kernel, blocks, (grad_in, b_routes, b_gates), 2 * one_dot, moved, after=(f_sent[0],)
+    )
+    g_rows = exchanged(g_sent, "expert")
+    projected = jax.ShapeDtypeStruct((slot_total, hidden_units), jnp.float32)
+    gate_pre, up_pre = local_call(
+        expert_again_kernel,
+        [projected, projected],
+        (*b_rows, weight_in),
+        2 * expert_flops,
+        expert_moved,
+        scratch=(rows_scratch,),
+        after=(g_sent[0],),
+    )
+    f_done = local_call(
+        expert_fwd_kernel,
+        blocks,
+        (*f_rows, weight_in, weight_out),
+        3 * expert_flops,
+        expert_moved,
+        scratch=(rows_scratch, pltpu.VMEM((slot_total, hidden_units), jnp.bfloat16)),
+        after=(gate_pre,),
+    )
+    f_back = exchanged(f_done, "expert")
+    b_done = local_call(
+        expert_bwd_kernel,
+        blocks,
+        (*g_rows, gate_pre, up_pre, weight_in, weight_out),
+        3 * expert_flops,
+        expert_moved,
+        scratch=(rows_scratch, pltpu.VMEM((slot_total, 2 * hidden_units), jnp.bfloat16)),
+        after=(f_back[1],),
+    )
+    b_back = exchanged(b_done, "expert")
+    fwd_block = local_call(
+        fwd_end_kernel,
+        whole,
+        (layer_in, f_routes, f_gates, *f_back),
+        2 * one_dot,
+        moved,
+        after=(b_done[0],),
+    )
+    bwd_block = local_call(
+        bwd_end_kernel,
+        whole,
+        (grad_in, saved, gain_row, b_routes, *b_back),
+        one_dot,
+        moved,
+    )
     return (fwd_block[None], bwd_block[None])
 
 

time: 98.1 us -> 97.4 us (level); the launches traced: 96.4 us -> 97.1 us
  matrix products: 17 us -> 0 us
  Pallas kernels: 8.86 us -> 18.1 us
  waiting for transfers between devices: 39 us -> 44.8 us
  local copies, waits for them, and re-layouts: 2.74 us -> 5.22 us
    dot_general x5 -> x0, matrix products: 17 us -> none  [the longest x1 6.82 us: expert_backward(): projected = jnp.dot(in_rows, weight_in, preferred_element_type=jnp.float32)]
    pallas_call x5 -> x8, Pallas kernels: 8.86 us -> 18.1 us  [local_call(): pl.pallas_call(body if after else kernel, out_shape=out_shapes, in_specs=...]
    ppermute x15, waiting for transfers between devices: 38.8 us -> 42.2 us  [swapped(): return lax.ppermute(value, axis, pairs)]
    unnamed x22 -> x18, local copies, waits for them, and re-layouts: 2.46 us -> 5.22 us
    ppermute x2, waiting for transfers between devices: 0.22 us -> 2.54 us  [passed_along(): return lax.ppermute(value, axis, pairs)]
  transfers between devices with their start and end apart: 17 -> 17, of which waited for: 9 -> 15; matrix products, arithmetic and copies ran while one was open for 19% -> 1% of each run, Pallas kernels for 7% -> 17%
where the time goes in v3:
time: 97.4 us; the launch traced here: 97.1 us
  waiting for transfers between devices  44.8 us (46%)
  starting transfers between devices  26.9 us (28%)
  Pallas kernels  18.1 us (19%)
  local copies, waits for them, and re-layouts  5.22 us (5%)
  other arithmetic  1.36 us (1%)
    ppermute x15, waiting for transfers between devices, swapped(): return lax.ppermute(value, axis, pairs)  42.2 us
    ppermute x15, starting transfers between devices, swapped(): return lax.ppermute(value, axis, pairs)  22.3 us
    pallas_call x8, Pallas kernels, local_call(): pl.pallas_call(body if after else kernel, out_shape=out_shapes, in_specs=...  18.1 us
    unnamed x18, local copies, waits for them, and re-layouts  5.22 us
    ppermute x2, starting transfers between devices, passed_along(): return lax.ppermute(value, axis, pairs)  4.61 us
    ppermute x2, waiting for transfers between devices, passed_along(): return lax.ppermute(value, axis, pairs)  2.54 us
  transfers between devices with their start and end apart: 17, of which 15 were waited for; matrix products, arithmetic and copies ran while one was open for 1% of the time, Pallas kernels for 17%

profile of v3, /device:TPU:0, one launch (start us, length us, event | category | flops | bytes accessed | tf_op | source)
XLA Modules:
  0.0 97.1 jit_solution(6095405297054872205)
XLA Ops:
  0.6 0.5 collective-permute-start
  1.1 4.1 %collective-permute-start.7 = (bf16[128,2048]{1,0:T(8,128)(2,1)}, bf16[128,2048]{1,0:T(8,128)(2,1)S(1)}, u32[]{:S(2)}, u32[]{:S(2)}) collective-permute-start(bf16[128,2048]{1,0:T(8,128)(2,1)} %bitcast.33), channel_id=1, source_target_pairs={{0,28},{4,0},{8,4},{12,8},{16,12},{20,16},{24,20},{28,24},{1,29},{... | collective-permute-start | bytes 1572872 | tf_op jit(solution)/shard_map/ppermute | solution.py:17
  5.2 0.7 xor_bitcast_fusion.routes_ref.refs_1_
  5.9 0.0 copy-start.3
  5.9 1.0 %copy-done.3 = bf16[1,128,2048]{2,1,0:T(8,128)(2,1)S(1)} copy-done((bf16[1,128,2048]{2,1,0:T(8,128)(2,1)S(1)}, bf16[1,128,2048]{2,1,0:T(8,128)(2,1)}, u32[]{:S(2)}) %copy-start.3) | copy-done | bytes 524312
  7.0 0.0 copy-start.5
  7.0 0.7 copy-done.5
  7.7 0.0 copy-start.2
  7.7 0.8 shard_map.113
  8.4 2.0 %collective-permute-start.4 = (bf16[96,2048]{1,0:T(8,128)(2,1)S(1)}, bf16[96,2048]{1,0:T(8,128)(2,1)S(1)}, u32[]{:S(2)}, u32[]{:S(2)}) collective-permute-start(bf16[96,2048]{1,0:T(8,128)(2,1)S(1)} %get-tuple-element.29), channel_id=1, source_target_pairs={{0,1},{1,0},{2,3},{3,2},{4,5},{5,4},{6,7},{7,6},{8,9},{9,8},{10,11... | collective-permute-start | bytes 1179656 | tf_op jit(solution)/shard_map/ppermute | solution.py:23
  10.4 1.5 %collective-permute-start.5 = (bf16[96,2048]{1,0:T(8,128)(2,1)S(1)}, bf16[96,2048]{1,0:T(8,128)(2,1)S(1)}, u32[]{:S(2)}, u32[]{:S(2)}) collective-permute-start(bf16[96,2048]{1,0:T(8,128)(2,1)S(1)} %get-tuple-element.30), channel_id=1, source_target_pairs={{0,2},{1,3},{2,0},{3,1},{4,6},{5,7},{6,4},{7,5},{8,10},{9,11},{10,... | collective-permute-start | bytes 1179656 | tf_op jit(solution)/shard_map/ppermute | solution.py:23
  11.9 0.0 collective-permute-start.6
  12.0 0.7 xor_bitcast_fusion.1.refs_1_
  12.7 2.5 %collective-permute-done.refs_0_ = bf16[128,2048]{1,0:T(8,128)(2,1)S(1)} collective-permute-done((bf16[128,2048]{1,0:T(8,128)(2,1)}, bf16[128,2048]{1,0:T(8,128)(2,1)S(1)}, u32[]{:S(2)}, u32[]{:S(2)}) %collective-permute-start) | collective-permute-done | bytes 524320 | tf_op jit(solution)/shard_map/ppermute | solution.py:17
  15.2 0.8 shard_map.114
  16.0 2.5 %collective-permute-start.1 = (bf16[96,2048]{1,0:T(8,128)(2,1)S(1)}, bf16[96,2048]{1,0:T(8,128)(2,1)S(1)}, u32[]{:S(2)}, u32[]{:S(2)}) collective-permute-start(bf16[96,2048]{1,0:T(8,128)(2,1)S(1)} %get-tuple-element.26), channel_id=1, source_target_pairs={{0,1},{1,0},{2,3},{3,2},{4,5},{5,4},{6,7},{7,6},{8,9},{9,8},{10,11... | collective-permute-start | bytes 1179656 | tf_op jit(solution)/shard_map/ppermute | solution.py:23
  18.5 2.0 %collective-permute-done.4.refs_1_ = bf16[96,2048]{1,0:T(8,128)(2,1)S(1)} collective-permute-done((bf16[96,2048]{1,0:T(8,128)(2,1)S(1)}, bf16[96,2048]{1,0:T(8,128)(2,1)S(1)}, u32[]{:S(2)}, u32[]{:S(2)}) %collective-permute-start.4) | collective-permute-done | bytes 393248 | tf_op jit(solution)/shard_map/ppermute | solution.py:23
  20.5 2.0 %collective-permute-start.2 = (bf16[96,2048]{1,0:T(8,128)(2,1)S(1)}, bf16[96,2048]{1,0:T(8,128)(2,1)S(1)}, u32[]{:S(2)}, u32[]{:S(2)}) collective-permute-start(bf16[96,2048]{1,0:T(8,128)(2,1)S(1)} %get-tuple-element.27), channel_id=1, source_target_pairs={{0,2},{1,3},{2,0},{3,1},{4,6},{5,7},{6,4},{7,5},{8,10},{9,11},{10,... | collective-permute-start | bytes 1179656 | tf_op jit(solution)/shard_map/ppermute | solution.py:23
  22.5 0.0 collective-permute-done.7.refs_0_.grads_ref
  22.5 1.4 %collective-permute-start.3 = (bf16[96,2048]{1,0:T(8,128)(2,1)S(1)}, bf16[96,2048]{1,0:T(8,128)(2,1)S(1)}, u32[]{:S(2)}, u32[]{:S(2)}) collective-permute-start(bf16[96,2048]{1,0:T(8,128)(2,1)S(1)} %get-tuple-element.28), channel_id=1, source_target_pairs={{0,3},{1,2},{2,1},{3,0},{4,7},{5,6},{6,5},{7,4},{8,11},{9,10},{10,... | collective-permute-start | bytes 1179656 | tf_op jit(solution)/shard_map/ppermute | solution.py:23
  23.9 0.0 copy-start.8
  23.9 0.7 copy-done.8
  24.6 1.1 %shard_map.115 = (bf16[96,2048]{1,0:T(8,128)(2,1)S(1)}, bf16[96,2048]{1,0:T(8,128)(2,1)S(1)}, bf16[96,2048]{1,0:T(8,128)(2,1)S(1)}, bf16[96,2048]{1,0:T(8,128)(2,1)S(1)}) custom-call(bf16[128,2048]{1,0:T(8,128)(2,1)S(1)} %collective-permute-done.7.refs_0_.grads_ref, s32[2,128]{1,0:T(2,128)S(1)} %xor_bitcast_fusion.routes_ref.refs_1_, f32[2,128]{1,0:T(2,128)S(1)} %bitcast.29, ...), custom_call_target="tpu_custom_call" | custom-call | flops 402653184 | bytes 2097152 | tf_op jit(solution)/shard_map/pallas_call | solution.py:242
  25.7 3.5 %collective-permute-done.5.refs_2_ = bf16[96,2048]{1,0:T(8,128)(2,1)S(1)} collective-permute-done((bf16[96,2048]{1,0:T(8,128)(2,1)S(1)}, bf16[96,2048]{1,0:T(8,128)(2,1)S(1)}, u32[]{:S(2)}, u32[]{:S(2)}) %collective-permute-start.5) | collective-permute-done | bytes 393248 | tf_op jit(solution)/shard_map/ppermute | solution.py:23
  29.3 0.0 collective-permute-start.11
  29.3 1.1 %collective-permute-done.6.refs_3_ = bf16[96,2048]{1,0:T(8,128)(2,1)S(1)} collective-permute-done((bf16[96,2048]{1,0:T(8,128)(2,1)S(1)}, bf16[96,2048]{1,0:T(8,128)(2,1)S(1)}, u32[]{:S(2)}, u32[]{:S(2)}) %collective-permute-start.6) | collective-permute-done | bytes 393248 | tf_op jit(solution)/shard_map/ppermute | solution.py:23
  30.4 1.4 %collective-permute-start.12 = (bf16[96,2048]{1,0:T(8,128)(2,1)S(1)}, bf16[96,2048]{1,0:T(8,128)(2,1)S(1)}, u32[]{:S(2)}, u32[]{:S(2)}) collective-permute-start(bf16[96,2048]{1,0:T(8,128)(2,1)S(1)} %get-tuple-element.39), channel_id=1, source_target_pairs={{0,2},{1,3},{2,0},{3,1},{4,6},{5,7},{6,4},{7,5},{8,10},{9,11},{10,... | collective-permute-start | bytes 1179656 | tf_op jit(solution)/shard_map/ppermute | solution.py:23
  31.8 0.0 copy-start
  31.8 2.8 %copy-done = bf16[1,1,2048,1536]{3,2,1,0:T(8,128)(2,1)S(1)} copy-done((bf16[1,1,2048,1536]{3,2,1,0:T(8,128)(2,1)S(1)}, bf16[1,1,2048,1536]{3,2,1,0:T(8,128)(2,1)}, u32[]{:S(2)}) %copy-start) | copy-done | bytes 6291480
  34.6 0.0 copy-start.1
  34.6 2.6 %shard_map.116 = (f32[384,768]{1,0:T(8,128)S(1)}, f32[384,768]{1,0:T(8,128)S(1)}) custom-call(bf16[96,2048]{1,0:T(8,128)(2,1)S(1)} %get-tuple-element.24.refs_3_.refs_0_, bf16[96,2048]{1,0:T(8,128)(2,1)S(1)} %collective-permute-done.4.refs_1_, bf16[96,2048]{1,0:T(8,128)(2,1)S(1)} %collective-permute-done.5.refs_2_, ...), custom_call_target="tpu_custom_call" | custom-call | flops 2415919104 | bytes 14155776 | tf_op jit(solution)/shard_map/pallas_call | solution.py:242
  37.1 0.3 collective-permute-done.1.refs_1_
  37.4 2.9 %collective-permute-start.13 = (bf16[96,2048]{1,0:T(8,128)(2,1)S(1)}, bf16[96,2048]{1,0:T(8,128)(2,1)S(1)}, u32[]{:S(2)}, u32[]{:S(2)}) collective-permute-start(bf16[96,2048]{1,0:T(8,128)(2,1)S(1)} %get-tuple-element.40), channel_id=1, source_target_pairs={{0,3},{1,2},{2,1},{3,0},{4,7},{5,6},{6,5},{7,4},{8,11},{9,10},{10,... | collective-permute-start | bytes 1179656 | tf_op jit(solution)/shard_map/ppermute | solution.py:23
  40.3 5.8 %collective-permute-done.2.refs_2_ = bf16[96,2048]{1,0:T(8,128)(2,1)S(1)} collective-permute-done((bf16[96,2048]{1,0:T(8,128)(2,1)S(1)}, bf16[96,2048]{1,0:T(8,128)(2,1)S(1)}, u32[]{:S(2)}, u32[]{:S(2)}) %collective-permute-start.2) | collective-permute-done | bytes 393248 | tf_op jit(solution)/shard_map/ppermute | solution.py:23
  46.1 1.2 %collective-permute-done.3.refs_3_ = bf16[96,2048]{1,0:T(8,128)(2,1)S(1)} collective-permute-done((bf16[96,2048]{1,0:T(8,128)(2,1)S(1)}, bf16[96,2048]{1,0:T(8,128)(2,1)S(1)}, u32[]{:S(2)}, u32[]{:S(2)}) %collective-permute-start.3) | collective-permute-done | bytes 393248 | tf_op jit(solution)/shard_map/ppermute | solution.py:23
  47.3 0.0 copy-done.2
  47.3 0.0 copy-done.1
  47.3 3.8 %shard_map.117 = (bf16[96,2048]{1,0:T(8,128)(2,1)S(1)}, bf16[96,2048]{1,0:T(8,128)(2,1)S(1)}, bf16[96,2048]{1,0:T(8,128)(2,1)S(1)}, bf16[96,2048]{1,0:T(8,128)(2,1)S(1)}) custom-call(bf16[96,2048]{1,0:T(8,128)(2,1)S(1)} %get-tuple-element.25.refs_3_.refs_0_, bf16[96,2048]{1,0:T(8,128)(2,1)S(1)} %collective-permute-done.1.refs_1_, ...), custom_call_target="tpu_custom_call" | custom-call | flops 3623878656 | bytes 14155776 | tf_op jit(solution)/shard_map/pallas_call | solution.py:242
  51.1 1.6 %collective-permute-start.8 = (bf16[96,2048]{1,0:T(8,128)(2,1)S(1)}, bf16[96,2048]{1,0:T(8,128)(2,1)S(1)}, u32[]{:S(2)}, u32[]{:S(2)}) collective-permute-start(bf16[96,2048]{1,0:T(8,128)(2,1)S(1)} %get-tuple-element.35), channel_id=1, source_target_pairs={{0,1},{1,0},{2,3},{3,2},{4,5},{5,4},{6,7},{7,6},{8,9},{9,8},{10,11... | collective-permute-start | bytes 1179656 | tf_op jit(solution)/shard_map/ppermute | solution.py:23
  52.7 0.5 collective-permute-start.9
  53.2 1.1 %collective-permute-done.11.refs_1_ = bf16[96,2048]{1,0:T(8,128)(2,1)S(1)} collective-permute-done((bf16[96,2048]{1,0:T(8,128)(2,1)S(1)}, bf16[96,2048]{1,0:T(8,128)(2,1)S(1)}, u32[]{:S(2)}, u32[]{:S(2)}) %collective-permute-start.11) | collective-permute-done | bytes 393248 | tf_op jit(solution)/shard_map/ppermute | solution.py:23
  54.3 2.9 %collective-permute-start.10 = (bf16[96,2048]{1,0:T(8,128)(2,1)S(1)}, bf16[96,2048]{1,0:T(8,128)(2,1)S(1)}, u32[]{:S(2)}, u32[]{:S(2)}) collective-permute-start(bf16[96,2048]{1,0:T(8,128)(2,1)S(1)} %get-tuple-element.37), channel_id=1, source_target_pairs={{0,3},{1,2},{2,1},{3,0},{4,7},{5,6},{6,5},{7,4},{8,11},{9,10},{10,... | collective-permute-start | bytes 1179656 | tf_op jit(solution)/shard_map/ppermute | solution.py:23
  57.2 5.8 %collective-permute-done.12.refs_2_ = bf16[96,2048]{1,0:T(8,128)(2,1)S(1)} collective-permute-done((bf16[96,2048]{1,0:T(8,128)(2,1)S(1)}, bf16[96,2048]{1,0:T(8,128)(2,1)S(1)}, u32[]{:S(2)}, u32[]{:S(2)}) %collective-permute-start.12) | collective-permute-done | bytes 393248 | tf_op jit(solution)/shard_map/ppermute | solution.py:23
  63.0 1.2 %collective-permute-done.13.refs_3_ = bf16[96,2048]{1,0:T(8,128)(2,1)S(1)} collective-permute-done((bf16[96,2048]{1,0:T(8,128)(2,1)S(1)}, bf16[96,2048]{1,0:T(8,128)(2,1)S(1)}, u32[]{:S(2)}, u32[]{:S(2)}) %collective-permute-start.13) | collective-permute-done | bytes 393248 | tf_op jit(solution)/shard_map/ppermute | solution.py:23
  64.2 7.0 %collective-permute-done.8.refs_8_.refs_4_ = bf16[96,2048]{1,0:T(8,128)(2,1)S(1)} collective-permute-done((bf16[96,2048]{1,0:T(8,128)(2,1)S(1)}, bf16[96,2048]{1,0:T(8,128)(2,1)S(1)}, u32[]{:S(2)}, u32[]{:S(2)}) %collective-permute-start.8) | collective-permute-done | bytes 393248 | tf_op jit(solution)/shard_map/ppermute | solution.py:23
  71.2 0.0 copy-start.7
  71.2 0.0 copy-start.6
  71.2 4.9 %shard_map.118 = (bf16[96,2048]{1,0:T(8,128)(2,1)S(1)}, bf16[96,2048]{1,0:T(8,128)(2,1)S(1)}, bf16[96,2048]{1,0:T(8,128)(2,1)S(1)}, bf16[96,2048]{1,0:T(8,128)(2,1)S(1)}) custom-call(bf16[96,2048]{1,0:T(8,128)(2,1)S(1)} %get-tuple-element.32.refs_5_.refs_0_, bf16[96,2048]{1,0:T(8,128)(2,1)S(1)} %collective-permute-done.11.refs_1_, ...), custom_call_target="tpu_custom_call" | custom-call | flops 3623878656 | bytes 14155776 | tf_op jit(solution)/shard_map/pallas_call | solution.py:242
  76.2 0.0 copy-start.4
  76.2 2.0 %collective-permute-start.14 = (bf16[96,2048]{1,0:T(8,128)(2,1)S(1)}, bf16[96,2048]{1,0:T(8,128)(2,1)S(1)}, u32[]{:S(2)}, u32[]{:S(2)}) collective-permute-start(bf16[96,2048]{1,0:T(8,128)(2,1)S(1)} %get-tuple-element.43), channel_id=1, source_target_pairs={{0,1},{1,0},{2,3},{3,2},{4,5},{5,4},{6,7},{7,6},{8,9},{9,8},{10,11... | collective-permute-start | bytes 1179656 | tf_op jit(solution)/shard_map/ppermute | solution.py:23
  78.2 1.5 %collective-permute-start.15 = (bf16[96,2048]{1,0:T(8,128)(2,1)S(1)}, bf16[96,2048]{1,0:T(8,128)(2,1)S(1)}, u32[]{:S(2)}, u32[]{:S(2)}) collective-permute-start(bf16[96,2048]{1,0:T(8,128)(2,1)S(1)} %get-tuple-element.44), channel_id=1, source_target_pairs={{0,2},{1,3},{2,0},{3,1},{4,6},{5,7},{6,4},{7,5},{8,10},{9,11},{10,... | collective-permute-start | bytes 1179656 | tf_op jit(solution)/shard_map/ppermute | solution.py:23
  79.7 0.0 collective-permute-start.16
  79.8 0.0 collective-permute-done.9.refs_5_
  79.8 1.3 %collective-permute-done.10.refs_6_ = bf16[96,2048]{1,0:T(8,128)(2,1)S(1)} collective-permute-done((bf16[96,2048]{1,0:T(8,128)(2,1)S(1)}, bf16[96,2048]{1,0:T(8,128)(2,1)S(1)}, u32[]{:S(2)}, u32[]{:S(2)}) %collective-permute-start.10) | collective-permute-done | bytes 393248 | tf_op jit(solution)/shard_map/ppermute | solution.py:23
  81.1 0.0 copy-done.7
  81.1 2.2 %shard_map.119 = bf16[128,2048]{1,0:T(8,128)(2,1)} custom-call(bf16[128,2048]{1,0:T(8,128)(2,1)S(1)} %collective-permute-done.refs_0_, s32[2,128]{1,0:T(2,128)S(1)} %xor_bitcast_fusion.1.refs_1_, f32[2,128]{1,0:T(2,128)S(1)} %bitcast.28, bf16[96,2048]{1,0:T(8,128)(2,1)S(1)} %get-tuple-element.34.refs_3_, ...), custom_call_target="tpu_custom_call" | custom-call | flops 402653184 | bytes 2097152 | tf_op jit(solution)/shard_map/pallas_call | solution.py:242
  83.3 5.0 %collective-permute-done.14.refs_1_ = bf16[96,2048]{1,0:T(8,128)(2,1)S(1)} collective-permute-done((bf16[96,2048]{1,0:T(8,128)(2,1)S(1)}, bf16[96,2048]{1,0:T(8,128)(2,1)S(1)}, u32[]{:S(2)}, u32[]{:S(2)}) %collective-permute-start.14) | collective-permute-done | bytes 393248 | tf_op jit(solution)/shard_map/ppermute | solution.py:23
  88.3 5.9 %collective-permute-done.15.refs_2_ = bf16[96,2048]{1,0:T(8,128)(2,1)S(1)} collective-permute-done((bf16[96,2048]{1,0:T(8,128)(2,1)S(1)}, bf16[96,2048]{1,0:T(8,128)(2,1)S(1)}, u32[]{:S(2)}, u32[]{:S(2)}) %collective-permute-start.15) | collective-permute-done | bytes 393248 | tf_op jit(solution)/shard_map/ppermute | solution.py:23
  94.2 1.0 collective-permute-done.16.refs_3_
  95.1 0.0 copy-done.6
  95.2 0.0 copy-done.4
  95.2 1.9 %shard_map.120 = bf16[128,2048]{1,0:T(8,128)(2,1)} custom-call(bf16[128,2048]{1,0:T(8,128)(2,1)S(1)} %collective-permute-done.7.refs_0_.grads_ref, bf16[128,2048]{1,0:T(8,128)(2,1)S(1)} %bitcast.27, f32[1,2048]{1,0:T(1,128)S(1)} %copy-done.6, s32[2,128]{1,0:T(2,128)S(1)} %xor_bitcast_fusion.routes_ref.refs_1_, ...), custom_call_target="tpu_custom_call" | custom-call | flops 201326592 | bytes 2097152 | tf_op jit(solution)/shard_map/pallas_call | solution.py:242
Async XLA Ops:
  0.6 14.6 %collective-permute-start = (bf16[128,2048]{1,0:T(8,128)(2,1)}, bf16[128,2048]{1,0:T(8,128)(2,1)S(1)}, u32[]{:S(2)}, u32[]{:S(2)}) collective-permute-start(bf16[128,2048]{1,0:T(8,128)(2,1)} %bitcast.32), channel_id=1, source_target_pairs={{0,4},{4,8},{8,12},{12,16},{16,20},{20,24},{24,28},{28,0},{1,5},{5... | collective-permute-start | bytes 1572872 | tf_op jit(solution)/shard_map/ppermute | solution.py:17
  1.1 21.4 %collective-permute-start.7 = (bf16[128,2048]{1,0:T(8,128)(2,1)}, bf16[128,2048]{1,0:T(8,128)(2,1)S(1)}, u32[]{:S(2)}, u32[]{:S(2)}) collective-permute-start(bf16[128,2048]{1,0:T(8,128)(2,1)} %bitcast.33), channel_id=1, source_target_pairs={{0,28},{4,0},{8,4},{12,8},{16,12},{20,16},{24,20},{28,24},{1,29},{... | collective-permute-start | bytes 1572872 | tf_op jit(solution)/shard_map/ppermute | solution.py:17
  5.9 1.0 %copy-start.3 = (bf16[1,128,2048]{2,1,0:T(8,128)(2,1)S(1)}, bf16[1,128,2048]{2,1,0:T(8,128)(2,1)}, u32[]{:S(2)}) copy-start(bf16[1,128,2048]{2,1,0:T(8,128)(2,1)} %param.12) | copy-start | bytes 1572868
  7.0 0.7 copy-start.5
  7.7 39.6 %copy-start.2 = (bf16[1,1,768,2048]{3,2,1,0:T(8,128)(2,1)S(1)}, bf16[1,1,768,2048]{3,2,1,0:T(8,128)(2,1)}, u32[]{:S(2)}) copy-start(bf16[1,1,768,2048]{3,2,1,0:T(8,128)(2,1)} %param.19) | copy-start | bytes 9437188
  8.4 12.1 %collective-permute-start.4 = (bf16[96,2048]{1,0:T(8,128)(2,1)S(1)}, bf16[96,2048]{1,0:T(8,128)(2,1)S(1)}, u32[]{:S(2)}, u32[]{:S(2)}) collective-permute-start(bf16[96,2048]{1,0:T(8,128)(2,1)S(1)} %get-tuple-element.29), channel_id=1, source_target_pairs={{0,1},{1,0},{2,3},{3,2},{4,5},{5,4},{6,7},{7,6},{8,9},{9,8},{10,11... | collective-permute-start | bytes 1179656 | tf_op jit(solution)/shard_map/ppermute | solution.py:23
  10.4 18.9 %collective-permute-start.5 = (bf16[96,2048]{1,0:T(8,128)(2,1)S(1)}, bf16[96,2048]{1,0:T(8,128)(2,1)S(1)}, u32[]{:S(2)}, u32[]{:S(2)}) collective-permute-start(bf16[96,2048]{1,0:T(8,128)(2,1)S(1)} %get-tuple-element.30), channel_id=1, source_target_pairs={{0,2},{1,3},{2,0},{3,1},{4,6},{5,7},{6,4},{7,5},{8,10},{9,11},{10,... | collective-permute-start | bytes 1179656 | tf_op jit(solution)/shard_map/ppermute | solution.py:23
  11.9 18.5 %collective-permute-start.6 = (bf16[96,2048]{1,0:T(8,128)(2,1)S(1)}, bf16[96,2048]{1,0:T(8,128)(2,1)S(1)}, u32[]{:S(2)}, u32[]{:S(2)}) collective-permute-start(bf16[96,2048]{1,0:T(8,128)(2,1)S(1)} %get-tuple-element.31), channel_id=1, source_target_pairs={{0,3},{1,2},{2,1},{3,0},{4,7},{5,6},{6,5},{7,4},{8,11},{9,10},{10,... | collective-permute-start | bytes 1179656 | tf_op jit(solution)/shard_map/ppermute | solution.py:23
  16.0 21.5 %collective-permute-start.1 = (bf16[96,2048]{1,0:T(8,128)(2,1)S(1)}, bf16[96,2048]{1,0:T(8,128)(2,1)S(1)}, u32[]{:S(2)}, u32[]{:S(2)}) collective-permute-start(bf16[96,2048]{1,0:T(8,128)(2,1)S(1)} %get-tuple-element.26), channel_id=1, source_target_pairs={{0,1},{1,0},{2,3},{3,2},{4,5},{5,4},{6,7},{7,6},{8,9},{9,8},{10,11... | collective-permute-start | bytes 1179656 | tf_op jit(solution)/shard_map/ppermute | solution.py:23
  20.5 25.6 %collective-permute-start.2 = (bf16[96,2048]{1,0:T(8,128)(2,1)S(1)}, bf16[96,2048]{1,0:T(8,128)(2,1)S(1)}, u32[]{:S(2)}, u32[]{:S(2)}) collective-permute-start(bf16[96,2048]{1,0:T(8,128)(2,1)S(1)} %get-tuple-element.27), channel_id=1, source_target_pairs={{0,2},{1,3},{2,0},{3,1},{4,6},{5,7},{6,4},{7,5},{8,10},{9,11},{10,... | collective-permute-start | bytes 1179656 | tf_op jit(solution)/shard_map/ppermute | solution.py:23
  22.5 24.8 %collective-permute-start.3 = (bf16[96,2048]{1,0:T(8,128)(2,1)S(1)}, bf16[96,2048]{1,0:T(8,128)(2,1)S(1)}, u32[]{:S(2)}, u32[]{:S(2)}) collective-permute-start(bf16[96,2048]{1,0:T(8,128)(2,1)S(1)} %get-tuple-element.28), channel_id=1, source_target_pairs={{0,3},{1,2},{2,1},{3,0},{4,7},{5,6},{6,5},{7,4},{8,11},{9,10},{10,... | collective-permute-start | bytes 1179656 | tf_op jit(solution)/shard_map/ppermute | solution.py:23
  23.9 0.7 copy-start.8
  29.3 25.1 %collective-permute-start.11 = (bf16[96,2048]{1,0:T(8,128)(2,1)S(1)}, bf16[96,2048]{1,0:T(8,128)(2,1)S(1)}, u32[]{:S(2)}, u32[]{:S(2)}) collective-permute-start(bf16[96,2048]{1,0:T(8,128)(2,1)S(1)} %get-tuple-element.38), channel_id=1, source_target_pairs={{0,1},{1,0},{2,3},{3,2},{4,5},{5,4},{6,7},{7,6},{8,9},{9,8},{10,11... | collective-permute-start | bytes 1179656 | tf_op jit(solution)/shard_map/ppermute | solution.py:23
  30.4 32.6 %collective-permute-start.12 = (bf16[96,2048]{1,0:T(8,128)(2,1)S(1)}, bf16[96,2048]{1,0:T(8,128)(2,1)S(1)}, u32[]{:S(2)}, u32[]{:S(2)}) collective-permute-start(bf16[96,2048]{1,0:T(8,128)(2,1)S(1)} %get-tuple-element.39), channel_id=1, source_target_pairs={{0,2},{1,3},{2,0},{3,1},{4,6},{5,7},{6,4},{7,5},{8,10},{9,11},{10,... | collective-permute-start | bytes 1179656 | tf_op jit(solution)/shard_map/ppermute | solution.py:23
  31.8 2.8 %copy-start = (bf16[1,1,2048,1536]{3,2,1,0:T(8,128)(2,1)S(1)}, bf16[1,1,2048,1536]{3,2,1,0:T(8,128)(2,1)}, u32[]{:S(2)}) copy-start(bf16[1,1,2048,1536]{3,2,1,0:T(8,128)(2,1)} %param.18) | copy-start | bytes 18874372
  34.6 12.8 %copy-start.1 = (bf16[1,1,2048,1536]{3,2,1,0:T(8,128)(2,1)S(1)}, bf16[1,1,2048,1536]{3,2,1,0:T(8,128)(2,1)}, u32[]{:S(2)}) copy-start(bf16[1,1,2048,1536]{3,2,1,0:T(8,128)(2,1)} %param.18) | copy-start | bytes 18874372
  37.4 26.8 %collective-permute-start.13 = (bf16[96,2048]{1,0:T(8,128)(2,1)S(1)}, bf16[96,2048]{1,0:T(8,128)(2,1)S(1)}, u32[]{:S(2)}, u32[]{:S(2)}) collective-permute-start(bf16[96,2048]{1,0:T(8,128)(2,1)S(1)} %get-tuple-element.40), channel_id=1, source_target_pairs={{0,3},{1,2},{2,1},{3,0},{4,7},{5,6},{6,5},{7,4},{8,11},{9,10},{10,... | collective-permute-start | bytes 1179656 | tf_op jit(solution)/shard_map/ppermute | solution.py:23
  51.1 20.1 %collective-permute-start.8 = (bf16[96,2048]{1,0:T(8,128)(2,1)S(1)}, bf16[96,2048]{1,0:T(8,128)(2,1)S(1)}, u32[]{:S(2)}, u32[]{:S(2)}) collective-permute-start(bf16[96,2048]{1,0:T(8,128)(2,1)S(1)} %get-tuple-element.35), channel_id=1, source_target_pairs={{0,1},{1,0},{2,3},{3,2},{4,5},{5,4},{6,7},{7,6},{8,9},{9,8},{10,11... | collective-permute-start | bytes 1179656 | tf_op jit(solution)/shard_map/ppermute | solution.py:23
  52.7 27.1 %collective-permute-start.9 = (bf16[96,2048]{1,0:T(8,128)(2,1)S(1)}, bf16[96,2048]{1,0:T(8,128)(2,1)S(1)}, u32[]{:S(2)}, u32[]{:S(2)}) collective-permute-start(bf16[96,2048]{1,0:T(8,128)(2,1)S(1)} %get-tuple-element.36), channel_id=1, source_target_pairs={{0,2},{1,3},{2,0},{3,1},{4,6},{5,7},{6,4},{7,5},{8,10},{9,11},{10,... | collective-permute-start | bytes 1179656 | tf_op jit(solution)/shard_map/ppermute | solution.py:23
  54.3 26.8 %collective-permute-start.10 = (bf16[96,2048]{1,0:T(8,128)(2,1)S(1)}, bf16[96,2048]{1,0:T(8,128)(2,1)S(1)}, u32[]{:S(2)}, u32[]{:S(2)}) collective-permute-start(bf16[96,2048]{1,0:T(8,128)(2,1)S(1)} %get-tuple-element.37), channel_id=1, source_target_pairs={{0,3},{1,2},{2,1},{3,0},{4,7},{5,6},{6,5},{7,4},{8,11},{9,10},{10,... | collective-permute-start | bytes 1179656 | tf_op jit(solution)/shard_map/ppermute | solution.py:23
  71.2 9.9 %copy-start.7 = (f32[1,128,2]{1,2,0:T(2,128)S(1)}, f32[1,128,2]{1,2,0:T(2,128)}, u32[]{:S(2)}) copy-start(f32[1,128,2]{1,2,0:T(2,128)} %param.14) | copy-start | bytes 3076
  71.2 23.9 %copy-start.6 = (f32[1,2048]{1,0:T(1,128)S(1)}, f32[1,2048]{1,0:T(1,128)}, u32[]{:S(2)}) copy-start(f32[1,2048]{1,0:T(1,128)} %gain_ref.3) | copy-start | bytes 24580
  76.2 19.0 %copy-start.4 = (bf16[1,128,2048]{2,1,0:T(8,128)(2,1)S(1)}, bf16[1,128,2048]{2,1,0:T(8,128)(2,1)}, u32[]{:S(2)}) copy-start(bf16[1,128,2048]{2,1,0:T(8,128)(2,1)} %param.12) | copy-start | bytes 1572868
  76.2 12.1 %collective-permute-start.14 = (bf16[96,2048]{1,0:T(8,128)(2,1)S(1)}, bf16[96,2048]{1,0:T(8,128)(2,1)S(1)}, u32[]{:S(2)}, u32[]{:S(2)}) collective-permute-start(bf16[96,2048]{1,0:T(8,128)(2,1)S(1)} %get-tuple-element.43), channel_id=1, source_target_pairs={{0,1},{1,0},{2,3},{3,2},{4,5},{5,4},{6,7},{7,6},{8,9},{9,8},{10,11... | collective-permute-start | bytes 1179656 | tf_op jit(solution)/shard_map/ppermute | solution.py:23
  78.2 16.0 %collective-permute-start.15 = (bf16[96,2048]{1,0:T(8,128)(2,1)S(1)}, bf16[96,2048]{1,0:T(8,128)(2,1)S(1)}, u32[]{:S(2)}, u32[]{:S(2)}) collective-permute-start(bf16[96,2048]{1,0:T(8,128)(2,1)S(1)} %get-tuple-element.44), channel_id=1, source_target_pairs={{0,2},{1,3},{2,0},{3,1},{4,6},{5,7},{6,4},{7,5},{8,10},{9,11},{10,... | collective-permute-start | bytes 1179656 | tf_op jit(solution)/shard_map/ppermute | solution.py:23
  79.7 15.4 %collective-permute-start.16 = (bf16[96,2048]{1,0:T(8,128)(2,1)S(1)}, bf16[96,2048]{1,0:T(8,128)(2,1)S(1)}, u32[]{:S(2)}, u32[]{:S(2)}) collective-permute-start(bf16[96,2048]{1,0:T(8,128)(2,1)S(1)} %get-tuple-element.45), channel_id=1, source_target_pairs={{0,3},{1,2},{2,1},{3,0},{4,7},{5,6},{6,5},{7,4},{8,11},{9,10},{10,... | collective-permute-start | bytes 1179656 | tf_op jit(solution)/shard_map/ppermute | solution.py:23

commit v4 on v3

--- a/solution.py
+++ b/solution.py
@@ -249,7 +249,7 @@
     )(*inputs, *after)
 
 
-def per_device(
+def per_device_direct(
     fwd_prev,
     bwd_prev,
     bwd_saved,
@@ -347,6 +347,463 @@
     return (fwd_block[None], bwd_block[None])
 
 
+def pick(table, expert, capacity, kind, top_count):
+    first = 0 if kind[0] == "f" else 2 * top_count
+    routes = table[first : first + top_count]
+    gates = table[first + top_count : first + 2 * top_count]
+    tok_rows = table.shape[1]
+    member = routes == float(expert)
+    held = jnp.sum(member.astype(jnp.float32), axis=0, keepdims=True)
+    before = lax.broadcasted_iota(jnp.int32, (tok_rows, tok_rows), 0) < lax.broadcasted_iota(
+        jnp.int32, (tok_rows, tok_rows), 1
+    )
+    slots = jnp.dot(
+        jnp.broadcast_to(held, (8, tok_rows)).astype(jnp.bfloat16),
+        before.astype(jnp.bfloat16),
+        preferred_element_type=jnp.float32,
+    )[0:1]
+    place = placement(jnp.where(held > 0.0, slots, -1.0), 0, capacity)
+    if len(kind) == 1:
+        return (place.astype(jnp.bfloat16),)
+    gate = jnp.sum(jnp.where(member, gates, 0.0), axis=0, keepdims=True)
+    return halves(jnp.where(place, gate, 0.0))
+
+
+def to_slots(weights, values):
+    total = None
+    for part in weights:
+        term = jnp.dot(part, values, preferred_element_type=jnp.float32)
+        total = term if total is None else total + term
+    return total.astype(jnp.bfloat16)
+
+
+def to_tokens(weights, rows):
+    total = None
+    for part in weights:
+        term = rows_dot(part, rows)
+        total = term if total is None else total + term
+    return total
+
+
+def three_parts(values):
+    high = values.astype(jnp.bfloat16)
+    rest = values - high.astype(jnp.float32)
+    mid = rest.astype(jnp.bfloat16)
+    low = (rest - mid.astype(jnp.float32)).astype(jnp.bfloat16)
+    return high, mid, low
+
+
+def normed_halves(wide, gain):
+    inv_rms = lax.rsqrt(jnp.mean(wide * wide, axis=-1, keepdims=True) + EPS)
+    return (wide * inv_rms * gain).astype(jnp.bfloat16)
+
+
+def first_kernel(top_count, me_ref, *refs):
+    sources, refs = refs[:6], refs[6:]
+    (left_ref, right_ref, table_ref), refs = refs[:3], refs[3:]
+    held, sems = refs[:6], refs[6]
+    copies = [pltpu.make_async_copy(sources[i], held[i], sems.at[i]) for i in range(6)]
+    for copy in copies:
+        copy.start()
+    for copy in copies[1:]:
+        copy.wait()
+    saved, gain, f_routes, f_gates, b_routes, b_gates = held
+    me = me_ref[0]
+    fr = (f_routes[...] ^ me).astype(jnp.float32)
+    br = (b_routes[...] ^ me).astype(jnp.float32)
+    fg = f_gates[...]
+    bg = b_gates[...]
+    table_ref[...] = jnp.concatenate([fr, fg, br, bg], axis=0)
+    packed = [fr.astype(jnp.bfloat16), br.astype(jnp.bfloat16), *three_parts(fg), *three_parts(bg)]
+    packed = jnp.concatenate([part.astype(jnp.float32) for part in packed], axis=0)
+    tok_rows, features = saved.shape
+    half = features // 2
+    copies[0].wait()
+    normed = normed_halves(saved[...].astype(jnp.float32), gain[...])
+    for half_ref, start in ((left_ref, 0), (right_ref, half)):
+        half_ref[:tok_rows, :] = normed[:, start : start + half]
+        half_ref[tok_rows:, :] = jnp.zeros((half_ref.shape[0] - tok_rows, half), jnp.bfloat16)
+        half_ref[tok_rows:, :tok_rows] = packed.astype(jnp.bfloat16)
+
+
+def unpacked(block, tok_rows, top_count):
+    rows = block[tok_rows:, :tok_rows].astype(jnp.float32)
+    k = top_count
+    fr, br = rows[0:k], rows[k : 2 * k]
+    fg = (rows[2 * k : 3 * k] + rows[3 * k : 4 * k]) + rows[4 * k : 5 * k]
+    bg = (rows[5 * k : 6 * k] + rows[6 * k : 7 * k]) + rows[7 * k : 8 * k]
+    return jnp.concatenate([fr, fg, br, bg], axis=0)
+
+
+def normed_kernel_halves(values_ref, gain_ref, left_ref, right_ref):
+    half = left_ref.shape[1]
+    normed = normed_halves(values_ref[...].astype(jnp.float32), gain_ref[...])
+    left_ref[...] = normed[:, :half]
+    right_ref[...] = normed[:, half:]
+
+
+def split_kernel(values_ref, left_ref, right_ref):
+    half = left_ref.shape[1]
+    left_ref[...] = values_ref[:, :half]
+    right_ref[...] = values_ref[:, half:]
+
+
+def tables_kernel(top_count, from_x, from_y, x_table, y_table):
+    tok_rows = x_table.shape[1]
+    x_table[...] = unpacked(from_x[...], tok_rows, top_count)
+    y_table[...] = unpacked(from_y[...], tok_rows, top_count)
+
+
+def hop_kernel(kind, top_count, own, x_tab, y_tab, left, right, from_x, from_y, to_y, to_x):
+    capacity = to_y.shape[0] // 2
+    tok_rows = own.shape[1]
+    to_y[:capacity, :] = to_slots(pick(own[...], 2, capacity, kind, top_count), left[:tok_rows, :])
+    to_y[capacity:, :] = to_slots(
+        pick(x_tab[...], 3, capacity, kind, top_count), from_x[:tok_rows, :]
+    )
+    to_x[:capacity, :] = to_slots(pick(own[...], 1, capacity, kind, top_count), right[:tok_rows, :])
+    to_x[capacity:, :] = to_slots(
+        pick(y_tab[...], 3, capacity, kind, top_count), from_y[:tok_rows, :]
+    )
+
+
+def assemble(kind, top_count, own, x_tab, y_tab, left, right, from_x, from_y, got_y, got_x, rows):
+    capacity = got_y.shape[0] // 2
+    half = got_y.shape[1]
+    tok_rows = own.shape[1]
+    mine = pick(own[...], 0, capacity, kind, top_count)
+    rows[:capacity, :half] = to_slots(mine, left[:tok_rows, :])
+    rows[:capacity, half:] = to_slots(mine, right[:tok_rows, :])
+    rows[capacity : 2 * capacity, :half] = to_slots(
+        pick(x_tab[...], 1, capacity, kind, top_count), from_x[:tok_rows, :]
+    )
+    rows[capacity : 2 * capacity, half:] = got_x[:capacity, :]
+    rows[2 * capacity : 3 * capacity, :half] = got_y[:capacity, :]
+    rows[2 * capacity : 3 * capacity, half:] = to_slots(
+        pick(y_tab[...], 2, capacity, kind, top_count), from_y[:tok_rows, :]
+    )
+    rows[3 * capacity :, :half] = got_y[capacity:, :]
+    rows[3 * capacity :, half:] = got_x[capacity:, :]
+
+
+def hand_out(out, start, capacity, half, keep, x_left, y_right, to_y, to_x):
+    size = out.shape[1]
+    rows = out.astype(jnp.bfloat16)
+    parts = [rows[d * capacity : (d + 1) * capacity] for d in range(4)]
+    keep[:, start : start + size] = parts[0]
+    if start < half:
+        x_left[:, start : start + size] = parts[1]
+        to_y[:capacity, start : start + size] = parts[2]
+        to_y[capacity:, start : start + size] = parts[3]
+    else:
+        at = start - half
+        to_x[:capacity, at : at + size] = parts[1]
+        y_right[:, at : at + size] = parts[2]
+        to_x[capacity:, at : at + size] = parts[3]
+
+
+def hop_again_kernel(top_count, *refs):
+    dispatch, (weight_in, gate_ref, up_ref, rows_ref) = refs[:9], refs[9:]
+    assemble("b", top_count, *dispatch, rows_ref)
+    hidden_units = gate_ref.shape[1]
+    for start, size in tiles(hidden_units, 256):
+        gate_ref[:, start : start + size] = jnp.dot(
+            rows_ref[...], weight_in[:, start : start + size], preferred_element_type=jnp.float32
+        )
+        up_ref[:, start : start + size] = jnp.dot(
+            rows_ref[...],
+            weight_in[:, hidden_units + start : hidden_units + start + size],
+            preferred_element_type=jnp.float32,
+        )
+
+
+def hop_fwd_kernel(top_count, *refs):
+    dispatch, refs = refs[:9], refs[9:]
+    weight_in, weight_out = refs[:2]
+    outs, (rows_ref, hidden_ref) = refs[2:7], refs[7:]
+    capacity = outs[0].shape[0]
+    hidden_units, features = weight_out.shape
+    assemble("f", top_count, *dispatch, rows_ref)
+    for start, size in tiles(hidden_units, 256):
+        gate = jnp.dot(
+            rows_ref[...], weight_in[:, start : start + size], preferred_element_type=jnp.float32
+        )
+        up = jnp.dot(
+            rows_ref[...],
+            weight_in[:, hidden_units + start : hidden_units + start + size],
+            preferred_element_type=jnp.float32,
+        )
+        hidden_ref[:, start : start + size] = (gate / (1.0 + jnp.exp(-gate)) * up).astype(
+            jnp.bfloat16
+        )
+    for start, size in tiles(features, features // 4):
+        out = jnp.dot(
+            hidden_ref[...], weight_out[:, start : start + size], preferred_element_type=jnp.float32
+        )
+        hand_out(out, start, capacity, features // 2, *outs)
+
+
+def hop_bwd_kernel(top_count, *refs):
+    dispatch, refs = refs[:9], refs[9:]
+    gate_ref, up_ref, weight_in, weight_out = refs[:4]
+    outs, (grads_ref, both_ref) = refs[4:9], refs[9:]
+    capacity = outs[0].shape[0]
+    hidden_units, features = weight_out.shape
+    assemble("bg", top_count, *dispatch, grads_ref)
+    for start, size in tiles(hidden_units, 256):
+        gate = gate_ref[:, start : start + size]
+        up = up_ref[:, start : start + size]
+        d_hidden = lax.dot_general(
+            grads_ref[...],
+            weight_out[start : start + size, :],
+            (((1,), (1,)), ((), ())),
+            preferred_element_type=jnp.float32,
+        )
+        sig = 1.0 / (1.0 + jnp.exp(-gate))
+        both_ref[:, start : start + size] = (
+            d_hidden * up * sig * (1.0 + gate * (1.0 - sig))
+        ).astype(jnp.bfloat16)
+        both_ref[:, hidden_units + start : hidden_units + start + size] = (
+            d_hidden * gate * sig
+        ).astype(jnp.bfloat16)
+    for start, size in tiles(features, features // 4):
+        out = lax.dot_general(
+            both_ref[...],
+            weight_in[start : start + size, :],
+            (((1,), (1,)), ((), ())),
+            preferred_element_type=jnp.float32,
+        )
+        hand_out(out, start, capacity, features // 2, *outs)
+
+
+def sums_kernel(kind, top_count, x_tab, y_tab, x_left, y_right, got_y, got_x, sum_x, sum_y):
+    capacity = x_left.shape[0]
+    for table, near, far, out in (
+        ((x_tab, 1), x_left, got_y, sum_x),
+        ((y_tab, 2), y_right, got_x, sum_y),
+    ):
+        tab = table[0][...]
+        out[...] = (
+            to_tokens(pick(tab, table[1], capacity, kind, top_count), near[...])
+            + to_tokens(pick(tab, 3, capacity, kind, top_count), far[capacity:, :])
+        ).astype(jnp.bfloat16)
+
+
+def summed(kind, top_count, own, keep, got_y, got_x, sum_x, sum_y):
+    capacity, features = keep.shape
+    half = features // 2
+    mine = pick(own[...], 0, capacity, kind, top_count)
+    near_y = pick(own[...], 2, capacity, kind, top_count)
+    near_x = pick(own[...], 1, capacity, kind, top_count)
+    left = to_tokens(mine, keep[:, :half]) + to_tokens(near_y, got_y[:capacity, :])
+    right = to_tokens(mine, keep[:, half:]) + to_tokens(near_x, got_x[:capacity, :])
+    return left + sum_x[...].astype(jnp.float32), right + sum_y[...].astype(jnp.float32)
+
+
+def hop_fwd_end_kernel(top_count, layer_ref, own, keep, got_y, got_x, sum_x, sum_y, out_ref):
+    half = got_y.shape[1]
+    left, right = summed("fg", top_count, own, keep, got_y, got_x, sum_x, sum_y)
+    out_ref[:, :half] = (layer_ref[:, :half].astype(jnp.float32) + left).astype(jnp.bfloat16)
+    out_ref[:, half:] = (layer_ref[:, half:].astype(jnp.float32) + right).astype(jnp.bfloat16)
+
+
+def hop_bwd_end_kernel(
+    top_count, grads_ref, saved_ref, gain_ref, own, keep, got_y, got_x, sum_x, sum_y, out_ref
+):
+    features = saved_ref.shape[1]
+    left, right = summed("b", top_count, own, keep, got_y, got_x, sum_x, sum_y)
+    wide = saved_ref[...].astype(jnp.float32)
+    inv_rms = lax.rsqrt(jnp.mean(wide * wide, axis=-1, keepdims=True) + EPS)
+    scaled = jnp.concatenate([left, right], axis=1) * gain_ref[...]
+    cubed = inv_rms * inv_rms * inv_rms
+    inner = jnp.sum(scaled * wide, axis=-1, keepdims=True)
+    out_ref[...] = (
+        grads_ref[...].astype(jnp.float32) + inv_rms * scaled - cubed / features * wide * inner
+    ).astype(jnp.bfloat16)
+
+
+def per_device_hops(
+    fwd_prev,
+    bwd_prev,
+    bwd_saved,
+    fwd_routes,
+    fwd_gates,
+    bwd_routes,
+    bwd_gates,
+    norm_gain,
+    w_in,
+    w_out,
+):
+    tok_rows, features = fwd_prev.shape[1:]
+    top_count = fwd_routes.shape[2]
+    hidden_units = w_in.shape[3] // 2
+    capacity = 3 * tok_rows * top_count // 8
+    half = features // 2
+    gain_row = norm_gain
+    weight_in = w_in[0, 0]
+    weight_out = w_out[0, 0]
+    me = lax.axis_index("expert").astype(jnp.int32).reshape(1)
+    saved = bwd_saved[0]
+    layer_in = passed_along(fwd_prev[0], "section", 1)
+    grad_in = passed_along(bwd_prev[0], "section", -1)
+
+    def shaped(rows, columns, dtype=jnp.bfloat16):
+        return jax.ShapeDtypeStruct((rows, columns), dtype)
+
+    def crossed(left, right):
+        return swapped(left, "expert", 1), swapped(right, "expert", 2)
+
+    slot_total = 4 * capacity
+    table_rows = 4 * top_count
+    one_hop = moved = 1024
+    expert_flops = 2 * slot_total * features * hidden_units
+    expert_moved = 2 * features * (3 * hidden_units + 3 * slot_total)
+    rows_scratch = pltpu.VMEM((slot_total, features), jnp.bfloat16)
+    halves_out = [shaped(tok_rows, half)] * 2
+    hop_out = [shaped(2 * capacity, half)] * 2
+    expert_out = [shaped(capacity, features), shaped(capacity, half), shaped(capacity, half)] + hop_out
+    table_shape = shaped(table_rows, tok_rows, jnp.float32)
+    first_rows = tok_rows + 8 * top_count
+
+    b_left, b_right, own = pl.pallas_call(
+        functools.partial(first_kernel, top_count),
+        out_shape=[shaped(first_rows, half), shaped(first_rows, half), table_shape],
+        in_specs=[pl.BlockSpec(memory_space=pltpu.SMEM)]
+        + [pl.BlockSpec(memory_space=pltpu.HBM)] * 6,
+        scratch_shapes=[
+            pltpu.VMEM((tok_rows, features), jnp.bfloat16),
+            pltpu.VMEM((1, features), jnp.float32),
+            pltpu.VMEM((top_count, tok_rows), jnp.int32),
+            pltpu.VMEM((top_count, tok_rows), jnp.float32),
+            pltpu.VMEM((top_count, tok_rows), jnp.int32),
+            pltpu.VMEM((top_count, tok_rows), jnp.float32),
+            pltpu.SemaphoreType.DMA((6,)),
+        ],
+        compiler_params=pltpu.CompilerParams(vmem_limit_bytes=VMEM_LIMIT),
+        cost_estimate=pl.CostEstimate(flops=one_hop, bytes_accessed=moved, transcendentals=0),
+    )(
+        me,
+        *[
+            pltpu.with_memory_space_constraint(value, pltpu.HBM)
+            for value in (
+                saved,
+                gain_row,
+                fwd_routes[0].T,
+                fwd_gates[0].T,
+                bwd_routes[0].T,
+                bwd_gates[0].T,
+            )
+        ],
+    )
+    b_from_x, b_from_y = crossed(b_left, b_right)
+    x_tab, y_tab = local_call(
+        functools.partial(tables_kernel, top_count),
+        [table_shape] * 2,
+        (b_from_x, b_from_y),
+        1024,
+        1024,
+    )
+    tabs = (own, x_tab, y_tab)
+
+    def onward(kind, sent, got, after):
+        to_y, to_x = local_call(
+            functools.partial(hop_kernel, kind, top_count),
+            hop_out,
+            (*tabs, *sent, *got),
+            one_hop,
+            moved,
+            after=after,
+        )
+        return swapped(to_y, "expert", 2), swapped(to_x, "expert", 1), to_y
+
+    b_got_y, b_got_x, b_to_y = onward("b", (b_left, b_right), (b_from_x, b_from_y), ())
+    f_left, f_right = local_call(
+        normed_kernel_halves, halves_out, (layer_in, gain_row), one_hop, moved, after=(b_to_y,)
+    )
+    f_from_x, f_from_y = crossed(f_left, f_right)
+    g_left, g_right = local_call(split_kernel, halves_out, (grad_in,), 1024, moved, after=(f_left,))
+    g_from_x, g_from_y = crossed(g_left, g_right)
+    f_got_y, f_got_x, f_to_y = onward("f", (f_left, f_right), (f_from_x, f_from_y), (g_left,))
+    gate_pre, up_pre = local_call(
+        functools.partial(hop_again_kernel, top_count),
+        [shaped(slot_total, hidden_units, jnp.float32)] * 2,
+        (*tabs, b_left, b_right, b_from_x, b_from_y, b_got_y, b_got_x, weight_in),
+        2 * expert_flops,
+        expert_moved,
+        scratch=(rows_scratch,),
+        after=(f_to_y,),
+    )
+    g_got_y, g_got_x, g_to_y = onward("bg", (g_left, g_right), (g_from_x, g_from_y), (gate_pre,))
+    f_keep, f_x_left, f_y_right, f_to_y, f_to_x = local_call(
+        functools.partial(hop_fwd_kernel, top_count),
+        expert_out,
+        (*tabs, f_left, f_right, f_from_x, f_from_y, f_got_y, f_got_x, weight_in, weight_out),
+        3 * expert_flops,
+        expert_moved,
+        scratch=(rows_scratch, pltpu.VMEM((slot_total, hidden_units), jnp.bfloat16)),
+        after=(g_to_y,),
+    )
+    f_ret_y, f_ret_x = swapped(f_to_y, "expert", 2), swapped(f_to_x, "expert", 1)
+    b_keep, b_x_left, b_y_right, b_to_y, b_to_x = local_call(
+        functools.partial(hop_bwd_kernel, top_count),
+        expert_out,
+        (
+            *tabs,
+            g_left,
+            g_right,
+            g_from_x,
+            g_from_y,
+            g_got_y,
+            g_got_x,
+            gate_pre,
+            up_pre,
+            weight_in,
+            weight_out,
+        ),
+        3 * expert_flops,
+        expert_moved,
+        scratch=(rows_scratch, pltpu.VMEM((slot_total, 2 * hidden_units), jnp.bfloat16)),
+        after=(f_keep,),
+    )
+    b_ret_y, b_ret_x = swapped(b_to_y, "expert", 2), swapped(b_to_x, "expert", 1)
+
+    def summed_call(kind, x_left, y_right, ret_y, ret_x, after):
+        sums = local_call(
+            functools.partial(sums_kernel, kind, top_count),
+            halves_out,
+            (x_tab, y_tab, x_left, y_right, ret_y, ret_x),
+            one_hop,
+            moved,
+            after=after,
+        )
+        return (*crossed(*sums), sums[0])
+
+    f_sum_x, f_sum_y, f_sum = summed_call("fg", f_x_left, f_y_right, f_ret_y, f_ret_x, (b_keep,))
+    b_sum_x, b_sum_y, b_sum = summed_call("b", b_x_left, b_y_right, b_ret_y, b_ret_x, (f_sum,))
+    fwd_block = local_call(
+        functools.partial(hop_fwd_end_kernel, top_count),
+        shaped(tok_rows, features),
+        (layer_in, own, f_keep, f_ret_y, f_ret_x, f_sum_x, f_sum_y),
+        one_hop,
+        moved,
+        after=(b_sum,),
+    )
+    bwd_block = local_call(
+        functools.partial(hop_bwd_end_kernel, top_count),
+        shaped(tok_rows, features),
+        (grad_in, saved, gain_row, own, b_keep, b_ret_y, b_ret_x, b_sum_x, b_sum_y),
+        one_hop,
+        moved,
+    )
+    return (fwd_block[None], bwd_block[None])
+
+
+def per_device(*arrays):
+    if lax.axis_size("expert") == 4:
+        return per_device_hops(*arrays)
+    return per_device_direct(*arrays)
+
+
 def solution(mesh):
     in_specs = (
         P("section", "expert", None),

time: 97.4 us -> 93.6 us (0.961)
  waiting for transfers between devices: 44.8 us -> 38.5 us
  Pallas kernels: 18.1 us -> 23.7 us
  local copies, waits for them, and re-layouts: 5.22 us -> 3.5 us
  other arithmetic: 1.36 us -> 0 us
    pallas_call x8 -> x13, Pallas kernels: 18.1 us -> 22.4 us  [local_call(): pl.pallas_call(body if after else kernel, out_shape=out_shapes, in_specs=...]
    ppermute x15 -> x20, waiting for transfers between devices: 42.2 us -> 38.5 us  [swapped(): return lax.ppermute(value, axis, pairs)]
    ppermute x2, waiting for transfers between devices: 2.54 us -> 0.01 us  [passed_along(): return lax.ppermute(value, axis, pairs)]
    unnamed x18 -> x12, local copies, waits for them, and re-layouts: 5.22 us -> 3.5 us
    transpose x2 -> x0, other arithmetic: 1.36 us -> none  [the longest x1 0.68 us: per_device(): b_routes = (bwd_routes[0] ^ me).T]
    pallas_call x0 -> x1, Pallas kernels: none -> 1.32 us  [per_device_hops(): pl.pallas_call(functools.partial(first_kernel, top_count), out_shape=[sha...]
    ppermute x2, starting transfers between devices: 4.61 us -> 3.47 us  [passed_along(): return lax.ppermute(value, axis, pairs)]
    ppermute x15 -> x20, starting transfers between devices: 22.3 us -> 23.4 us  [swapped(): return lax.ppermute(value, axis, pairs)]
  transfers between devices with their start and end apart: 17 -> 22, of which waited for: 15 -> 10; matrix products, arithmetic and copies ran while one was open for 1% -> 0% of each run, Pallas kernels for 17% -> 24%
where the time goes in v4:
time: 93.6 us; the launch traced here: 93.4 us
  waiting for transfers between devices  38.5 us (41%)
  starting transfers between devices  26.8 us (29%)
  Pallas kernels  23.7 us (25%)
  local copies, waits for them, and re-layouts  3.5 us (4%)
    ppermute x20, waiting for transfers between devices, swapped(): return lax.ppermute(value, axis, pairs)  38.5 us
    ppermute x20, starting transfers between devices, swapped(): return lax.ppermute(value, axis, pairs)  23.4 us
    pallas_call x13, Pallas kernels, local_call(): pl.pallas_call(body if after else kernel, out_shape=out_shapes, in_specs=...  22.4 us
    unnamed x12, local copies, waits for them, and re-layouts  3.5 us
    ppermute x2, starting transfers between devices, passed_along(): return lax.ppermute(value, axis, pairs)  3.47 us
  transfers between devices with their start and end apart: 22, of which 10 were waited for; matrix products, arithmetic and copies ran while one was open for 0% of the time, Pallas kernels for 24%

profile of v4, /device:TPU:0, one launch (start us, length us, event | category | flops | bytes accessed | tf_op | source)
XLA Modules:
  0.0 93.4 jit_solution(8913772953095140663)
XLA Ops:
  0.6 0.5 collective-permute-start
  1.1 1.3 %shard_map.113 = (bf16[144,1024]{1,0:T(8,128)(2,1)S(1)}, bf16[144,1024]{1,0:T(8,128)(2,1)S(1)}, f32[8,128]{1,0:T(8,128)S(1)}) custom-call(s32[1]{0:T(128)} %bitcast.1.me_ref, bf16[128,2048]{1,0:T(8,128)(2,1)} %bitcast.25, f32[1,2048]{1,0:T(1,128)} %gain_ref.1, s32[2,128]{1,0:T(2,128)} %bitcast.29, f32[2,128]{1,0:T(2,128)} %bitcast.30, s32[2,128]{1,0:T(2,128)} %bitcast.31, ...), custom_call_target="tpu_custom_call" | custom-call | flops 1024 | bytes 1024 | tf_op jit(solution)/shard_map/pallas_call | solution.py:668
  2.5 2.6 %collective-permute-start.1 = (bf16[144,1024]{1,0:T(8,128)(2,1)S(1)}, bf16[144,1024]{1,0:T(8,128)(2,1)S(1)}, u32[]{:S(2)}, u32[]{:S(2)}) collective-permute-start(bf16[144,1024]{1,0:T(8,128)(2,1)S(1)} %get-tuple-element.34.left.refs_3_), channel_id=1, source_target_pairs={{0,1},{1,0},{2,3},{3,2},{4,5},{5,4},{6,7},{7,6},{8,9},{9,8},{10,11... | collective-permute-start | bytes 884744 | tf_op jit(solution)/shard_map/ppermute | solution.py:23
  5.0 1.5 %collective-permute-start.2 = (bf16[144,1024]{1,0:T(8,128)(2,1)S(1)}, bf16[144,1024]{1,0:T(8,128)(2,1)S(1)}, u32[]{:S(2)}, u32[]{:S(2)}) collective-permute-start(bf16[144,1024]{1,0:T(8,128)(2,1)S(1)} %get-tuple-element.35.right.refs_4_), channel_id=1, source_target_pairs={{0,2},{1,3},{2,0},{3,1},{4,6},{5,7},{6,4},{7,5},{8,10},{9,11},{10,... | collective-permute-start | bytes 884744 | tf_op jit(solution)/shard_map/ppermute | solution.py:23
  6.6 3.0 %collective-permute-start.5 = (bf16[128,2048]{1,0:T(8,128)(2,1)}, bf16[128,2048]{1,0:T(8,128)(2,1)S(1)}, u32[]{:S(2)}, u32[]{:S(2)}) collective-permute-start(bf16[128,2048]{1,0:T(8,128)(2,1)} %bitcast.34), channel_id=1, source_target_pairs={{0,28},{4,0},{8,4},{12,8},{16,12},{20,16},{24,20},{28,24},{1,29},{... | collective-permute-start | bytes 1572872 | tf_op jit(solution)/shard_map/ppermute | solution.py:17
  9.5 2.3 %collective-permute-done.1.from_x.refs_5_ = bf16[144,1024]{1,0:T(8,128)(2,1)S(1)} collective-permute-done((bf16[144,1024]{1,0:T(8,128)(2,1)S(1)}, bf16[144,1024]{1,0:T(8,128)(2,1)S(1)}, u32[]{:S(2)}, u32[]{:S(2)}) %collective-permute-start.1) | collective-permute-done | bytes 294944 | tf_op jit(solution)/shard_map/ppermute | solution.py:23
  11.8 2.8 %collective-permute-done.2.from_y.refs_6_ = bf16[144,1024]{1,0:T(8,128)(2,1)S(1)} collective-permute-done((bf16[144,1024]{1,0:T(8,128)(2,1)S(1)}, bf16[144,1024]{1,0:T(8,128)(2,1)S(1)}, u32[]{:S(2)}, u32[]{:S(2)}) %collective-permute-start.2) | collective-permute-done | bytes 294944 | tf_op jit(solution)/shard_map/ppermute | solution.py:23
  14.6 0.9 shard_map.115
  15.5 0.1 collective-permute-start.11
  15.5 2.0 %collective-permute-start.10 = (bf16[192,1024]{1,0:T(8,128)(2,1)S(1)}, bf16[192,1024]{1,0:T(8,128)(2,1)S(1)}, u32[]{:S(2)}, u32[]{:S(2)}) collective-permute-start(bf16[192,1024]{1,0:T(8,128)(2,1)S(1)} %get-tuple-element.38.refs_2_), channel_id=1, source_target_pairs={{0,2},{1,3},{2,0},{3,1},{4,6},{5,7},{6,4},{7,5},{8,10},{9,11},{10,... | collective-permute-start | bytes 1179656 | tf_op jit(solution)/shard_map/ppermute | solution.py:23
  17.6 0.0 collective-permute-done.refs_0_
  17.6 0.7 copy-done.4
  18.3 0.2 shard_map.116
  18.5 0.1 collective-permute-start.4
  18.6 1.9 %collective-permute-start.3 = (bf16[128,1024]{1,0:T(8,128)(2,1)S(1)}, bf16[128,1024]{1,0:T(8,128)(2,1)S(1)}, u32[]{:S(2)}, u32[]{:S(2)}) collective-permute-start(bf16[128,1024]{1,0:T(8,128)(2,1)S(1)} %get-tuple-element.39.refs_1_.refs_3_), channel_id=1, source_target_pairs={{0,1},{1,0},{2,3},{3,2},{4,5},{5,4},{6,7},{7,6},{8,9},{9,8},{10,11... | collective-permute-start | bytes 786440 | tf_op jit(solution)/shard_map/ppermute | solution.py:23
  20.6 0.0 collective-permute-done.5.refs_0_.grads_ref
  20.6 12.0 %collective-permute-done.4.refs_6_ = bf16[128,1024]{1,0:T(8,128)(2,1)S(1)} collective-permute-done((bf16[128,1024]{1,0:T(8,128)(2,1)S(1)}, bf16[128,1024]{1,0:T(8,128)(2,1)S(1)}, u32[]{:S(2)}, u32[]{:S(2)}) %collective-permute-start.4) | collective-permute-done | bytes 262176 | tf_op jit(solution)/shard_map/ppermute | solution.py:23
  32.7 0.0 collective-permute-done.3.refs_5_
  32.7 0.9 shard_map.118
  33.5 1.5 %collective-permute-start.7 = (bf16[192,1024]{1,0:T(8,128)(2,1)S(1)}, bf16[192,1024]{1,0:T(8,128)(2,1)S(1)}, u32[]{:S(2)}, u32[]{:S(2)}) collective-permute-start(bf16[192,1024]{1,0:T(8,128)(2,1)S(1)} %get-tuple-element.43), channel_id=1, source_target_pairs={{0,1},{1,0},{2,3},{3,2},{4,5},{5,4},{6,7},{7,6},{8,9},{9,8},{10,11... | collective-permute-start | bytes 1179656 | tf_op jit(solution)/shard_map/ppermute | solution.py:23
  35.0 1.5 %collective-permute-start.6 = (bf16[192,1024]{1,0:T(8,128)(2,1)S(1)}, bf16[192,1024]{1,0:T(8,128)(2,1)S(1)}, u32[]{:S(2)}, u32[]{:S(2)}) collective-permute-start(bf16[192,1024]{1,0:T(8,128)(2,1)S(1)} %get-tuple-element.42.refs_10_), channel_id=1, source_target_pairs={{0,2},{1,3},{2,0},{3,1},{4,6},{5,7},{6,4},{7,5},{8,10},{9,11},{10,... | collective-permute-start | bytes 1179656 | tf_op jit(solution)/shard_map/ppermute | solution.py:23
  36.5 0.5 collective-permute-start.9
  37.1 0.0 collective-permute-done.11.refs_8_
  37.1 0.6 collective-permute-start.8
  37.7 0.0 collective-permute-done.10.refs_7_
  37.7 2.8 %copy-done = bf16[1,1,2048,1536]{3,2,1,0:T(8,128)(2,1)S(1)} copy-done((bf16[1,1,2048,1536]{3,2,1,0:T(8,128)(2,1)S(1)}, bf16[1,1,2048,1536]{3,2,1,0:T(8,128)(2,1)}, u32[]{:S(2)}) %copy-start) | copy-done | bytes 6291480
  40.4 3.2 %shard_map.119 = (f32[384,768]{1,0:T(8,128)S(1)}, f32[384,768]{1,0:T(8,128)S(1)}) custom-call(f32[8,128]{1,0:T(8,128)S(1)} %get-tuple-element.33.own.refs_0_.refs_1_, f32[8,128]{1,0:T(8,128)S(1)} %get-tuple-element.36.x_tab.refs_1_.refs_0_, f32[8,128]{1,0:T(8,128)S(1)} %get-tuple-element.37.y_tab.refs_2_.refs_1_, ...), custom_call_target="tpu_custom_call" | custom-call | flops 2415919104 | bytes 14155776 | tf_op jit(solution)/shard_map/pallas_call | solution.py:242
  43.7 6.7 %collective-permute-done.9.refs_6_ = bf16[128,1024]{1,0:T(8,128)(2,1)S(1)} collective-permute-done((bf16[128,1024]{1,0:T(8,128)(2,1)S(1)}, bf16[128,1024]{1,0:T(8,128)(2,1)S(1)}, u32[]{:S(2)}, u32[]{:S(2)}) %collective-permute-start.9) | collective-permute-done | bytes 262176 | tf_op jit(solution)/shard_map/ppermute | solution.py:23
  50.4 0.0 collective-permute-done.8.refs_5_
  50.4 1.1 %shard_map.120 = (bf16[192,1024]{1,0:T(8,128)(2,1)S(1)}, bf16[192,1024]{1,0:T(8,128)(2,1)S(1)}) custom-call(f32[8,128]{1,0:T(8,128)S(1)} %get-tuple-element.33.own.refs_0_.refs_1_, f32[8,128]{1,0:T(8,128)S(1)} %get-tuple-element.36.x_tab.refs_1_.refs_0_, f32[8,128]{1,0:T(8,128)S(1)} %get-tuple-element.37.y_tab.refs_2_.refs_1_, ...), custom_call_target="tpu_custom_call" | custom-call | flops 1024 | bytes 1024 | tf_op jit(solution)/shard_map/pallas_call | solution.py:242
  51.5 1.3 %collective-permute-start.15 = (bf16[192,1024]{1,0:T(8,128)(2,1)S(1)}, bf16[192,1024]{1,0:T(8,128)(2,1)S(1)}, u32[]{:S(2)}, u32[]{:S(2)}) collective-permute-start(bf16[192,1024]{1,0:T(8,128)(2,1)S(1)} %get-tuple-element.53), channel_id=1, source_target_pairs={{0,1},{1,0},{2,3},{3,2},{4,5},{5,4},{6,7},{7,6},{8,9},{9,8},{10,11... | collective-permute-start | bytes 1179656 | tf_op jit(solution)/shard_map/ppermute | solution.py:23
  52.8 1.5 %collective-permute-start.14 = (bf16[192,1024]{1,0:T(8,128)(2,1)S(1)}, bf16[192,1024]{1,0:T(8,128)(2,1)S(1)}, u32[]{:S(2)}, u32[]{:S(2)}) collective-permute-start(bf16[192,1024]{1,0:T(8,128)(2,1)S(1)} %get-tuple-element.47.refs_11_), channel_id=1, source_target_pairs={{0,2},{1,3},{2,0},{3,1},{4,6},{5,7},{6,4},{7,5},{8,10},{9,11},{10,... | collective-permute-start | bytes 1179656 | tf_op jit(solution)/shard_map/ppermute | solution.py:23
  54.3 0.0 collective-permute-done.7.refs_8_
  54.3 0.0 collective-permute-done.6.refs_7_
  54.3 0.0 copy-done.1
  54.3 0.0 copy-done.2
  54.3 4.5 %shard_map.121 = (bf16[96,2048]{1,0:T(8,128)(2,1)S(1)}, bf16[96,1024]{1,0:T(8,128)(2,1)S(1)}, bf16[96,1024]{1,0:T(8,128)(2,1)S(1)}, bf16[192,1024]{1,0:T(8,128)(2,1)S(1)}, bf16[192,1024]{1,0:T(8,128)(2,1)S(1)}) custom-call(f32[8,128]{1,0:T(8,128)S(1)} %get-tuple-element.33.own.refs_0_.refs_1_, f32[8,128]{1,0:T(8,128)S(1)} %get-tuple-element.36.x_tab.refs_1_.refs_0_, ...), custom_call_target="tpu_custom_call" | custom-call | flops 3623878656 | bytes 14155776 | tf_op jit(solution)/shard_map/pallas_call | solution.py:242
  58.8 0.6 collective-permute-start.12
  59.4 0.8 collective-permute-start.13
  60.2 1.7 %collective-permute-done.15.refs_8_ = bf16[192,1024]{1,0:T(8,128)(2,1)S(1)} collective-permute-done((bf16[192,1024]{1,0:T(8,128)(2,1)S(1)}, bf16[192,1024]{1,0:T(8,128)(2,1)S(1)}, u32[]{:S(2)}, u32[]{:S(2)}) %collective-permute-start.15) | collective-permute-done | bytes 393248 | tf_op jit(solution)/shard_map/ppermute | solution.py:23
  61.9 2.9 %collective-permute-done.14.refs_7_ = bf16[192,1024]{1,0:T(8,128)(2,1)S(1)} collective-permute-done((bf16[192,1024]{1,0:T(8,128)(2,1)S(1)}, bf16[192,1024]{1,0:T(8,128)(2,1)S(1)}, u32[]{:S(2)}, u32[]{:S(2)}) %collective-permute-start.14) | collective-permute-done | bytes 393248 | tf_op jit(solution)/shard_map/ppermute | solution.py:23
  64.9 6.0 %shard_map.122 = (bf16[96,2048]{1,0:T(8,128)(2,1)S(1)}, bf16[96,1024]{1,0:T(8,128)(2,1)S(1)}, bf16[96,1024]{1,0:T(8,128)(2,1)S(1)}, bf16[192,1024]{1,0:T(8,128)(2,1)S(1)}, bf16[192,1024]{1,0:T(8,128)(2,1)S(1)}) custom-call(f32[8,128]{1,0:T(8,128)S(1)} %get-tuple-element.33.own.refs_0_.refs_1_, f32[8,128]{1,0:T(8,128)S(1)} %get-tuple-element.36.x_tab.refs_1_.refs_0_, ...), custom_call_target="tpu_custom_call" | custom-call | flops 3623878656 | bytes 14155776 | tf_op jit(solution)/shard_map/pallas_call | solution.py:242
  70.8 0.0 copy-start.3
  70.8 0.0 copy-start.5
  70.8 1.5 %collective-permute-start.18 = (bf16[192,1024]{1,0:T(8,128)(2,1)S(1)}, bf16[192,1024]{1,0:T(8,128)(2,1)S(1)}, u32[]{:S(2)}, u32[]{:S(2)}) collective-permute-start(bf16[192,1024]{1,0:T(8,128)(2,1)S(1)} %get-tuple-element.60), channel_id=1, source_target_pairs={{0,2},{1,3},{2,0},{3,1},{4,6},{5,7},{6,4},{7,5},{8,10},{9,11},{10,... | collective-permute-start | bytes 1179656 | tf_op jit(solution)/shard_map/ppermute | solution.py:23
  72.4 0.6 collective-permute-start.19
  73.0 0.0 collective-permute-done.12.refs_4_.refs_3_
  73.0 0.0 collective-permute-done.13.refs_5_.refs_4_
  73.0 1.4 %shard_map.123 = (bf16[128,1024]{1,0:T(8,128)(2,1)S(1)}, bf16[128,1024]{1,0:T(8,128)(2,1)S(1)}) custom-call(f32[8,128]{1,0:T(8,128)S(1)} %get-tuple-element.36.x_tab.refs_1_.refs_0_, f32[8,128]{1,0:T(8,128)S(1)} %get-tuple-element.37.y_tab.refs_2_.refs_1_, bf16[96,1024]{1,0:T(8,128)(2,1)S(1)} %get-tuple-element.51.refs_2_, ...), custom_call_target="tpu_custom_call" | custom-call | flops 1024 | bytes 1024 | tf_op jit(solution)/shard_map/pallas_call | solution.py:242
  74.4 1.4 %collective-permute-start.17 = (bf16[128,1024]{1,0:T(8,128)(2,1)S(1)}, bf16[128,1024]{1,0:T(8,128)(2,1)S(1)}, u32[]{:S(2)}, u32[]{:S(2)}) collective-permute-start(bf16[128,1024]{1,0:T(8,128)(2,1)S(1)} %get-tuple-element.57), channel_id=1, source_target_pairs={{0,2},{1,3},{2,0},{3,1},{4,6},{5,7},{6,4},{7,5},{8,10},{9,11},{10,... | collective-permute-start | bytes 786440 | tf_op jit(solution)/shard_map/ppermute | solution.py:23
  75.9 0.6 collective-permute-start.16
  76.5 6.5 %collective-permute-done.18.refs_4_.got_y = bf16[192,1024]{1,0:T(8,128)(2,1)S(1)} collective-permute-done((bf16[192,1024]{1,0:T(8,128)(2,1)S(1)}, bf16[192,1024]{1,0:T(8,128)(2,1)S(1)}, u32[]{:S(2)}, u32[]{:S(2)}) %collective-permute-start.18) | collective-permute-done | bytes 393248 | tf_op jit(solution)/shard_map/ppermute | solution.py:23
  83.0 0.0 collective-permute-done.19.refs_5_.got_x
  83.0 0.8 shard_map.124
  83.8 1.5 %collective-permute-start.21 = (bf16[128,1024]{1,0:T(8,128)(2,1)S(1)}, bf16[128,1024]{1,0:T(8,128)(2,1)S(1)}, u32[]{:S(2)}, u32[]{:S(2)}) collective-permute-start(bf16[128,1024]{1,0:T(8,128)(2,1)S(1)} %get-tuple-element.63), channel_id=1, source_target_pairs={{0,2},{1,3},{2,0},{3,1},{4,6},{5,7},{6,4},{7,5},{8,10},{9,11},{10,... | collective-permute-start | bytes 786440 | tf_op jit(solution)/shard_map/ppermute | solution.py:23
  85.3 1.1 %collective-permute-start.20 = (bf16[128,1024]{1,0:T(8,128)(2,1)S(1)}, bf16[128,1024]{1,0:T(8,128)(2,1)S(1)}, u32[]{:S(2)}, u32[]{:S(2)}) collective-permute-start(bf16[128,1024]{1,0:T(8,128)(2,1)S(1)} %get-tuple-element.62.refs_7_), channel_id=1, source_target_pairs={{0,1},{1,0},{2,3},{3,2},{4,5},{5,4},{6,7},{7,6},{8,9},{9,8},{10,11... | collective-permute-start | bytes 786440 | tf_op jit(solution)/shard_map/ppermute | solution.py:23
  86.4 0.9 collective-permute-done.17.refs_6_
  87.2 0.0 collective-permute-done.16.refs_5_
  87.2 1.7 %shard_map.125 = bf16[128,2048]{1,0:T(8,128)(2,1)} custom-call(bf16[128,2048]{1,0:T(8,128)(2,1)S(1)} %collective-permute-done.refs_0_, f32[8,128]{1,0:T(8,128)S(1)} %get-tuple-element.33.own.refs_0_.refs_1_, bf16[96,2048]{1,0:T(8,128)(2,1)S(1)} %get-tuple-element.48.refs_13_.refs_2_, bf16[192,1024]{1,0:T(8,128)(2,1)S(1)} %collective-permute-done.12.refs_4_.refs_3_, ...), custom_call_target="tpu_custom_call" | custom-call | flops 1024 | bytes 1024 | tf_op jit(solution)/shard_map/pallas_call | solution.py:242
  88.9 1.3 %collective-permute-done.21.sum_y = bf16[128,1024]{1,0:T(8,128)(2,1)S(1)} collective-permute-done((bf16[128,1024]{1,0:T(8,128)(2,1)S(1)}, bf16[128,1024]{1,0:T(8,128)(2,1)S(1)}, u32[]{:S(2)}, u32[]{:S(2)}) %collective-permute-start.21) | collective-permute-done | bytes 262176 | tf_op jit(solution)/shard_map/ppermute | solution.py:23
  90.2 1.5 %collective-permute-done.20.sum_x = bf16[128,1024]{1,0:T(8,128)(2,1)S(1)} collective-permute-done((bf16[128,1024]{1,0:T(8,128)(2,1)S(1)}, bf16[128,1024]{1,0:T(8,128)(2,1)S(1)}, u32[]{:S(2)}, u32[]{:S(2)}) %collective-permute-start.20) | collective-permute-done | bytes 262176 | tf_op jit(solution)/shard_map/ppermute | solution.py:23
  91.7 0.0 copy-done.3
  91.7 0.0 copy-done.5
  91.7 1.7 %shard_map.126 = bf16[128,2048]{1,0:T(8,128)(2,1)} custom-call(bf16[128,2048]{1,0:T(8,128)(2,1)S(1)} %collective-permute-done.5.refs_0_.grads_ref, bf16[128,2048]{1,0:T(8,128)(2,1)S(1)} %bitcast.26, f32[1,2048]{1,0:T(1,128)S(1)} %copy-done.5, f32[8,128]{1,0:T(8,128)S(1)} %get-tuple-element.33.own.refs_0_.refs_1_, ...), custom_call_target="tpu_custom_call" | custom-call | flops 1024 | bytes 1024 | tf_op jit(solution)/shard_map/pallas_call | solution.py:242
  (6 shorter events, 0.1 us)
Async XLA Ops:
  0.6 17.0 %collective-permute-start = (bf16[128,2048]{1,0:T(8,128)(2,1)}, bf16[128,2048]{1,0:T(8,128)(2,1)S(1)}, u32[]{:S(2)}, u32[]{:S(2)}) collective-permute-start(bf16[128,2048]{1,0:T(8,128)(2,1)} %bitcast.33), channel_id=1, source_target_pairs={{0,4},{4,8},{8,12},{12,16},{16,20},{20,24},{24,28},{28,0},{1,5},{5... | collective-permute-start | bytes 1572872 | tf_op jit(solution)/shard_map/ppermute | solution.py:17
  2.5 9.3 %collective-permute-start.1 = (bf16[144,1024]{1,0:T(8,128)(2,1)S(1)}, bf16[144,1024]{1,0:T(8,128)(2,1)S(1)}, u32[]{:S(2)}, u32[]{:S(2)}) collective-permute-start(bf16[144,1024]{1,0:T(8,128)(2,1)S(1)} %get-tuple-element.34.left.refs_3_), channel_id=1, source_target_pairs={{0,1},{1,0},{2,3},{3,2},{4,5},{5,4},{6,7},{7,6},{8,9},{9,8},{10,11... | collective-permute-start | bytes 884744 | tf_op jit(solution)/shard_map/ppermute | solution.py:23
  5.0 9.5 %collective-permute-start.2 = (bf16[144,1024]{1,0:T(8,128)(2,1)S(1)}, bf16[144,1024]{1,0:T(8,128)(2,1)S(1)}, u32[]{:S(2)}, u32[]{:S(2)}) collective-permute-start(bf16[144,1024]{1,0:T(8,128)(2,1)S(1)} %get-tuple-element.35.right.refs_4_), channel_id=1, source_target_pairs={{0,2},{1,3},{2,0},{3,1},{4,6},{5,7},{6,4},{7,5},{8,10},{9,11},{10,... | collective-permute-start | bytes 884744 | tf_op jit(solution)/shard_map/ppermute | solution.py:23
  6.6 14.0 %collective-permute-start.5 = (bf16[128,2048]{1,0:T(8,128)(2,1)}, bf16[128,2048]{1,0:T(8,128)(2,1)S(1)}, u32[]{:S(2)}, u32[]{:S(2)}) collective-permute-start(bf16[128,2048]{1,0:T(8,128)(2,1)} %bitcast.34), channel_id=1, source_target_pairs={{0,28},{4,0},{8,4},{12,8},{16,12},{20,16},{24,20},{28,24},{1,29},{... | collective-permute-start | bytes 1572872 | tf_op jit(solution)/shard_map/ppermute | solution.py:17
  15.5 21.6 %collective-permute-start.11 = (bf16[192,1024]{1,0:T(8,128)(2,1)S(1)}, bf16[192,1024]{1,0:T(8,128)(2,1)S(1)}, u32[]{:S(2)}, u32[]{:S(2)}) collective-permute-start(bf16[192,1024]{1,0:T(8,128)(2,1)S(1)} %get-tuple-element.45), channel_id=1, source_target_pairs={{0,1},{1,0},{2,3},{3,2},{4,5},{5,4},{6,7},{7,6},{8,9},{9,8},{10,11... | collective-permute-start | bytes 1179656 | tf_op jit(solution)/shard_map/ppermute | solution.py:23
  15.5 22.1 %collective-permute-start.10 = (bf16[192,1024]{1,0:T(8,128)(2,1)S(1)}, bf16[192,1024]{1,0:T(8,128)(2,1)S(1)}, u32[]{:S(2)}, u32[]{:S(2)}) collective-permute-start(bf16[192,1024]{1,0:T(8,128)(2,1)S(1)} %get-tuple-element.38.refs_2_), channel_id=1, source_target_pairs={{0,2},{1,3},{2,0},{3,1},{4,6},{5,7},{6,4},{7,5},{8,10},{9,11},{10,... | collective-permute-start | bytes 1179656 | tf_op jit(solution)/shard_map/ppermute | solution.py:23
  17.6 0.7 copy-start.4
  18.5 14.1 %collective-permute-start.4 = (bf16[128,1024]{1,0:T(8,128)(2,1)S(1)}, bf16[128,1024]{1,0:T(8,128)(2,1)S(1)}, u32[]{:S(2)}, u32[]{:S(2)}) collective-permute-start(bf16[128,1024]{1,0:T(8,128)(2,1)S(1)} %get-tuple-element.40.refs_4_), channel_id=1, source_target_pairs={{0,2},{1,3},{2,0},{3,1},{4,6},{5,7},{6,4},{7,5},{8,10},{9,11},{10,... | collective-permute-start | bytes 786440 | tf_op jit(solution)/shard_map/ppermute | solution.py:23
  18.6 14.0 %collective-permute-start.3 = (bf16[128,1024]{1,0:T(8,128)(2,1)S(1)}, bf16[128,1024]{1,0:T(8,128)(2,1)S(1)}, u32[]{:S(2)}, u32[]{:S(2)}) collective-permute-start(bf16[128,1024]{1,0:T(8,128)(2,1)S(1)} %get-tuple-element.39.refs_1_.refs_3_), channel_id=1, source_target_pairs={{0,1},{1,0},{2,3},{3,2},{4,5},{5,4},{6,7},{7,6},{8,9},{9,8},{10,11... | collective-permute-start | bytes 786440 | tf_op jit(solution)/shard_map/ppermute | solution.py:23
  33.5 20.8 %collective-permute-start.7 = (bf16[192,1024]{1,0:T(8,128)(2,1)S(1)}, bf16[192,1024]{1,0:T(8,128)(2,1)S(1)}, u32[]{:S(2)}, u32[]{:S(2)}) collective-permute-start(bf16[192,1024]{1,0:T(8,128)(2,1)S(1)} %get-tuple-element.43), channel_id=1, source_target_pairs={{0,1},{1,0},{2,3},{3,2},{4,5},{5,4},{6,7},{7,6},{8,9},{9,8},{10,11... | collective-permute-start | bytes 1179656 | tf_op jit(solution)/shard_map/ppermute | solution.py:23
  35.0 19.3 %collective-permute-start.6 = (bf16[192,1024]{1,0:T(8,128)(2,1)S(1)}, bf16[192,1024]{1,0:T(8,128)(2,1)S(1)}, u32[]{:S(2)}, u32[]{:S(2)}) collective-permute-start(bf16[192,1024]{1,0:T(8,128)(2,1)S(1)} %get-tuple-element.42.refs_10_), channel_id=1, source_target_pairs={{0,2},{1,3},{2,0},{3,1},{4,6},{5,7},{6,4},{7,5},{8,10},{9,11},{10,... | collective-permute-start | bytes 1179656 | tf_op jit(solution)/shard_map/ppermute | solution.py:23
  36.5 13.9 %collective-permute-start.9 = (bf16[128,1024]{1,0:T(8,128)(2,1)S(1)}, bf16[128,1024]{1,0:T(8,128)(2,1)S(1)}, u32[]{:S(2)}, u32[]{:S(2)}) collective-permute-start(bf16[128,1024]{1,0:T(8,128)(2,1)S(1)} %get-tuple-element.44.refs_4_), channel_id=1, source_target_pairs={{0,2},{1,3},{2,0},{3,1},{4,6},{5,7},{6,4},{7,5},{8,10},{9,11},{10,... | collective-permute-start | bytes 786440 | tf_op jit(solution)/shard_map/ppermute | solution.py:23
  37.1 13.3 %collective-permute-start.8 = (bf16[128,1024]{1,0:T(8,128)(2,1)S(1)}, bf16[128,1024]{1,0:T(8,128)(2,1)S(1)}, u32[]{:S(2)}, u32[]{:S(2)}) collective-permute-start(bf16[128,1024]{1,0:T(8,128)(2,1)S(1)} %get-tuple-element.41.refs_7_.refs_3_), channel_id=1, source_target_pairs={{0,1},{1,0},{2,3},{3,2},{4,5},{5,4},{6,7},{7,6},{8,9},{9,8},{10,11... | collective-permute-start | bytes 786440 | tf_op jit(solution)/shard_map/ppermute | solution.py:23
  37.7 2.8 %copy-start = (bf16[1,1,2048,1536]{3,2,1,0:T(8,128)(2,1)S(1)}, bf16[1,1,2048,1536]{3,2,1,0:T(8,128)(2,1)}, u32[]{:S(2)}) copy-start(bf16[1,1,2048,1536]{3,2,1,0:T(8,128)(2,1)} %param.18) | copy-start | bytes 18874372
  40.4 13.8 %copy-start.1 = (bf16[1,1,2048,1536]{3,2,1,0:T(8,128)(2,1)S(1)}, bf16[1,1,2048,1536]{3,2,1,0:T(8,128)(2,1)}, u32[]{:S(2)}) copy-start(bf16[1,1,2048,1536]{3,2,1,0:T(8,128)(2,1)} %param.18) | copy-start | bytes 18874372
  40.4 13.9 %copy-start.2 = (bf16[1,1,768,2048]{3,2,1,0:T(8,128)(2,1)S(1)}, bf16[1,1,768,2048]{3,2,1,0:T(8,128)(2,1)}, u32[]{:S(2)}) copy-start(bf16[1,1,768,2048]{3,2,1,0:T(8,128)(2,1)} %param.19) | copy-start | bytes 9437188
  51.5 10.4 %collective-permute-start.15 = (bf16[192,1024]{1,0:T(8,128)(2,1)S(1)}, bf16[192,1024]{1,0:T(8,128)(2,1)S(1)}, u32[]{:S(2)}, u32[]{:S(2)}) collective-permute-start(bf16[192,1024]{1,0:T(8,128)(2,1)S(1)} %get-tuple-element.53), channel_id=1, source_target_pairs={{0,1},{1,0},{2,3},{3,2},{4,5},{5,4},{6,7},{7,6},{8,9},{9,8},{10,11... | collective-permute-start | bytes 1179656 | tf_op jit(solution)/shard_map/ppermute | solution.py:23
  52.8 12.1 %collective-permute-start.14 = (bf16[192,1024]{1,0:T(8,128)(2,1)S(1)}, bf16[192,1024]{1,0:T(8,128)(2,1)S(1)}, u32[]{:S(2)}, u32[]{:S(2)}) collective-permute-start(bf16[192,1024]{1,0:T(8,128)(2,1)S(1)} %get-tuple-element.47.refs_11_), channel_id=1, source_target_pairs={{0,2},{1,3},{2,0},{3,1},{4,6},{5,7},{6,4},{7,5},{8,10},{9,11},{10,... | collective-permute-start | bytes 1179656 | tf_op jit(solution)/shard_map/ppermute | solution.py:23
  58.8 14.2 %collective-permute-start.12 = (bf16[192,1024]{1,0:T(8,128)(2,1)S(1)}, bf16[192,1024]{1,0:T(8,128)(2,1)S(1)}, u32[]{:S(2)}, u32[]{:S(2)}) collective-permute-start(bf16[192,1024]{1,0:T(8,128)(2,1)S(1)} %get-tuple-element.49), channel_id=1, source_target_pairs={{0,2},{1,3},{2,0},{3,1},{4,6},{5,7},{6,4},{7,5},{8,10},{9,11},{10,... | collective-permute-start | bytes 1179656 | tf_op jit(solution)/shard_map/ppermute | solution.py:23
  59.4 13.6 %collective-permute-start.13 = (bf16[192,1024]{1,0:T(8,128)(2,1)S(1)}, bf16[192,1024]{1,0:T(8,128)(2,1)S(1)}, u32[]{:S(2)}, u32[]{:S(2)}) collective-permute-start(bf16[192,1024]{1,0:T(8,128)(2,1)S(1)} %get-tuple-element.50), channel_id=1, source_target_pairs={{0,1},{1,0},{2,3},{3,2},{4,5},{5,4},{6,7},{7,6},{8,9},{9,8},{10,11... | collective-permute-start | bytes 1179656 | tf_op jit(solution)/shard_map/ppermute | solution.py:23
  70.8 20.9 %copy-start.3 = (bf16[1,128,2048]{2,1,0:T(8,128)(2,1)S(1)}, bf16[1,128,2048]{2,1,0:T(8,128)(2,1)}, u32[]{:S(2)}) copy-start(bf16[1,128,2048]{2,1,0:T(8,128)(2,1)} %param.12) | copy-start | bytes 1572868
  70.8 20.8 %copy-start.5 = (f32[1,2048]{1,0:T(1,128)S(1)}, f32[1,2048]{1,0:T(1,128)}, u32[]{:S(2)}) copy-start(f32[1,2048]{1,0:T(1,128)} %gain_ref.1) | copy-start | bytes 24580
  70.8 12.1 %collective-permute-start.18 = (bf16[192,1024]{1,0:T(8,128)(2,1)S(1)}, bf16[192,1024]{1,0:T(8,128)(2,1)S(1)}, u32[]{:S(2)}, u32[]{:S(2)}) collective-permute-start(bf16[192,1024]{1,0:T(8,128)(2,1)S(1)} %get-tuple-element.60), channel_id=1, source_target_pairs={{0,2},{1,3},{2,0},{3,1},{4,6},{5,7},{6,4},{7,5},{8,10},{9,11},{10,... | collective-permute-start | bytes 1179656 | tf_op jit(solution)/shard_map/ppermute | solution.py:23
  72.4 10.6 %collective-permute-start.19 = (bf16[192,1024]{1,0:T(8,128)(2,1)S(1)}, bf16[192,1024]{1,0:T(8,128)(2,1)S(1)}, u32[]{:S(2)}, u32[]{:S(2)}) collective-permute-start(bf16[192,1024]{1,0:T(8,128)(2,1)S(1)} %get-tuple-element.61), channel_id=1, source_target_pairs={{0,1},{1,0},{2,3},{3,2},{4,5},{5,4},{6,7},{7,6},{8,9},{9,8},{10,11... | collective-permute-start | bytes 1179656 | tf_op jit(solution)/shard_map/ppermute | solution.py:23
  74.4 12.8 %collective-permute-start.17 = (bf16[128,1024]{1,0:T(8,128)(2,1)S(1)}, bf16[128,1024]{1,0:T(8,128)(2,1)S(1)}, u32[]{:S(2)}, u32[]{:S(2)}) collective-permute-start(bf16[128,1024]{1,0:T(8,128)(2,1)S(1)} %get-tuple-element.57), channel_id=1, source_target_pairs={{0,2},{1,3},{2,0},{3,1},{4,6},{5,7},{6,4},{7,5},{8,10},{9,11},{10,... | collective-permute-start | bytes 786440 | tf_op jit(solution)/shard_map/ppermute | solution.py:23
  75.9 11.4 %collective-permute-start.16 = (bf16[128,1024]{1,0:T(8,128)(2,1)S(1)}, bf16[128,1024]{1,0:T(8,128)(2,1)S(1)}, u32[]{:S(2)}, u32[]{:S(2)}) collective-permute-start(bf16[128,1024]{1,0:T(8,128)(2,1)S(1)} %get-tuple-element.56.refs_6_), channel_id=1, source_target_pairs={{0,1},{1,0},{2,3},{3,2},{4,5},{5,4},{6,7},{7,6},{8,9},{9,8},{10,11... | collective-permute-start | bytes 786440 | tf_op jit(solution)/shard_map/ppermute | solution.py:23
  83.8 6.4 %collective-permute-start.21 = (bf16[128,1024]{1,0:T(8,128)(2,1)S(1)}, bf16[128,1024]{1,0:T(8,128)(2,1)S(1)}, u32[]{:S(2)}, u32[]{:S(2)}) collective-permute-start(bf16[128,1024]{1,0:T(8,128)(2,1)S(1)} %get-tuple-element.63), channel_id=1, source_target_pairs={{0,2},{1,3},{2,0},{3,1},{4,6},{5,7},{6,4},{7,5},{8,10},{9,11},{10,... | collective-permute-start | bytes 786440 | tf_op jit(solution)/shard_map/ppermute | solution.py:23
  85.3 6.4 %collective-permute-start.20 = (bf16[128,1024]{1,0:T(8,128)(2,1)S(1)}, bf16[128,1024]{1,0:T(8,128)(2,1)S(1)}, u32[]{:S(2)}, u32[]{:S(2)}) collective-permute-start(bf16[128,1024]{1,0:T(8,128)(2,1)S(1)} %get-tuple-element.62.refs_7_), channel_id=1, source_target_pairs={{0,1},{1,0},{2,3},{3,2},{4,5},{5,4},{6,7},{7,6},{8,9},{9,8},{10,11... | collective-permute-start | bytes 786440 | tf_op jit(solution)/shard_map/ppermute | solution.py:23

commit v5 on v4

--- a/solution.py
+++ b/solution.py
@@ -400,7 +400,7 @@
 
 def first_kernel(top_count, me_ref, *refs):
     sources, refs = refs[:6], refs[6:]
-    (left_ref, right_ref, table_ref), refs = refs[:3], refs[3:]
+    (left_ref, right_ref, table_ref, gain_out), refs = refs[:4], refs[4:]
     held, sems = refs[:6], refs[6]
     copies = [pltpu.make_async_copy(sources[i], held[i], sems.at[i]) for i in range(6)]
     for copy in copies:
@@ -416,6 +416,7 @@
     table_ref[...] = jnp.concatenate([fr, fg, br, bg], axis=0)
     packed = [fr.astype(jnp.bfloat16), br.astype(jnp.bfloat16), *three_parts(fg), *three_parts(bg)]
     packed = jnp.concatenate([part.astype(jnp.float32) for part in packed], axis=0)
+    gain_out[...] = gain[...]
     tok_rows, features = saved.shape
     half = features // 2
     copies[0].wait()
@@ -486,20 +487,47 @@
     rows[3 * capacity :, half:] = got_x[capacity:, :]
 
 
-def hand_out(out, start, capacity, half, keep, x_left, y_right, to_y, to_x):
+def hand_out(out, at, capacity, to_left, keep, near, onward):
     size = out.shape[1]
     rows = out.astype(jnp.bfloat16)
-    parts = [rows[d * capacity : (d + 1) * capacity] for d in range(4)]
-    keep[:, start : start + size] = parts[0]
-    if start < half:
-        x_left[:, start : start + size] = parts[1]
-        to_y[:capacity, start : start + size] = parts[2]
-        to_y[capacity:, start : start + size] = parts[3]
-    else:
-        at = start - half
-        to_x[:capacity, at : at + size] = parts[1]
-        y_right[:, at : at + size] = parts[2]
-        to_x[capacity:, at : at + size] = parts[3]
+    mine, from_x, from_y, far = [rows[d * capacity : (d + 1) * capacity] for d in range(4)]
+    keep[:, at : at + size] = mine
+    near[:, at : at + size] = from_x if to_left else from_y
+    onward[:capacity, at : at + size] = from_y if to_left else from_x
+    onward[capacity:, at : at + size] = far
+
+
+def fwd_half(hidden_ref, weight_out, to_left, keep, near, onward):
+    capacity, half = keep.shape
+    first = 0 if to_left else half
+    for at, size in tiles(half, 512):
+        out = jnp.dot(
+            hidden_ref[...],
+            weight_out[:, first + at : first + at + size],
+            preferred_element_type=jnp.float32,
+        )
+        hand_out(out, at, capacity, to_left, keep, near, onward)
+
+
+def bwd_half(both_ref, weight_in, to_left, keep, near, onward):
+    capacity, half = keep.shape
+    first = 0 if to_left else half
+    for at, size in tiles(half, 512):
+        out = lax.dot_general(
+            both_ref[...],
+            weight_in[first + at : first + at + size, :],
+            (((1,), (1,)), ((), ())),
+            preferred_element_type=jnp.float32,
+        )
+        hand_out(out, at, capacity, to_left, keep, near, onward)
+
+
+def fwd_right_kernel(hidden_ref, weight_out, keep, near, onward):
+    fwd_half(hidden_ref, weight_out, False, keep, near, onward)
+
+
+def bwd_right_kernel(both_ref, weight_in, keep, near, onward):
+    bwd_half(both_ref, weight_in, False, keep, near, onward)
 
 
 def hop_again_kernel(top_count, *refs):
@@ -520,9 +548,8 @@
 def hop_fwd_kernel(top_count, *refs):
     dispatch, refs = refs[:9], refs[9:]
     weight_in, weight_out = refs[:2]
-    outs, (rows_ref, hidden_ref) = refs[2:7], refs[7:]
-    capacity = outs[0].shape[0]
-    hidden_units, features = weight_out.shape
+    outs, hidden_ref, rows_ref = refs[2:5], refs[5], refs[6]
+    hidden_units = weight_out.shape[0]
     assemble("f", top_count, *dispatch, rows_ref)
     for start, size in tiles(hidden_units, 256):
         gate = jnp.dot(
@@ -536,19 +563,14 @@
         hidden_ref[:, start : start + size] = (gate / (1.0 + jnp.exp(-gate)) * up).astype(
             jnp.bfloat16
         )
-    for start, size in tiles(features, features // 4):
-        out = jnp.dot(
-            hidden_ref[...], weight_out[:, start : start + size], preferred_element_type=jnp.float32
-        )
-        hand_out(out, start, capacity, features // 2, *outs)
+    fwd_half(hidden_ref, weight_out, True, *outs)
 
 
 def hop_bwd_kernel(top_count, *refs):
     dispatch, refs = refs[:9], refs[9:]
     gate_ref, up_ref, weight_in, weight_out = refs[:4]
-    outs, (grads_ref, both_ref) = refs[4:9], refs[9:]
-    capacity = outs[0].shape[0]
-    hidden_units, features = weight_out.shape
+    outs, both_ref, grads_ref = refs[4:7], refs[7], refs[8]
+    hidden_units = weight_out.shape[0]
     assemble("bg", top_count, *dispatch, grads_ref)
     for start, size in tiles(hidden_units, 256):
         gate = gate_ref[:, start : start + size]
@@ -566,52 +588,40 @@
         both_ref[:, hidden_units + start : hidden_units + start + size] = (
             d_hidden * gate * sig
         ).astype(jnp.bfloat16)
-    for start, size in tiles(features, features // 4):
-        out = lax.dot_general(
-            both_ref[...],
-            weight_in[start : start + size, :],
-            (((1,), (1,)), ((), ())),
-            preferred_element_type=jnp.float32,
-        )
-        hand_out(out, start, capacity, features // 2, *outs)
-
-
-def sums_kernel(kind, top_count, x_tab, y_tab, x_left, y_right, got_y, got_x, sum_x, sum_y):
-    capacity = x_left.shape[0]
-    for table, near, far, out in (
-        ((x_tab, 1), x_left, got_y, sum_x),
-        ((y_tab, 2), y_right, got_x, sum_y),
-    ):
-        tab = table[0][...]
-        out[...] = (
-            to_tokens(pick(tab, table[1], capacity, kind, top_count), near[...])
-            + to_tokens(pick(tab, 3, capacity, kind, top_count), far[capacity:, :])
-        ).astype(jnp.bfloat16)
-
-
-def summed(kind, top_count, own, keep, got_y, got_x, sum_x, sum_y):
-    capacity, features = keep.shape
-    half = features // 2
+    bwd_half(both_ref, weight_in, True, *outs)
+
+
+def sums_kernel(kind, top_count, here, table_ref, near, far, out):
+    capacity = near.shape[0]
+    table = table_ref[...]
+    out[...] = (
+        to_tokens(pick(table, here, capacity, kind, top_count), near[...])
+        + to_tokens(pick(table, 3, capacity, kind, top_count), far[capacity:, :])
+    ).astype(jnp.bfloat16)
+
+
+def summed(kind, top_count, own, keep_left, keep_right, got_y, got_x, sum_x, sum_y):
+    capacity = keep_left.shape[0]
     mine = pick(own[...], 0, capacity, kind, top_count)
     near_y = pick(own[...], 2, capacity, kind, top_count)
     near_x = pick(own[...], 1, capacity, kind, top_count)
-    left = to_tokens(mine, keep[:, :half]) + to_tokens(near_y, got_y[:capacity, :])
-    right = to_tokens(mine, keep[:, half:]) + to_tokens(near_x, got_x[:capacity, :])
+    left = to_tokens(mine, keep_left[...]) + to_tokens(near_y, got_y[:capacity, :])
+    right = to_tokens(mine, keep_right[...]) + to_tokens(near_x, got_x[:capacity, :])
     return left + sum_x[...].astype(jnp.float32), right + sum_y[...].astype(jnp.float32)
 
 
-def hop_fwd_end_kernel(top_count, layer_ref, own, keep, got_y, got_x, sum_x, sum_y, out_ref):
-    half = got_y.shape[1]
-    left, right = summed("fg", top_count, own, keep, got_y, got_x, sum_x, sum_y)
+def hop_fwd_end_kernel(top_count, layer_ref, *refs):
+    out_ref = refs[-1]
+    half = layer_ref.shape[1] // 2
+    left, right = summed("fg", top_count, *refs[:-1])
     out_ref[:, :half] = (layer_ref[:, :half].astype(jnp.float32) + left).astype(jnp.bfloat16)
     out_ref[:, half:] = (layer_ref[:, half:].astype(jnp.float32) + right).astype(jnp.bfloat16)
 
 
-def hop_bwd_end_kernel(
-    top_count, grads_ref, saved_ref, gain_ref, own, keep, got_y, got_x, sum_x, sum_y, out_ref
-):
+def hop_bwd_end_kernel(top_count, grads_ref, saved_ref, gain_ref, *refs):
+    out_ref = refs[-1]
     features = saved_ref.shape[1]
-    left, right = summed("b", top_count, own, keep, got_y, got_x, sum_x, sum_y)
+    left, right = summed("b", top_count, *refs[:-1])
     wide = saved_ref[...].astype(jnp.float32)
     inv_rms = lax.rsqrt(jnp.mean(wide * wide, axis=-1, keepdims=True) + EPS)
     scaled = jnp.concatenate([left, right], axis=1) * gain_ref[...]
@@ -661,13 +671,20 @@
     rows_scratch = pltpu.VMEM((slot_total, features), jnp.bfloat16)
     halves_out = [shaped(tok_rows, half)] * 2
     hop_out = [shaped(2 * capacity, half)] * 2
-    expert_out = [shaped(capacity, features), shaped(capacity, half), shaped(capacity, half)] + hop_out
+    half_out = [shaped(capacity, half), shaped(capacity, half), shaped(2 * capacity, half)]
+    hidden_shape = shaped(slot_total, hidden_units)
+    both_shape = shaped(slot_total, 2 * hidden_units)
     table_shape = shaped(table_rows, tok_rows, jnp.float32)
     first_rows = tok_rows + 8 * top_count
 
-    b_left, b_right, own = pl.pallas_call(
+    b_left, b_right, own, gain_here = pl.pallas_call(
         functools.partial(first_kernel, top_count),
-        out_shape=[shaped(first_rows, half), shaped(first_rows, half), table_shape],
+        out_shape=[
+            shaped(first_rows, half),
+            shaped(first_rows, half),
+            table_shape,
+            shaped(1, features, jnp.float32),
+        ],
         in_specs=[pl.BlockSpec(memory_space=pltpu.SMEM)]
         + [pl.BlockSpec(memory_space=pltpu.HBM)] * 6,
         scratch_shapes=[
@@ -718,12 +735,13 @@
 
     b_got_y, b_got_x, b_to_y = onward("b", (b_left, b_right), (b_from_x, b_from_y), ())
     f_left, f_right = local_call(
-        normed_kernel_halves, halves_out, (layer_in, gain_row), one_hop, moved, after=(b_to_y,)
+        normed_kernel_halves, halves_out, (layer_in, gain_here), one_hop, moved, after=(b_to_y,)
     )
     f_from_x, f_from_y = crossed(f_left, f_right)
     g_left, g_right = local_call(split_kernel, halves_out, (grad_in,), 1024, moved, after=(f_left,))
     g_from_x, g_from_y = crossed(g_left, g_right)
     f_got_y, f_got_x, f_to_y = onward("f", (f_left, f_right), (f_from_x, f_from_y), (g_left,))
+    g_got_y, g_got_x, g_to_y = onward("bg", (g_left, g_right), (g_from_x, g_from_y), (f_to_y,))
     gate_pre, up_pre = local_call(
         functools.partial(hop_again_kernel, top_count),
         [shaped(slot_total, hidden_units, jnp.float32)] * 2,
@@ -731,22 +749,25 @@
         2 * expert_flops,
         expert_moved,
         scratch=(rows_scratch,),
-        after=(f_to_y,),
-    )
-    g_got_y, g_got_x, g_to_y = onward("bg", (g_left, g_right), (g_from_x, g_from_y), (gate_pre,))
-    f_keep, f_x_left, f_y_right, f_to_y, f_to_x = local_call(
+        after=(g_to_y,),
+    )
+    f_keep_l, f_near_l, f_on_l, hidden = local_call(
         functools.partial(hop_fwd_kernel, top_count),
-        expert_out,
+        half_out + [hidden_shape],
         (*tabs, f_left, f_right, f_from_x, f_from_y, f_got_y, f_got_x, weight_in, weight_out),
-        3 * expert_flops,
+        5 * expert_flops // 2,
         expert_moved,
-        scratch=(rows_scratch, pltpu.VMEM((slot_total, hidden_units), jnp.bfloat16)),
-        after=(g_to_y,),
-    )
-    f_ret_y, f_ret_x = swapped(f_to_y, "expert", 2), swapped(f_to_x, "expert", 1)
-    b_keep, b_x_left, b_y_right, b_to_y, b_to_x = local_call(
+        scratch=(rows_scratch,),
+        after=(gate_pre,),
+    )
+    f_ret_y = swapped(f_on_l, "expert", 2)
+    f_keep_r, f_near_r, f_on_r = local_call(
+        fwd_right_kernel, half_out, (hidden, weight_out), 1024, 1024
+    )
+    f_ret_x = swapped(f_on_r, "expert", 1)
+    b_keep_l, b_near_l, b_on_l, both = local_call(
         functools.partial(hop_bwd_kernel, top_count),
-        expert_out,
+        half_out + [both_shape],
         (
             *tabs,
             g_left,
@@ -760,38 +781,46 @@
             weight_in,
             weight_out,
         ),
-        3 * expert_flops,
+        2 * expert_flops,
         expert_moved,
-        scratch=(rows_scratch, pltpu.VMEM((slot_total, 2 * hidden_units), jnp.bfloat16)),
-        after=(f_keep,),
-    )
-    b_ret_y, b_ret_x = swapped(b_to_y, "expert", 2), swapped(b_to_x, "expert", 1)
-
-    def summed_call(kind, x_left, y_right, ret_y, ret_x, after):
-        sums = local_call(
-            functools.partial(sums_kernel, kind, top_count),
-            halves_out,
-            (x_tab, y_tab, x_left, y_right, ret_y, ret_x),
+        scratch=(rows_scratch,),
+        after=(f_keep_r,),
+    )
+    b_ret_y = swapped(b_on_l, "expert", 2)
+    b_keep_r, b_near_r, b_on_r = local_call(
+        bwd_right_kernel, half_out, (both, weight_in), 1024, 1024
+    )
+    b_ret_x = swapped(b_on_r, "expert", 1)
+
+    def summed_call(kind, here, table, near, far, after):
+        part = local_call(
+            functools.partial(sums_kernel, kind, top_count, here),
+            shaped(tok_rows, half),
+            (table, near, far),
             one_hop,
             moved,
             after=after,
         )
-        return (*crossed(*sums), sums[0])
-
-    f_sum_x, f_sum_y, f_sum = summed_call("fg", f_x_left, f_y_right, f_ret_y, f_ret_x, (b_keep,))
-    b_sum_x, b_sum_y, b_sum = summed_call("b", b_x_left, b_y_right, b_ret_y, b_ret_x, (f_sum,))
+        return swapped(part, "expert", here), part
+
+    f_sum_x, last = summed_call("fg", 1, x_tab, f_near_l, f_ret_y, (b_keep_r,))
+    f_sum_y, last = summed_call("fg", 2, y_tab, f_near_r, f_ret_x, (last,))
+    b_sum_x, last = summed_call("b", 1, x_tab, b_near_l, b_ret_y, (last,))
+    b_sum_y, last = summed_call("b", 2, y_tab, b_near_r, b_ret_x, (last,))
+    f_keep = (f_keep_l, f_keep_r)
+    b_keep = (b_keep_l, b_keep_r)
     fwd_block = local_call(
         functools.partial(hop_fwd_end_kernel, top_count),
         shaped(tok_rows, features),
-        (layer_in, own, f_keep, f_ret_y, f_ret_x, f_sum_x, f_sum_y),
+        (layer_in, own, *f_keep, f_ret_y, f_ret_x, f_sum_x, f_sum_y),
         one_hop,
         moved,
-        after=(b_sum,),
+        after=(last,),
     )
     bwd_block = local_call(
         functools.partial(hop_bwd_end_kernel, top_count),
         shaped(tok_rows, features),
-        (grad_in, saved, gain_row, own, b_keep, b_ret_y, b_ret_x, b_sum_x, b_sum_y),
+        (grad_in, saved, gain_here, own, *b_keep, b_ret_y, b_ret_x, b_sum_x, b_sum_y),
         one_hop,
         moved,
     )

time: 93.6 us -> 86.2 us (0.921)
  waiting for transfers between devices: 38.5 us -> 32.3 us
  local copies, waits for them, and re-layouts: 3.5 us -> 0.01 us
  starting transfers between devices: 26.8 us -> 28.7 us
    ppermute x20, waiting for transfers between devices: 38.5 us -> 32.3 us  [swapped(): return lax.ppermute(value, axis, pairs)]
    unnamed x12 -> x6, local copies, waits for them, and re-layouts: 3.5 us -> 0.01 us
    ppermute x2, starting transfers between devices: 3.47 us -> 4.61 us  [passed_along(): return lax.ppermute(value, axis, pairs)]
    pallas_call x13 -> x17, Pallas kernels: 22.4 us -> 23 us  [local_call(): pl.pallas_call(body if after else kernel, out_shape=out_shapes, in_specs=...]
  transfers between devices with their start and end apart: 22 -> 22, of which waited for: 10 -> 13; matrix products, arithmetic and copies ran while one was open for 0% -> 0% of each run, Pallas kernels for 24% -> 26%
where the time goes in v5:
time: 86.2 us; the launch traced here: 86.1 us
  waiting for transfers between devices  32.3 us (37%)
  starting transfers between devices  28.7 us (33%)
  Pallas kernels  24.3 us (28%)
    ppermute x20, waiting for transfers between devices, swapped(): return lax.ppermute(value, axis, pairs)  32.3 us
    ppermute x20, starting transfers between devices, swapped(): return lax.ppermute(value, axis, pairs)  24.1 us
    pallas_call x17, Pallas kernels, local_call(): pl.pallas_call(body if after else kernel, out_shape=out_shapes, in_specs=...  23 us
    ppermute x2, starting transfers between devices, passed_along(): return lax.ppermute(value, axis, pairs)  4.61 us
  transfers between devices with their start and end apart: 22, of which 13 were waited for; matrix products, arithmetic and copies ran while one was open for 0% of the time, Pallas kernels for 26%

profile of v5, /device:TPU:0, one launch (start us, length us, event | category | flops | bytes accessed | tf_op | source)
XLA Modules:
  0.0 86.1 jit_solution(11140588492748463146)
XLA Ops:
  0.6 0.5 collective-permute-start
  1.1 4.1 %collective-permute-start.5 = (bf16[128,2048]{1,0:T(8,128)(2,1)}, bf16[128,2048]{1,0:T(8,128)(2,1)S(1)}, u32[]{:S(2)}, u32[]{:S(2)}) collective-permute-start(bf16[128,2048]{1,0:T(8,128)(2,1)} %bitcast.36), channel_id=1, source_target_pairs={{0,28},{4,0},{8,4},{12,8},{16,12},{20,16},{24,20},{28,24},{1,29},{... | collective-permute-start | bytes 1572872 | tf_op jit(solution)/shard_map/ppermute | solution.py:17
  5.2 1.3 %shard_map.113 = (bf16[144,1024]{1,0:T(8,128)(2,1)S(1)}, bf16[144,1024]{1,0:T(8,128)(2,1)S(1)}, f32[8,128]{1,0:T(8,128)S(1)}, f32[1,2048]{1,0:T(1,128)S(1)}) custom-call(s32[1]{0:T(128)} %bitcast.1.me_ref, bf16[128,2048]{1,0:T(8,128)(2,1)} %bitcast.27, f32[1,2048]{1,0:T(1,128)} %refs_1_.1, s32[2,128]{1,0:T(2,128)} %bitcast.31, f32[2,128]{1,0:T(2,128)} %bitcast.32, ...), custom_call_target="tpu_custom_call" | custom-call | flops 1024 | bytes 1024 | tf_op jit(solution)/shard_map/pallas_call | solution.py:680
  6.6 2.0 %collective-permute-start.1 = (bf16[144,1024]{1,0:T(8,128)(2,1)S(1)}, bf16[144,1024]{1,0:T(8,128)(2,1)S(1)}, u32[]{:S(2)}, u32[]{:S(2)}) collective-permute-start(bf16[144,1024]{1,0:T(8,128)(2,1)S(1)} %get-tuple-element.35.left.refs_3_), channel_id=1, source_target_pairs={{0,1},{1,0},{2,3},{3,2},{4,5},{5,4},{6,7},{7,6},{8,9},{9,8},{10,11... | collective-permute-start | bytes 884744 | tf_op jit(solution)/shard_map/ppermute | solution.py:23
  8.6 1.5 %collective-permute-start.2 = (bf16[144,1024]{1,0:T(8,128)(2,1)S(1)}, bf16[144,1024]{1,0:T(8,128)(2,1)S(1)}, u32[]{:S(2)}, u32[]{:S(2)}) collective-permute-start(bf16[144,1024]{1,0:T(8,128)(2,1)S(1)} %get-tuple-element.36.right.refs_4_), channel_id=1, source_target_pairs={{0,2},{1,3},{2,0},{3,1},{4,6},{5,7},{6,4},{7,5},{8,10},{9,11},{10,... | collective-permute-start | bytes 884744 | tf_op jit(solution)/shard_map/ppermute | solution.py:23
  10.1 4.1 %collective-permute-done.1.from_x.refs_5_ = bf16[144,1024]{1,0:T(8,128)(2,1)S(1)} collective-permute-done((bf16[144,1024]{1,0:T(8,128)(2,1)S(1)}, bf16[144,1024]{1,0:T(8,128)(2,1)S(1)}, u32[]{:S(2)}, u32[]{:S(2)}) %collective-permute-start.1) | collective-permute-done | bytes 294944 | tf_op jit(solution)/shard_map/ppermute | solution.py:23
  14.1 1.2 %collective-permute-done.2.from_y.refs_6_ = bf16[144,1024]{1,0:T(8,128)(2,1)S(1)} collective-permute-done((bf16[144,1024]{1,0:T(8,128)(2,1)S(1)}, bf16[144,1024]{1,0:T(8,128)(2,1)S(1)}, u32[]{:S(2)}, u32[]{:S(2)}) %collective-permute-start.2) | collective-permute-done | bytes 294944 | tf_op jit(solution)/shard_map/ppermute | solution.py:23
  15.3 0.0 copy-start
  15.4 0.9 %shard_map.115 = (bf16[192,1024]{1,0:T(8,128)(2,1)S(1)}, bf16[192,1024]{1,0:T(8,128)(2,1)S(1)}) custom-call(f32[8,128]{1,0:T(8,128)S(1)} %get-tuple-element.34.own.refs_0_.refs_1_, f32[8,128]{1,0:T(8,128)S(1)} %get-tuple-element.37.x_tab.refs_1_.refs_0_, f32[8,128]{1,0:T(8,128)S(1)} %get-tuple-element.38.y_tab.refs_2_.refs_0_, ...), custom_call_target="tpu_custom_call" | custom-call | flops 1024 | bytes 1024 | tf_op jit(solution)/shard_map/pallas_call | solution.py:242
  16.2 0.0 collective-permute-done.refs_0_
  16.2 0.2 shard_map.116
  16.5 1.6 %collective-permute-start.4 = (bf16[128,1024]{1,0:T(8,128)(2,1)S(1)}, bf16[128,1024]{1,0:T(8,128)(2,1)S(1)}, u32[]{:S(2)}, u32[]{:S(2)}) collective-permute-start(bf16[128,1024]{1,0:T(8,128)(2,1)S(1)} %get-tuple-element.42.refs_4_), channel_id=1, source_target_pairs={{0,2},{1,3},{2,0},{3,1},{4,6},{5,7},{6,4},{7,5},{8,10},{9,11},{10,... | collective-permute-start | bytes 786440 | tf_op jit(solution)/shard_map/ppermute | solution.py:23
  18.1 1.4 %collective-permute-start.3 = (bf16[128,1024]{1,0:T(8,128)(2,1)S(1)}, bf16[128,1024]{1,0:T(8,128)(2,1)S(1)}, u32[]{:S(2)}, u32[]{:S(2)}) collective-permute-start(bf16[128,1024]{1,0:T(8,128)(2,1)S(1)} %get-tuple-element.41.refs_1_.refs_3_), channel_id=1, source_target_pairs={{0,1},{1,0},{2,3},{3,2},{4,5},{5,4},{6,7},{7,6},{8,9},{9,8},{10,11... | collective-permute-start | bytes 786440 | tf_op jit(solution)/shard_map/ppermute | solution.py:23
  19.5 0.0 collective-permute-done.5.refs_0_.grads_ref
  19.5 0.6 collective-permute-start.11
  20.1 0.6 collective-permute-start.9
  20.7 1.5 %collective-permute-start.8 = (bf16[192,1024]{1,0:T(8,128)(2,1)S(1)}, bf16[192,1024]{1,0:T(8,128)(2,1)S(1)}, u32[]{:S(2)}, u32[]{:S(2)}) collective-permute-start(bf16[192,1024]{1,0:T(8,128)(2,1)S(1)} %get-tuple-element.40.refs_2_), channel_id=1, source_target_pairs={{0,2},{1,3},{2,0},{3,1},{4,6},{5,7},{6,4},{7,5},{8,10},{9,11},{10,... | collective-permute-start | bytes 1179656 | tf_op jit(solution)/shard_map/ppermute | solution.py:23
  22.2 3.0 %collective-permute-done.4.refs_6_ = bf16[128,1024]{1,0:T(8,128)(2,1)S(1)} collective-permute-done((bf16[128,1024]{1,0:T(8,128)(2,1)S(1)}, bf16[128,1024]{1,0:T(8,128)(2,1)S(1)}, u32[]{:S(2)}, u32[]{:S(2)}) %collective-permute-start.4) | collective-permute-done | bytes 262176 | tf_op jit(solution)/shard_map/ppermute | solution.py:23
  25.2 1.1 %collective-permute-start.10 = (bf16[128,1024]{1,0:T(8,128)(2,1)S(1)}, bf16[128,1024]{1,0:T(8,128)(2,1)S(1)}, u32[]{:S(2)}, u32[]{:S(2)}) collective-permute-start(bf16[128,1024]{1,0:T(8,128)(2,1)S(1)} %get-tuple-element.43.refs_7_.refs_3_), channel_id=1, source_target_pairs={{0,1},{1,0},{2,3},{3,2},{4,5},{5,4},{6,7},{7,6},{8,9},{9,8},{10,11... | collective-permute-start | bytes 786440 | tf_op jit(solution)/shard_map/ppermute | solution.py:23
  26.4 0.4 collective-permute-done.3.refs_5_
  26.8 0.9 %shard_map.118 = (bf16[192,1024]{1,0:T(8,128)(2,1)S(1)}, bf16[192,1024]{1,0:T(8,128)(2,1)S(1)}) custom-call(f32[8,128]{1,0:T(8,128)S(1)} %get-tuple-element.34.own.refs_0_.refs_1_, f32[8,128]{1,0:T(8,128)S(1)} %get-tuple-element.37.x_tab.refs_1_.refs_0_, f32[8,128]{1,0:T(8,128)S(1)} %get-tuple-element.38.y_tab.refs_2_.refs_0_, ...), custom_call_target="tpu_custom_call" | custom-call | flops 1024 | bytes 1024 | tf_op jit(solution)/shard_map/pallas_call | solution.py:242
  27.7 1.5 %collective-permute-start.7 = (bf16[192,1024]{1,0:T(8,128)(2,1)S(1)}, bf16[192,1024]{1,0:T(8,128)(2,1)S(1)}, u32[]{:S(2)}, u32[]{:S(2)}) collective-permute-start(bf16[192,1024]{1,0:T(8,128)(2,1)S(1)} %get-tuple-element.45), channel_id=1, source_target_pairs={{0,1},{1,0},{2,3},{3,2},{4,5},{5,4},{6,7},{7,6},{8,9},{9,8},{10,11... | collective-permute-start | bytes 1179656 | tf_op jit(solution)/shard_map/ppermute | solution.py:23
  29.1 1.7 %collective-permute-done.11.refs_6_ = bf16[128,1024]{1,0:T(8,128)(2,1)S(1)} collective-permute-done((bf16[128,1024]{1,0:T(8,128)(2,1)S(1)}, bf16[128,1024]{1,0:T(8,128)(2,1)S(1)}, u32[]{:S(2)}, u32[]{:S(2)}) %collective-permute-start.11) | collective-permute-done | bytes 262176 | tf_op jit(solution)/shard_map/ppermute | solution.py:23
  30.8 1.3 %collective-permute-start.6 = (bf16[192,1024]{1,0:T(8,128)(2,1)S(1)}, bf16[192,1024]{1,0:T(8,128)(2,1)S(1)}, u32[]{:S(2)}, u32[]{:S(2)}) collective-permute-start(bf16[192,1024]{1,0:T(8,128)(2,1)S(1)} %get-tuple-element.44.refs_7_), channel_id=1, source_target_pairs={{0,2},{1,3},{2,0},{3,1},{4,6},{5,7},{6,4},{7,5},{8,10},{9,11},{10,... | collective-permute-start | bytes 1179656 | tf_op jit(solution)/shard_map/ppermute | solution.py:23
  32.1 8.7 %collective-permute-done.10.refs_5_ = bf16[128,1024]{1,0:T(8,128)(2,1)S(1)} collective-permute-done((bf16[128,1024]{1,0:T(8,128)(2,1)S(1)}, bf16[128,1024]{1,0:T(8,128)(2,1)S(1)}, u32[]{:S(2)}, u32[]{:S(2)}) %collective-permute-start.10) | collective-permute-done | bytes 262176 | tf_op jit(solution)/shard_map/ppermute | solution.py:23
  40.9 1.1 %shard_map.119 = (bf16[192,1024]{1,0:T(8,128)(2,1)S(1)}, bf16[192,1024]{1,0:T(8,128)(2,1)S(1)}) custom-call(f32[8,128]{1,0:T(8,128)S(1)} %get-tuple-element.34.own.refs_0_.refs_1_, f32[8,128]{1,0:T(8,128)S(1)} %get-tuple-element.37.x_tab.refs_1_.refs_0_, f32[8,128]{1,0:T(8,128)S(1)} %get-tuple-element.38.y_tab.refs_2_.refs_0_, ...), custom_call_target="tpu_custom_call" | custom-call | flops 1024 | bytes 1024 | tf_op jit(solution)/shard_map/pallas_call | solution.py:242
  42.0 1.5 %collective-permute-start.15 = (bf16[192,1024]{1,0:T(8,128)(2,1)S(1)}, bf16[192,1024]{1,0:T(8,128)(2,1)S(1)}, u32[]{:S(2)}, u32[]{:S(2)}) collective-permute-start(bf16[192,1024]{1,0:T(8,128)(2,1)S(1)} %get-tuple-element.56), channel_id=1, source_target_pairs={{0,1},{1,0},{2,3},{3,2},{4,5},{5,4},{6,7},{7,6},{8,9},{9,8},{10,11... | collective-permute-start | bytes 1179656 | tf_op jit(solution)/shard_map/ppermute | solution.py:23
  43.4 0.0 collective-permute-done.9.refs_8_
  43.5 0.5 collective-permute-start.14
  44.0 0.0 collective-permute-done.8.refs_7_
  44.0 0.0 copy-done
  44.0 3.2 %shard_map.120 = (f32[384,768]{1,0:T(8,128)S(1)}, f32[384,768]{1,0:T(8,128)S(1)}) custom-call(f32[8,128]{1,0:T(8,128)S(1)} %get-tuple-element.34.own.refs_0_.refs_1_, f32[8,128]{1,0:T(8,128)S(1)} %get-tuple-element.37.x_tab.refs_1_.refs_0_, f32[8,128]{1,0:T(8,128)S(1)} %get-tuple-element.38.y_tab.refs_2_.refs_0_, ...), custom_call_target="tpu_custom_call" | custom-call | flops 2415919104 | bytes 14155776 | tf_op jit(solution)/shard_map/pallas_call | solution.py:242
  47.2 2.1 %collective-permute-done.7.refs_8_ = bf16[192,1024]{1,0:T(8,128)(2,1)S(1)} collective-permute-done((bf16[192,1024]{1,0:T(8,128)(2,1)S(1)}, bf16[192,1024]{1,0:T(8,128)(2,1)S(1)}, u32[]{:S(2)}, u32[]{:S(2)}) %collective-permute-start.7) | collective-permute-done | bytes 393248 | tf_op jit(solution)/shard_map/ppermute | solution.py:23
  49.3 0.0 collective-permute-done.6.refs_7_
  49.3 0.0 copy-done.1
  49.3 3.9 %shard_map.121 = (bf16[96,1024]{1,0:T(8,128)(2,1)S(1)}, bf16[96,1024]{1,0:T(8,128)(2,1)S(1)}, bf16[192,1024]{1,0:T(8,128)(2,1)S(1)}, bf16[384,768]{1,0:T(8,128)(2,1)S(1)}) custom-call(f32[8,128]{1,0:T(8,128)S(1)} %get-tuple-element.34.own.refs_0_.refs_1_, f32[8,128]{1,0:T(8,128)S(1)} %get-tuple-element.37.x_tab.refs_1_.refs_0_, ...), custom_call_target="tpu_custom_call" | custom-call | flops 3019898880 | bytes 14155776 | tf_op jit(solution)/shard_map/pallas_call | solution.py:242
  53.2 0.7 collective-permute-start.12
  53.9 0.8 shard_map.122
  54.7 1.3 %collective-permute-start.13 = (bf16[192,1024]{1,0:T(8,128)(2,1)S(1)}, bf16[192,1024]{1,0:T(8,128)(2,1)S(1)}, u32[]{:S(2)}, u32[]{:S(2)}) collective-permute-start(bf16[192,1024]{1,0:T(8,128)(2,1)S(1)} %get-tuple-element.54), channel_id=1, source_target_pairs={{0,1},{1,0},{2,3},{3,2},{4,5},{5,4},{6,7},{7,6},{8,9},{9,8},{10,11... | collective-permute-start | bytes 1179656 | tf_op jit(solution)/shard_map/ppermute | solution.py:23
  56.0 1.7 %collective-permute-done.15.refs_8_ = bf16[192,1024]{1,0:T(8,128)(2,1)S(1)} collective-permute-done((bf16[192,1024]{1,0:T(8,128)(2,1)S(1)}, bf16[192,1024]{1,0:T(8,128)(2,1)S(1)}, u32[]{:S(2)}, u32[]{:S(2)}) %collective-permute-start.15) | collective-permute-done | bytes 393248 | tf_op jit(solution)/shard_map/ppermute | solution.py:23
  57.7 0.0 collective-permute-done.14.refs_7_
  57.7 4.7 %shard_map.123 = (bf16[96,1024]{1,0:T(8,128)(2,1)S(1)}, bf16[96,1024]{1,0:T(8,128)(2,1)S(1)}, bf16[192,1024]{1,0:T(8,128)(2,1)S(1)}, bf16[384,1536]{1,0:T(8,128)(2,1)S(1)}) custom-call(f32[8,128]{1,0:T(8,128)S(1)} %get-tuple-element.34.own.refs_0_.refs_1_, f32[8,128]{1,0:T(8,128)S(1)} %get-tuple-element.37.x_tab.refs_1_.refs_0_, ...), custom_call_target="tpu_custom_call" | custom-call | flops 2415919104 | bytes 14155776 | tf_op jit(solution)/shard_map/pallas_call | solution.py:242
  62.4 0.2 collective-permute-start.19
  62.6 1.4 %shard_map.124 = (bf16[96,1024]{1,0:T(8,128)(2,1)S(1)}, bf16[96,1024]{1,0:T(8,128)(2,1)S(1)}, bf16[192,1024]{1,0:T(8,128)(2,1)S(1)}) custom-call(bf16[384,1536]{1,0:T(8,128)(2,1)S(1)} %get-tuple-element.58.both_ref, bf16[2048,1536]{1,0:T(8,128)(2,1)S(1)} %bitcast.23), custom_call_target="tpu_custom_call" | custom-call | flops 1024 | bytes 1024 | tf_op jit(solution)/shard_map/pallas_call | solution.py:242
  64.0 1.5 %collective-permute-start.18 = (bf16[192,1024]{1,0:T(8,128)(2,1)S(1)}, bf16[192,1024]{1,0:T(8,128)(2,1)S(1)}, u32[]{:S(2)}, u32[]{:S(2)}) collective-permute-start(bf16[192,1024]{1,0:T(8,128)(2,1)S(1)} %get-tuple-element.62), channel_id=1, source_target_pairs={{0,1},{1,0},{2,3},{3,2},{4,5},{5,4},{6,7},{7,6},{8,9},{9,8},{10,11... | collective-permute-start | bytes 1179656 | tf_op jit(solution)/shard_map/ppermute | solution.py:23
  65.5 0.0 collective-permute-done.12.refs_2_.refs_4_
  65.5 0.8 shard_map.125.refs_3_
  66.3 0.7 collective-permute-start.16
  67.0 0.0 collective-permute-done.13.refs_2_.refs_5_
  67.0 0.8 shard_map.126.refs_3_
  67.8 1.9 %collective-permute-start.17 = (bf16[128,1024]{1,0:T(8,128)(2,1)S(1)}, bf16[128,1024]{1,0:T(8,128)(2,1)S(1)}, u32[]{:S(2)}, u32[]{:S(2)}) collective-permute-start(bf16[128,1024]{1,0:T(8,128)(2,1)S(1)} %shard_map.126.refs_3_), channel_id=1, source_target_pairs={{0,2},{1,3},{2,0},{3,1},{4,6},{5,7},{6,4},{7,5},{8,10},{9,11},{10,... | collective-permute-start | bytes 786440 | tf_op jit(solution)/shard_map/ppermute | solution.py:23
  69.7 4.8 %collective-permute-done.19.refs_2_.refs_3_ = bf16[192,1024]{1,0:T(8,128)(2,1)S(1)} collective-permute-done((bf16[192,1024]{1,0:T(8,128)(2,1)S(1)}, bf16[192,1024]{1,0:T(8,128)(2,1)S(1)}, u32[]{:S(2)}, u32[]{:S(2)}) %collective-permute-start.19) | collective-permute-done | bytes 393248 | tf_op jit(solution)/shard_map/ppermute | solution.py:23
  74.5 0.4 shard_map.127.refs_3_
  75.0 1.2 %collective-permute-done.18.refs_2_.refs_4_ = bf16[192,1024]{1,0:T(8,128)(2,1)S(1)} collective-permute-done((bf16[192,1024]{1,0:T(8,128)(2,1)S(1)}, bf16[192,1024]{1,0:T(8,128)(2,1)S(1)}, u32[]{:S(2)}, u32[]{:S(2)}) %collective-permute-start.18) | collective-permute-done | bytes 393248 | tf_op jit(solution)/shard_map/ppermute | solution.py:23
  76.2 0.5 shard_map.128.refs_8_
  76.6 1.4 %collective-permute-start.21 = (bf16[128,1024]{1,0:T(8,128)(2,1)S(1)}, bf16[128,1024]{1,0:T(8,128)(2,1)S(1)}, u32[]{:S(2)}, u32[]{:S(2)}) collective-permute-start(bf16[128,1024]{1,0:T(8,128)(2,1)S(1)} %shard_map.128.refs_8_), channel_id=1, source_target_pairs={{0,2},{1,3},{2,0},{3,1},{4,6},{5,7},{6,4},{7,5},{8,10},{9,11},{10,... | collective-permute-start | bytes 786440 | tf_op jit(solution)/shard_map/ppermute | solution.py:23
  78.0 1.4 %collective-permute-start.20 = (bf16[128,1024]{1,0:T(8,128)(2,1)S(1)}, bf16[128,1024]{1,0:T(8,128)(2,1)S(1)}, u32[]{:S(2)}, u32[]{:S(2)}) collective-permute-start(bf16[128,1024]{1,0:T(8,128)(2,1)S(1)} %shard_map.127.refs_3_), channel_id=1, source_target_pairs={{0,1},{1,0},{2,3},{3,2},{4,5},{5,4},{6,7},{7,6},{8,9},{9,8},{10,11... | collective-permute-start | bytes 786440 | tf_op jit(solution)/shard_map/ppermute | solution.py:23
  79.4 1.2 %collective-permute-done.16.refs_6_ = bf16[128,1024]{1,0:T(8,128)(2,1)S(1)} collective-permute-done((bf16[128,1024]{1,0:T(8,128)(2,1)S(1)}, bf16[128,1024]{1,0:T(8,128)(2,1)S(1)}, u32[]{:S(2)}, u32[]{:S(2)}) %collective-permute-start.16) | collective-permute-done | bytes 262176 | tf_op jit(solution)/shard_map/ppermute | solution.py:23
  80.6 0.0 collective-permute-done.17.refs_7_
  80.6 1.7 %shard_map.129 = bf16[128,2048]{1,0:T(8,128)(2,1)} custom-call(bf16[128,2048]{1,0:T(8,128)(2,1)S(1)} %collective-permute-done.refs_0_, f32[8,128]{1,0:T(8,128)S(1)} %get-tuple-element.34.own.refs_0_.refs_1_, bf16[96,1024]{1,0:T(8,128)(2,1)S(1)} %get-tuple-element.50.refs_2_, bf16[96,1024]{1,0:T(8,128)(2,1)S(1)} %get-tuple-element.52.refs_13_.refs_3_, ...), custom_call_target="tpu_custom_call" | custom-call | flops 1024 | bytes 1024 | tf_op jit(solution)/shard_map/pallas_call | solution.py:242
  82.3 0.7 collective-permute-done.21.refs_6_
  83.1 1.3 %collective-permute-done.20.refs_5_ = bf16[128,1024]{1,0:T(8,128)(2,1)S(1)} collective-permute-done((bf16[128,1024]{1,0:T(8,128)(2,1)S(1)}, bf16[128,1024]{1,0:T(8,128)(2,1)S(1)}, u32[]{:S(2)}, u32[]{:S(2)}) %collective-permute-start.20) | collective-permute-done | bytes 262176 | tf_op jit(solution)/shard_map/ppermute | solution.py:23
  84.4 0.0 copy-done.2
  84.4 1.7 %shard_map.130 = bf16[128,2048]{1,0:T(8,128)(2,1)} custom-call(bf16[128,2048]{1,0:T(8,128)(2,1)S(1)} %collective-permute-done.5.refs_0_.grads_ref, bf16[128,2048]{1,0:T(8,128)(2,1)S(1)} %bitcast.28, f32[1,2048]{1,0:T(1,128)S(1)} %get-tuple-element.39.refs_1_.gain_ref, f32[8,128]{1,0:T(8,128)S(1)} %get-tuple-element.34.own.refs_0_.refs_1_, ...), custom_call_target="tpu_custom_call" | custom-call | flops 1024 | bytes 1024 | tf_op jit(solution)/shard_map/pallas_call | solution.py:242
  (4 shorter events, 0.0 us)
Async XLA Ops:
  0.6 15.6 %collective-permute-start = (bf16[128,2048]{1,0:T(8,128)(2,1)}, bf16[128,2048]{1,0:T(8,128)(2,1)S(1)}, u32[]{:S(2)}, u32[]{:S(2)}) collective-permute-start(bf16[128,2048]{1,0:T(8,128)(2,1)} %bitcast.35), channel_id=1, source_target_pairs={{0,4},{4,8},{8,12},{12,16},{16,20},{20,24},{24,28},{28,0},{1,5},{5... | collective-permute-start | bytes 1572872 | tf_op jit(solution)/shard_map/ppermute | solution.py:17
  1.1 18.4 %collective-permute-start.5 = (bf16[128,2048]{1,0:T(8,128)(2,1)}, bf16[128,2048]{1,0:T(8,128)(2,1)S(1)}, u32[]{:S(2)}, u32[]{:S(2)}) collective-permute-start(bf16[128,2048]{1,0:T(8,128)(2,1)} %bitcast.36), channel_id=1, source_target_pairs={{0,28},{4,0},{8,4},{12,8},{16,12},{20,16},{24,20},{28,24},{1,29},{... | collective-permute-start | bytes 1572872 | tf_op jit(solution)/shard_map/ppermute | solution.py:17
  6.6 7.6 %collective-permute-start.1 = (bf16[144,1024]{1,0:T(8,128)(2,1)S(1)}, bf16[144,1024]{1,0:T(8,128)(2,1)S(1)}, u32[]{:S(2)}, u32[]{:S(2)}) collective-permute-start(bf16[144,1024]{1,0:T(8,128)(2,1)S(1)} %get-tuple-element.35.left.refs_3_), channel_id=1, source_target_pairs={{0,1},{1,0},{2,3},{3,2},{4,5},{5,4},{6,7},{7,6},{8,9},{9,8},{10,11... | collective-permute-start | bytes 884744 | tf_op jit(solution)/shard_map/ppermute | solution.py:23
  8.6 6.8 %collective-permute-start.2 = (bf16[144,1024]{1,0:T(8,128)(2,1)S(1)}, bf16[144,1024]{1,0:T(8,128)(2,1)S(1)}, u32[]{:S(2)}, u32[]{:S(2)}) collective-permute-start(bf16[144,1024]{1,0:T(8,128)(2,1)S(1)} %get-tuple-element.36.right.refs_4_), channel_id=1, source_target_pairs={{0,2},{1,3},{2,0},{3,1},{4,6},{5,7},{6,4},{7,5},{8,10},{9,11},{10,... | collective-permute-start | bytes 884744 | tf_op jit(solution)/shard_map/ppermute | solution.py:23
  15.3 28.6 %copy-start = (bf16[1,1,2048,1536]{3,2,1,0:T(8,128)(2,1)S(1)}, bf16[1,1,2048,1536]{3,2,1,0:T(8,128)(2,1)}, u32[]{:S(2)}) copy-start(bf16[1,1,2048,1536]{3,2,1,0:T(8,128)(2,1)} %param.18) | copy-start | bytes 18874372
  16.5 8.8 %collective-permute-start.4 = (bf16[128,1024]{1,0:T(8,128)(2,1)S(1)}, bf16[128,1024]{1,0:T(8,128)(2,1)S(1)}, u32[]{:S(2)}, u32[]{:S(2)}) collective-permute-start(bf16[128,1024]{1,0:T(8,128)(2,1)S(1)} %get-tuple-element.42.refs_4_), channel_id=1, source_target_pairs={{0,2},{1,3},{2,0},{3,1},{4,6},{5,7},{6,4},{7,5},{8,10},{9,11},{10,... | collective-permute-start | bytes 786440 | tf_op jit(solution)/shard_map/ppermute | solution.py:23
  18.1 8.7 %collective-permute-start.3 = (bf16[128,1024]{1,0:T(8,128)(2,1)S(1)}, bf16[128,1024]{1,0:T(8,128)(2,1)S(1)}, u32[]{:S(2)}, u32[]{:S(2)}) collective-permute-start(bf16[128,1024]{1,0:T(8,128)(2,1)S(1)} %get-tuple-element.41.refs_1_.refs_3_), channel_id=1, source_target_pairs={{0,1},{1,0},{2,3},{3,2},{4,5},{5,4},{6,7},{7,6},{8,9},{9,8},{10,11... | collective-permute-start | bytes 786440 | tf_op jit(solution)/shard_map/ppermute | solution.py:23
  19.5 11.3 %collective-permute-start.11 = (bf16[128,1024]{1,0:T(8,128)(2,1)S(1)}, bf16[128,1024]{1,0:T(8,128)(2,1)S(1)}, u32[]{:S(2)}, u32[]{:S(2)}) collective-permute-start(bf16[128,1024]{1,0:T(8,128)(2,1)S(1)} %get-tuple-element.47.refs_4_), channel_id=1, source_target_pairs={{0,2},{1,3},{2,0},{3,1},{4,6},{5,7},{6,4},{7,5},{8,10},{9,11},{10,... | collective-permute-start | bytes 786440 | tf_op jit(solution)/shard_map/ppermute | solution.py:23
  20.1 23.3 %collective-permute-start.9 = (bf16[192,1024]{1,0:T(8,128)(2,1)S(1)}, bf16[192,1024]{1,0:T(8,128)(2,1)S(1)}, u32[]{:S(2)}, u32[]{:S(2)}) collective-permute-start(bf16[192,1024]{1,0:T(8,128)(2,1)S(1)} %get-tuple-element.46), channel_id=1, source_target_pairs={{0,1},{1,0},{2,3},{3,2},{4,5},{5,4},{6,7},{7,6},{8,9},{9,8},{10,11... | collective-permute-start | bytes 1179656 | tf_op jit(solution)/shard_map/ppermute | solution.py:23
  20.7 23.3 %collective-permute-start.8 = (bf16[192,1024]{1,0:T(8,128)(2,1)S(1)}, bf16[192,1024]{1,0:T(8,128)(2,1)S(1)}, u32[]{:S(2)}, u32[]{:S(2)}) collective-permute-start(bf16[192,1024]{1,0:T(8,128)(2,1)S(1)} %get-tuple-element.40.refs_2_), channel_id=1, source_target_pairs={{0,2},{1,3},{2,0},{3,1},{4,6},{5,7},{6,4},{7,5},{8,10},{9,11},{10,... | collective-permute-start | bytes 1179656 | tf_op jit(solution)/shard_map/ppermute | solution.py:23
  25.2 15.6 %collective-permute-start.10 = (bf16[128,1024]{1,0:T(8,128)(2,1)S(1)}, bf16[128,1024]{1,0:T(8,128)(2,1)S(1)}, u32[]{:S(2)}, u32[]{:S(2)}) collective-permute-start(bf16[128,1024]{1,0:T(8,128)(2,1)S(1)} %get-tuple-element.43.refs_7_.refs_3_), channel_id=1, source_target_pairs={{0,1},{1,0},{2,3},{3,2},{4,5},{5,4},{6,7},{7,6},{8,9},{9,8},{10,11... | collective-permute-start | bytes 786440 | tf_op jit(solution)/shard_map/ppermute | solution.py:23
  27.7 21.6 %collective-permute-start.7 = (bf16[192,1024]{1,0:T(8,128)(2,1)S(1)}, bf16[192,1024]{1,0:T(8,128)(2,1)S(1)}, u32[]{:S(2)}, u32[]{:S(2)}) collective-permute-start(bf16[192,1024]{1,0:T(8,128)(2,1)S(1)} %get-tuple-element.45), channel_id=1, source_target_pairs={{0,1},{1,0},{2,3},{3,2},{4,5},{5,4},{6,7},{7,6},{8,9},{9,8},{10,11... | collective-permute-start | bytes 1179656 | tf_op jit(solution)/shard_map/ppermute | solution.py:23
  30.8 18.4 %collective-permute-start.6 = (bf16[192,1024]{1,0:T(8,128)(2,1)S(1)}, bf16[192,1024]{1,0:T(8,128)(2,1)S(1)}, u32[]{:S(2)}, u32[]{:S(2)}) collective-permute-start(bf16[192,1024]{1,0:T(8,128)(2,1)S(1)} %get-tuple-element.44.refs_7_), channel_id=1, source_target_pairs={{0,2},{1,3},{2,0},{3,1},{4,6},{5,7},{6,4},{7,5},{8,10},{9,11},{10,... | collective-permute-start | bytes 1179656 | tf_op jit(solution)/shard_map/ppermute | solution.py:23
  42.0 15.7 %collective-permute-start.15 = (bf16[192,1024]{1,0:T(8,128)(2,1)S(1)}, bf16[192,1024]{1,0:T(8,128)(2,1)S(1)}, u32[]{:S(2)}, u32[]{:S(2)}) collective-permute-start(bf16[192,1024]{1,0:T(8,128)(2,1)S(1)} %get-tuple-element.56), channel_id=1, source_target_pairs={{0,1},{1,0},{2,3},{3,2},{4,5},{5,4},{6,7},{7,6},{8,9},{9,8},{10,11... | collective-permute-start | bytes 1179656 | tf_op jit(solution)/shard_map/ppermute | solution.py:23
  43.5 14.3 %collective-permute-start.14 = (bf16[192,1024]{1,0:T(8,128)(2,1)S(1)}, bf16[192,1024]{1,0:T(8,128)(2,1)S(1)}, u32[]{:S(2)}, u32[]{:S(2)}) collective-permute-start(bf16[192,1024]{1,0:T(8,128)(2,1)S(1)} %get-tuple-element.48.refs_10_), channel_id=1, source_target_pairs={{0,2},{1,3},{2,0},{3,1},{4,6},{5,7},{6,4},{7,5},{8,10},{9,11},{10,... | collective-permute-start | bytes 1179656 | tf_op jit(solution)/shard_map/ppermute | solution.py:23
  44.0 5.3 %copy-start.1 = (bf16[1,1,768,2048]{3,2,1,0:T(8,128)(2,1)S(1)}, bf16[1,1,768,2048]{3,2,1,0:T(8,128)(2,1)}, u32[]{:S(2)}) copy-start(bf16[1,1,768,2048]{3,2,1,0:T(8,128)(2,1)} %param.19) | copy-start | bytes 9437188
  53.2 12.3 %collective-permute-start.12 = (bf16[192,1024]{1,0:T(8,128)(2,1)S(1)}, bf16[192,1024]{1,0:T(8,128)(2,1)S(1)}, u32[]{:S(2)}, u32[]{:S(2)}) collective-permute-start(bf16[192,1024]{1,0:T(8,128)(2,1)S(1)} %get-tuple-element.53), channel_id=1, source_target_pairs={{0,2},{1,3},{2,0},{3,1},{4,6},{5,7},{6,4},{7,5},{8,10},{9,11},{10,... | collective-permute-start | bytes 1179656 | tf_op jit(solution)/shard_map/ppermute | solution.py:23
  54.7 12.3 %collective-permute-start.13 = (bf16[192,1024]{1,0:T(8,128)(2,1)S(1)}, bf16[192,1024]{1,0:T(8,128)(2,1)S(1)}, u32[]{:S(2)}, u32[]{:S(2)}) collective-permute-start(bf16[192,1024]{1,0:T(8,128)(2,1)S(1)} %get-tuple-element.54), channel_id=1, source_target_pairs={{0,1},{1,0},{2,3},{3,2},{4,5},{5,4},{6,7},{7,6},{8,9},{9,8},{10,11... | collective-permute-start | bytes 1179656 | tf_op jit(solution)/shard_map/ppermute | solution.py:23
  62.4 12.1 %collective-permute-start.19 = (bf16[192,1024]{1,0:T(8,128)(2,1)S(1)}, bf16[192,1024]{1,0:T(8,128)(2,1)S(1)}, u32[]{:S(2)}, u32[]{:S(2)}) collective-permute-start(bf16[192,1024]{1,0:T(8,128)(2,1)S(1)} %get-tuple-element.64), channel_id=1, source_target_pairs={{0,2},{1,3},{2,0},{3,1},{4,6},{5,7},{6,4},{7,5},{8,10},{9,11},{10,... | collective-permute-start | bytes 1179656 | tf_op jit(solution)/shard_map/ppermute | solution.py:23
  64.0 12.1 %collective-permute-start.18 = (bf16[192,1024]{1,0:T(8,128)(2,1)S(1)}, bf16[192,1024]{1,0:T(8,128)(2,1)S(1)}, u32[]{:S(2)}, u32[]{:S(2)}) collective-permute-start(bf16[192,1024]{1,0:T(8,128)(2,1)S(1)} %get-tuple-element.62), channel_id=1, source_target_pairs={{0,1},{1,0},{2,3},{3,2},{4,5},{5,4},{6,7},{7,6},{8,9},{9,8},{10,11... | collective-permute-start | bytes 1179656 | tf_op jit(solution)/shard_map/ppermute | solution.py:23
  66.3 14.3 %collective-permute-start.16 = (bf16[128,1024]{1,0:T(8,128)(2,1)S(1)}, bf16[128,1024]{1,0:T(8,128)(2,1)S(1)}, u32[]{:S(2)}, u32[]{:S(2)}) collective-permute-start(bf16[128,1024]{1,0:T(8,128)(2,1)S(1)} %shard_map.125.refs_3_), channel_id=1, source_target_pairs={{0,1},{1,0},{2,3},{3,2},{4,5},{5,4},{6,7},{7,6},{8,9},{9,8},{10,11... | collective-permute-start | bytes 786440 | tf_op jit(solution)/shard_map/ppermute | solution.py:23
  67.8 12.8 %collective-permute-start.17 = (bf16[128,1024]{1,0:T(8,128)(2,1)S(1)}, bf16[128,1024]{1,0:T(8,128)(2,1)S(1)}, u32[]{:S(2)}, u32[]{:S(2)}) collective-permute-start(bf16[128,1024]{1,0:T(8,128)(2,1)S(1)} %shard_map.126.refs_3_), channel_id=1, source_target_pairs={{0,2},{1,3},{2,0},{3,1},{4,6},{5,7},{6,4},{7,5},{8,10},{9,11},{10,... | collective-permute-start | bytes 786440 | tf_op jit(solution)/shard_map/ppermute | solution.py:23
  76.6 6.4 %collective-permute-start.21 = (bf16[128,1024]{1,0:T(8,128)(2,1)S(1)}, bf16[128,1024]{1,0:T(8,128)(2,1)S(1)}, u32[]{:S(2)}, u32[]{:S(2)}) collective-permute-start(bf16[128,1024]{1,0:T(8,128)(2,1)S(1)} %shard_map.128.refs_8_), channel_id=1, source_target_pairs={{0,2},{1,3},{2,0},{3,1},{4,6},{5,7},{6,4},{7,5},{8,10},{9,11},{10,... | collective-permute-start | bytes 786440 | tf_op jit(solution)/shard_map/ppermute | solution.py:23
  78.0 6.4 %collective-permute-start.20 = (bf16[128,1024]{1,0:T(8,128)(2,1)S(1)}, bf16[128,1024]{1,0:T(8,128)(2,1)S(1)}, u32[]{:S(2)}, u32[]{:S(2)}) collective-permute-start(bf16[128,1024]{1,0:T(8,128)(2,1)S(1)} %shard_map.127.refs_3_), channel_id=1, source_target_pairs={{0,1},{1,0},{2,3},{3,2},{4,5},{5,4},{6,7},{7,6},{8,9},{9,8},{10,11... | collective-permute-start | bytes 786440 | tf_op jit(solution)/shard_map/ppermute | solution.py:23
  80.6 3.8 %copy-start.2 = (bf16[1,128,2048]{2,1,0:T(8,128)(2,1)S(1)}, bf16[1,128,2048]{2,1,0:T(8,128)(2,1)}, u32[]{:S(2)}) copy-start(bf16[1,128,2048]{2,1,0:T(8,128)(2,1)} %param.12) | copy-start | bytes 1572868

commit v6 on v5

--- a/solution.py
+++ b/solution.py
@@ -399,15 +399,16 @@
 
 
 def first_kernel(top_count, me_ref, *refs):
-    sources, refs = refs[:6], refs[6:]
-    (left_ref, right_ref, table_ref, gain_out), refs = refs[:4], refs[4:]
-    held, sems = refs[:6], refs[6]
-    copies = [pltpu.make_async_copy(sources[i], held[i], sems.at[i]) for i in range(6)]
+    sources, refs = refs[:8], refs[8:]
+    (left_ref, right_ref, table_ref, gain_out, fwd_out, bwd_out), refs = refs[:6], refs[6:]
+    sems = refs[6]
+    held = (*refs[:6], fwd_out, bwd_out)
+    copies = [pltpu.make_async_copy(sources[i], held[i], sems.at[i]) for i in range(8)]
     for copy in copies:
         copy.start()
-    for copy in copies[1:]:
+    for copy in copies[1:6]:
         copy.wait()
-    saved, gain, f_routes, f_gates, b_routes, b_gates = held
+    saved, gain, f_routes, f_gates, b_routes, b_gates = held[:6]
     me = me_ref[0]
     fr = (f_routes[...] ^ me).astype(jnp.float32)
     br = (b_routes[...] ^ me).astype(jnp.float32)
@@ -425,6 +426,8 @@
         half_ref[:tok_rows, :] = normed[:, start : start + half]
         half_ref[tok_rows:, :] = jnp.zeros((half_ref.shape[0] - tok_rows, half), jnp.bfloat16)
         half_ref[tok_rows:, :tok_rows] = packed.astype(jnp.bfloat16)
+    for copy in copies[6:]:
+        copy.wait()
 
 
 def unpacked(block, tok_rows, top_count):
@@ -654,8 +657,6 @@
     weight_out = w_out[0, 0]
     me = lax.axis_index("expert").astype(jnp.int32).reshape(1)
     saved = bwd_saved[0]
-    layer_in = passed_along(fwd_prev[0], "section", 1)
-    grad_in = passed_along(bwd_prev[0], "section", -1)
 
     def shaped(rows, columns, dtype=jnp.bfloat16):
         return jax.ShapeDtypeStruct((rows, columns), dtype)
@@ -677,16 +678,18 @@
     table_shape = shaped(table_rows, tok_rows, jnp.float32)
     first_rows = tok_rows + 8 * top_count
 
-    b_left, b_right, own, gain_here = pl.pallas_call(
+    b_left, b_right, own, gain_here, fwd_here, bwd_here = pl.pallas_call(
         functools.partial(first_kernel, top_count),
         out_shape=[
             shaped(first_rows, half),
             shaped(first_rows, half),
             table_shape,
             shaped(1, features, jnp.float32),
+            shaped(tok_rows, features),
+            shaped(tok_rows, features),
         ],
         in_specs=[pl.BlockSpec(memory_space=pltpu.SMEM)]
-        + [pl.BlockSpec(memory_space=pltpu.HBM)] * 6,
+        + [pl.BlockSpec(memory_space=pltpu.HBM)] * 8,
         scratch_shapes=[
             pltpu.VMEM((tok_rows, features), jnp.bfloat16),
             pltpu.VMEM((1, features), jnp.float32),
@@ -694,7 +697,7 @@
             pltpu.VMEM((top_count, tok_rows), jnp.float32),
             pltpu.VMEM((top_count, tok_rows), jnp.int32),
             pltpu.VMEM((top_count, tok_rows), jnp.float32),
-            pltpu.SemaphoreType.DMA((6,)),
+            pltpu.SemaphoreType.DMA((8,)),
         ],
         compiler_params=pltpu.CompilerParams(vmem_limit_bytes=VMEM_LIMIT),
         cost_estimate=pl.CostEstimate(flops=one_hop, bytes_accessed=moved, transcendentals=0),
@@ -709,16 +712,27 @@
                 fwd_gates[0].T,
                 bwd_routes[0].T,
                 bwd_gates[0].T,
+                fwd_prev[0],
+                bwd_prev[0],
             )
         ],
     )
+    layer_in = passed_along(fwd_here, "section", 1)
+    grad_in = passed_along(bwd_here, "section", -1)
     b_from_x, b_from_y = crossed(b_left, b_right)
+    f_left, f_right = local_call(
+        normed_kernel_halves, halves_out, (layer_in, gain_here), one_hop, moved, after=(b_left,)
+    )
+    f_from_x, f_from_y = crossed(f_left, f_right)
+    g_left, g_right = local_call(split_kernel, halves_out, (grad_in,), 1024, moved, after=(f_left,))
+    g_from_x, g_from_y = crossed(g_left, g_right)
     x_tab, y_tab = local_call(
         functools.partial(tables_kernel, top_count),
         [table_shape] * 2,
         (b_from_x, b_from_y),
         1024,
         1024,
+        after=(g_left,),
     )
     tabs = (own, x_tab, y_tab)
 
@@ -733,14 +747,8 @@
         )
         return swapped(to_y, "expert", 2), swapped(to_x, "expert", 1), to_y
 
-    b_got_y, b_got_x, b_to_y = onward("b", (b_left, b_right), (b_from_x, b_from_y), ())
-    f_left, f_right = local_call(
-        normed_kernel_halves, halves_out, (layer_in, gain_here), one_hop, moved, after=(b_to_y,)
-    )
-    f_from_x, f_from_y = crossed(f_left, f_right)
-    g_left, g_right = local_call(split_kernel, halves_out, (grad_in,), 1024, moved, after=(f_left,))
-    g_from_x, g_from_y = crossed(g_left, g_right)
-    f_got_y, f_got_x, f_to_y = onward("f", (f_left, f_right), (f_from_x, f_from_y), (g_left,))
+    b_got_y, b_got_x, b_to_y = onward("b", (b_left, b_right), (b_from_x, b_from_y), (g_left,))
+    f_got_y, f_got_x, f_to_y = onward("f", (f_left, f_right), (f_from_x, f_from_y), (b_to_y,))
     g_got_y, g_got_x, g_to_y = onward("bg", (g_left, g_right), (g_from_x, g_from_y), (f_to_y,))
     gate_pre, up_pre = local_call(
         functools.partial(hop_again_kernel, top_count),

time: 86.2 us -> 87.2 us (1.012)
  starting transfers between devices: 28.7 us -> 31.8 us
  waiting for transfers between devices: 32.3 us -> 29.6 us
    ppermute x20, waiting for transfers between devices: 32.3 us -> 23.3 us  [swapped(): return lax.ppermute(value, axis, pairs)]
    ppermute x2, waiting for transfers between devices: 0.01 us -> 6.31 us  [passed_along(): return lax.ppermute(value, axis, pairs)]
    ppermute x20, starting transfers between devices: 24.1 us -> 27.2 us  [swapped(): return lax.ppermute(value, axis, pairs)]
  transfers between devices with their start and end apart: 22 -> 22, of which waited for: 13 -> 11; matrix products, arithmetic and copies ran while one was open for 0% -> 0% of each run, Pallas kernels for 26% -> 25%
where the time goes in v6:
time: 87.2 us; the launch traced here: 86.8 us
  starting transfers between devices  31.8 us (36%)
  waiting for transfers between devices  29.6 us (34%)
  Pallas kernels  24.5 us (28%)
    ppermute x20, starting transfers between devices, swapped(): return lax.ppermute(value, axis, pairs)  27.2 us
    ppermute x20, waiting for transfers between devices, swapped(): return lax.ppermute(value, axis, pairs)  23.3 us
    pallas_call x17, Pallas kernels, local_call(): pl.pallas_call(body if after else kernel, out_shape=out_shapes, in_specs=...  23 us
    ppermute x2, waiting for transfers between devices, passed_along(): return lax.ppermute(value, axis, pairs)  6.31 us
    ppermute x2, starting transfers between devices, passed_along(): return lax.ppermute(value, axis, pairs)  4.61 us
  transfers between devices with their start and end apart: 22, of which 11 were waited for; matrix products, arithmetic and copies ran while one was open for 0% of the time, Pallas kernels for 25%

profile of v6, /device:TPU:0, one launch (start us, length us, event | category | flops | bytes accessed | tf_op | source)
XLA Modules:
  0.0 86.8 jit_solution(8969202958143724098)
XLA Ops:
  0.6 1.5 %shard_map.113 = (bf16[144,1024]{1,0:T(8,128)(2,1)S(1)}, bf16[144,1024]{1,0:T(8,128)(2,1)S(1)}, f32[8,128]{1,0:T(8,128)S(1)}, f32[1,2048]{1,0:T(1,128)S(1)}, bf1...) custom-call(s32[1]{0:T(128)} %bitcast.me_ref, bf16[128,2048]{1,0:T(8,128)(2,1)} %bitcast.27, f32[1,2048]{1,0:T(1,128)} %refs_1_.1, ...), custom_call_target="tpu_custom_call" | custom-call | flops 1024 | bytes 1024 | tf_op jit(solution)/shard_map/pallas_call | solution.py:681
  2.2 0.5 collective-permute-start
  2.7 4.1 %collective-permute-start.3 = (bf16[128,2048]{1,0:T(8,128)(2,1)S(1)}, bf16[128,2048]{1,0:T(8,128)(2,1)S(1)}, u32[]{:S(2)}, u32[]{:S(2)}) collective-permute-start(bf16[128,2048]{1,0:T(8,128)(2,1)S(1)} %get-tuple-element.40), channel_id=1, source_target_pairs={{0,28},{4,0},{8,4},{12,8},{16,12},{20,16},{24,20},{28,24},{1,29},{... | collective-permute-start | bytes 1572872 | tf_op jit(solution)/shard_map/ppermute | solution.py:17
  6.8 2.0 %collective-permute-start.2 = (bf16[144,1024]{1,0:T(8,128)(2,1)S(1)}, bf16[144,1024]{1,0:T(8,128)(2,1)S(1)}, u32[]{:S(2)}, u32[]{:S(2)}) collective-permute-start(bf16[144,1024]{1,0:T(8,128)(2,1)S(1)} %get-tuple-element.39.refs_4_), channel_id=1, source_target_pairs={{0,2},{1,3},{2,0},{3,1},{4,6},{5,7},{6,4},{7,5},{8,10},{9,11},{10,... | collective-permute-start | bytes 884744 | tf_op jit(solution)/shard_map/ppermute | solution.py:23
  8.7 1.5 %collective-permute-start.1 = (bf16[144,1024]{1,0:T(8,128)(2,1)S(1)}, bf16[144,1024]{1,0:T(8,128)(2,1)S(1)}, u32[]{:S(2)}, u32[]{:S(2)}) collective-permute-start(bf16[144,1024]{1,0:T(8,128)(2,1)S(1)} %get-tuple-element.38.refs_2_.refs_3_), channel_id=1, source_target_pairs={{0,1},{1,0},{2,3},{3,2},{4,5},{5,4},{6,7},{7,6},{8,9},{9,8},{10,11... | collective-permute-start | bytes 884744 | tf_op jit(solution)/shard_map/ppermute | solution.py:23
  10.2 6.3 %collective-permute-done.refs_0_ = bf16[128,2048]{1,0:T(8,128)(2,1)S(1)} collective-permute-done((bf16[128,2048]{1,0:T(8,128)(2,1)S(1)}, bf16[128,2048]{1,0:T(8,128)(2,1)S(1)}, u32[]{:S(2)}, u32[]{:S(2)}) %collective-permute-start) | collective-permute-done | bytes 524320 | tf_op jit(solution)/shard_map/ppermute | solution.py:17
  16.5 0.0 copy-start
  16.5 0.2 shard_map.114
  16.7 2.6 %collective-permute-start.5 = (bf16[128,1024]{1,0:T(8,128)(2,1)S(1)}, bf16[128,1024]{1,0:T(8,128)(2,1)S(1)}, u32[]{:S(2)}, u32[]{:S(2)}) collective-permute-start(bf16[128,1024]{1,0:T(8,128)(2,1)S(1)} %get-tuple-element.46.refs_4_), channel_id=1, source_target_pairs={{0,2},{1,3},{2,0},{3,1},{4,6},{5,7},{6,4},{7,5},{8,10},{9,11},{10,... | collective-permute-start | bytes 786440 | tf_op jit(solution)/shard_map/ppermute | solution.py:23
  19.3 1.5 %collective-permute-start.4 = (bf16[128,1024]{1,0:T(8,128)(2,1)S(1)}, bf16[128,1024]{1,0:T(8,128)(2,1)S(1)}, u32[]{:S(2)}, u32[]{:S(2)}) collective-permute-start(bf16[128,1024]{1,0:T(8,128)(2,1)S(1)} %get-tuple-element.42.refs_1_.refs_3_), channel_id=1, source_target_pairs={{0,1},{1,0},{2,3},{3,2},{4,5},{5,4},{6,7},{7,6},{8,9},{9,8},{10,11... | collective-permute-start | bytes 786440 | tf_op jit(solution)/shard_map/ppermute | solution.py:23
  20.8 0.0 collective-permute-done.3.refs_0_.grads_ref
  20.9 0.6 collective-permute-start.11
  21.4 0.0 collective-permute-done.2.refs_1_.refs_6_
  21.4 0.0 collective-permute-done.1.refs_0_.refs_5_
  21.5 0.9 shard_map.117
  22.3 0.2 collective-permute-start.9
  22.5 1.9 %collective-permute-start.8 = (bf16[192,1024]{1,0:T(8,128)(2,1)S(1)}, bf16[192,1024]{1,0:T(8,128)(2,1)S(1)}, u32[]{:S(2)}, u32[]{:S(2)}) collective-permute-start(bf16[192,1024]{1,0:T(8,128)(2,1)S(1)} %get-tuple-element.47.refs_7_), channel_id=1, source_target_pairs={{0,2},{1,3},{2,0},{3,1},{4,6},{5,7},{6,4},{7,5},{8,10},{9,11},{10,... | collective-permute-start | bytes 1179656 | tf_op jit(solution)/shard_map/ppermute | solution.py:23
  24.5 0.9 %collective-permute-done.5.refs_6_ = bf16[128,1024]{1,0:T(8,128)(2,1)S(1)} collective-permute-done((bf16[128,1024]{1,0:T(8,128)(2,1)S(1)}, bf16[128,1024]{1,0:T(8,128)(2,1)S(1)}, u32[]{:S(2)}, u32[]{:S(2)}) %collective-permute-start.5) | collective-permute-done | bytes 262176 | tf_op jit(solution)/shard_map/ppermute | solution.py:23
  25.4 2.3 %collective-permute-start.10 = (bf16[128,1024]{1,0:T(8,128)(2,1)S(1)}, bf16[128,1024]{1,0:T(8,128)(2,1)S(1)}, u32[]{:S(2)}, u32[]{:S(2)}) collective-permute-start(bf16[128,1024]{1,0:T(8,128)(2,1)S(1)} %get-tuple-element.43.refs_2_.refs_7_.refs_3_), channel_id=1, source_target_pairs={{0,1},{1,0},{2,3},{3,2},{4,5},{5,4},{6,7},{7,6},{8,9},{9,8},{10,11... | collective-permute-start | bytes 786440 | tf_op jit(solution)/shard_map/ppermute | solution.py:23
  27.7 0.0 collective-permute-done.4.refs_5_
  27.7 0.9 shard_map.118
  28.6 0.8 collective-permute-start.7
  29.4 1.6 %collective-permute-done.11.refs_6_ = bf16[128,1024]{1,0:T(8,128)(2,1)S(1)} collective-permute-done((bf16[128,1024]{1,0:T(8,128)(2,1)S(1)}, bf16[128,1024]{1,0:T(8,128)(2,1)S(1)}, u32[]{:S(2)}, u32[]{:S(2)}) %collective-permute-start.11) | collective-permute-done | bytes 262176 | tf_op jit(solution)/shard_map/ppermute | solution.py:23
  31.0 2.3 %collective-permute-start.6 = (bf16[192,1024]{1,0:T(8,128)(2,1)S(1)}, bf16[192,1024]{1,0:T(8,128)(2,1)S(1)}, u32[]{:S(2)}, u32[]{:S(2)}) collective-permute-start(bf16[192,1024]{1,0:T(8,128)(2,1)S(1)} %get-tuple-element.48.refs_7_), channel_id=1, source_target_pairs={{0,2},{1,3},{2,0},{3,1},{4,6},{5,7},{6,4},{7,5},{8,10},{9,11},{10,... | collective-permute-start | bytes 1179656 | tf_op jit(solution)/shard_map/ppermute | solution.py:23
  33.3 7.7 %collective-permute-done.10.refs_5_ = bf16[128,1024]{1,0:T(8,128)(2,1)S(1)} collective-permute-done((bf16[128,1024]{1,0:T(8,128)(2,1)S(1)}, bf16[128,1024]{1,0:T(8,128)(2,1)S(1)}, u32[]{:S(2)}, u32[]{:S(2)}) %collective-permute-start.10) | collective-permute-done | bytes 262176 | tf_op jit(solution)/shard_map/ppermute | solution.py:23
  41.0 1.1 %shard_map.119 = (bf16[192,1024]{1,0:T(8,128)(2,1)S(1)}, bf16[192,1024]{1,0:T(8,128)(2,1)S(1)}) custom-call(f32[8,128]{1,0:T(8,128)S(1)} %get-tuple-element.37.refs_0_.refs_1_, f32[8,128]{1,0:T(8,128)S(1)} %get-tuple-element.44.refs_1_.refs_0_, f32[8,128]{1,0:T(8,128)S(1)} %get-tuple-element.45.refs_2_.refs_0_, ...), custom_call_target="tpu_custom_call" | custom-call | flops 1024 | bytes 1024 | tf_op jit(solution)/shard_map/pallas_call | solution.py:242
  42.1 1.6 %collective-permute-start.15 = (bf16[192,1024]{1,0:T(8,128)(2,1)S(1)}, bf16[192,1024]{1,0:T(8,128)(2,1)S(1)}, u32[]{:S(2)}, u32[]{:S(2)}) collective-permute-start(bf16[192,1024]{1,0:T(8,128)(2,1)S(1)} %get-tuple-element.60), channel_id=1, source_target_pairs={{0,1},{1,0},{2,3},{3,2},{4,5},{5,4},{6,7},{7,6},{8,9},{9,8},{10,11... | collective-permute-start | bytes 1179656 | tf_op jit(solution)/shard_map/ppermute | solution.py:23
  43.7 0.0 collective-permute-done.9.refs_8_
  43.7 0.5 collective-permute-start.14
  44.2 0.0 collective-permute-done.8.refs_7_
  44.2 0.0 copy-done
  44.2 3.2 %shard_map.120 = (f32[384,768]{1,0:T(8,128)S(1)}, f32[384,768]{1,0:T(8,128)S(1)}) custom-call(f32[8,128]{1,0:T(8,128)S(1)} %get-tuple-element.37.refs_0_.refs_1_, f32[8,128]{1,0:T(8,128)S(1)} %get-tuple-element.44.refs_1_.refs_0_, f32[8,128]{1,0:T(8,128)S(1)} %get-tuple-element.45.refs_2_.refs_0_, bf16[144,1024]{1,0:T(8,128)(2,1)S(1)} %get-tuple-element.38.refs_2_.refs_3_, ...), custom_call_target="tpu_custom_call" | custom-call | flops 2415919104 | bytes 14155776 | tf_op jit(solution)/shard_map/pallas_call | solution.py:242
  47.4 2.0 %collective-permute-done.7.refs_8_ = bf16[192,1024]{1,0:T(8,128)(2,1)S(1)} collective-permute-done((bf16[192,1024]{1,0:T(8,128)(2,1)S(1)}, bf16[192,1024]{1,0:T(8,128)(2,1)S(1)}, u32[]{:S(2)}, u32[]{:S(2)}) %collective-permute-start.7) | collective-permute-done | bytes 393248 | tf_op jit(solution)/shard_map/ppermute | solution.py:23
  49.4 0.0 collective-permute-done.6.refs_7_
  49.4 0.0 copy-done.1
  49.4 3.9 %shard_map.121 = (bf16[96,1024]{1,0:T(8,128)(2,1)S(1)}, bf16[96,1024]{1,0:T(8,128)(2,1)S(1)}, bf16[192,1024]{1,0:T(8,128)(2,1)S(1)}, bf16[384,768]{1,0:T(8,128)(2,1)S(1)}) custom-call(f32[8,128]{1,0:T(8,128)S(1)} %get-tuple-element.37.refs_0_.refs_1_, f32[8,128]{1,0:T(8,128)S(1)} %get-tuple-element.44.refs_1_.refs_0_, ...), custom_call_target="tpu_custom_call" | custom-call | flops 3019898880 | bytes 14155776 | tf_op jit(solution)/shard_map/pallas_call | solution.py:242
  53.3 0.8 collective-permute-start.12
  54.1 0.8 shard_map.122
  54.9 1.6 %collective-permute-start.13 = (bf16[192,1024]{1,0:T(8,128)(2,1)S(1)}, bf16[192,1024]{1,0:T(8,128)(2,1)S(1)}, u32[]{:S(2)}, u32[]{:S(2)}) collective-permute-start(bf16[192,1024]{1,0:T(8,128)(2,1)S(1)} %get-tuple-element.58), channel_id=1, source_target_pairs={{0,1},{1,0},{2,3},{3,2},{4,5},{5,4},{6,7},{7,6},{8,9},{9,8},{10,11... | collective-permute-start | bytes 1179656 | tf_op jit(solution)/shard_map/ppermute | solution.py:23
  56.5 1.4 %collective-permute-done.15.refs_8_ = bf16[192,1024]{1,0:T(8,128)(2,1)S(1)} collective-permute-done((bf16[192,1024]{1,0:T(8,128)(2,1)S(1)}, bf16[192,1024]{1,0:T(8,128)(2,1)S(1)}, u32[]{:S(2)}, u32[]{:S(2)}) %collective-permute-start.15) | collective-permute-done | bytes 393248 | tf_op jit(solution)/shard_map/ppermute | solution.py:23
  57.8 0.0 collective-permute-done.14.refs_7_
  57.8 4.7 %shard_map.123 = (bf16[96,1024]{1,0:T(8,128)(2,1)S(1)}, bf16[96,1024]{1,0:T(8,128)(2,1)S(1)}, bf16[192,1024]{1,0:T(8,128)(2,1)S(1)}, bf16[384,1536]{1,0:T(8,128)(2,1)S(1)}) custom-call(f32[8,128]{1,0:T(8,128)S(1)} %get-tuple-element.37.refs_0_.refs_1_, f32[8,128]{1,0:T(8,128)S(1)} %get-tuple-element.44.refs_1_.refs_0_, ...), custom_call_target="tpu_custom_call" | custom-call | flops 2415919104 | bytes 14155776 | tf_op jit(solution)/shard_map/pallas_call | solution.py:242
  62.5 0.8 collective-permute-start.19
  63.4 1.4 %shard_map.124 = (bf16[96,1024]{1,0:T(8,128)(2,1)S(1)}, bf16[96,1024]{1,0:T(8,128)(2,1)S(1)}, bf16[192,1024]{1,0:T(8,128)(2,1)S(1)}) custom-call(bf16[384,1536]{1,0:T(8,128)(2,1)S(1)} %get-tuple-element.62.both_ref, bf16[2048,1536]{1,0:T(8,128)(2,1)S(1)} %bitcast.23), custom_call_target="tpu_custom_call" | custom-call | flops 1024 | bytes 1024 | tf_op jit(solution)/shard_map/pallas_call | solution.py:242
  64.8 1.6 %collective-permute-start.18 = (bf16[192,1024]{1,0:T(8,128)(2,1)S(1)}, bf16[192,1024]{1,0:T(8,128)(2,1)S(1)}, u32[]{:S(2)}, u32[]{:S(2)}) collective-permute-start(bf16[192,1024]{1,0:T(8,128)(2,1)S(1)} %get-tuple-element.66), channel_id=1, source_target_pairs={{0,1},{1,0},{2,3},{3,2},{4,5},{5,4},{6,7},{7,6},{8,9},{9,8},{10,11... | collective-permute-start | bytes 1179656 | tf_op jit(solution)/shard_map/ppermute | solution.py:23
  66.4 0.0 collective-permute-done.12.refs_2_.refs_4_
  66.4 0.8 shard_map.125.refs_3_
  67.2 0.6 collective-permute-start.16
  67.7 0.0 collective-permute-done.13.refs_2_.refs_5_
  67.7 0.8 shard_map.126.refs_3_
  68.5 1.3 %collective-permute-start.17 = (bf16[128,1024]{1,0:T(8,128)(2,1)S(1)}, bf16[128,1024]{1,0:T(8,128)(2,1)S(1)}, u32[]{:S(2)}, u32[]{:S(2)}) collective-permute-start(bf16[128,1024]{1,0:T(8,128)(2,1)S(1)} %shard_map.126.refs_3_), channel_id=1, source_target_pairs={{0,2},{1,3},{2,0},{3,1},{4,6},{5,7},{6,4},{7,5},{8,10},{9,11},{10,... | collective-permute-start | bytes 786440 | tf_op jit(solution)/shard_map/ppermute | solution.py:23
  69.9 4.8 %collective-permute-done.19.refs_2_.refs_3_ = bf16[192,1024]{1,0:T(8,128)(2,1)S(1)} collective-permute-done((bf16[192,1024]{1,0:T(8,128)(2,1)S(1)}, bf16[192,1024]{1,0:T(8,128)(2,1)S(1)}, u32[]{:S(2)}, u32[]{:S(2)}) %collective-permute-start.19) | collective-permute-done | bytes 393248 | tf_op jit(solution)/shard_map/ppermute | solution.py:23
  74.7 0.5 shard_map.127.refs_3_
  75.1 1.8 %collective-permute-done.18.refs_2_.refs_4_ = bf16[192,1024]{1,0:T(8,128)(2,1)S(1)} collective-permute-done((bf16[192,1024]{1,0:T(8,128)(2,1)S(1)}, bf16[192,1024]{1,0:T(8,128)(2,1)S(1)}, u32[]{:S(2)}, u32[]{:S(2)}) %collective-permute-start.18) | collective-permute-done | bytes 393248 | tf_op jit(solution)/shard_map/ppermute | solution.py:23
  76.9 0.5 shard_map.128.refs_8_
  77.4 1.3 %collective-permute-start.21 = (bf16[128,1024]{1,0:T(8,128)(2,1)S(1)}, bf16[128,1024]{1,0:T(8,128)(2,1)S(1)}, u32[]{:S(2)}, u32[]{:S(2)}) collective-permute-start(bf16[128,1024]{1,0:T(8,128)(2,1)S(1)} %shard_map.128.refs_8_), channel_id=1, source_target_pairs={{0,2},{1,3},{2,0},{3,1},{4,6},{5,7},{6,4},{7,5},{8,10},{9,11},{10,... | collective-permute-start | bytes 786440 | tf_op jit(solution)/shard_map/ppermute | solution.py:23
  78.7 1.5 %collective-permute-start.20 = (bf16[128,1024]{1,0:T(8,128)(2,1)S(1)}, bf16[128,1024]{1,0:T(8,128)(2,1)S(1)}, u32[]{:S(2)}, u32[]{:S(2)}) collective-permute-start(bf16[128,1024]{1,0:T(8,128)(2,1)S(1)} %shard_map.127.refs_3_), channel_id=1, source_target_pairs={{0,1},{1,0},{2,3},{3,2},{4,5},{5,4},{6,7},{7,6},{8,9},{9,8},{10,11... | collective-permute-start | bytes 786440 | tf_op jit(solution)/shard_map/ppermute | solution.py:23
  80.2 1.7 %collective-permute-done.16.refs_6_ = bf16[128,1024]{1,0:T(8,128)(2,1)S(1)} collective-permute-done((bf16[128,1024]{1,0:T(8,128)(2,1)S(1)}, bf16[128,1024]{1,0:T(8,128)(2,1)S(1)}, u32[]{:S(2)}, u32[]{:S(2)}) %collective-permute-start.16) | collective-permute-done | bytes 262176 | tf_op jit(solution)/shard_map/ppermute | solution.py:23
  81.9 0.0 collective-permute-done.17.refs_7_
  81.9 1.7 %shard_map.129 = bf16[128,2048]{1,0:T(8,128)(2,1)} custom-call(bf16[128,2048]{1,0:T(8,128)(2,1)S(1)} %collective-permute-done.refs_0_, f32[8,128]{1,0:T(8,128)S(1)} %get-tuple-element.37.refs_0_.refs_1_, bf16[96,1024]{1,0:T(8,128)(2,1)S(1)} %get-tuple-element.54.refs_2_, bf16[96,1024]{1,0:T(8,128)(2,1)S(1)} %get-tuple-element.56.refs_13_.refs_3_, ...), custom_call_target="tpu_custom_call" | custom-call | flops 1024 | bytes 1024 | tf_op jit(solution)/shard_map/pallas_call | solution.py:242
  83.6 0.2 collective-permute-done.21.refs_6_
  83.8 1.3 %collective-permute-done.20.refs_5_ = bf16[128,1024]{1,0:T(8,128)(2,1)S(1)} collective-permute-done((bf16[128,1024]{1,0:T(8,128)(2,1)S(1)}, bf16[128,1024]{1,0:T(8,128)(2,1)S(1)}, u32[]{:S(2)}, u32[]{:S(2)}) %collective-permute-start.20) | collective-permute-done | bytes 262176 | tf_op jit(solution)/shard_map/ppermute | solution.py:23
  85.1 0.0 copy-done.2
  85.1 1.7 %shard_map.130 = bf16[128,2048]{1,0:T(8,128)(2,1)} custom-call(bf16[128,2048]{1,0:T(8,128)(2,1)S(1)} %collective-permute-done.3.refs_0_.grads_ref, bf16[128,2048]{1,0:T(8,128)(2,1)S(1)} %bitcast.28, f32[1,2048]{1,0:T(1,128)S(1)} %get-tuple-element.41.refs_1_.gain_ref, f32[8,128]{1,0:T(8,128)S(1)} %get-tuple-element.37.refs_0_.refs_1_, ...), custom_call_target="tpu_custom_call" | custom-call | flops 1024 | bytes 1024 | tf_op jit(solution)/shard_map/pallas_call | solution.py:242
  (4 shorter events, 0.0 us)
Async XLA Ops:
  2.2 14.4 %collective-permute-start = (bf16[128,2048]{1,0:T(8,128)(2,1)S(1)}, bf16[128,2048]{1,0:T(8,128)(2,1)S(1)}, u32[]{:S(2)}, u32[]{:S(2)}) collective-permute-start(bf16[128,2048]{1,0:T(8,128)(2,1)S(1)} %get-tuple-element.36), channel_id=1, source_target_pairs={{0,4},{4,8},{8,12},{12,16},{16,20},{20,24},{24,28},{28,0},{1,5},{5... | collective-permute-start | bytes 1572872 | tf_op jit(solution)/shard_map/ppermute | solution.py:17
  2.7 18.2 %collective-permute-start.3 = (bf16[128,2048]{1,0:T(8,128)(2,1)S(1)}, bf16[128,2048]{1,0:T(8,128)(2,1)S(1)}, u32[]{:S(2)}, u32[]{:S(2)}) collective-permute-start(bf16[128,2048]{1,0:T(8,128)(2,1)S(1)} %get-tuple-element.40), channel_id=1, source_target_pairs={{0,28},{4,0},{8,4},{12,8},{16,12},{20,16},{24,20},{28,24},{1,29},{... | collective-permute-start | bytes 1572872 | tf_op jit(solution)/shard_map/ppermute | solution.py:17
  6.8 14.7 %collective-permute-start.2 = (bf16[144,1024]{1,0:T(8,128)(2,1)S(1)}, bf16[144,1024]{1,0:T(8,128)(2,1)S(1)}, u32[]{:S(2)}, u32[]{:S(2)}) collective-permute-start(bf16[144,1024]{1,0:T(8,128)(2,1)S(1)} %get-tuple-element.39.refs_4_), channel_id=1, source_target_pairs={{0,2},{1,3},{2,0},{3,1},{4,6},{5,7},{6,4},{7,5},{8,10},{9,11},{10,... | collective-permute-start | bytes 884744 | tf_op jit(solution)/shard_map/ppermute | solution.py:23
  8.7 12.7 %collective-permute-start.1 = (bf16[144,1024]{1,0:T(8,128)(2,1)S(1)}, bf16[144,1024]{1,0:T(8,128)(2,1)S(1)}, u32[]{:S(2)}, u32[]{:S(2)}) collective-permute-start(bf16[144,1024]{1,0:T(8,128)(2,1)S(1)} %get-tuple-element.38.refs_2_.refs_3_), channel_id=1, source_target_pairs={{0,1},{1,0},{2,3},{3,2},{4,5},{5,4},{6,7},{7,6},{8,9},{9,8},{10,11... | collective-permute-start | bytes 884744 | tf_op jit(solution)/shard_map/ppermute | solution.py:23
  16.5 27.7 %copy-start = (bf16[1,1,2048,1536]{3,2,1,0:T(8,128)(2,1)S(1)}, bf16[1,1,2048,1536]{3,2,1,0:T(8,128)(2,1)}, u32[]{:S(2)}) copy-start(bf16[1,1,2048,1536]{3,2,1,0:T(8,128)(2,1)} %param.18) | copy-start | bytes 18874372
  16.7 8.6 %collective-permute-start.5 = (bf16[128,1024]{1,0:T(8,128)(2,1)S(1)}, bf16[128,1024]{1,0:T(8,128)(2,1)S(1)}, u32[]{:S(2)}, u32[]{:S(2)}) collective-permute-start(bf16[128,1024]{1,0:T(8,128)(2,1)S(1)} %get-tuple-element.46.refs_4_), channel_id=1, source_target_pairs={{0,2},{1,3},{2,0},{3,1},{4,6},{5,7},{6,4},{7,5},{8,10},{9,11},{10,... | collective-permute-start | bytes 786440 | tf_op jit(solution)/shard_map/ppermute | solution.py:23
  19.3 8.4 %collective-permute-start.4 = (bf16[128,1024]{1,0:T(8,128)(2,1)S(1)}, bf16[128,1024]{1,0:T(8,128)(2,1)S(1)}, u32[]{:S(2)}, u32[]{:S(2)}) collective-permute-start(bf16[128,1024]{1,0:T(8,128)(2,1)S(1)} %get-tuple-element.42.refs_1_.refs_3_), channel_id=1, source_target_pairs={{0,1},{1,0},{2,3},{3,2},{4,5},{5,4},{6,7},{7,6},{8,9},{9,8},{10,11... | collective-permute-start | bytes 786440 | tf_op jit(solution)/shard_map/ppermute | solution.py:23
  20.9 10.1 %collective-permute-start.11 = (bf16[128,1024]{1,0:T(8,128)(2,1)S(1)}, bf16[128,1024]{1,0:T(8,128)(2,1)S(1)}, u32[]{:S(2)}, u32[]{:S(2)}) collective-permute-start(bf16[128,1024]{1,0:T(8,128)(2,1)S(1)} %get-tuple-element.51.refs_4_), channel_id=1, source_target_pairs={{0,2},{1,3},{2,0},{3,1},{4,6},{5,7},{6,4},{7,5},{8,10},{9,11},{10,... | collective-permute-start | bytes 786440 | tf_op jit(solution)/shard_map/ppermute | solution.py:23
  22.3 21.3 %collective-permute-start.9 = (bf16[192,1024]{1,0:T(8,128)(2,1)S(1)}, bf16[192,1024]{1,0:T(8,128)(2,1)S(1)}, u32[]{:S(2)}, u32[]{:S(2)}) collective-permute-start(bf16[192,1024]{1,0:T(8,128)(2,1)S(1)} %get-tuple-element.50), channel_id=1, source_target_pairs={{0,1},{1,0},{2,3},{3,2},{4,5},{5,4},{6,7},{7,6},{8,9},{9,8},{10,11... | collective-permute-start | bytes 1179656 | tf_op jit(solution)/shard_map/ppermute | solution.py:23
  22.5 21.7 %collective-permute-start.8 = (bf16[192,1024]{1,0:T(8,128)(2,1)S(1)}, bf16[192,1024]{1,0:T(8,128)(2,1)S(1)}, u32[]{:S(2)}, u32[]{:S(2)}) collective-permute-start(bf16[192,1024]{1,0:T(8,128)(2,1)S(1)} %get-tuple-element.47.refs_7_), channel_id=1, source_target_pairs={{0,2},{1,3},{2,0},{3,1},{4,6},{5,7},{6,4},{7,5},{8,10},{9,11},{10,... | collective-permute-start | bytes 1179656 | tf_op jit(solution)/shard_map/ppermute | solution.py:23
  25.4 15.6 %collective-permute-start.10 = (bf16[128,1024]{1,0:T(8,128)(2,1)S(1)}, bf16[128,1024]{1,0:T(8,128)(2,1)S(1)}, u32[]{:S(2)}, u32[]{:S(2)}) collective-permute-start(bf16[128,1024]{1,0:T(8,128)(2,1)S(1)} %get-tuple-element.43.refs_2_.refs_7_.refs_3_), channel_id=1, source_target_pairs={{0,1},{1,0},{2,3},{3,2},{4,5},{5,4},{6,7},{7,6},{8,9},{9,8},{10,11... | collective-permute-start | bytes 786440 | tf_op jit(solution)/shard_map/ppermute | solution.py:23
  28.6 20.9 %collective-permute-start.7 = (bf16[192,1024]{1,0:T(8,128)(2,1)S(1)}, bf16[192,1024]{1,0:T(8,128)(2,1)S(1)}, u32[]{:S(2)}, u32[]{:S(2)}) collective-permute-start(bf16[192,1024]{1,0:T(8,128)(2,1)S(1)} %get-tuple-element.49), channel_id=1, source_target_pairs={{0,1},{1,0},{2,3},{3,2},{4,5},{5,4},{6,7},{7,6},{8,9},{9,8},{10,11... | collective-permute-start | bytes 1179656 | tf_op jit(solution)/shard_map/ppermute | solution.py:23
  31.0 18.4 %collective-permute-start.6 = (bf16[192,1024]{1,0:T(8,128)(2,1)S(1)}, bf16[192,1024]{1,0:T(8,128)(2,1)S(1)}, u32[]{:S(2)}, u32[]{:S(2)}) collective-permute-start(bf16[192,1024]{1,0:T(8,128)(2,1)S(1)} %get-tuple-element.48.refs_7_), channel_id=1, source_target_pairs={{0,2},{1,3},{2,0},{3,1},{4,6},{5,7},{6,4},{7,5},{8,10},{9,11},{10,... | collective-permute-start | bytes 1179656 | tf_op jit(solution)/shard_map/ppermute | solution.py:23
  42.1 15.7 %collective-permute-start.15 = (bf16[192,1024]{1,0:T(8,128)(2,1)S(1)}, bf16[192,1024]{1,0:T(8,128)(2,1)S(1)}, u32[]{:S(2)}, u32[]{:S(2)}) collective-permute-start(bf16[192,1024]{1,0:T(8,128)(2,1)S(1)} %get-tuple-element.60), channel_id=1, source_target_pairs={{0,1},{1,0},{2,3},{3,2},{4,5},{5,4},{6,7},{7,6},{8,9},{9,8},{10,11... | collective-permute-start | bytes 1179656 | tf_op jit(solution)/shard_map/ppermute | solution.py:23
  43.7 14.2 %collective-permute-start.14 = (bf16[192,1024]{1,0:T(8,128)(2,1)S(1)}, bf16[192,1024]{1,0:T(8,128)(2,1)S(1)}, u32[]{:S(2)}, u32[]{:S(2)}) collective-permute-start(bf16[192,1024]{1,0:T(8,128)(2,1)S(1)} %get-tuple-element.52.refs_10_), channel_id=1, source_target_pairs={{0,2},{1,3},{2,0},{3,1},{4,6},{5,7},{6,4},{7,5},{8,10},{9,11},{10,... | collective-permute-start | bytes 1179656 | tf_op jit(solution)/shard_map/ppermute | solution.py:23
  44.2 5.2 %copy-start.1 = (bf16[1,1,768,2048]{3,2,1,0:T(8,128)(2,1)S(1)}, bf16[1,1,768,2048]{3,2,1,0:T(8,128)(2,1)}, u32[]{:S(2)}) copy-start(bf16[1,1,768,2048]{3,2,1,0:T(8,128)(2,1)} %param.19) | copy-start | bytes 9437188
  53.3 13.1 %collective-permute-start.12 = (bf16[192,1024]{1,0:T(8,128)(2,1)S(1)}, bf16[192,1024]{1,0:T(8,128)(2,1)S(1)}, u32[]{:S(2)}, u32[]{:S(2)}) collective-permute-start(bf16[192,1024]{1,0:T(8,128)(2,1)S(1)} %get-tuple-element.57), channel_id=1, source_target_pairs={{0,2},{1,3},{2,0},{3,1},{4,6},{5,7},{6,4},{7,5},{8,10},{9,11},{10,... | collective-permute-start | bytes 1179656 | tf_op jit(solution)/shard_map/ppermute | solution.py:23
  54.9 12.9 %collective-permute-start.13 = (bf16[192,1024]{1,0:T(8,128)(2,1)S(1)}, bf16[192,1024]{1,0:T(8,128)(2,1)S(1)}, u32[]{:S(2)}, u32[]{:S(2)}) collective-permute-start(bf16[192,1024]{1,0:T(8,128)(2,1)S(1)} %get-tuple-element.58), channel_id=1, source_target_pairs={{0,1},{1,0},{2,3},{3,2},{4,5},{5,4},{6,7},{7,6},{8,9},{9,8},{10,11... | collective-permute-start | bytes 1179656 | tf_op jit(solution)/shard_map/ppermute | solution.py:23
  62.5 12.1 %collective-permute-start.19 = (bf16[192,1024]{1,0:T(8,128)(2,1)S(1)}, bf16[192,1024]{1,0:T(8,128)(2,1)S(1)}, u32[]{:S(2)}, u32[]{:S(2)}) collective-permute-start(bf16[192,1024]{1,0:T(8,128)(2,1)S(1)} %get-tuple-element.68), channel_id=1, source_target_pairs={{0,2},{1,3},{2,0},{3,1},{4,6},{5,7},{6,4},{7,5},{8,10},{9,11},{10,... | collective-permute-start | bytes 1179656 | tf_op jit(solution)/shard_map/ppermute | solution.py:23
  64.8 12.1 %collective-permute-start.18 = (bf16[192,1024]{1,0:T(8,128)(2,1)S(1)}, bf16[192,1024]{1,0:T(8,128)(2,1)S(1)}, u32[]{:S(2)}, u32[]{:S(2)}) collective-permute-start(bf16[192,1024]{1,0:T(8,128)(2,1)S(1)} %get-tuple-element.66), channel_id=1, source_target_pairs={{0,1},{1,0},{2,3},{3,2},{4,5},{5,4},{6,7},{7,6},{8,9},{9,8},{10,11... | collective-permute-start | bytes 1179656 | tf_op jit(solution)/shard_map/ppermute | solution.py:23
  67.2 14.7 %collective-permute-start.16 = (bf16[128,1024]{1,0:T(8,128)(2,1)S(1)}, bf16[128,1024]{1,0:T(8,128)(2,1)S(1)}, u32[]{:S(2)}, u32[]{:S(2)}) collective-permute-start(bf16[128,1024]{1,0:T(8,128)(2,1)S(1)} %shard_map.125.refs_3_), channel_id=1, source_target_pairs={{0,1},{1,0},{2,3},{3,2},{4,5},{5,4},{6,7},{7,6},{8,9},{9,8},{10,11... | collective-permute-start | bytes 786440 | tf_op jit(solution)/shard_map/ppermute | solution.py:23
  68.5 13.3 %collective-permute-start.17 = (bf16[128,1024]{1,0:T(8,128)(2,1)S(1)}, bf16[128,1024]{1,0:T(8,128)(2,1)S(1)}, u32[]{:S(2)}, u32[]{:S(2)}) collective-permute-start(bf16[128,1024]{1,0:T(8,128)(2,1)S(1)} %shard_map.126.refs_3_), channel_id=1, source_target_pairs={{0,2},{1,3},{2,0},{3,1},{4,6},{5,7},{6,4},{7,5},{8,10},{9,11},{10,... | collective-permute-start | bytes 786440 | tf_op jit(solution)/shard_map/ppermute | solution.py:23
  77.4 6.4 %collective-permute-start.21 = (bf16[128,1024]{1,0:T(8,128)(2,1)S(1)}, bf16[128,1024]{1,0:T(8,128)(2,1)S(1)}, u32[]{:S(2)}, u32[]{:S(2)}) collective-permute-start(bf16[128,1024]{1,0:T(8,128)(2,1)S(1)} %shard_map.128.refs_8_), channel_id=1, source_target_pairs={{0,2},{1,3},{2,0},{3,1},{4,6},{5,7},{6,4},{7,5},{8,10},{9,11},{10,... | collective-permute-start | bytes 786440 | tf_op jit(solution)/shard_map/ppermute | solution.py:23
  78.7 6.4 %collective-permute-start.20 = (bf16[128,1024]{1,0:T(8,128)(2,1)S(1)}, bf16[128,1024]{1,0:T(8,128)(2,1)S(1)}, u32[]{:S(2)}, u32[]{:S(2)}) collective-permute-start(bf16[128,1024]{1,0:T(8,128)(2,1)S(1)} %shard_map.127.refs_3_), channel_id=1, source_target_pairs={{0,1},{1,0},{2,3},{3,2},{4,5},{5,4},{6,7},{7,6},{8,9},{9,8},{10,11... | collective-permute-start | bytes 786440 | tf_op jit(solution)/shard_map/ppermute | solution.py:23
  81.9 3.2 %copy-start.2 = (bf16[1,128,2048]{2,1,0:T(8,128)(2,1)S(1)}, bf16[1,128,2048]{2,1,0:T(8,128)(2,1)}, u32[]{:S(2)}) copy-start(bf16[1,128,2048]{2,1,0:T(8,128)(2,1)} %param.12) | copy-start | bytes 1572868

commit v7 on v5

--- a/solution.py
+++ b/solution.py
@@ -449,10 +449,13 @@
     right_ref[...] = values_ref[:, half:]
 
 
-def tables_kernel(top_count, from_x, from_y, x_table, y_table):
+def tables_kernel(top_count, from_x, from_y, kept_ref, x_table, y_table, handed_ref, sem):
+    copy = pltpu.make_async_copy(kept_ref, handed_ref, sem)
+    copy.start()
     tok_rows = x_table.shape[1]
     x_table[...] = unpacked(from_x[...], tok_rows, top_count)
     y_table[...] = unpacked(from_y[...], tok_rows, top_count)
+    copy.wait()
 
 
 def hop_kernel(kind, top_count, own, x_tab, y_tab, left, right, from_x, from_y, to_y, to_x):
@@ -655,7 +658,6 @@
     me = lax.axis_index("expert").astype(jnp.int32).reshape(1)
     saved = bwd_saved[0]
     layer_in = passed_along(fwd_prev[0], "section", 1)
-    grad_in = passed_along(bwd_prev[0], "section", -1)
 
     def shaped(rows, columns, dtype=jnp.bfloat16):
         return jax.ShapeDtypeStruct((rows, columns), dtype)
@@ -713,13 +715,16 @@
         ],
     )
     b_from_x, b_from_y = crossed(b_left, b_right)
-    x_tab, y_tab = local_call(
+    x_tab, y_tab, bwd_here = pl.pallas_call(
         functools.partial(tables_kernel, top_count),
-        [table_shape] * 2,
-        (b_from_x, b_from_y),
-        1024,
-        1024,
-    )
+        out_shape=[table_shape, table_shape, shaped(tok_rows, features)],
+        in_specs=[pl.BlockSpec(memory_space=pltpu.VMEM)] * 2
+        + [pl.BlockSpec(memory_space=pltpu.HBM)],
+        scratch_shapes=[pltpu.SemaphoreType.DMA(())],
+        compiler_params=pltpu.CompilerParams(vmem_limit_bytes=VMEM_LIMIT),
+        cost_estimate=pl.CostEstimate(flops=one_hop, bytes_accessed=moved, transcendentals=0),
+    )(b_from_x, b_from_y, pltpu.with_memory_space_constraint(bwd_prev[0], pltpu.HBM))
+    grad_in = passed_along(bwd_here, "section", -1)
     tabs = (own, x_tab, y_tab)
 
     def onward(kind, sent, got, after):

time: 86.2 us -> 88.4 us (1.026)
  waiting for transfers between devices: 32.3 us -> 37.7 us
  starting transfers between devices: 28.7 us -> 24.3 us
  Pallas kernels: 24.3 us -> 25.5 us
    ppermute x2, waiting for transfers between devices: 0.01 us -> 3.4 us  [passed_along(): return lax.ppermute(value, axis, pairs)]
    ppermute x2, starting transfers between devices: 4.61 us -> 1.91 us  [passed_along(): return lax.ppermute(value, axis, pairs)]
    ppermute x20, waiting for transfers between devices: 32.3 us -> 34.3 us  [swapped(): return lax.ppermute(value, axis, pairs)]
    ppermute x20, starting transfers between devices: 24.1 us -> 22.4 us  [swapped(): return lax.ppermute(value, axis, pairs)]
    pallas_call x0 -> x1, Pallas kernels: none -> 1.2 us  [per_device_hops(): pl.pallas_call(functools.partial(tables_kernel, top_count), out_shape=[ta...]
    pallas_call x17 -> x16, Pallas kernels: 23 us -> 23 us  [local_call(): pl.pallas_call(body if after else kernel, out_shape=out_shapes, in_specs=...]
  transfers between devices with their start and end apart: 22 -> 22, of which waited for: 13 -> 12; matrix products, arithmetic and copies ran while one was open for 0% -> 0% of each run, Pallas kernels for 26% -> 26%
where the time goes in v7:
time: 88.4 us; the launch traced here: 88.2 us
  waiting for transfers between devices  37.7 us (43%)
  Pallas kernels  25.5 us (29%)
  starting transfers between devices  24.3 us (27%)
    ppermute x20, waiting for transfers between devices, swapped(): return lax.ppermute(value, axis, pairs)  34.3 us
    pallas_call x16, Pallas kernels, local_call(): pl.pallas_call(body if after else kernel, out_shape=out_shapes, in_specs=...  23 us
    ppermute x20, starting transfers between devices, swapped(): return lax.ppermute(value, axis, pairs)  22.4 us
    ppermute x2, waiting for transfers between devices, passed_along(): return lax.ppermute(value, axis, pairs)  3.4 us
    ppermute x2, starting transfers between devices, passed_along(): return lax.ppermute(value, axis, pairs)  1.91 us
  transfers between devices with their start and end apart: 22, of which 12 were waited for; matrix products, arithmetic and copies ran while one was open for 0% of the time, Pallas kernels for 26%

profile of v7, /device:TPU:0, one launch (start us, length us, event | category | flops | bytes accessed | tf_op | source)
XLA Modules:
  0.0 88.2 jit_solution(11299719599162569212)
XLA Ops:
  0.6 1.3 %shard_map.113 = (bf16[144,1024]{1,0:T(8,128)(2,1)S(1)}, bf16[144,1024]{1,0:T(8,128)(2,1)S(1)}, f32[8,128]{1,0:T(8,128)S(1)}, f32[1,2048]{1,0:T(1,128)S(1)}) custom-call(s32[1]{0:T(128)} %bitcast.1.me_ref, bf16[128,2048]{1,0:T(8,128)(2,1)} %bitcast.27, f32[1,2048]{1,0:T(1,128)} %refs_1_.1, s32[2,128]{1,0:T(2,128)} %bitcast.32, f32[2,128]{1,0:T(2,128)} %bitcast.33, ...), custom_call_target="tpu_custom_call" | custom-call | flops 1024 | bytes 1024 | tf_op jit(solution)/shard_map/pallas_call | solution.py:682
  2.0 3.0 %collective-permute-start.1 = (bf16[144,1024]{1,0:T(8,128)(2,1)S(1)}, bf16[144,1024]{1,0:T(8,128)(2,1)S(1)}, u32[]{:S(2)}, u32[]{:S(2)}) collective-permute-start(bf16[144,1024]{1,0:T(8,128)(2,1)S(1)} %get-tuple-element.36.left.refs_3_), channel_id=1, source_target_pairs={{0,1},{1,0},{2,3},{3,2},{4,5},{5,4},{6,7},{7,6},{8,9},{9,8},{10,11... | collective-permute-start | bytes 884744 | tf_op jit(solution)/shard_map/ppermute | solution.py:23
  5.0 1.5 %collective-permute-start.2 = (bf16[144,1024]{1,0:T(8,128)(2,1)S(1)}, bf16[144,1024]{1,0:T(8,128)(2,1)S(1)}, u32[]{:S(2)}, u32[]{:S(2)}) collective-permute-start(bf16[144,1024]{1,0:T(8,128)(2,1)S(1)} %get-tuple-element.37.right.refs_4_), channel_id=1, source_target_pairs={{0,2},{1,3},{2,0},{3,1},{4,6},{5,7},{6,4},{7,5},{8,10},{9,11},{10,... | collective-permute-start | bytes 884744 | tf_op jit(solution)/shard_map/ppermute | solution.py:23
  6.5 0.0 collective-permute-start
  6.5 5.5 %collective-permute-done.1.from_x.refs_5_ = bf16[144,1024]{1,0:T(8,128)(2,1)S(1)} collective-permute-done((bf16[144,1024]{1,0:T(8,128)(2,1)S(1)}, bf16[144,1024]{1,0:T(8,128)(2,1)S(1)}, u32[]{:S(2)}, u32[]{:S(2)}) %collective-permute-start.1) | collective-permute-done | bytes 294944 | tf_op jit(solution)/shard_map/ppermute | solution.py:23
  12.0 1.5 %collective-permute-done.2.from_y.refs_6_ = bf16[144,1024]{1,0:T(8,128)(2,1)S(1)} collective-permute-done((bf16[144,1024]{1,0:T(8,128)(2,1)S(1)}, bf16[144,1024]{1,0:T(8,128)(2,1)S(1)}, u32[]{:S(2)}, u32[]{:S(2)}) %collective-permute-start.2) | collective-permute-done | bytes 294944 | tf_op jit(solution)/shard_map/ppermute | solution.py:23
  13.4 1.2 %shard_map.114 = (f32[8,128]{1,0:T(8,128)S(1)}, f32[8,128]{1,0:T(8,128)S(1)}, bf16[128,2048]{1,0:T(8,128)(2,1)S(1)}) custom-call(bf16[144,1024]{1,0:T(8,128)(2,1)S(1)} %collective-permute-done.1.from_x.refs_5_, bf16[144,1024]{1,0:T(8,128)(2,1)S(1)} %collective-permute-done.2.from_y.refs_6_, bf16[128,2048]{1,0:T(8,128)(2,1)} %bitcast.30), custom_call_target="tpu_custom_call" | custom-call | flops 1024 | bytes 1024 | tf_op jit(solution)/shard_map/pallas_call | solution.py:718
  14.6 1.9 %collective-permute-start.5 = (bf16[128,2048]{1,0:T(8,128)(2,1)S(1)}, bf16[128,2048]{1,0:T(8,128)(2,1)S(1)}, u32[]{:S(2)}, u32[]{:S(2)}) collective-permute-start(bf16[128,2048]{1,0:T(8,128)(2,1)S(1)} %get-tuple-element.44), channel_id=1, source_target_pairs={{0,28},{4,0},{8,4},{12,8},{16,12},{20,16},{24,20},{28,24},{1,29},{... | collective-permute-start | bytes 1572872 | tf_op jit(solution)/shard_map/ppermute | solution.py:17
  16.6 0.9 shard_map.115
  17.4 0.0 collective-permute-done.refs_0_
  17.4 0.2 shard_map.116
  17.7 1.6 %collective-permute-start.4 = (bf16[128,1024]{1,0:T(8,128)(2,1)S(1)}, bf16[128,1024]{1,0:T(8,128)(2,1)S(1)}, u32[]{:S(2)}, u32[]{:S(2)}) collective-permute-start(bf16[128,1024]{1,0:T(8,128)(2,1)S(1)} %get-tuple-element.43.refs_4_), channel_id=1, source_target_pairs={{0,2},{1,3},{2,0},{3,1},{4,6},{5,7},{6,4},{7,5},{8,10},{9,11},{10,... | collective-permute-start | bytes 786440 | tf_op jit(solution)/shard_map/ppermute | solution.py:23
  19.3 0.6 collective-permute-start.3
  19.9 3.4 %collective-permute-done.5.refs_0_.grads_ref = bf16[128,2048]{1,0:T(8,128)(2,1)S(1)} collective-permute-done((bf16[128,2048]{1,0:T(8,128)(2,1)S(1)}, bf16[128,2048]{1,0:T(8,128)(2,1)S(1)}, u32[]{:S(2)}, u32[]{:S(2)}) %collective-permute-start.5) | collective-permute-done | bytes 524320 | tf_op jit(solution)/shard_map/ppermute | solution.py:17
  23.3 1.6 %collective-permute-start.11 = (bf16[128,1024]{1,0:T(8,128)(2,1)S(1)}, bf16[128,1024]{1,0:T(8,128)(2,1)S(1)}, u32[]{:S(2)}, u32[]{:S(2)}) collective-permute-start(bf16[128,1024]{1,0:T(8,128)(2,1)S(1)} %get-tuple-element.49.refs_4_), channel_id=1, source_target_pairs={{0,2},{1,3},{2,0},{3,1},{4,6},{5,7},{6,4},{7,5},{8,10},{9,11},{10,... | collective-permute-start | bytes 786440 | tf_op jit(solution)/shard_map/ppermute | solution.py:23
  24.9 0.6 collective-permute-start.9
  25.5 0.5 collective-permute-start.8
  26.0 0.0 collective-permute-done.4.refs_6_
  26.0 1.4 %collective-permute-start.10 = (bf16[128,1024]{1,0:T(8,128)(2,1)S(1)}, bf16[128,1024]{1,0:T(8,128)(2,1)S(1)}, u32[]{:S(2)}, u32[]{:S(2)}) collective-permute-start(bf16[128,1024]{1,0:T(8,128)(2,1)S(1)} %get-tuple-element.45.refs_7_.refs_3_), channel_id=1, source_target_pairs={{0,1},{1,0},{2,3},{3,2},{4,5},{5,4},{6,7},{7,6},{8,9},{9,8},{10,11... | collective-permute-start | bytes 786440 | tf_op jit(solution)/shard_map/ppermute | solution.py:23
  27.4 0.0 collective-permute-done.3.refs_5_
  27.4 0.9 shard_map.118
  28.3 0.7 collective-permute-start.7
  29.0 3.5 %collective-permute-done.11.refs_6_ = bf16[128,1024]{1,0:T(8,128)(2,1)S(1)} collective-permute-done((bf16[128,1024]{1,0:T(8,128)(2,1)S(1)}, bf16[128,1024]{1,0:T(8,128)(2,1)S(1)}, u32[]{:S(2)}, u32[]{:S(2)}) %collective-permute-start.11) | collective-permute-done | bytes 262176 | tf_op jit(solution)/shard_map/ppermute | solution.py:23
  32.5 1.5 %collective-permute-start.6 = (bf16[192,1024]{1,0:T(8,128)(2,1)S(1)}, bf16[192,1024]{1,0:T(8,128)(2,1)S(1)}, u32[]{:S(2)}, u32[]{:S(2)}) collective-permute-start(bf16[192,1024]{1,0:T(8,128)(2,1)S(1)} %get-tuple-element.46.refs_7_), channel_id=1, source_target_pairs={{0,2},{1,3},{2,0},{3,1},{4,6},{5,7},{6,4},{7,5},{8,10},{9,11},{10,... | collective-permute-start | bytes 1179656 | tf_op jit(solution)/shard_map/ppermute | solution.py:23
  34.0 8.5 %collective-permute-done.10.refs_5_ = bf16[128,1024]{1,0:T(8,128)(2,1)S(1)} collective-permute-done((bf16[128,1024]{1,0:T(8,128)(2,1)S(1)}, bf16[128,1024]{1,0:T(8,128)(2,1)S(1)}, u32[]{:S(2)}, u32[]{:S(2)}) %collective-permute-start.10) | collective-permute-done | bytes 262176 | tf_op jit(solution)/shard_map/ppermute | solution.py:23
  42.5 1.1 %shard_map.119 = (bf16[192,1024]{1,0:T(8,128)(2,1)S(1)}, bf16[192,1024]{1,0:T(8,128)(2,1)S(1)}) custom-call(f32[8,128]{1,0:T(8,128)S(1)} %get-tuple-element.35.own.refs_0_.refs_1_, f32[8,128]{1,0:T(8,128)S(1)} %get-tuple-element.38.x_tab.refs_1_.refs_0_, f32[8,128]{1,0:T(8,128)S(1)} %get-tuple-element.39.y_tab.refs_2_.refs_0_, ...), custom_call_target="tpu_custom_call" | custom-call | flops 1024 | bytes 1024 | tf_op jit(solution)/shard_map/pallas_call | solution.py:242
  43.6 0.7 collective-permute-start.15
  44.3 0.0 collective-permute-done.9.refs_8_
  44.3 0.5 collective-permute-start.14
  44.8 0.0 collective-permute-done.8.refs_7_
  44.8 0.0 copy-done
  44.8 3.2 %shard_map.120 = (f32[384,768]{1,0:T(8,128)S(1)}, f32[384,768]{1,0:T(8,128)S(1)}) custom-call(f32[8,128]{1,0:T(8,128)S(1)} %get-tuple-element.35.own.refs_0_.refs_1_, f32[8,128]{1,0:T(8,128)S(1)} %get-tuple-element.38.x_tab.refs_1_.refs_0_, f32[8,128]{1,0:T(8,128)S(1)} %get-tuple-element.39.y_tab.refs_2_.refs_0_, ...), custom_call_target="tpu_custom_call" | custom-call | flops 2415919104 | bytes 14155776 | tf_op jit(solution)/shard_map/pallas_call | solution.py:242
  48.0 2.8 %collective-permute-done.7.refs_8_ = bf16[192,1024]{1,0:T(8,128)(2,1)S(1)} collective-permute-done((bf16[192,1024]{1,0:T(8,128)(2,1)S(1)}, bf16[192,1024]{1,0:T(8,128)(2,1)S(1)}, u32[]{:S(2)}, u32[]{:S(2)}) %collective-permute-start.7) | collective-permute-done | bytes 393248 | tf_op jit(solution)/shard_map/ppermute | solution.py:23
  50.9 0.0 collective-permute-done.6.refs_7_
  50.9 0.0 copy-done.1
  50.9 3.9 %shard_map.121 = (bf16[96,1024]{1,0:T(8,128)(2,1)S(1)}, bf16[96,1024]{1,0:T(8,128)(2,1)S(1)}, bf16[192,1024]{1,0:T(8,128)(2,1)S(1)}, bf16[384,768]{1,0:T(8,128)(2,1)S(1)}) custom-call(f32[8,128]{1,0:T(8,128)S(1)} %get-tuple-element.35.own.refs_0_.refs_1_, f32[8,128]{1,0:T(8,128)S(1)} %get-tuple-element.38.x_tab.refs_1_.refs_0_, ...), custom_call_target="tpu_custom_call" | custom-call | flops 3019898880 | bytes 14155776 | tf_op jit(solution)/shard_map/pallas_call | solution.py:242
  54.8 0.6 collective-permute-start.12
  55.4 0.8 shard_map.122
  56.2 0.7 collective-permute-start.13
  56.8 2.5 %collective-permute-done.15.refs_8_ = bf16[192,1024]{1,0:T(8,128)(2,1)S(1)} collective-permute-done((bf16[192,1024]{1,0:T(8,128)(2,1)S(1)}, bf16[192,1024]{1,0:T(8,128)(2,1)S(1)}, u32[]{:S(2)}, u32[]{:S(2)}) %collective-permute-start.15) | collective-permute-done | bytes 393248 | tf_op jit(solution)/shard_map/ppermute | solution.py:23
  59.3 0.0 collective-permute-done.14.refs_7_
  59.3 4.7 %shard_map.123 = (bf16[96,1024]{1,0:T(8,128)(2,1)S(1)}, bf16[96,1024]{1,0:T(8,128)(2,1)S(1)}, bf16[192,1024]{1,0:T(8,128)(2,1)S(1)}, bf16[384,1536]{1,0:T(8,128)(2,1)S(1)}) custom-call(f32[8,128]{1,0:T(8,128)S(1)} %get-tuple-element.35.own.refs_0_.refs_1_, f32[8,128]{1,0:T(8,128)S(1)} %get-tuple-element.38.x_tab.refs_1_.refs_0_, ...), custom_call_target="tpu_custom_call" | custom-call | flops 2415919104 | bytes 14155776 | tf_op jit(solution)/shard_map/pallas_call | solution.py:242
  64.0 0.2 collective-permute-start.19
  64.2 1.4 %shard_map.124 = (bf16[96,1024]{1,0:T(8,128)(2,1)S(1)}, bf16[96,1024]{1,0:T(8,128)(2,1)S(1)}, bf16[192,1024]{1,0:T(8,128)(2,1)S(1)}) custom-call(bf16[384,1536]{1,0:T(8,128)(2,1)S(1)} %get-tuple-element.60.both_ref, bf16[2048,1536]{1,0:T(8,128)(2,1)S(1)} %bitcast.23), custom_call_target="tpu_custom_call" | custom-call | flops 1024 | bytes 1024 | tf_op jit(solution)/shard_map/pallas_call | solution.py:242
  65.6 0.7 collective-permute-start.18
  66.3 0.0 collective-permute-done.12.refs_2_.refs_4_
  66.3 0.8 shard_map.125.refs_3_
  67.1 1.5 %collective-permute-start.16 = (bf16[128,1024]{1,0:T(8,128)(2,1)S(1)}, bf16[128,1024]{1,0:T(8,128)(2,1)S(1)}, u32[]{:S(2)}, u32[]{:S(2)}) collective-permute-start(bf16[128,1024]{1,0:T(8,128)(2,1)S(1)} %shard_map.125.refs_3_), channel_id=1, source_target_pairs={{0,1},{1,0},{2,3},{3,2},{4,5},{5,4},{6,7},{7,6},{8,9},{9,8},{10,11... | collective-permute-start | bytes 786440 | tf_op jit(solution)/shard_map/ppermute | solution.py:23
  68.6 0.0 collective-permute-done.13.refs_2_.refs_5_
  68.6 0.8 shard_map.126.refs_3_
  69.4 2.0 %collective-permute-start.17 = (bf16[128,1024]{1,0:T(8,128)(2,1)S(1)}, bf16[128,1024]{1,0:T(8,128)(2,1)S(1)}, u32[]{:S(2)}, u32[]{:S(2)}) collective-permute-start(bf16[128,1024]{1,0:T(8,128)(2,1)S(1)} %shard_map.126.refs_3_), channel_id=1, source_target_pairs={{0,2},{1,3},{2,0},{3,1},{4,6},{5,7},{6,4},{7,5},{8,10},{9,11},{10,... | collective-permute-start | bytes 786440 | tf_op jit(solution)/shard_map/ppermute | solution.py:23
  71.3 4.8 %collective-permute-done.19.refs_2_.refs_3_ = bf16[192,1024]{1,0:T(8,128)(2,1)S(1)} collective-permute-done((bf16[192,1024]{1,0:T(8,128)(2,1)S(1)}, bf16[192,1024]{1,0:T(8,128)(2,1)S(1)}, u32[]{:S(2)}, u32[]{:S(2)}) %collective-permute-start.19) | collective-permute-done | bytes 393248 | tf_op jit(solution)/shard_map/ppermute | solution.py:23
  76.1 0.5 shard_map.127.refs_3_
  76.6 1.1 %collective-permute-done.18.refs_2_.refs_4_ = bf16[192,1024]{1,0:T(8,128)(2,1)S(1)} collective-permute-done((bf16[192,1024]{1,0:T(8,128)(2,1)S(1)}, bf16[192,1024]{1,0:T(8,128)(2,1)S(1)}, u32[]{:S(2)}, u32[]{:S(2)}) %collective-permute-start.18) | collective-permute-done | bytes 393248 | tf_op jit(solution)/shard_map/ppermute | solution.py:23
  77.7 0.5 shard_map.128.refs_8_
  78.2 2.0 %collective-permute-start.21 = (bf16[128,1024]{1,0:T(8,128)(2,1)S(1)}, bf16[128,1024]{1,0:T(8,128)(2,1)S(1)}, u32[]{:S(2)}, u32[]{:S(2)}) collective-permute-start(bf16[128,1024]{1,0:T(8,128)(2,1)S(1)} %shard_map.128.refs_8_), channel_id=1, source_target_pairs={{0,2},{1,3},{2,0},{3,1},{4,6},{5,7},{6,4},{7,5},{8,10},{9,11},{10,... | collective-permute-start | bytes 786440 | tf_op jit(solution)/shard_map/ppermute | solution.py:23
  80.2 0.6 collective-permute-start.20
  80.8 2.5 %collective-permute-done.16.refs_6_ = bf16[128,1024]{1,0:T(8,128)(2,1)S(1)} collective-permute-done((bf16[128,1024]{1,0:T(8,128)(2,1)S(1)}, bf16[128,1024]{1,0:T(8,128)(2,1)S(1)}, u32[]{:S(2)}, u32[]{:S(2)}) %collective-permute-start.16) | collective-permute-done | bytes 262176 | tf_op jit(solution)/shard_map/ppermute | solution.py:23
  83.3 0.0 collective-permute-done.17.refs_7_
  83.4 1.7 %shard_map.129 = bf16[128,2048]{1,0:T(8,128)(2,1)} custom-call(bf16[128,2048]{1,0:T(8,128)(2,1)S(1)} %collective-permute-done.refs_0_, f32[8,128]{1,0:T(8,128)S(1)} %get-tuple-element.35.own.refs_0_.refs_1_, bf16[96,1024]{1,0:T(8,128)(2,1)S(1)} %get-tuple-element.52.refs_2_, bf16[96,1024]{1,0:T(8,128)(2,1)S(1)} %get-tuple-element.54.refs_13_.refs_3_, ...), custom_call_target="tpu_custom_call" | custom-call | flops 1024 | bytes 1024 | tf_op jit(solution)/shard_map/pallas_call | solution.py:242
  85.1 0.2 collective-permute-done.21.refs_6_
  85.2 1.3 %collective-permute-done.20.refs_5_ = bf16[128,1024]{1,0:T(8,128)(2,1)S(1)} collective-permute-done((bf16[128,1024]{1,0:T(8,128)(2,1)S(1)}, bf16[128,1024]{1,0:T(8,128)(2,1)S(1)}, u32[]{:S(2)}, u32[]{:S(2)}) %collective-permute-start.20) | collective-permute-done | bytes 262176 | tf_op jit(solution)/shard_map/ppermute | solution.py:23
  86.5 0.0 copy-done.2
  86.6 1.7 %shard_map.130 = bf16[128,2048]{1,0:T(8,128)(2,1)} custom-call(bf16[128,2048]{1,0:T(8,128)(2,1)S(1)} %collective-permute-done.5.refs_0_.grads_ref, bf16[128,2048]{1,0:T(8,128)(2,1)S(1)} %bitcast.28, f32[1,2048]{1,0:T(1,128)S(1)} %get-tuple-element.40.refs_1_.gain_ref, f32[8,128]{1,0:T(8,128)S(1)} %get-tuple-element.35.own.refs_0_.refs_1_, ...), custom_call_target="tpu_custom_call" | custom-call | flops 1024 | bytes 1024 | tf_op jit(solution)/shard_map/pallas_call | solution.py:242
  (4 shorter events, 0.0 us)
Async XLA Ops:
  2.0 10.0 %collective-permute-start.1 = (bf16[144,1024]{1,0:T(8,128)(2,1)S(1)}, bf16[144,1024]{1,0:T(8,128)(2,1)S(1)}, u32[]{:S(2)}, u32[]{:S(2)}) collective-permute-start(bf16[144,1024]{1,0:T(8,128)(2,1)S(1)} %get-tuple-element.36.left.refs_3_), channel_id=1, source_target_pairs={{0,1},{1,0},{2,3},{3,2},{4,5},{5,4},{6,7},{7,6},{8,9},{9,8},{10,11... | collective-permute-start | bytes 884744 | tf_op jit(solution)/shard_map/ppermute | solution.py:23
  5.0 8.5 %collective-permute-start.2 = (bf16[144,1024]{1,0:T(8,128)(2,1)S(1)}, bf16[144,1024]{1,0:T(8,128)(2,1)S(1)}, u32[]{:S(2)}, u32[]{:S(2)}) collective-permute-start(bf16[144,1024]{1,0:T(8,128)(2,1)S(1)} %get-tuple-element.37.right.refs_4_), channel_id=1, source_target_pairs={{0,2},{1,3},{2,0},{3,1},{4,6},{5,7},{6,4},{7,5},{8,10},{9,11},{10,... | collective-permute-start | bytes 884744 | tf_op jit(solution)/shard_map/ppermute | solution.py:23
  6.5 10.9 %collective-permute-start = (bf16[128,2048]{1,0:T(8,128)(2,1)}, bf16[128,2048]{1,0:T(8,128)(2,1)S(1)}, u32[]{:S(2)}, u32[]{:S(2)}) collective-permute-start(bf16[128,2048]{1,0:T(8,128)(2,1)} %bitcast.36), channel_id=1, source_target_pairs={{0,4},{4,8},{8,12},{12,16},{16,20},{20,24},{24,28},{28,0},{1,5},{5... | collective-permute-start | bytes 1572872 | tf_op jit(solution)/shard_map/ppermute | solution.py:17
  13.4 31.4 %copy-start = (bf16[1,1,2048,1536]{3,2,1,0:T(8,128)(2,1)S(1)}, bf16[1,1,2048,1536]{3,2,1,0:T(8,128)(2,1)}, u32[]{:S(2)}) copy-start(bf16[1,1,2048,1536]{3,2,1,0:T(8,128)(2,1)} %param.18) | copy-start | bytes 18874372
  14.6 8.6 %collective-permute-start.5 = (bf16[128,2048]{1,0:T(8,128)(2,1)S(1)}, bf16[128,2048]{1,0:T(8,128)(2,1)S(1)}, u32[]{:S(2)}, u32[]{:S(2)}) collective-permute-start(bf16[128,2048]{1,0:T(8,128)(2,1)S(1)} %get-tuple-element.44), channel_id=1, source_target_pairs={{0,28},{4,0},{8,4},{12,8},{16,12},{20,16},{24,20},{28,24},{1,29},{... | collective-permute-start | bytes 1572872 | tf_op jit(solution)/shard_map/ppermute | solution.py:17
  17.7 8.3 %collective-permute-start.4 = (bf16[128,1024]{1,0:T(8,128)(2,1)S(1)}, bf16[128,1024]{1,0:T(8,128)(2,1)S(1)}, u32[]{:S(2)}, u32[]{:S(2)}) collective-permute-start(bf16[128,1024]{1,0:T(8,128)(2,1)S(1)} %get-tuple-element.43.refs_4_), channel_id=1, source_target_pairs={{0,2},{1,3},{2,0},{3,1},{4,6},{5,7},{6,4},{7,5},{8,10},{9,11},{10,... | collective-permute-start | bytes 786440 | tf_op jit(solution)/shard_map/ppermute | solution.py:23
  19.3 8.2 %collective-permute-start.3 = (bf16[128,1024]{1,0:T(8,128)(2,1)S(1)}, bf16[128,1024]{1,0:T(8,128)(2,1)S(1)}, u32[]{:S(2)}, u32[]{:S(2)}) collective-permute-start(bf16[128,1024]{1,0:T(8,128)(2,1)S(1)} %get-tuple-element.42.refs_1_.refs_3_), channel_id=1, source_target_pairs={{0,1},{1,0},{2,3},{3,2},{4,5},{5,4},{6,7},{7,6},{8,9},{9,8},{10,11... | collective-permute-start | bytes 786440 | tf_op jit(solution)/shard_map/ppermute | solution.py:23
  23.3 9.2 %collective-permute-start.11 = (bf16[128,1024]{1,0:T(8,128)(2,1)S(1)}, bf16[128,1024]{1,0:T(8,128)(2,1)S(1)}, u32[]{:S(2)}, u32[]{:S(2)}) collective-permute-start(bf16[128,1024]{1,0:T(8,128)(2,1)S(1)} %get-tuple-element.49.refs_4_), channel_id=1, source_target_pairs={{0,2},{1,3},{2,0},{3,1},{4,6},{5,7},{6,4},{7,5},{8,10},{9,11},{10,... | collective-permute-start | bytes 786440 | tf_op jit(solution)/shard_map/ppermute | solution.py:23
  24.9 19.4 %collective-permute-start.9 = (bf16[192,1024]{1,0:T(8,128)(2,1)S(1)}, bf16[192,1024]{1,0:T(8,128)(2,1)S(1)}, u32[]{:S(2)}, u32[]{:S(2)}) collective-permute-start(bf16[192,1024]{1,0:T(8,128)(2,1)S(1)} %get-tuple-element.48), channel_id=1, source_target_pairs={{0,1},{1,0},{2,3},{3,2},{4,5},{5,4},{6,7},{7,6},{8,9},{9,8},{10,11... | collective-permute-start | bytes 1179656 | tf_op jit(solution)/shard_map/ppermute | solution.py:23
  25.5 19.3 %collective-permute-start.8 = (bf16[192,1024]{1,0:T(8,128)(2,1)S(1)}, bf16[192,1024]{1,0:T(8,128)(2,1)S(1)}, u32[]{:S(2)}, u32[]{:S(2)}) collective-permute-start(bf16[192,1024]{1,0:T(8,128)(2,1)S(1)} %get-tuple-element.41.refs_2_), channel_id=1, source_target_pairs={{0,2},{1,3},{2,0},{3,1},{4,6},{5,7},{6,4},{7,5},{8,10},{9,11},{10,... | collective-permute-start | bytes 1179656 | tf_op jit(solution)/shard_map/ppermute | solution.py:23
  26.0 16.5 %collective-permute-start.10 = (bf16[128,1024]{1,0:T(8,128)(2,1)S(1)}, bf16[128,1024]{1,0:T(8,128)(2,1)S(1)}, u32[]{:S(2)}, u32[]{:S(2)}) collective-permute-start(bf16[128,1024]{1,0:T(8,128)(2,1)S(1)} %get-tuple-element.45.refs_7_.refs_3_), channel_id=1, source_target_pairs={{0,1},{1,0},{2,3},{3,2},{4,5},{5,4},{6,7},{7,6},{8,9},{9,8},{10,11... | collective-permute-start | bytes 786440 | tf_op jit(solution)/shard_map/ppermute | solution.py:23
  28.3 22.6 %collective-permute-start.7 = (bf16[192,1024]{1,0:T(8,128)(2,1)S(1)}, bf16[192,1024]{1,0:T(8,128)(2,1)S(1)}, u32[]{:S(2)}, u32[]{:S(2)}) collective-permute-start(bf16[192,1024]{1,0:T(8,128)(2,1)S(1)} %get-tuple-element.47), channel_id=1, source_target_pairs={{0,1},{1,0},{2,3},{3,2},{4,5},{5,4},{6,7},{7,6},{8,9},{9,8},{10,11... | collective-permute-start | bytes 1179656 | tf_op jit(solution)/shard_map/ppermute | solution.py:23
  32.5 18.4 %collective-permute-start.6 = (bf16[192,1024]{1,0:T(8,128)(2,1)S(1)}, bf16[192,1024]{1,0:T(8,128)(2,1)S(1)}, u32[]{:S(2)}, u32[]{:S(2)}) collective-permute-start(bf16[192,1024]{1,0:T(8,128)(2,1)S(1)} %get-tuple-element.46.refs_7_), channel_id=1, source_target_pairs={{0,2},{1,3},{2,0},{3,1},{4,6},{5,7},{6,4},{7,5},{8,10},{9,11},{10,... | collective-permute-start | bytes 1179656 | tf_op jit(solution)/shard_map/ppermute | solution.py:23
  43.6 15.7 %collective-permute-start.15 = (bf16[192,1024]{1,0:T(8,128)(2,1)S(1)}, bf16[192,1024]{1,0:T(8,128)(2,1)S(1)}, u32[]{:S(2)}, u32[]{:S(2)}) collective-permute-start(bf16[192,1024]{1,0:T(8,128)(2,1)S(1)} %get-tuple-element.58), channel_id=1, source_target_pairs={{0,1},{1,0},{2,3},{3,2},{4,5},{5,4},{6,7},{7,6},{8,9},{9,8},{10,11... | collective-permute-start | bytes 1179656 | tf_op jit(solution)/shard_map/ppermute | solution.py:23
  44.3 15.0 %collective-permute-start.14 = (bf16[192,1024]{1,0:T(8,128)(2,1)S(1)}, bf16[192,1024]{1,0:T(8,128)(2,1)S(1)}, u32[]{:S(2)}, u32[]{:S(2)}) collective-permute-start(bf16[192,1024]{1,0:T(8,128)(2,1)S(1)} %get-tuple-element.50.refs_10_), channel_id=1, source_target_pairs={{0,2},{1,3},{2,0},{3,1},{4,6},{5,7},{6,4},{7,5},{8,10},{9,11},{10,... | collective-permute-start | bytes 1179656 | tf_op jit(solution)/shard_map/ppermute | solution.py:23
  44.8 6.1 %copy-start.1 = (bf16[1,1,768,2048]{3,2,1,0:T(8,128)(2,1)S(1)}, bf16[1,1,768,2048]{3,2,1,0:T(8,128)(2,1)}, u32[]{:S(2)}) copy-start(bf16[1,1,768,2048]{3,2,1,0:T(8,128)(2,1)} %param.19) | copy-start | bytes 9437188
  54.8 11.5 %collective-permute-start.12 = (bf16[192,1024]{1,0:T(8,128)(2,1)S(1)}, bf16[192,1024]{1,0:T(8,128)(2,1)S(1)}, u32[]{:S(2)}, u32[]{:S(2)}) collective-permute-start(bf16[192,1024]{1,0:T(8,128)(2,1)S(1)} %get-tuple-element.55), channel_id=1, source_target_pairs={{0,2},{1,3},{2,0},{3,1},{4,6},{5,7},{6,4},{7,5},{8,10},{9,11},{10,... | collective-permute-start | bytes 1179656 | tf_op jit(solution)/shard_map/ppermute | solution.py:23
  56.2 12.4 %collective-permute-start.13 = (bf16[192,1024]{1,0:T(8,128)(2,1)S(1)}, bf16[192,1024]{1,0:T(8,128)(2,1)S(1)}, u32[]{:S(2)}, u32[]{:S(2)}) collective-permute-start(bf16[192,1024]{1,0:T(8,128)(2,1)S(1)} %get-tuple-element.56), channel_id=1, source_target_pairs={{0,1},{1,0},{2,3},{3,2},{4,5},{5,4},{6,7},{7,6},{8,9},{9,8},{10,11... | collective-permute-start | bytes 1179656 | tf_op jit(solution)/shard_map/ppermute | solution.py:23
  64.0 12.1 %collective-permute-start.19 = (bf16[192,1024]{1,0:T(8,128)(2,1)S(1)}, bf16[192,1024]{1,0:T(8,128)(2,1)S(1)}, u32[]{:S(2)}, u32[]{:S(2)}) collective-permute-start(bf16[192,1024]{1,0:T(8,128)(2,1)S(1)} %get-tuple-element.66), channel_id=1, source_target_pairs={{0,2},{1,3},{2,0},{3,1},{4,6},{5,7},{6,4},{7,5},{8,10},{9,11},{10,... | collective-permute-start | bytes 1179656 | tf_op jit(solution)/shard_map/ppermute | solution.py:23
  65.6 12.1 %collective-permute-start.18 = (bf16[192,1024]{1,0:T(8,128)(2,1)S(1)}, bf16[192,1024]{1,0:T(8,128)(2,1)S(1)}, u32[]{:S(2)}, u32[]{:S(2)}) collective-permute-start(bf16[192,1024]{1,0:T(8,128)(2,1)S(1)} %get-tuple-element.64), channel_id=1, source_target_pairs={{0,1},{1,0},{2,3},{3,2},{4,5},{5,4},{6,7},{7,6},{8,9},{9,8},{10,11... | collective-permute-start | bytes 1179656 | tf_op jit(solution)/shard_map/ppermute | solution.py:23
  67.1 16.3 %collective-permute-start.16 = (bf16[128,1024]{1,0:T(8,128)(2,1)S(1)}, bf16[128,1024]{1,0:T(8,128)(2,1)S(1)}, u32[]{:S(2)}, u32[]{:S(2)}) collective-permute-start(bf16[128,1024]{1,0:T(8,128)(2,1)S(1)} %shard_map.125.refs_3_), channel_id=1, source_target_pairs={{0,1},{1,0},{2,3},{3,2},{4,5},{5,4},{6,7},{7,6},{8,9},{9,8},{10,11... | collective-permute-start | bytes 786440 | tf_op jit(solution)/shard_map/ppermute | solution.py:23
  69.4 14.0 %collective-permute-start.17 = (bf16[128,1024]{1,0:T(8,128)(2,1)S(1)}, bf16[128,1024]{1,0:T(8,128)(2,1)S(1)}, u32[]{:S(2)}, u32[]{:S(2)}) collective-permute-start(bf16[128,1024]{1,0:T(8,128)(2,1)S(1)} %shard_map.126.refs_3_), channel_id=1, source_target_pairs={{0,2},{1,3},{2,0},{3,1},{4,6},{5,7},{6,4},{7,5},{8,10},{9,11},{10,... | collective-permute-start | bytes 786440 | tf_op jit(solution)/shard_map/ppermute | solution.py:23
  78.2 7.0 %collective-permute-start.21 = (bf16[128,1024]{1,0:T(8,128)(2,1)S(1)}, bf16[128,1024]{1,0:T(8,128)(2,1)S(1)}, u32[]{:S(2)}, u32[]{:S(2)}) collective-permute-start(bf16[128,1024]{1,0:T(8,128)(2,1)S(1)} %shard_map.128.refs_8_), channel_id=1, source_target_pairs={{0,2},{1,3},{2,0},{3,1},{4,6},{5,7},{6,4},{7,5},{8,10},{9,11},{10,... | collective-permute-start | bytes 786440 | tf_op jit(solution)/shard_map/ppermute | solution.py:23
  80.2 6.4 %collective-permute-start.20 = (bf16[128,1024]{1,0:T(8,128)(2,1)S(1)}, bf16[128,1024]{1,0:T(8,128)(2,1)S(1)}, u32[]{:S(2)}, u32[]{:S(2)}) collective-permute-start(bf16[128,1024]{1,0:T(8,128)(2,1)S(1)} %shard_map.127.refs_3_), channel_id=1, source_target_pairs={{0,1},{1,0},{2,3},{3,2},{4,5},{5,4},{6,7},{7,6},{8,9},{9,8},{10,11... | collective-permute-start | bytes 786440 | tf_op jit(solution)/shard_map/ppermute | solution.py:23
  83.4 3.2 %copy-start.2 = (bf16[1,128,2048]{2,1,0:T(8,128)(2,1)S(1)}, bf16[1,128,2048]{2,1,0:T(8,128)(2,1)}, u32[]{:S(2)}) copy-start(bf16[1,128,2048]{2,1,0:T(8,128)(2,1)} %param.12) | copy-start | bytes 1572868

commit v8 on v5

--- a/solution.py
+++ b/solution.py
@@ -413,7 +413,8 @@
     br = (b_routes[...] ^ me).astype(jnp.float32)
     fg = f_gates[...]
     bg = b_gates[...]
-    table_ref[...] = jnp.concatenate([fr, fg, br, bg], axis=0)
+    table = jnp.concatenate([fr, fg, br, bg], axis=0)
+    table_ref[...] = table
     packed = [fr.astype(jnp.bfloat16), br.astype(jnp.bfloat16), *three_parts(fg), *three_parts(bg)]
     packed = jnp.concatenate([part.astype(jnp.float32) for part in packed], axis=0)
     gain_out[...] = gain[...]
@@ -421,14 +422,20 @@
     half = features // 2
     copies[0].wait()
     normed = normed_halves(saved[...].astype(jnp.float32), gain[...])
-    for half_ref, start in ((left_ref, 0), (right_ref, half)):
+    capacity = left_ref.shape[0] - tok_rows - packed.shape[0]
+    near = tok_rows + packed.shape[0]
+    for half_ref, start, expert in ((left_ref, 0, 1), (right_ref, half, 2)):
         half_ref[:tok_rows, :] = normed[:, start : start + half]
-        half_ref[tok_rows:, :] = jnp.zeros((half_ref.shape[0] - tok_rows, half), jnp.bfloat16)
-        half_ref[tok_rows:, :tok_rows] = packed.astype(jnp.bfloat16)
+        half_ref[tok_rows:near, :] = jnp.zeros((near - tok_rows, half), jnp.bfloat16)
+        half_ref[tok_rows:near, :tok_rows] = packed.astype(jnp.bfloat16)
+        other = half - start
+        half_ref[near:, :] = to_slots(
+            pick(table, expert, capacity, "b", top_count), normed[:, other : other + half]
+        )
 
 
 def unpacked(block, tok_rows, top_count):
-    rows = block[tok_rows:, :tok_rows].astype(jnp.float32)
+    rows = block[tok_rows : tok_rows + 8 * top_count, :tok_rows].astype(jnp.float32)
     k = top_count
     fr, br = rows[0:k], rows[k : 2 * k]
     fg = (rows[2 * k : 3 * k] + rows[3 * k : 4 * k]) + rows[4 * k : 5 * k]
@@ -468,8 +475,15 @@
     )
 
 
+def far_kernel(kind, top_count, x_tab, y_tab, from_x, from_y, to_y, to_x):
+    capacity = to_y.shape[0]
+    tok_rows = x_tab.shape[1]
+    to_y[...] = to_slots(pick(x_tab[...], 3, capacity, kind, top_count), from_x[:tok_rows, :])
+    to_x[...] = to_slots(pick(y_tab[...], 3, capacity, kind, top_count), from_y[:tok_rows, :])
+
+
 def assemble(kind, top_count, own, x_tab, y_tab, left, right, from_x, from_y, got_y, got_x, rows):
-    capacity = got_y.shape[0] // 2
+    capacity = rows.shape[0] // 4
     half = got_y.shape[1]
     tok_rows = own.shape[1]
     mine = pick(own[...], 0, capacity, kind, top_count)
@@ -478,13 +492,17 @@
     rows[capacity : 2 * capacity, :half] = to_slots(
         pick(x_tab[...], 1, capacity, kind, top_count), from_x[:tok_rows, :]
     )
-    rows[capacity : 2 * capacity, half:] = got_x[:capacity, :]
-    rows[2 * capacity : 3 * capacity, :half] = got_y[:capacity, :]
     rows[2 * capacity : 3 * capacity, half:] = to_slots(
         pick(y_tab[...], 2, capacity, kind, top_count), from_y[:tok_rows, :]
     )
-    rows[3 * capacity :, :half] = got_y[capacity:, :]
-    rows[3 * capacity :, half:] = got_x[capacity:, :]
+    if got_y.shape[0] == capacity:
+        near_x, near_y = from_x[-capacity:, :], from_y[-capacity:, :]
+    else:
+        near_x, near_y = got_x[:capacity, :], got_y[:capacity, :]
+    rows[capacity : 2 * capacity, half:] = near_x
+    rows[2 * capacity : 3 * capacity, :half] = near_y
+    rows[3 * capacity :, :half] = got_y[-capacity:, :]
+    rows[3 * capacity :, half:] = got_x[-capacity:, :]
 
 
 def hand_out(out, at, capacity, to_left, keep, near, onward):
@@ -611,9 +629,10 @@
 
 
 def hop_fwd_end_kernel(top_count, layer_ref, *refs):
-    out_ref = refs[-1]
+    out_ref, order_ref = refs[-2:]
+    order_ref[...] = jnp.zeros_like(order_ref)
     half = layer_ref.shape[1] // 2
-    left, right = summed("fg", top_count, *refs[:-1])
+    left, right = summed("fg", top_count, *refs[:-2])
     out_ref[:, :half] = (layer_ref[:, :half].astype(jnp.float32) + left).astype(jnp.bfloat16)
     out_ref[:, half:] = (layer_ref[:, half:].astype(jnp.float32) + right).astype(jnp.bfloat16)
 
@@ -675,7 +694,7 @@
     hidden_shape = shaped(slot_total, hidden_units)
     both_shape = shaped(slot_total, 2 * hidden_units)
     table_shape = shaped(table_rows, tok_rows, jnp.float32)
-    first_rows = tok_rows + 8 * top_count
+    first_rows = tok_rows + 8 * top_count + capacity
 
     b_left, b_right, own, gain_here = pl.pallas_call(
         functools.partial(first_kernel, top_count),
@@ -733,15 +752,37 @@
         )
         return swapped(to_y, "expert", 2), swapped(to_x, "expert", 1), to_y
 
-    b_got_y, b_got_x, b_to_y = onward("b", (b_left, b_right), (b_from_x, b_from_y), ())
     f_left, f_right = local_call(
-        normed_kernel_halves, halves_out, (layer_in, gain_here), one_hop, moved, after=(b_to_y,)
+        normed_kernel_halves, halves_out, (layer_in, gain_here), one_hop, moved, after=(x_tab,)
     )
     f_from_x, f_from_y = crossed(f_left, f_right)
     g_left, g_right = local_call(split_kernel, halves_out, (grad_in,), 1024, moved, after=(f_left,))
     g_from_x, g_from_y = crossed(g_left, g_right)
+    b_to_y, b_to_x = local_call(
+        functools.partial(far_kernel, "b", top_count),
+        [shaped(capacity, half)] * 2,
+        (x_tab, y_tab, b_from_x, b_from_y),
+        one_hop,
+        moved,
+        after=(g_left,),
+    )
+    b_got_y, b_got_x = swapped(b_to_y, "expert", 2), swapped(b_to_x, "expert", 1)
     f_got_y, f_got_x, f_to_y = onward("f", (f_left, f_right), (f_from_x, f_from_y), (g_left,))
     g_got_y, g_got_x, g_to_y = onward("bg", (g_left, g_right), (g_from_x, g_from_y), (f_to_y,))
+    f_keep_l, f_near_l, f_on_l, hidden = local_call(
+        functools.partial(hop_fwd_kernel, top_count),
+        half_out + [hidden_shape],
+        (*tabs, f_left, f_right, f_from_x, f_from_y, f_got_y, f_got_x, weight_in, weight_out),
+        5 * expert_flops // 2,
+        expert_moved,
+        scratch=(rows_scratch,),
+        after=(g_to_y,),
+    )
+    f_ret_y = swapped(f_on_l, "expert", 2)
+    f_keep_r, f_near_r, f_on_r = local_call(
+        fwd_right_kernel, half_out, (hidden, weight_out), 1024, 1024
+    )
+    f_ret_x = swapped(f_on_r, "expert", 1)
     gate_pre, up_pre = local_call(
         functools.partial(hop_again_kernel, top_count),
         [shaped(slot_total, hidden_units, jnp.float32)] * 2,
@@ -749,22 +790,8 @@
         2 * expert_flops,
         expert_moved,
         scratch=(rows_scratch,),
-        after=(g_to_y,),
-    )
-    f_keep_l, f_near_l, f_on_l, hidden = local_call(
-        functools.partial(hop_fwd_kernel, top_count),
-        half_out + [hidden_shape],
-        (*tabs, f_left, f_right, f_from_x, f_from_y, f_got_y, f_got_x, weight_in, weight_out),
-        5 * expert_flops // 2,
-        expert_moved,
-        scratch=(rows_scratch,),
-        after=(gate_pre,),
-    )
-    f_ret_y = swapped(f_on_l, "expert", 2)
-    f_keep_r, f_near_r, f_on_r = local_call(
-        fwd_right_kernel, half_out, (hidden, weight_out), 1024, 1024
-    )
-    f_ret_x = swapped(f_on_r, "expert", 1)
+        after=(f_keep_r,),
+    )
     b_keep_l, b_near_l, b_on_l, both = local_call(
         functools.partial(hop_bwd_kernel, top_count),
         half_out + [both_shape],
@@ -809,9 +836,9 @@
     b_sum_y, last = summed_call("b", 2, y_tab, b_near_r, b_ret_x, (last,))
     f_keep = (f_keep_l, f_keep_r)
     b_keep = (b_keep_l, b_keep_r)
-    fwd_block = local_call(
+    fwd_block, order = local_call(
         functools.partial(hop_fwd_end_kernel, top_count),
-        shaped(tok_rows, features),
+        [shaped(tok_rows, features), shaped(8, 128, jnp.float32)],
         (layer_in, own, *f_keep, f_ret_y, f_ret_x, f_sum_x, f_sum_y),
         one_hop,
         moved,
@@ -823,6 +850,7 @@
         (grad_in, saved, gain_here, own, *b_keep, b_ret_y, b_ret_x, b_sum_x, b_sum_y),
         one_hop,
         moved,
+        after=(order,),
     )
     return (fwd_block[None], bwd_block[None])
 

time: 86.2 us -> 92.5 us (1.073)
  waiting for transfers between devices: 32.3 us -> 38.9 us
  starting transfers between devices: 28.7 us -> 26.5 us
  local copies, waits for them, and re-layouts: 0.01 us -> 1.9 us
    ppermute x20, waiting for transfers between devices: 32.3 us -> 38.9 us  [swapped(): return lax.ppermute(value, axis, pairs)]
    unnamed x6 -> x8, local copies, waits for them, and re-layouts: 0.01 us -> 1.9 us
    ppermute x20, starting transfers between devices: 24.1 us -> 23 us  [swapped(): return lax.ppermute(value, axis, pairs)]
    ppermute x2, starting transfers between devices: 4.61 us -> 3.46 us  [passed_along(): return lax.ppermute(value, axis, pairs)]
  transfers between devices with their start and end apart: 22 -> 22, of which waited for: 13 -> 10; matrix products, arithmetic and copies ran while one was open for 0% -> 0% of each run, Pallas kernels for 26% -> 24%
where the time goes in v8:
time: 92.5 us; the launch traced here: 92.3 us
  waiting for transfers between devices  38.9 us (42%)
  starting transfers between devices  26.5 us (29%)
  Pallas kernels  24.3 us (26%)
  local copies, waits for them, and re-layouts  1.9 us (2%)
    ppermute x20, waiting for transfers between devices, swapped(): return lax.ppermute(value, axis, pairs)  38.9 us
    ppermute x20, starting transfers between devices, swapped(): return lax.ppermute(value, axis, pairs)  23 us
    pallas_call x17, Pallas kernels, local_call(): pl.pallas_call(body if after else kernel, out_shape=out_shapes, in_specs=...  22.6 us
    ppermute x2, starting transfers between devices, passed_along(): return lax.ppermute(value, axis, pairs)  3.46 us
    unnamed x8, local copies, waits for them, and re-layouts  1.9 us
  transfers between devices with their start and end apart: 22, of which 10 were waited for; matrix products, arithmetic and copies ran while one was open for 0% of the time, Pallas kernels for 24%

profile of v8, /device:TPU:0, one launch (start us, length us, event | category | flops | bytes accessed | tf_op | source)
XLA Modules:
  0.0 92.3 jit_solution(12315966448360786637)
XLA Ops:
  0.6 0.5 collective-permute-start
  1.1 1.7 %shard_map.113 = (bf16[240,1024]{1,0:T(8,128)(2,1)S(1)}, bf16[240,1024]{1,0:T(8,128)(2,1)S(1)}, f32[8,128]{1,0:T(8,128)S(1)}, f32[1,2048]{1,0:T(1,128)S(1)}) custom-call(s32[1]{0:T(128)} %bitcast.1.me_ref, bf16[128,2048]{1,0:T(8,128)(2,1)} %bitcast.27, f32[1,2048]{1,0:T(1,128)} %refs_1_.1, s32[2,128]{1,0:T(2,128)} %bitcast.30, f32[2,128]{1,0:T(2,128)} %bitcast.31, ...), custom_call_target="tpu_custom_call" | custom-call | flops 1024 | bytes 1024 | tf_op jit(solution)/shard_map/pallas_call | solution.py:699
  2.8 2.6 %collective-permute-start.1 = (bf16[240,1024]{1,0:T(8,128)(2,1)S(1)}, bf16[240,1024]{1,0:T(8,128)(2,1)S(1)}, u32[]{:S(2)}, u32[]{:S(2)}) collective-permute-start(bf16[240,1024]{1,0:T(8,128)(2,1)S(1)} %get-tuple-element.37.refs_3_), channel_id=1, source_target_pairs={{0,1},{1,0},{2,3},{3,2},{4,5},{5,4},{6,7},{7,6},{8,9},{9,8},{10,11... | collective-permute-start | bytes 1474568 | tf_op jit(solution)/shard_map/ppermute | solution.py:23
  5.4 1.5 %collective-permute-start.2 = (bf16[240,1024]{1,0:T(8,128)(2,1)S(1)}, bf16[240,1024]{1,0:T(8,128)(2,1)S(1)}, u32[]{:S(2)}, u32[]{:S(2)}) collective-permute-start(bf16[240,1024]{1,0:T(8,128)(2,1)S(1)} %get-tuple-element.38.refs_4_), channel_id=1, source_target_pairs={{0,2},{1,3},{2,0},{3,1},{4,6},{5,7},{6,4},{7,5},{8,10},{9,11},{10,... | collective-permute-start | bytes 1474568 | tf_op jit(solution)/shard_map/ppermute | solution.py:23
  6.9 3.0 %collective-permute-start.5 = (bf16[128,2048]{1,0:T(8,128)(2,1)}, bf16[128,2048]{1,0:T(8,128)(2,1)S(1)}, u32[]{:S(2)}, u32[]{:S(2)}) collective-permute-start(bf16[128,2048]{1,0:T(8,128)(2,1)} %bitcast.35), channel_id=1, source_target_pairs={{0,28},{4,0},{8,4},{12,8},{16,12},{20,16},{24,20},{28,24},{1,29},{... | collective-permute-start | bytes 1572872 | tf_op jit(solution)/shard_map/ppermute | solution.py:17
  9.9 6.5 %collective-permute-done.1.from_x.refs_2_.refs_5_ = bf16[240,1024]{1,0:T(8,128)(2,1)S(1)} collective-permute-done((bf16[240,1024]{1,0:T(8,128)(2,1)S(1)}, bf16[240,1024]{1,0:T(8,128)(2,1)S(1)}, u32[]{:S(2)}, u32[]{:S(2)}) %collective-permute-start.1) | collective-permute-done | bytes 491552 | tf_op jit(solution)/shard_map/ppermute | solution.py:23
  16.4 2.8 %collective-permute-done.2.from_y.refs_3_.refs_6_ = bf16[240,1024]{1,0:T(8,128)(2,1)S(1)} collective-permute-done((bf16[240,1024]{1,0:T(8,128)(2,1)S(1)}, bf16[240,1024]{1,0:T(8,128)(2,1)S(1)}, u32[]{:S(2)}, u32[]{:S(2)}) %collective-permute-start.2) | collective-permute-done | bytes 491552 | tf_op jit(solution)/shard_map/ppermute | solution.py:23
  19.2 0.0 collective-permute-done.refs_0_
  19.2 0.2 shard_map.115
  19.4 1.6 %collective-permute-start.4 = (bf16[128,1024]{1,0:T(8,128)(2,1)S(1)}, bf16[128,1024]{1,0:T(8,128)(2,1)S(1)}, u32[]{:S(2)}, u32[]{:S(2)}) collective-permute-start(bf16[128,1024]{1,0:T(8,128)(2,1)S(1)} %get-tuple-element.43.refs_4_), channel_id=1, source_target_pairs={{0,2},{1,3},{2,0},{3,1},{4,6},{5,7},{6,4},{7,5},{8,10},{9,11},{10,... | collective-permute-start | bytes 786440 | tf_op jit(solution)/shard_map/ppermute | solution.py:23
  21.0 0.5 collective-permute-start.3
  21.5 0.0 collective-permute-done.5.refs_0_
  21.6 6.3 %collective-permute-done.4.refs_6_ = bf16[128,1024]{1,0:T(8,128)(2,1)S(1)} collective-permute-done((bf16[128,1024]{1,0:T(8,128)(2,1)S(1)}, bf16[128,1024]{1,0:T(8,128)(2,1)S(1)}, u32[]{:S(2)}, u32[]{:S(2)}) %collective-permute-start.4) | collective-permute-done | bytes 262176 | tf_op jit(solution)/shard_map/ppermute | solution.py:23
  27.8 1.2 %collective-permute-done.3.refs_5_ = bf16[128,1024]{1,0:T(8,128)(2,1)S(1)} collective-permute-done((bf16[128,1024]{1,0:T(8,128)(2,1)S(1)}, bf16[128,1024]{1,0:T(8,128)(2,1)S(1)}, u32[]{:S(2)}, u32[]{:S(2)}) %collective-permute-start.3) | collective-permute-done | bytes 262176 | tf_op jit(solution)/shard_map/ppermute | solution.py:23
  29.1 0.9 shard_map.117
  30.0 0.6 collective-permute-start.7
  30.6 0.4 collective-permute-start.6
  30.9 1.7 %collective-permute-start.9 = (bf16[128,1024]{1,0:T(8,128)(2,1)S(1)}, bf16[128,1024]{1,0:T(8,128)(2,1)S(1)}, u32[]{:S(2)}, u32[]{:S(2)}) collective-permute-start(bf16[128,1024]{1,0:T(8,128)(2,1)S(1)} %get-tuple-element.47.refs_4_), channel_id=1, source_target_pairs={{0,2},{1,3},{2,0},{3,1},{4,6},{5,7},{6,4},{7,5},{8,10},{9,11},{10,... | collective-permute-start | bytes 786440 | tf_op jit(solution)/shard_map/ppermute | solution.py:23
  32.6 1.5 %collective-permute-start.8 = (bf16[128,1024]{1,0:T(8,128)(2,1)S(1)}, bf16[128,1024]{1,0:T(8,128)(2,1)S(1)}, u32[]{:S(2)}, u32[]{:S(2)}) collective-permute-start(bf16[128,1024]{1,0:T(8,128)(2,1)S(1)} %get-tuple-element.44.refs_7_.refs_3_.refs_4_), channel_id=1, source_target_pairs={{0,1},{1,0},{2,3},{3,2},{4,5},{5,4},{6,7},{7,6},{8,9},{9,8},{10,11... | collective-permute-start | bytes 786440 | tf_op jit(solution)/shard_map/ppermute | solution.py:23
  34.1 0.5 shard_map.121
  34.6 0.6 collective-permute-start.14
  35.2 12.9 %collective-permute-done.9.refs_6_ = bf16[128,1024]{1,0:T(8,128)(2,1)S(1)} collective-permute-done((bf16[128,1024]{1,0:T(8,128)(2,1)S(1)}, bf16[128,1024]{1,0:T(8,128)(2,1)S(1)}, u32[]{:S(2)}, u32[]{:S(2)}) %collective-permute-start.9) | collective-permute-done | bytes 262176 | tf_op jit(solution)/shard_map/ppermute | solution.py:23
  48.0 1.5 %collective-permute-start.15 = (bf16[96,1024]{1,0:T(8,128)(2,1)S(1)}, bf16[96,1024]{1,0:T(8,128)(2,1)S(1)}, u32[]{:S(2)}, u32[]{:S(2)}) collective-permute-start(bf16[96,1024]{1,0:T(8,128)(2,1)S(1)} %get-tuple-element.57), channel_id=1, source_target_pairs={{0,1},{1,0},{2,3},{3,2},{4,5},{5,4},{6,7},{7,6},{8,9},{9,8},{10,11... | collective-permute-start | bytes 589832 | tf_op jit(solution)/shard_map/ppermute | solution.py:23
  49.5 0.0 collective-permute-done.8.refs_5_
  49.5 1.1 %shard_map.118 = (bf16[192,1024]{1,0:T(8,128)(2,1)S(1)}, bf16[192,1024]{1,0:T(8,128)(2,1)S(1)}) custom-call(f32[8,128]{1,0:T(8,128)S(1)} %get-tuple-element.36.refs_0_.refs_1_.refs_3_, f32[8,128]{1,0:T(8,128)S(1)} %get-tuple-element.39.refs_2_.refs_1_.refs_0_, f32[8,128]{1,0:T(8,128)S(1)} %get-tuple-element.40.refs_2_.refs_1_.refs_0_, ...), custom_call_target="tpu_custom_call" | custom-call | flops 1024 | bytes 1024 | tf_op jit(solution)/shard_map/pallas_call | solution.py:242
  50.7 0.6 collective-permute-start.13
  51.3 0.0 collective-permute-done.7.refs_8_
  51.3 0.6 collective-permute-start.12
  51.8 0.0 collective-permute-done.6.refs_7_
  51.8 0.0 copy-done
  51.8 1.9 %copy-done.1 = bf16[1,1,768,2048]{3,2,1,0:T(8,128)(2,1)S(1)} copy-done((bf16[1,1,768,2048]{3,2,1,0:T(8,128)(2,1)S(1)}, bf16[1,1,768,2048]{3,2,1,0:T(8,128)(2,1)}, u32[]{:S(2)}) %copy-start.1) | copy-done | bytes 3145752
  53.7 3.9 %shard_map.119 = (bf16[96,1024]{1,0:T(8,128)(2,1)S(1)}, bf16[96,1024]{1,0:T(8,128)(2,1)S(1)}, bf16[192,1024]{1,0:T(8,128)(2,1)S(1)}, bf16[384,768]{1,0:T(8,128)(2,1)S(1)}) custom-call(f32[8,128]{1,0:T(8,128)S(1)} %get-tuple-element.36.refs_0_.refs_1_.refs_3_, f32[8,128]{1,0:T(8,128)S(1)} %get-tuple-element.39.refs_2_.refs_1_.refs_0_, ...), custom_call_target="tpu_custom_call" | custom-call | flops 3019898880 | bytes 14155776 | tf_op jit(solution)/shard_map/pallas_call | solution.py:242
  57.6 1.5 %collective-permute-start.10 = (bf16[192,1024]{1,0:T(8,128)(2,1)S(1)}, bf16[192,1024]{1,0:T(8,128)(2,1)S(1)}, u32[]{:S(2)}, u32[]{:S(2)}) collective-permute-start(bf16[192,1024]{1,0:T(8,128)(2,1)S(1)} %get-tuple-element.52), channel_id=1, source_target_pairs={{0,2},{1,3},{2,0},{3,1},{4,6},{5,7},{6,4},{7,5},{8,10},{9,11},{10,... | collective-permute-start | bytes 1179656 | tf_op jit(solution)/shard_map/ppermute | solution.py:23
  59.1 0.0 copy-done.2
  59.1 0.8 shard_map.120
  59.9 0.0 collective-permute-done.14.refs_7_
  59.9 1.6 %collective-permute-start.11 = (bf16[192,1024]{1,0:T(8,128)(2,1)S(1)}, bf16[192,1024]{1,0:T(8,128)(2,1)S(1)}, u32[]{:S(2)}, u32[]{:S(2)}) collective-permute-start(bf16[192,1024]{1,0:T(8,128)(2,1)S(1)} %get-tuple-element.53), channel_id=1, source_target_pairs={{0,1},{1,0},{2,3},{3,2},{4,5},{5,4},{6,7},{7,6},{8,9},{9,8},{10,11... | collective-permute-start | bytes 1179656 | tf_op jit(solution)/shard_map/ppermute | solution.py:23
  61.5 0.0 collective-permute-done.15.refs_8_
  61.5 3.2 %shard_map.122 = (f32[384,768]{1,0:T(8,128)S(1)}, f32[384,768]{1,0:T(8,128)S(1)}) custom-call(f32[8,128]{1,0:T(8,128)S(1)} %get-tuple-element.36.refs_0_.refs_1_.refs_3_, f32[8,128]{1,0:T(8,128)S(1)} %get-tuple-element.39.refs_2_.refs_1_.refs_0_, f32[8,128]{1,0:T(8,128)S(1)} %get-tuple-element.40.refs_2_.refs_1_.refs_0_, ...), custom_call_target="tpu_custom_call" | custom-call | flops 2415919104 | bytes 14155776 | tf_op jit(solution)/shard_map/pallas_call | solution.py:242
  64.7 0.0 collective-permute-done.13.refs_8_
  64.7 0.0 collective-permute-done.12.refs_7_
  64.8 4.7 %shard_map.123 = (bf16[96,1024]{1,0:T(8,128)(2,1)S(1)}, bf16[96,1024]{1,0:T(8,128)(2,1)S(1)}, bf16[192,1024]{1,0:T(8,128)(2,1)S(1)}, bf16[384,1536]{1,0:T(8,128)(2,1)S(1)}) custom-call(f32[8,128]{1,0:T(8,128)S(1)} %get-tuple-element.36.refs_0_.refs_1_.refs_3_, f32[8,128]{1,0:T(8,128)S(1)} %get-tuple-element.39.refs_2_.refs_1_.refs_0_, ...), custom_call_target="tpu_custom_call" | custom-call | flops 2415919104 | bytes 14155776 | tf_op jit(solution)/shard_map/pallas_call | solution.py:242
  69.5 0.7 collective-permute-start.19
  70.1 1.4 %shard_map.124 = (bf16[96,1024]{1,0:T(8,128)(2,1)S(1)}, bf16[96,1024]{1,0:T(8,128)(2,1)S(1)}, bf16[192,1024]{1,0:T(8,128)(2,1)S(1)}) custom-call(bf16[384,1536]{1,0:T(8,128)(2,1)S(1)} %get-tuple-element.60.both_ref, bf16[2048,1536]{1,0:T(8,128)(2,1)S(1)} %bitcast.23), custom_call_target="tpu_custom_call" | custom-call | flops 1024 | bytes 1024 | tf_op jit(solution)/shard_map/pallas_call | solution.py:242
  71.5 0.5 collective-permute-start.18
  72.1 0.0 collective-permute-done.10.refs_2_.refs_4_
  72.1 0.8 shard_map.125.refs_3_
  72.9 1.6 %collective-permute-start.16 = (bf16[128,1024]{1,0:T(8,128)(2,1)S(1)}, bf16[128,1024]{1,0:T(8,128)(2,1)S(1)}, u32[]{:S(2)}, u32[]{:S(2)}) collective-permute-start(bf16[128,1024]{1,0:T(8,128)(2,1)S(1)} %shard_map.125.refs_3_), channel_id=1, source_target_pairs={{0,1},{1,0},{2,3},{3,2},{4,5},{5,4},{6,7},{7,6},{8,9},{9,8},{10,11... | collective-permute-start | bytes 786440 | tf_op jit(solution)/shard_map/ppermute | solution.py:23
  74.5 0.0 collective-permute-done.11.refs_2_.refs_5_
  74.5 0.8 shard_map.126.refs_3_
  75.3 1.5 %collective-permute-start.17 = (bf16[128,1024]{1,0:T(8,128)(2,1)S(1)}, bf16[128,1024]{1,0:T(8,128)(2,1)S(1)}, u32[]{:S(2)}, u32[]{:S(2)}) collective-permute-start(bf16[128,1024]{1,0:T(8,128)(2,1)S(1)} %shard_map.126.refs_3_), channel_id=1, source_target_pairs={{0,2},{1,3},{2,0},{3,1},{4,6},{5,7},{6,4},{7,5},{8,10},{9,11},{10,... | collective-permute-start | bytes 786440 | tf_op jit(solution)/shard_map/ppermute | solution.py:23
  76.8 4.7 %collective-permute-done.19.refs_2_.refs_6_ = bf16[192,1024]{1,0:T(8,128)(2,1)S(1)} collective-permute-done((bf16[192,1024]{1,0:T(8,128)(2,1)S(1)}, bf16[192,1024]{1,0:T(8,128)(2,1)S(1)}, u32[]{:S(2)}, u32[]{:S(2)}) %collective-permute-start.19) | collective-permute-done | bytes 393248 | tf_op jit(solution)/shard_map/ppermute | solution.py:23
  81.5 0.5 shard_map.127.refs_3_
  82.0 0.2 collective-permute-done.18.refs_2_.refs_7_
  82.2 0.5 shard_map.128.refs_8_
  82.7 1.5 %collective-permute-start.21 = (bf16[128,1024]{1,0:T(8,128)(2,1)S(1)}, bf16[128,1024]{1,0:T(8,128)(2,1)S(1)}, u32[]{:S(2)}, u32[]{:S(2)}) collective-permute-start(bf16[128,1024]{1,0:T(8,128)(2,1)S(1)} %shard_map.128.refs_8_), channel_id=1, source_target_pairs={{0,2},{1,3},{2,0},{3,1},{4,6},{5,7},{6,4},{7,5},{8,10},{9,11},{10,... | collective-permute-start | bytes 786440 | tf_op jit(solution)/shard_map/ppermute | solution.py:23
  84.2 0.5 collective-permute-start.20
  84.7 0.4 collective-permute-done.16.refs_6_
  85.2 0.0 collective-permute-done.17.refs_7_
  85.2 1.7 %shard_map.129 = (bf16[128,2048]{1,0:T(8,128)(2,1)}, f32[8,128]{1,0:T(8,128)S(1)}) custom-call(bf16[128,2048]{1,0:T(8,128)(2,1)S(1)} %collective-permute-done.refs_0_, f32[8,128]{1,0:T(8,128)S(1)} %get-tuple-element.36.refs_0_.refs_1_.refs_3_, bf16[96,1024]{1,0:T(8,128)(2,1)S(1)} %get-tuple-element.49.refs_2_, ...), custom_call_target="tpu_custom_call" | custom-call | flops 1024 | bytes 1024 | tf_op jit(solution)/shard_map/pallas_call | solution.py:242
  86.9 2.2 %collective-permute-done.21.refs_9_ = bf16[128,1024]{1,0:T(8,128)(2,1)S(1)} collective-permute-done((bf16[128,1024]{1,0:T(8,128)(2,1)S(1)}, bf16[128,1024]{1,0:T(8,128)(2,1)S(1)}, u32[]{:S(2)}, u32[]{:S(2)}) %collective-permute-start.21) | collective-permute-done | bytes 262176 | tf_op jit(solution)/shard_map/ppermute | solution.py:23
  89.1 1.5 %collective-permute-done.20.refs_8_ = bf16[128,1024]{1,0:T(8,128)(2,1)S(1)} collective-permute-done((bf16[128,1024]{1,0:T(8,128)(2,1)S(1)}, bf16[128,1024]{1,0:T(8,128)(2,1)S(1)}, u32[]{:S(2)}, u32[]{:S(2)}) %collective-permute-start.20) | collective-permute-done | bytes 262176 | tf_op jit(solution)/shard_map/ppermute | solution.py:23
  90.6 0.0 copy-done.3
  90.6 1.7 %shard_map.130 = bf16[128,2048]{1,0:T(8,128)(2,1)} custom-call(bf16[128,2048]{1,0:T(8,128)(2,1)S(1)} %collective-permute-done.5.refs_0_, bf16[128,2048]{1,0:T(8,128)(2,1)S(1)} %bitcast.28, f32[1,2048]{1,0:T(1,128)S(1)} %get-tuple-element.41.refs_1_.refs_2_, f32[8,128]{1,0:T(8,128)S(1)} %get-tuple-element.36.refs_0_.refs_1_.refs_3_, ...), custom_call_target="tpu_custom_call" | custom-call | flops 1024 | bytes 1024 | tf_op jit(solution)/shard_map/pallas_call | solution.py:242
  (6 shorter events, 0.1 us)
Async XLA Ops:
  0.6 18.5 %collective-permute-start = (bf16[128,2048]{1,0:T(8,128)(2,1)}, bf16[128,2048]{1,0:T(8,128)(2,1)S(1)}, u32[]{:S(2)}, u32[]{:S(2)}) collective-permute-start(bf16[128,2048]{1,0:T(8,128)(2,1)} %bitcast.34), channel_id=1, source_target_pairs={{0,4},{4,8},{8,12},{12,16},{16,20},{20,24},{24,28},{28,0},{1,5},{5... | collective-permute-start | bytes 1572872 | tf_op jit(solution)/shard_map/ppermute | solution.py:17
  2.8 13.5 %collective-permute-start.1 = (bf16[240,1024]{1,0:T(8,128)(2,1)S(1)}, bf16[240,1024]{1,0:T(8,128)(2,1)S(1)}, u32[]{:S(2)}, u32[]{:S(2)}) collective-permute-start(bf16[240,1024]{1,0:T(8,128)(2,1)S(1)} %get-tuple-element.37.refs_3_), channel_id=1, source_target_pairs={{0,1},{1,0},{2,3},{3,2},{4,5},{5,4},{6,7},{7,6},{8,9},{9,8},{10,11... | collective-permute-start | bytes 1474568 | tf_op jit(solution)/shard_map/ppermute | solution.py:23
  5.4 13.8 %collective-permute-start.2 = (bf16[240,1024]{1,0:T(8,128)(2,1)S(1)}, bf16[240,1024]{1,0:T(8,128)(2,1)S(1)}, u32[]{:S(2)}, u32[]{:S(2)}) collective-permute-start(bf16[240,1024]{1,0:T(8,128)(2,1)S(1)} %get-tuple-element.38.refs_4_), channel_id=1, source_target_pairs={{0,2},{1,3},{2,0},{3,1},{4,6},{5,7},{6,4},{7,5},{8,10},{9,11},{10,... | collective-permute-start | bytes 1474568 | tf_op jit(solution)/shard_map/ppermute | solution.py:23
  6.9 14.6 %collective-permute-start.5 = (bf16[128,2048]{1,0:T(8,128)(2,1)}, bf16[128,2048]{1,0:T(8,128)(2,1)S(1)}, u32[]{:S(2)}, u32[]{:S(2)}) collective-permute-start(bf16[128,2048]{1,0:T(8,128)(2,1)} %bitcast.35), channel_id=1, source_target_pairs={{0,28},{4,0},{8,4},{12,8},{16,12},{20,16},{24,20},{28,24},{1,29},{... | collective-permute-start | bytes 1572872 | tf_op jit(solution)/shard_map/ppermute | solution.py:17
  19.2 32.7 %copy-start = (bf16[1,1,2048,1536]{3,2,1,0:T(8,128)(2,1)S(1)}, bf16[1,1,2048,1536]{3,2,1,0:T(8,128)(2,1)}, u32[]{:S(2)}) copy-start(bf16[1,1,2048,1536]{3,2,1,0:T(8,128)(2,1)} %param.18) | copy-start | bytes 18874372
  19.4 8.4 %collective-permute-start.4 = (bf16[128,1024]{1,0:T(8,128)(2,1)S(1)}, bf16[128,1024]{1,0:T(8,128)(2,1)S(1)}, u32[]{:S(2)}, u32[]{:S(2)}) collective-permute-start(bf16[128,1024]{1,0:T(8,128)(2,1)S(1)} %get-tuple-element.43.refs_4_), channel_id=1, source_target_pairs={{0,2},{1,3},{2,0},{3,1},{4,6},{5,7},{6,4},{7,5},{8,10},{9,11},{10,... | collective-permute-start | bytes 786440 | tf_op jit(solution)/shard_map/ppermute | solution.py:23
  21.0 8.1 %collective-permute-start.3 = (bf16[128,1024]{1,0:T(8,128)(2,1)S(1)}, bf16[128,1024]{1,0:T(8,128)(2,1)S(1)}, u32[]{:S(2)}, u32[]{:S(2)}) collective-permute-start(bf16[128,1024]{1,0:T(8,128)(2,1)S(1)} %get-tuple-element.42.refs_1_.refs_3_), channel_id=1, source_target_pairs={{0,1},{1,0},{2,3},{3,2},{4,5},{5,4},{6,7},{7,6},{8,9},{9,8},{10,11... | collective-permute-start | bytes 786440 | tf_op jit(solution)/shard_map/ppermute | solution.py:23
  30.0 21.3 %collective-permute-start.7 = (bf16[192,1024]{1,0:T(8,128)(2,1)S(1)}, bf16[192,1024]{1,0:T(8,128)(2,1)S(1)}, u32[]{:S(2)}, u32[]{:S(2)}) collective-permute-start(bf16[192,1024]{1,0:T(8,128)(2,1)S(1)} %get-tuple-element.46), channel_id=1, source_target_pairs={{0,1},{1,0},{2,3},{3,2},{4,5},{5,4},{6,7},{7,6},{8,9},{9,8},{10,11... | collective-permute-start | bytes 1179656 | tf_op jit(solution)/shard_map/ppermute | solution.py:23
  30.6 21.3 %collective-permute-start.6 = (bf16[192,1024]{1,0:T(8,128)(2,1)S(1)}, bf16[192,1024]{1,0:T(8,128)(2,1)S(1)}, u32[]{:S(2)}, u32[]{:S(2)}) collective-permute-start(bf16[192,1024]{1,0:T(8,128)(2,1)S(1)} %get-tuple-element.45.refs_7_), channel_id=1, source_target_pairs={{0,2},{1,3},{2,0},{3,1},{4,6},{5,7},{6,4},{7,5},{8,10},{9,11},{10,... | collective-permute-start | bytes 1179656 | tf_op jit(solution)/shard_map/ppermute | solution.py:23
  30.9 17.1 %collective-permute-start.9 = (bf16[128,1024]{1,0:T(8,128)(2,1)S(1)}, bf16[128,1024]{1,0:T(8,128)(2,1)S(1)}, u32[]{:S(2)}, u32[]{:S(2)}) collective-permute-start(bf16[128,1024]{1,0:T(8,128)(2,1)S(1)} %get-tuple-element.47.refs_4_), channel_id=1, source_target_pairs={{0,2},{1,3},{2,0},{3,1},{4,6},{5,7},{6,4},{7,5},{8,10},{9,11},{10,... | collective-permute-start | bytes 786440 | tf_op jit(solution)/shard_map/ppermute | solution.py:23
  32.6 17.0 %collective-permute-start.8 = (bf16[128,1024]{1,0:T(8,128)(2,1)S(1)}, bf16[128,1024]{1,0:T(8,128)(2,1)S(1)}, u32[]{:S(2)}, u32[]{:S(2)}) collective-permute-start(bf16[128,1024]{1,0:T(8,128)(2,1)S(1)} %get-tuple-element.44.refs_7_.refs_3_.refs_4_), channel_id=1, source_target_pairs={{0,1},{1,0},{2,3},{3,2},{4,5},{5,4},{6,7},{7,6},{8,9},{9,8},{10,11... | collective-permute-start | bytes 786440 | tf_op jit(solution)/shard_map/ppermute | solution.py:23
  34.6 25.3 %collective-permute-start.14 = (bf16[96,1024]{1,0:T(8,128)(2,1)S(1)}, bf16[96,1024]{1,0:T(8,128)(2,1)S(1)}, u32[]{:S(2)}, u32[]{:S(2)}) collective-permute-start(bf16[96,1024]{1,0:T(8,128)(2,1)S(1)} %get-tuple-element.56), channel_id=1, source_target_pairs={{0,2},{1,3},{2,0},{3,1},{4,6},{5,7},{6,4},{7,5},{8,10},{9,11},{10,... | collective-permute-start | bytes 589832 | tf_op jit(solution)/shard_map/ppermute | solution.py:23
  48.0 13.5 %collective-permute-start.15 = (bf16[96,1024]{1,0:T(8,128)(2,1)S(1)}, bf16[96,1024]{1,0:T(8,128)(2,1)S(1)}, u32[]{:S(2)}, u32[]{:S(2)}) collective-permute-start(bf16[96,1024]{1,0:T(8,128)(2,1)S(1)} %get-tuple-element.57), channel_id=1, source_target_pairs={{0,1},{1,0},{2,3},{3,2},{4,5},{5,4},{6,7},{7,6},{8,9},{9,8},{10,11... | collective-permute-start | bytes 589832 | tf_op jit(solution)/shard_map/ppermute | solution.py:23
  50.7 14.1 %collective-permute-start.13 = (bf16[192,1024]{1,0:T(8,128)(2,1)S(1)}, bf16[192,1024]{1,0:T(8,128)(2,1)S(1)}, u32[]{:S(2)}, u32[]{:S(2)}) collective-permute-start(bf16[192,1024]{1,0:T(8,128)(2,1)S(1)} %get-tuple-element.55), channel_id=1, source_target_pairs={{0,1},{1,0},{2,3},{3,2},{4,5},{5,4},{6,7},{7,6},{8,9},{9,8},{10,11... | collective-permute-start | bytes 1179656 | tf_op jit(solution)/shard_map/ppermute | solution.py:23
  51.3 13.5 %collective-permute-start.12 = (bf16[192,1024]{1,0:T(8,128)(2,1)S(1)}, bf16[192,1024]{1,0:T(8,128)(2,1)S(1)}, u32[]{:S(2)}, u32[]{:S(2)}) collective-permute-start(bf16[192,1024]{1,0:T(8,128)(2,1)S(1)} %get-tuple-element.48.refs_11_), channel_id=1, source_target_pairs={{0,2},{1,3},{2,0},{3,1},{4,6},{5,7},{6,4},{7,5},{8,10},{9,11},{10,... | collective-permute-start | bytes 1179656 | tf_op jit(solution)/shard_map/ppermute | solution.py:23
  51.8 1.9 %copy-start.1 = (bf16[1,1,768,2048]{3,2,1,0:T(8,128)(2,1)S(1)}, bf16[1,1,768,2048]{3,2,1,0:T(8,128)(2,1)}, u32[]{:S(2)}) copy-start(bf16[1,1,768,2048]{3,2,1,0:T(8,128)(2,1)} %param.19) | copy-start | bytes 9437188
  53.7 5.4 %copy-start.2 = (bf16[1,1,768,2048]{3,2,1,0:T(8,128)(2,1)S(1)}, bf16[1,1,768,2048]{3,2,1,0:T(8,128)(2,1)}, u32[]{:S(2)}) copy-start(bf16[1,1,768,2048]{3,2,1,0:T(8,128)(2,1)} %param.19) | copy-start | bytes 9437188
  57.6 14.5 %collective-permute-start.10 = (bf16[192,1024]{1,0:T(8,128)(2,1)S(1)}, bf16[192,1024]{1,0:T(8,128)(2,1)S(1)}, u32[]{:S(2)}, u32[]{:S(2)}) collective-permute-start(bf16[192,1024]{1,0:T(8,128)(2,1)S(1)} %get-tuple-element.52), channel_id=1, source_target_pairs={{0,2},{1,3},{2,0},{3,1},{4,6},{5,7},{6,4},{7,5},{8,10},{9,11},{10,... | collective-permute-start | bytes 1179656 | tf_op jit(solution)/shard_map/ppermute | solution.py:23
  59.9 14.6 %collective-permute-start.11 = (bf16[192,1024]{1,0:T(8,128)(2,1)S(1)}, bf16[192,1024]{1,0:T(8,128)(2,1)S(1)}, u32[]{:S(2)}, u32[]{:S(2)}) collective-permute-start(bf16[192,1024]{1,0:T(8,128)(2,1)S(1)} %get-tuple-element.53), channel_id=1, source_target_pairs={{0,1},{1,0},{2,3},{3,2},{4,5},{5,4},{6,7},{7,6},{8,9},{9,8},{10,11... | collective-permute-start | bytes 1179656 | tf_op jit(solution)/shard_map/ppermute | solution.py:23
  69.5 12.1 %collective-permute-start.19 = (bf16[192,1024]{1,0:T(8,128)(2,1)S(1)}, bf16[192,1024]{1,0:T(8,128)(2,1)S(1)}, u32[]{:S(2)}, u32[]{:S(2)}) collective-permute-start(bf16[192,1024]{1,0:T(8,128)(2,1)S(1)} %get-tuple-element.66), channel_id=1, source_target_pairs={{0,2},{1,3},{2,0},{3,1},{4,6},{5,7},{6,4},{7,5},{8,10},{9,11},{10,... | collective-permute-start | bytes 1179656 | tf_op jit(solution)/shard_map/ppermute | solution.py:23
  71.5 10.7 %collective-permute-start.18 = (bf16[192,1024]{1,0:T(8,128)(2,1)S(1)}, bf16[192,1024]{1,0:T(8,128)(2,1)S(1)}, u32[]{:S(2)}, u32[]{:S(2)}) collective-permute-start(bf16[192,1024]{1,0:T(8,128)(2,1)S(1)} %get-tuple-element.64), channel_id=1, source_target_pairs={{0,1},{1,0},{2,3},{3,2},{4,5},{5,4},{6,7},{7,6},{8,9},{9,8},{10,11... | collective-permute-start | bytes 1179656 | tf_op jit(solution)/shard_map/ppermute | solution.py:23
  72.9 12.3 %collective-permute-start.16 = (bf16[128,1024]{1,0:T(8,128)(2,1)S(1)}, bf16[128,1024]{1,0:T(8,128)(2,1)S(1)}, u32[]{:S(2)}, u32[]{:S(2)}) collective-permute-start(bf16[128,1024]{1,0:T(8,128)(2,1)S(1)} %shard_map.125.refs_3_), channel_id=1, source_target_pairs={{0,1},{1,0},{2,3},{3,2},{4,5},{5,4},{6,7},{7,6},{8,9},{9,8},{10,11... | collective-permute-start | bytes 786440 | tf_op jit(solution)/shard_map/ppermute | solution.py:23
  75.3 9.9 %collective-permute-start.17 = (bf16[128,1024]{1,0:T(8,128)(2,1)S(1)}, bf16[128,1024]{1,0:T(8,128)(2,1)S(1)}, u32[]{:S(2)}, u32[]{:S(2)}) collective-permute-start(bf16[128,1024]{1,0:T(8,128)(2,1)S(1)} %shard_map.126.refs_3_), channel_id=1, source_target_pairs={{0,2},{1,3},{2,0},{3,1},{4,6},{5,7},{6,4},{7,5},{8,10},{9,11},{10,... | collective-permute-start | bytes 786440 | tf_op jit(solution)/shard_map/ppermute | solution.py:23
  82.7 6.4 %collective-permute-start.21 = (bf16[128,1024]{1,0:T(8,128)(2,1)S(1)}, bf16[128,1024]{1,0:T(8,128)(2,1)S(1)}, u32[]{:S(2)}, u32[]{:S(2)}) collective-permute-start(bf16[128,1024]{1,0:T(8,128)(2,1)S(1)} %shard_map.128.refs_8_), channel_id=1, source_target_pairs={{0,2},{1,3},{2,0},{3,1},{4,6},{5,7},{6,4},{7,5},{8,10},{9,11},{10,... | collective-permute-start | bytes 786440 | tf_op jit(solution)/shard_map/ppermute | solution.py:23
  84.2 6.4 %collective-permute-start.20 = (bf16[128,1024]{1,0:T(8,128)(2,1)S(1)}, bf16[128,1024]{1,0:T(8,128)(2,1)S(1)}, u32[]{:S(2)}, u32[]{:S(2)}) collective-permute-start(bf16[128,1024]{1,0:T(8,128)(2,1)S(1)} %shard_map.127.refs_3_), channel_id=1, source_target_pairs={{0,1},{1,0},{2,3},{3,2},{4,5},{5,4},{6,7},{7,6},{8,9},{9,8},{10,11... | collective-permute-start | bytes 786440 | tf_op jit(solution)/shard_map/ppermute | solution.py:23
  85.2 5.4 %copy-start.3 = (bf16[1,128,2048]{2,1,0:T(8,128)(2,1)S(1)}, bf16[1,128,2048]{2,1,0:T(8,128)(2,1)}, u32[]{:S(2)}) copy-start(bf16[1,128,2048]{2,1,0:T(8,128)(2,1)} %param.12) | copy-start | bytes 1572868

commit v9 on v8

--- a/solution.py
+++ b/solution.py
@@ -732,14 +732,6 @@
         ],
     )
     b_from_x, b_from_y = crossed(b_left, b_right)
-    x_tab, y_tab = local_call(
-        functools.partial(tables_kernel, top_count),
-        [table_shape] * 2,
-        (b_from_x, b_from_y),
-        1024,
-        1024,
-    )
-    tabs = (own, x_tab, y_tab)
 
     def onward(kind, sent, got, after):
         to_y, to_x = local_call(
@@ -753,11 +745,20 @@
         return swapped(to_y, "expert", 2), swapped(to_x, "expert", 1), to_y
 
     f_left, f_right = local_call(
-        normed_kernel_halves, halves_out, (layer_in, gain_here), one_hop, moved, after=(x_tab,)
+        normed_kernel_halves, halves_out, (layer_in, gain_here), one_hop, moved, after=(b_left,)
     )
     f_from_x, f_from_y = crossed(f_left, f_right)
     g_left, g_right = local_call(split_kernel, halves_out, (grad_in,), 1024, moved, after=(f_left,))
     g_from_x, g_from_y = crossed(g_left, g_right)
+    x_tab, y_tab = local_call(
+        functools.partial(tables_kernel, top_count),
+        [table_shape] * 2,
+        (b_from_x, b_from_y),
+        1024,
+        1024,
+        after=(g_left,),
+    )
+    tabs = (own, x_tab, y_tab)
     b_to_y, b_to_x = local_call(
         functools.partial(far_kernel, "b", top_count),
         [shaped(capacity, half)] * 2,
@@ -767,8 +768,17 @@
         after=(g_left,),
     )
     b_got_y, b_got_x = swapped(b_to_y, "expert", 2), swapped(b_to_x, "expert", 1)
-    f_got_y, f_got_x, f_to_y = onward("f", (f_left, f_right), (f_from_x, f_from_y), (g_left,))
+    f_got_y, f_got_x, f_to_y = onward("f", (f_left, f_right), (f_from_x, f_from_y), (b_to_y,))
     g_got_y, g_got_x, g_to_y = onward("bg", (g_left, g_right), (g_from_x, g_from_y), (f_to_y,))
+    gate_pre, up_pre = local_call(
+        functools.partial(hop_again_kernel, top_count),
+        [shaped(slot_total, hidden_units, jnp.float32)] * 2,
+        (*tabs, b_left, b_right, b_from_x, b_from_y, b_got_y, b_got_x, weight_in),
+        2 * expert_flops,
+        expert_moved,
+        scratch=(rows_scratch,),
+        after=(g_to_y,),
+    )
     f_keep_l, f_near_l, f_on_l, hidden = local_call(
         functools.partial(hop_fwd_kernel, top_count),
         half_out + [hidden_shape],
@@ -776,22 +786,13 @@
         5 * expert_flops // 2,
         expert_moved,
         scratch=(rows_scratch,),
-        after=(g_to_y,),
+        after=(gate_pre,),
     )
     f_ret_y = swapped(f_on_l, "expert", 2)
     f_keep_r, f_near_r, f_on_r = local_call(
         fwd_right_kernel, half_out, (hidden, weight_out), 1024, 1024
     )
     f_ret_x = swapped(f_on_r, "expert", 1)
-    gate_pre, up_pre = local_call(
-        functools.partial(hop_again_kernel, top_count),
-        [shaped(slot_total, hidden_units, jnp.float32)] * 2,
-        (*tabs, b_left, b_right, b_from_x, b_from_y, b_got_y, b_got_x, weight_in),
-        2 * expert_flops,
-        expert_moved,
-        scratch=(rows_scratch,),
-        after=(f_keep_r,),
-    )
     b_keep_l, b_near_l, b_on_l, both = local_call(
         functools.partial(hop_bwd_kernel, top_count),
         half_out + [both_shape],

time: 92.5 us -> 82.8 us (0.90)
  waiting for transfers between devices: 38.9 us -> 25.7 us
  starting transfers between devices: 26.5 us -> 31.8 us
  local copies, waits for them, and re-layouts: 1.9 us -> 0.01 us
    ppermute x20, waiting for transfers between devices: 38.9 us -> 21 us  [swapped(): return lax.ppermute(value, axis, pairs)]
    ppermute x2, waiting for transfers between devices: 0.01 us -> 4.77 us  [passed_along(): return lax.ppermute(value, axis, pairs)]
    ppermute x20, starting transfers between devices: 23 us -> 27.2 us  [swapped(): return lax.ppermute(value, axis, pairs)]
    unnamed x8 -> x6, local copies, waits for them, and re-layouts: 1.9 us -> 0.01 us
    ppermute x2, starting transfers between devices: 3.46 us -> 4.61 us  [passed_along(): return lax.ppermute(value, axis, pairs)]
  transfers between devices with their start and end apart: 22 -> 22, of which waited for: 10 -> 12; matrix products, arithmetic and copies ran while one was open for 0% -> 0% of each run, Pallas kernels for 24% -> 27%
where the time goes in v9:
time: 82.8 us; the launch traced here: 82.7 us
  starting transfers between devices  31.8 us (38%)
  waiting for transfers between devices  25.7 us (31%)
  Pallas kernels  24.3 us (29%)
    ppermute x20, starting transfers between devices, swapped(): return lax.ppermute(value, axis, pairs)  27.2 us
    pallas_call x17, Pallas kernels, local_call(): pl.pallas_call(body if after else kernel, out_shape=out_shapes, in_specs=...  22.7 us
    ppermute x20, waiting for transfers between devices, swapped(): return lax.ppermute(value, axis, pairs)  21 us
    ppermute x2, waiting for transfers between devices, passed_along(): return lax.ppermute(value, axis, pairs)  4.77 us
    ppermute x2, starting transfers between devices, passed_along(): return lax.ppermute(value, axis, pairs)  4.61 us
    pallas_call x1, Pallas kernels, per_device_hops(): pl.pallas_call(functools.partial(first_kernel, top_count), out_shape=[sha...  1.67 us
  transfers between devices with their start and end apart: 22, of which 12 were waited for; matrix products, arithmetic and copies ran while one was open for 0% of the time, Pallas kernels for 27%

profile of v9, /device:TPU:0, one launch (start us, length us, event | category | flops | bytes accessed | tf_op | source)
XLA Modules:
  0.0 82.7 jit_solution(11151601902392734585)
XLA Ops:
  0.6 0.5 collective-permute-start
  1.1 4.1 %collective-permute-start.3 = (bf16[128,2048]{1,0:T(8,128)(2,1)}, bf16[128,2048]{1,0:T(8,128)(2,1)S(1)}, u32[]{:S(2)}, u32[]{:S(2)}) collective-permute-start(bf16[128,2048]{1,0:T(8,128)(2,1)} %bitcast.35), channel_id=1, source_target_pairs={{0,28},{4,0},{8,4},{12,8},{16,12},{20,16},{24,20},{28,24},{1,29},{... | collective-permute-start | bytes 1572872 | tf_op jit(solution)/shard_map/ppermute | solution.py:17
  5.2 1.7 %shard_map.113 = (bf16[240,1024]{1,0:T(8,128)(2,1)S(1)}, bf16[240,1024]{1,0:T(8,128)(2,1)S(1)}, f32[8,128]{1,0:T(8,128)S(1)}, f32[1,2048]{1,0:T(1,128)S(1)}) custom-call(s32[1]{0:T(128)} %bitcast.1.me_ref, bf16[128,2048]{1,0:T(8,128)(2,1)} %bitcast.27, f32[1,2048]{1,0:T(1,128)} %refs_1_.1, s32[2,128]{1,0:T(2,128)} %bitcast.30, f32[2,128]{1,0:T(2,128)} %bitcast.31, ...), custom_call_target="tpu_custom_call" | custom-call | flops 1024 | bytes 1024 | tf_op jit(solution)/shard_map/pallas_call | solution.py:699
  6.9 2.0 %collective-permute-start.2 = (bf16[240,1024]{1,0:T(8,128)(2,1)S(1)}, bf16[240,1024]{1,0:T(8,128)(2,1)S(1)}, u32[]{:S(2)}, u32[]{:S(2)}) collective-permute-start(bf16[240,1024]{1,0:T(8,128)(2,1)S(1)} %get-tuple-element.38.refs_4_), channel_id=1, source_target_pairs={{0,2},{1,3},{2,0},{3,1},{4,6},{5,7},{6,4},{7,5},{8,10},{9,11},{10,... | collective-permute-start | bytes 1474568 | tf_op jit(solution)/shard_map/ppermute | solution.py:23
  8.9 1.5 %collective-permute-start.1 = (bf16[240,1024]{1,0:T(8,128)(2,1)S(1)}, bf16[240,1024]{1,0:T(8,128)(2,1)S(1)}, u32[]{:S(2)}, u32[]{:S(2)}) collective-permute-start(bf16[240,1024]{1,0:T(8,128)(2,1)S(1)} %get-tuple-element.37.refs_2_.refs_3_), channel_id=1, source_target_pairs={{0,1},{1,0},{2,3},{3,2},{4,5},{5,4},{6,7},{7,6},{8,9},{9,8},{10,11... | collective-permute-start | bytes 1474568 | tf_op jit(solution)/shard_map/ppermute | solution.py:23
  10.4 4.8 %collective-permute-done.refs_0_ = bf16[128,2048]{1,0:T(8,128)(2,1)S(1)} collective-permute-done((bf16[128,2048]{1,0:T(8,128)(2,1)}, bf16[128,2048]{1,0:T(8,128)(2,1)S(1)}, u32[]{:S(2)}, u32[]{:S(2)}) %collective-permute-start) | collective-permute-done | bytes 524320 | tf_op jit(solution)/shard_map/ppermute | solution.py:17
  15.2 0.0 copy-start
  15.2 0.2 shard_map.114
  15.4 2.6 %collective-permute-start.5 = (bf16[128,1024]{1,0:T(8,128)(2,1)S(1)}, bf16[128,1024]{1,0:T(8,128)(2,1)S(1)}, u32[]{:S(2)}, u32[]{:S(2)}) collective-permute-start(bf16[128,1024]{1,0:T(8,128)(2,1)S(1)} %get-tuple-element.44.refs_4_), channel_id=1, source_target_pairs={{0,2},{1,3},{2,0},{3,1},{4,6},{5,7},{6,4},{7,5},{8,10},{9,11},{10,... | collective-permute-start | bytes 786440 | tf_op jit(solution)/shard_map/ppermute | solution.py:23
  18.0 1.5 %collective-permute-start.4 = (bf16[128,1024]{1,0:T(8,128)(2,1)S(1)}, bf16[128,1024]{1,0:T(8,128)(2,1)S(1)}, u32[]{:S(2)}, u32[]{:S(2)}) collective-permute-start(bf16[128,1024]{1,0:T(8,128)(2,1)S(1)} %get-tuple-element.40.refs_1_.refs_3_), channel_id=1, source_target_pairs={{0,1},{1,0},{2,3},{3,2},{4,5},{5,4},{6,7},{7,6},{8,9},{9,8},{10,11... | collective-permute-start | bytes 786440 | tf_op jit(solution)/shard_map/ppermute | solution.py:23
  19.5 0.0 collective-permute-done.3.refs_0_
  19.5 0.6 collective-permute-start.11
  20.1 0.6 collective-permute-done.2.refs_1_.refs_3_.refs_6_
  20.7 1.9 %collective-permute-start.10 = (bf16[128,1024]{1,0:T(8,128)(2,1)S(1)}, bf16[128,1024]{1,0:T(8,128)(2,1)S(1)}, u32[]{:S(2)}, u32[]{:S(2)}) collective-permute-start(bf16[128,1024]{1,0:T(8,128)(2,1)S(1)} %get-tuple-element.41.refs_2_.refs_4_.refs_3_), channel_id=1, source_target_pairs={{0,1},{1,0},{2,3},{3,2},{4,5},{5,4},{6,7},{7,6},{8,9},{9,8},{10,11... | collective-permute-start | bytes 786440 | tf_op jit(solution)/shard_map/ppermute | solution.py:23
  22.7 0.0 collective-permute-done.1.refs_0_.refs_2_.refs_5_
  22.7 0.5 shard_map.117
  23.2 1.3 %collective-permute-start.9 = (bf16[96,1024]{1,0:T(8,128)(2,1)S(1)}, bf16[96,1024]{1,0:T(8,128)(2,1)S(1)}, u32[]{:S(2)}, u32[]{:S(2)}) collective-permute-start(bf16[96,1024]{1,0:T(8,128)(2,1)S(1)} %get-tuple-element.48), channel_id=1, source_target_pairs={{0,1},{1,0},{2,3},{3,2},{4,5},{5,4},{6,7},{7,6},{8,9},{9,8},{10,11... | collective-permute-start | bytes 589832 | tf_op jit(solution)/shard_map/ppermute | solution.py:23
  24.5 1.9 %collective-permute-done.5.refs_6_ = bf16[128,1024]{1,0:T(8,128)(2,1)S(1)} collective-permute-done((bf16[128,1024]{1,0:T(8,128)(2,1)S(1)}, bf16[128,1024]{1,0:T(8,128)(2,1)S(1)}, u32[]{:S(2)}, u32[]{:S(2)}) %collective-permute-start.5) | collective-permute-done | bytes 262176 | tf_op jit(solution)/shard_map/ppermute | solution.py:23
  26.4 2.0 %collective-permute-start.8 = (bf16[96,1024]{1,0:T(8,128)(2,1)S(1)}, bf16[96,1024]{1,0:T(8,128)(2,1)S(1)}, u32[]{:S(2)}, u32[]{:S(2)}) collective-permute-start(bf16[96,1024]{1,0:T(8,128)(2,1)S(1)} %get-tuple-element.45.refs_7_), channel_id=1, source_target_pairs={{0,2},{1,3},{2,0},{3,1},{4,6},{5,7},{6,4},{7,5},{8,10},{9,11},{10,... | collective-permute-start | bytes 589832 | tf_op jit(solution)/shard_map/ppermute | solution.py:23
  28.3 0.0 collective-permute-done.4.refs_5_
  28.3 0.9 %shard_map.118 = (bf16[192,1024]{1,0:T(8,128)(2,1)S(1)}, bf16[192,1024]{1,0:T(8,128)(2,1)S(1)}) custom-call(f32[8,128]{1,0:T(8,128)S(1)} %get-tuple-element.36.refs_0_.refs_1_.refs_3_, f32[8,128]{1,0:T(8,128)S(1)} %get-tuple-element.42.refs_0_.refs_1_, f32[8,128]{1,0:T(8,128)S(1)} %get-tuple-element.43.refs_1_.refs_2_.refs_0_, ...), custom_call_target="tpu_custom_call" | custom-call | flops 1024 | bytes 1024 | tf_op jit(solution)/shard_map/pallas_call | solution.py:242
  29.2 1.5 %collective-permute-start.7 = (bf16[192,1024]{1,0:T(8,128)(2,1)S(1)}, bf16[192,1024]{1,0:T(8,128)(2,1)S(1)}, u32[]{:S(2)}, u32[]{:S(2)}) collective-permute-start(bf16[192,1024]{1,0:T(8,128)(2,1)S(1)} %get-tuple-element.47), channel_id=1, source_target_pairs={{0,1},{1,0},{2,3},{3,2},{4,5},{5,4},{6,7},{7,6},{8,9},{9,8},{10,11... | collective-permute-start | bytes 1179656 | tf_op jit(solution)/shard_map/ppermute | solution.py:23
  30.7 1.2 %collective-permute-done.11.refs_6_ = bf16[128,1024]{1,0:T(8,128)(2,1)S(1)} collective-permute-done((bf16[128,1024]{1,0:T(8,128)(2,1)S(1)}, bf16[128,1024]{1,0:T(8,128)(2,1)S(1)}, u32[]{:S(2)}, u32[]{:S(2)}) %collective-permute-start.11) | collective-permute-done | bytes 262176 | tf_op jit(solution)/shard_map/ppermute | solution.py:23
  32.0 2.0 %collective-permute-start.6 = (bf16[192,1024]{1,0:T(8,128)(2,1)S(1)}, bf16[192,1024]{1,0:T(8,128)(2,1)S(1)}, u32[]{:S(2)}, u32[]{:S(2)}) collective-permute-start(bf16[192,1024]{1,0:T(8,128)(2,1)S(1)} %get-tuple-element.46.refs_7_), channel_id=1, source_target_pairs={{0,2},{1,3},{2,0},{3,1},{4,6},{5,7},{6,4},{7,5},{8,10},{9,11},{10,... | collective-permute-start | bytes 1179656 | tf_op jit(solution)/shard_map/ppermute | solution.py:23
  33.9 0.0 collective-permute-done.10.refs_5_
  33.9 1.1 %shard_map.119 = (bf16[192,1024]{1,0:T(8,128)(2,1)S(1)}, bf16[192,1024]{1,0:T(8,128)(2,1)S(1)}) custom-call(f32[8,128]{1,0:T(8,128)S(1)} %get-tuple-element.36.refs_0_.refs_1_.refs_3_, f32[8,128]{1,0:T(8,128)S(1)} %get-tuple-element.42.refs_0_.refs_1_, f32[8,128]{1,0:T(8,128)S(1)} %get-tuple-element.43.refs_1_.refs_2_.refs_0_, ...), custom_call_target="tpu_custom_call" | custom-call | flops 1024 | bytes 1024 | tf_op jit(solution)/shard_map/pallas_call | solution.py:242
  35.1 1.5 %collective-permute-start.15 = (bf16[192,1024]{1,0:T(8,128)(2,1)S(1)}, bf16[192,1024]{1,0:T(8,128)(2,1)S(1)}, u32[]{:S(2)}, u32[]{:S(2)}) collective-permute-start(bf16[192,1024]{1,0:T(8,128)(2,1)S(1)} %get-tuple-element.58), channel_id=1, source_target_pairs={{0,1},{1,0},{2,3},{3,2},{4,5},{5,4},{6,7},{7,6},{8,9},{9,8},{10,11... | collective-permute-start | bytes 1179656 | tf_op jit(solution)/shard_map/ppermute | solution.py:23
  36.6 1.2 %collective-permute-done.9.refs_8_ = bf16[96,1024]{1,0:T(8,128)(2,1)S(1)} collective-permute-done((bf16[96,1024]{1,0:T(8,128)(2,1)S(1)}, bf16[96,1024]{1,0:T(8,128)(2,1)S(1)}, u32[]{:S(2)}, u32[]{:S(2)}) %collective-permute-start.9) | collective-permute-done | bytes 196640 | tf_op jit(solution)/shard_map/ppermute | solution.py:23
  37.9 0.1 collective-permute-start.14
  37.9 0.0 collective-permute-done.8.refs_7_
  37.9 0.0 copy-done
  37.9 3.2 %shard_map.120 = (f32[384,768]{1,0:T(8,128)S(1)}, f32[384,768]{1,0:T(8,128)S(1)}) custom-call(f32[8,128]{1,0:T(8,128)S(1)} %get-tuple-element.36.refs_0_.refs_1_.refs_3_, f32[8,128]{1,0:T(8,128)S(1)} %get-tuple-element.42.refs_0_.refs_1_, f32[8,128]{1,0:T(8,128)S(1)} %get-tuple-element.43.refs_1_.refs_2_.refs_0_, ...), custom_call_target="tpu_custom_call" | custom-call | flops 2415919104 | bytes 14155776 | tf_op jit(solution)/shard_map/pallas_call | solution.py:242
  41.2 5.1 %collective-permute-done.7.refs_8_ = bf16[192,1024]{1,0:T(8,128)(2,1)S(1)} collective-permute-done((bf16[192,1024]{1,0:T(8,128)(2,1)S(1)}, bf16[192,1024]{1,0:T(8,128)(2,1)S(1)}, u32[]{:S(2)}, u32[]{:S(2)}) %collective-permute-start.7) | collective-permute-done | bytes 393248 | tf_op jit(solution)/shard_map/ppermute | solution.py:23
  46.3 0.0 collective-permute-done.6.refs_7_
  46.3 0.0 copy-done.1
  46.3 3.9 %shard_map.121 = (bf16[96,1024]{1,0:T(8,128)(2,1)S(1)}, bf16[96,1024]{1,0:T(8,128)(2,1)S(1)}, bf16[192,1024]{1,0:T(8,128)(2,1)S(1)}, bf16[384,768]{1,0:T(8,128)(2,1)S(1)}) custom-call(f32[8,128]{1,0:T(8,128)S(1)} %get-tuple-element.36.refs_0_.refs_1_.refs_3_, f32[8,128]{1,0:T(8,128)S(1)} %get-tuple-element.42.refs_0_.refs_1_, ...), custom_call_target="tpu_custom_call" | custom-call | flops 3019898880 | bytes 14155776 | tf_op jit(solution)/shard_map/pallas_call | solution.py:242
  50.2 0.3 collective-permute-start.12
  50.5 0.8 shard_map.122
  51.3 1.8 %collective-permute-start.13 = (bf16[192,1024]{1,0:T(8,128)(2,1)S(1)}, bf16[192,1024]{1,0:T(8,128)(2,1)S(1)}, u32[]{:S(2)}, u32[]{:S(2)}) collective-permute-start(bf16[192,1024]{1,0:T(8,128)(2,1)S(1)} %get-tuple-element.56), channel_id=1, source_target_pairs={{0,1},{1,0},{2,3},{3,2},{4,5},{5,4},{6,7},{7,6},{8,9},{9,8},{10,11... | collective-permute-start | bytes 1179656 | tf_op jit(solution)/shard_map/ppermute | solution.py:23
  53.1 1.6 %collective-permute-done.15.refs_8_ = bf16[192,1024]{1,0:T(8,128)(2,1)S(1)} collective-permute-done((bf16[192,1024]{1,0:T(8,128)(2,1)S(1)}, bf16[192,1024]{1,0:T(8,128)(2,1)S(1)}, u32[]{:S(2)}, u32[]{:S(2)}) %collective-permute-start.15) | collective-permute-done | bytes 393248 | tf_op jit(solution)/shard_map/ppermute | solution.py:23
  54.7 0.0 collective-permute-done.14.refs_7_
  54.7 4.7 %shard_map.123 = (bf16[96,1024]{1,0:T(8,128)(2,1)S(1)}, bf16[96,1024]{1,0:T(8,128)(2,1)S(1)}, bf16[192,1024]{1,0:T(8,128)(2,1)S(1)}, bf16[384,1536]{1,0:T(8,128)(2,1)S(1)}) custom-call(f32[8,128]{1,0:T(8,128)S(1)} %get-tuple-element.36.refs_0_.refs_1_.refs_3_, f32[8,128]{1,0:T(8,128)S(1)} %get-tuple-element.42.refs_0_.refs_1_, ...), custom_call_target="tpu_custom_call" | custom-call | flops 2415919104 | bytes 14155776 | tf_op jit(solution)/shard_map/pallas_call | solution.py:242
  59.4 0.3 collective-permute-start.19
  59.8 1.4 %shard_map.124 = (bf16[96,1024]{1,0:T(8,128)(2,1)S(1)}, bf16[96,1024]{1,0:T(8,128)(2,1)S(1)}, bf16[192,1024]{1,0:T(8,128)(2,1)S(1)}) custom-call(bf16[384,1536]{1,0:T(8,128)(2,1)S(1)} %get-tuple-element.60.both_ref, bf16[2048,1536]{1,0:T(8,128)(2,1)S(1)} %bitcast.23), custom_call_target="tpu_custom_call" | custom-call | flops 1024 | bytes 1024 | tf_op jit(solution)/shard_map/pallas_call | solution.py:242
  61.2 1.5 %collective-permute-start.18 = (bf16[192,1024]{1,0:T(8,128)(2,1)S(1)}, bf16[192,1024]{1,0:T(8,128)(2,1)S(1)}, u32[]{:S(2)}, u32[]{:S(2)}) collective-permute-start(bf16[192,1024]{1,0:T(8,128)(2,1)S(1)} %get-tuple-element.64), channel_id=1, source_target_pairs={{0,1},{1,0},{2,3},{3,2},{4,5},{5,4},{6,7},{7,6},{8,9},{9,8},{10,11... | collective-permute-start | bytes 1179656 | tf_op jit(solution)/shard_map/ppermute | solution.py:23
  62.7 0.0 collective-permute-done.12.refs_2_.refs_4_
  62.7 0.8 shard_map.125.refs_3_
  63.5 0.6 collective-permute-start.16
  64.1 0.0 collective-permute-done.13.refs_2_.refs_5_
  64.1 0.8 shard_map.126.refs_3_
  64.9 1.8 %collective-permute-start.17 = (bf16[128,1024]{1,0:T(8,128)(2,1)S(1)}, bf16[128,1024]{1,0:T(8,128)(2,1)S(1)}, u32[]{:S(2)}, u32[]{:S(2)}) collective-permute-start(bf16[128,1024]{1,0:T(8,128)(2,1)S(1)} %shard_map.126.refs_3_), channel_id=1, source_target_pairs={{0,2},{1,3},{2,0},{3,1},{4,6},{5,7},{6,4},{7,5},{8,10},{9,11},{10,... | collective-permute-start | bytes 786440 | tf_op jit(solution)/shard_map/ppermute | solution.py:23
  66.8 4.8 %collective-permute-done.19.refs_2_.refs_6_ = bf16[192,1024]{1,0:T(8,128)(2,1)S(1)} collective-permute-done((bf16[192,1024]{1,0:T(8,128)(2,1)S(1)}, bf16[192,1024]{1,0:T(8,128)(2,1)S(1)}, u32[]{:S(2)}, u32[]{:S(2)}) %collective-permute-start.19) | collective-permute-done | bytes 393248 | tf_op jit(solution)/shard_map/ppermute | solution.py:23
  71.6 0.5 shard_map.127.refs_3_
  72.0 1.3 %collective-permute-done.18.refs_2_.refs_7_ = bf16[192,1024]{1,0:T(8,128)(2,1)S(1)} collective-permute-done((bf16[192,1024]{1,0:T(8,128)(2,1)S(1)}, bf16[192,1024]{1,0:T(8,128)(2,1)S(1)}, u32[]{:S(2)}, u32[]{:S(2)}) %collective-permute-start.18) | collective-permute-done | bytes 393248 | tf_op jit(solution)/shard_map/ppermute | solution.py:23
  73.3 0.5 shard_map.128.refs_8_
  73.8 0.8 %collective-permute-start.21 = (bf16[128,1024]{1,0:T(8,128)(2,1)S(1)}, bf16[128,1024]{1,0:T(8,128)(2,1)S(1)}, u32[]{:S(2)}, u32[]{:S(2)}) collective-permute-start(bf16[128,1024]{1,0:T(8,128)(2,1)S(1)} %shard_map.128.refs_8_), channel_id=1, source_target_pairs={{0,2},{1,3},{2,0},{3,1},{4,6},{5,7},{6,4},{7,5},{8,10},{9,11},{10,... | collective-permute-start | bytes 786440 | tf_op jit(solution)/shard_map/ppermute | solution.py:23
  74.6 1.5 %collective-permute-start.20 = (bf16[128,1024]{1,0:T(8,128)(2,1)S(1)}, bf16[128,1024]{1,0:T(8,128)(2,1)S(1)}, u32[]{:S(2)}, u32[]{:S(2)}) collective-permute-start(bf16[128,1024]{1,0:T(8,128)(2,1)S(1)} %shard_map.127.refs_3_), channel_id=1, source_target_pairs={{0,1},{1,0},{2,3},{3,2},{4,5},{5,4},{6,7},{7,6},{8,9},{9,8},{10,11... | collective-permute-start | bytes 786440 | tf_op jit(solution)/shard_map/ppermute | solution.py:23
  76.1 1.4 %collective-permute-done.16.refs_6_ = bf16[128,1024]{1,0:T(8,128)(2,1)S(1)} collective-permute-done((bf16[128,1024]{1,0:T(8,128)(2,1)S(1)}, bf16[128,1024]{1,0:T(8,128)(2,1)S(1)}, u32[]{:S(2)}, u32[]{:S(2)}) %collective-permute-start.16) | collective-permute-done | bytes 262176 | tf_op jit(solution)/shard_map/ppermute | solution.py:23
  77.5 0.0 collective-permute-done.17.refs_7_
  77.5 1.7 %shard_map.129 = (bf16[128,2048]{1,0:T(8,128)(2,1)}, f32[8,128]{1,0:T(8,128)S(1)}) custom-call(bf16[128,2048]{1,0:T(8,128)(2,1)S(1)} %collective-permute-done.refs_0_, f32[8,128]{1,0:T(8,128)S(1)} %get-tuple-element.36.refs_0_.refs_1_.refs_3_, bf16[96,1024]{1,0:T(8,128)(2,1)S(1)} %get-tuple-element.52.refs_2_, ...), custom_call_target="tpu_custom_call" | custom-call | flops 1024 | bytes 1024 | tf_op jit(solution)/shard_map/pallas_call | solution.py:242
  79.2 1.0 %collective-permute-done.21.refs_9_ = bf16[128,1024]{1,0:T(8,128)(2,1)S(1)} collective-permute-done((bf16[128,1024]{1,0:T(8,128)(2,1)S(1)}, bf16[128,1024]{1,0:T(8,128)(2,1)S(1)}, u32[]{:S(2)}, u32[]{:S(2)}) %collective-permute-start.21) | collective-permute-done | bytes 262176 | tf_op jit(solution)/shard_map/ppermute | solution.py:23
  80.2 0.8 collective-permute-done.20.refs_8_
  81.0 0.0 copy-done.2
  81.0 1.7 %shard_map.130 = bf16[128,2048]{1,0:T(8,128)(2,1)} custom-call(bf16[128,2048]{1,0:T(8,128)(2,1)S(1)} %collective-permute-done.3.refs_0_, bf16[128,2048]{1,0:T(8,128)(2,1)S(1)} %bitcast.28, f32[1,2048]{1,0:T(1,128)S(1)} %get-tuple-element.39.refs_1_.refs_2_, f32[8,128]{1,0:T(8,128)S(1)} %get-tuple-element.36.refs_0_.refs_1_.refs_3_, ...), custom_call_target="tpu_custom_call" | custom-call | flops 1024 | bytes 1024 | tf_op jit(solution)/shard_map/pallas_call | solution.py:242
  (4 shorter events, 0.0 us)
Async XLA Ops:
  0.6 14.6 %collective-permute-start = (bf16[128,2048]{1,0:T(8,128)(2,1)}, bf16[128,2048]{1,0:T(8,128)(2,1)S(1)}, u32[]{:S(2)}, u32[]{:S(2)}) collective-permute-start(bf16[128,2048]{1,0:T(8,128)(2,1)} %bitcast.34), channel_id=1, source_target_pairs={{0,4},{4,8},{8,12},{12,16},{16,20},{20,24},{24,28},{28,0},{1,5},{5... | collective-permute-start | bytes 1572872 | tf_op jit(solution)/shard_map/ppermute | solution.py:17
  1.1 18.4 %collective-permute-start.3 = (bf16[128,2048]{1,0:T(8,128)(2,1)}, bf16[128,2048]{1,0:T(8,128)(2,1)S(1)}, u32[]{:S(2)}, u32[]{:S(2)}) collective-permute-start(bf16[128,2048]{1,0:T(8,128)(2,1)} %bitcast.35), channel_id=1, source_target_pairs={{0,28},{4,0},{8,4},{12,8},{16,12},{20,16},{24,20},{28,24},{1,29},{... | collective-permute-start | bytes 1572872 | tf_op jit(solution)/shard_map/ppermute | solution.py:17
  6.9 13.8 %collective-permute-start.2 = (bf16[240,1024]{1,0:T(8,128)(2,1)S(1)}, bf16[240,1024]{1,0:T(8,128)(2,1)S(1)}, u32[]{:S(2)}, u32[]{:S(2)}) collective-permute-start(bf16[240,1024]{1,0:T(8,128)(2,1)S(1)} %get-tuple-element.38.refs_4_), channel_id=1, source_target_pairs={{0,2},{1,3},{2,0},{3,1},{4,6},{5,7},{6,4},{7,5},{8,10},{9,11},{10,... | collective-permute-start | bytes 1474568 | tf_op jit(solution)/shard_map/ppermute | solution.py:23
  8.9 13.7 %collective-permute-start.1 = (bf16[240,1024]{1,0:T(8,128)(2,1)S(1)}, bf16[240,1024]{1,0:T(8,128)(2,1)S(1)}, u32[]{:S(2)}, u32[]{:S(2)}) collective-permute-start(bf16[240,1024]{1,0:T(8,128)(2,1)S(1)} %get-tuple-element.37.refs_2_.refs_3_), channel_id=1, source_target_pairs={{0,1},{1,0},{2,3},{3,2},{4,5},{5,4},{6,7},{7,6},{8,9},{9,8},{10,11... | collective-permute-start | bytes 1474568 | tf_op jit(solution)/shard_map/ppermute | solution.py:23
  15.2 22.7 %copy-start = (bf16[1,1,2048,1536]{3,2,1,0:T(8,128)(2,1)S(1)}, bf16[1,1,2048,1536]{3,2,1,0:T(8,128)(2,1)}, u32[]{:S(2)}) copy-start(bf16[1,1,2048,1536]{3,2,1,0:T(8,128)(2,1)} %param.18) | copy-start | bytes 18874372
  15.4 10.9 %collective-permute-start.5 = (bf16[128,1024]{1,0:T(8,128)(2,1)S(1)}, bf16[128,1024]{1,0:T(8,128)(2,1)S(1)}, u32[]{:S(2)}, u32[]{:S(2)}) collective-permute-start(bf16[128,1024]{1,0:T(8,128)(2,1)S(1)} %get-tuple-element.44.refs_4_), channel_id=1, source_target_pairs={{0,2},{1,3},{2,0},{3,1},{4,6},{5,7},{6,4},{7,5},{8,10},{9,11},{10,... | collective-permute-start | bytes 786440 | tf_op jit(solution)/shard_map/ppermute | solution.py:23
  18.0 10.3 %collective-permute-start.4 = (bf16[128,1024]{1,0:T(8,128)(2,1)S(1)}, bf16[128,1024]{1,0:T(8,128)(2,1)S(1)}, u32[]{:S(2)}, u32[]{:S(2)}) collective-permute-start(bf16[128,1024]{1,0:T(8,128)(2,1)S(1)} %get-tuple-element.40.refs_1_.refs_3_), channel_id=1, source_target_pairs={{0,1},{1,0},{2,3},{3,2},{4,5},{5,4},{6,7},{7,6},{8,9},{9,8},{10,11... | collective-permute-start | bytes 786440 | tf_op jit(solution)/shard_map/ppermute | solution.py:23
  19.5 12.4 %collective-permute-start.11 = (bf16[128,1024]{1,0:T(8,128)(2,1)S(1)}, bf16[128,1024]{1,0:T(8,128)(2,1)S(1)}, u32[]{:S(2)}, u32[]{:S(2)}) collective-permute-start(bf16[128,1024]{1,0:T(8,128)(2,1)S(1)} %get-tuple-element.49.refs_4_), channel_id=1, source_target_pairs={{0,2},{1,3},{2,0},{3,1},{4,6},{5,7},{6,4},{7,5},{8,10},{9,11},{10,... | collective-permute-start | bytes 786440 | tf_op jit(solution)/shard_map/ppermute | solution.py:23
  20.7 13.2 %collective-permute-start.10 = (bf16[128,1024]{1,0:T(8,128)(2,1)S(1)}, bf16[128,1024]{1,0:T(8,128)(2,1)S(1)}, u32[]{:S(2)}, u32[]{:S(2)}) collective-permute-start(bf16[128,1024]{1,0:T(8,128)(2,1)S(1)} %get-tuple-element.41.refs_2_.refs_4_.refs_3_), channel_id=1, source_target_pairs={{0,1},{1,0},{2,3},{3,2},{4,5},{5,4},{6,7},{7,6},{8,9},{9,8},{10,11... | collective-permute-start | bytes 786440 | tf_op jit(solution)/shard_map/ppermute | solution.py:23
  23.2 14.7 %collective-permute-start.9 = (bf16[96,1024]{1,0:T(8,128)(2,1)S(1)}, bf16[96,1024]{1,0:T(8,128)(2,1)S(1)}, u32[]{:S(2)}, u32[]{:S(2)}) collective-permute-start(bf16[96,1024]{1,0:T(8,128)(2,1)S(1)} %get-tuple-element.48), channel_id=1, source_target_pairs={{0,1},{1,0},{2,3},{3,2},{4,5},{5,4},{6,7},{7,6},{8,9},{9,8},{10,11... | collective-permute-start | bytes 589832 | tf_op jit(solution)/shard_map/ppermute | solution.py:23
  26.4 11.6 %collective-permute-start.8 = (bf16[96,1024]{1,0:T(8,128)(2,1)S(1)}, bf16[96,1024]{1,0:T(8,128)(2,1)S(1)}, u32[]{:S(2)}, u32[]{:S(2)}) collective-permute-start(bf16[96,1024]{1,0:T(8,128)(2,1)S(1)} %get-tuple-element.45.refs_7_), channel_id=1, source_target_pairs={{0,2},{1,3},{2,0},{3,1},{4,6},{5,7},{6,4},{7,5},{8,10},{9,11},{10,... | collective-permute-start | bytes 589832 | tf_op jit(solution)/shard_map/ppermute | solution.py:23
  29.2 17.1 %collective-permute-start.7 = (bf16[192,1024]{1,0:T(8,128)(2,1)S(1)}, bf16[192,1024]{1,0:T(8,128)(2,1)S(1)}, u32[]{:S(2)}, u32[]{:S(2)}) collective-permute-start(bf16[192,1024]{1,0:T(8,128)(2,1)S(1)} %get-tuple-element.47), channel_id=1, source_target_pairs={{0,1},{1,0},{2,3},{3,2},{4,5},{5,4},{6,7},{7,6},{8,9},{9,8},{10,11... | collective-permute-start | bytes 1179656 | tf_op jit(solution)/shard_map/ppermute | solution.py:23
  32.0 14.3 %collective-permute-start.6 = (bf16[192,1024]{1,0:T(8,128)(2,1)S(1)}, bf16[192,1024]{1,0:T(8,128)(2,1)S(1)}, u32[]{:S(2)}, u32[]{:S(2)}) collective-permute-start(bf16[192,1024]{1,0:T(8,128)(2,1)S(1)} %get-tuple-element.46.refs_7_), channel_id=1, source_target_pairs={{0,2},{1,3},{2,0},{3,1},{4,6},{5,7},{6,4},{7,5},{8,10},{9,11},{10,... | collective-permute-start | bytes 1179656 | tf_op jit(solution)/shard_map/ppermute | solution.py:23
  35.1 19.6 %collective-permute-start.15 = (bf16[192,1024]{1,0:T(8,128)(2,1)S(1)}, bf16[192,1024]{1,0:T(8,128)(2,1)S(1)}, u32[]{:S(2)}, u32[]{:S(2)}) collective-permute-start(bf16[192,1024]{1,0:T(8,128)(2,1)S(1)} %get-tuple-element.58), channel_id=1, source_target_pairs={{0,1},{1,0},{2,3},{3,2},{4,5},{5,4},{6,7},{7,6},{8,9},{9,8},{10,11... | collective-permute-start | bytes 1179656 | tf_op jit(solution)/shard_map/ppermute | solution.py:23
  37.9 16.9 %collective-permute-start.14 = (bf16[192,1024]{1,0:T(8,128)(2,1)S(1)}, bf16[192,1024]{1,0:T(8,128)(2,1)S(1)}, u32[]{:S(2)}, u32[]{:S(2)}) collective-permute-start(bf16[192,1024]{1,0:T(8,128)(2,1)S(1)} %get-tuple-element.50.refs_10_), channel_id=1, source_target_pairs={{0,2},{1,3},{2,0},{3,1},{4,6},{5,7},{6,4},{7,5},{8,10},{9,11},{10,... | collective-permute-start | bytes 1179656 | tf_op jit(solution)/shard_map/ppermute | solution.py:23
  37.9 8.4 %copy-start.1 = (bf16[1,1,768,2048]{3,2,1,0:T(8,128)(2,1)S(1)}, bf16[1,1,768,2048]{3,2,1,0:T(8,128)(2,1)}, u32[]{:S(2)}) copy-start(bf16[1,1,768,2048]{3,2,1,0:T(8,128)(2,1)} %param.19) | copy-start | bytes 9437188
  50.2 12.5 %collective-permute-start.12 = (bf16[192,1024]{1,0:T(8,128)(2,1)S(1)}, bf16[192,1024]{1,0:T(8,128)(2,1)S(1)}, u32[]{:S(2)}, u32[]{:S(2)}) collective-permute-start(bf16[192,1024]{1,0:T(8,128)(2,1)S(1)} %get-tuple-element.55), channel_id=1, source_target_pairs={{0,2},{1,3},{2,0},{3,1},{4,6},{5,7},{6,4},{7,5},{8,10},{9,11},{10,... | collective-permute-start | bytes 1179656 | tf_op jit(solution)/shard_map/ppermute | solution.py:23
  51.3 12.8 %collective-permute-start.13 = (bf16[192,1024]{1,0:T(8,128)(2,1)S(1)}, bf16[192,1024]{1,0:T(8,128)(2,1)S(1)}, u32[]{:S(2)}, u32[]{:S(2)}) collective-permute-start(bf16[192,1024]{1,0:T(8,128)(2,1)S(1)} %get-tuple-element.56), channel_id=1, source_target_pairs={{0,1},{1,0},{2,3},{3,2},{4,5},{5,4},{6,7},{7,6},{8,9},{9,8},{10,11... | collective-permute-start | bytes 1179656 | tf_op jit(solution)/shard_map/ppermute | solution.py:23
  59.4 12.1 %collective-permute-start.19 = (bf16[192,1024]{1,0:T(8,128)(2,1)S(1)}, bf16[192,1024]{1,0:T(8,128)(2,1)S(1)}, u32[]{:S(2)}, u32[]{:S(2)}) collective-permute-start(bf16[192,1024]{1,0:T(8,128)(2,1)S(1)} %get-tuple-element.66), channel_id=1, source_target_pairs={{0,2},{1,3},{2,0},{3,1},{4,6},{5,7},{6,4},{7,5},{8,10},{9,11},{10,... | collective-permute-start | bytes 1179656 | tf_op jit(solution)/shard_map/ppermute | solution.py:23
  61.2 12.1 %collective-permute-start.18 = (bf16[192,1024]{1,0:T(8,128)(2,1)S(1)}, bf16[192,1024]{1,0:T(8,128)(2,1)S(1)}, u32[]{:S(2)}, u32[]{:S(2)}) collective-permute-start(bf16[192,1024]{1,0:T(8,128)(2,1)S(1)} %get-tuple-element.64), channel_id=1, source_target_pairs={{0,1},{1,0},{2,3},{3,2},{4,5},{5,4},{6,7},{7,6},{8,9},{9,8},{10,11... | collective-permute-start | bytes 1179656 | tf_op jit(solution)/shard_map/ppermute | solution.py:23
  63.5 14.0 %collective-permute-start.16 = (bf16[128,1024]{1,0:T(8,128)(2,1)S(1)}, bf16[128,1024]{1,0:T(8,128)(2,1)S(1)}, u32[]{:S(2)}, u32[]{:S(2)}) collective-permute-start(bf16[128,1024]{1,0:T(8,128)(2,1)S(1)} %shard_map.125.refs_3_), channel_id=1, source_target_pairs={{0,1},{1,0},{2,3},{3,2},{4,5},{5,4},{6,7},{7,6},{8,9},{9,8},{10,11... | collective-permute-start | bytes 786440 | tf_op jit(solution)/shard_map/ppermute | solution.py:23
  64.9 12.6 %collective-permute-start.17 = (bf16[128,1024]{1,0:T(8,128)(2,1)S(1)}, bf16[128,1024]{1,0:T(8,128)(2,1)S(1)}, u32[]{:S(2)}, u32[]{:S(2)}) collective-permute-start(bf16[128,1024]{1,0:T(8,128)(2,1)S(1)} %shard_map.126.refs_3_), channel_id=1, source_target_pairs={{0,2},{1,3},{2,0},{3,1},{4,6},{5,7},{6,4},{7,5},{8,10},{9,11},{10,... | collective-permute-start | bytes 786440 | tf_op jit(solution)/shard_map/ppermute | solution.py:23
  73.8 6.4 %collective-permute-start.21 = (bf16[128,1024]{1,0:T(8,128)(2,1)S(1)}, bf16[128,1024]{1,0:T(8,128)(2,1)S(1)}, u32[]{:S(2)}, u32[]{:S(2)}) collective-permute-start(bf16[128,1024]{1,0:T(8,128)(2,1)S(1)} %shard_map.128.refs_8_), channel_id=1, source_target_pairs={{0,2},{1,3},{2,0},{3,1},{4,6},{5,7},{6,4},{7,5},{8,10},{9,11},{10,... | collective-permute-start | bytes 786440 | tf_op jit(solution)/shard_map/ppermute | solution.py:23
  74.6 6.4 %collective-permute-start.20 = (bf16[128,1024]{1,0:T(8,128)(2,1)S(1)}, bf16[128,1024]{1,0:T(8,128)(2,1)S(1)}, u32[]{:S(2)}, u32[]{:S(2)}) collective-permute-start(bf16[128,1024]{1,0:T(8,128)(2,1)S(1)} %shard_map.127.refs_3_), channel_id=1, source_target_pairs={{0,1},{1,0},{2,3},{3,2},{4,5},{5,4},{6,7},{7,6},{8,9},{9,8},{10,11... | collective-permute-start | bytes 786440 | tf_op jit(solution)/shard_map/ppermute | solution.py:23
  77.5 3.5 %copy-start.2 = (bf16[1,128,2048]{2,1,0:T(8,128)(2,1)S(1)}, bf16[1,128,2048]{2,1,0:T(8,128)(2,1)}, u32[]{:S(2)}) copy-start(bf16[1,128,2048]{2,1,0:T(8,128)(2,1)} %param.12) | copy-start | bytes 1572868

commit v10 on v9

--- a/solution.py
+++ b/solution.py
@@ -637,18 +637,33 @@
     out_ref[:, half:] = (layer_ref[:, half:].astype(jnp.float32) + right).astype(jnp.bfloat16)
 
 
-def hop_bwd_end_kernel(top_count, grads_ref, saved_ref, gain_ref, *refs):
-    out_ref = refs[-1]
+def hop_bwd_near_kernel(top_count, own, keep_left, keep_right, got_y, got_x, left_ref, right_ref):
+    capacity = keep_left.shape[0]
+    mine = pick(own[...], 0, capacity, "b", top_count)
+    near_y = pick(own[...], 2, capacity, "b", top_count)
+    near_x = pick(own[...], 1, capacity, "b", top_count)
+    left_ref[...] = to_tokens(mine, keep_left[...]) + to_tokens(near_y, got_y[:capacity, :])
+    right_ref[...] = to_tokens(mine, keep_right[...]) + to_tokens(near_x, got_x[:capacity, :])
+
+
+def hop_bwd_end_kernel(grads_ref, saved_ref, gain_ref, left_ref, right_ref, sum_x, sum_y, out_ref):
     features = saved_ref.shape[1]
-    left, right = summed("b", top_count, *refs[:-1])
-    wide = saved_ref[...].astype(jnp.float32)
-    inv_rms = lax.rsqrt(jnp.mean(wide * wide, axis=-1, keepdims=True) + EPS)
-    scaled = jnp.concatenate([left, right], axis=1) * gain_ref[...]
-    cubed = inv_rms * inv_rms * inv_rms
-    inner = jnp.sum(scaled * wide, axis=-1, keepdims=True)
-    out_ref[...] = (
-        grads_ref[...].astype(jnp.float32) + inv_rms * scaled - cubed / features * wide * inner
-    ).astype(jnp.bfloat16)
+    half = features // 2
+    parts = []
+    for start, near, far in ((0, left_ref, sum_x), (half, right_ref, sum_y)):
+        wide = saved_ref[:, start : start + half].astype(jnp.float32)
+        scaled = (near[...] + far[...].astype(jnp.float32)) * gain_ref[:, start : start + half]
+        parts.append((start, wide, scaled))
+    square = sum(jnp.sum(wide * wide, axis=-1, keepdims=True) for _, wide, _ in parts)
+    inner = sum(jnp.sum(scaled * wide, axis=-1, keepdims=True) for _, wide, scaled in parts)
+    inv_rms = lax.rsqrt(square / features + EPS)
+    factor = inv_rms * inv_rms * inv_rms / features * inner
+    for start, wide, scaled in parts:
+        out_ref[:, start : start + half] = (
+            grads_ref[:, start : start + half].astype(jnp.float32)
+            + inv_rms * scaled
+            - factor * wide
+        ).astype(jnp.bfloat16)
 
 
 def per_device_hops(
@@ -845,10 +860,18 @@
         moved,
         after=(last,),
     )
+    b_near = local_call(
+        functools.partial(hop_bwd_near_kernel, top_count),
+        [shaped(tok_rows, half, jnp.float32)] * 2,
+        (own, *b_keep, b_ret_y, b_ret_x),
+        one_hop,
+        moved,
+        after=(last,),
+    )
     bwd_block = local_call(
-        functools.partial(hop_bwd_end_kernel, top_count),
+        hop_bwd_end_kernel,
         shaped(tok_rows, features),
-        (grad_in, saved, gain_here, own, *b_keep, b_ret_y, b_ret_x, b_sum_x, b_sum_y),
+        (grad_in, saved, gain_here, *b_near, b_sum_x, b_sum_y),
         one_hop,
         moved,
         after=(order,),

time: 82.8 us -> 82.5 us (level)
    pallas_call x17 -> x18, Pallas kernels: 22.7 us -> 22.9 us  [local_call(): pl.pallas_call(body if after else kernel, out_shape=out_shapes, in_specs=...]
  transfers between devices with their start and end apart: 22 -> 22, of which waited for: 12 -> 12; matrix products, arithmetic and copies ran while one was open for 0% -> 0% of each run, Pallas kernels for 27% -> 28%
where the time goes in v10:
time: 82.5 us; the launch traced here: 82.3 us
  starting transfers between devices  31.8 us (39%)
  waiting for transfers between devices  25.1 us (30%)
  Pallas kernels  24.5 us (30%)
    ppermute x20, starting transfers between devices, swapped(): return lax.ppermute(value, axis, pairs)  27.2 us
    pallas_call x18, Pallas kernels, local_call(): pl.pallas_call(body if after else kernel, out_shape=out_shapes, in_specs=...  22.9 us
    ppermute x20, waiting for transfers between devices, swapped(): return lax.ppermute(value, axis, pairs)  20.4 us
    ppermute x2, waiting for transfers between devices, passed_along(): return lax.ppermute(value, axis, pairs)  4.77 us
    ppermute x2, starting transfers between devices, passed_along(): return lax.ppermute(value, axis, pairs)  4.61 us
    pallas_call x1, Pallas kernels, per_device_hops(): pl.pallas_call(functools.partial(first_kernel, top_count), out_shape=[sha...  1.67 us
  transfers between devices with their start and end apart: 22, of which 12 were waited for; matrix products, arithmetic and copies ran while one was open for 0% of the time, Pallas kernels for 28%

profile of v10, /device:TPU:0, one launch (start us, length us, event | category | flops | bytes accessed | tf_op | source)
XLA Modules:
  0.0 82.3 jit_solution(18315988748675373824)
XLA Ops:
  0.6 0.5 collective-permute-start
  1.1 4.1 %collective-permute-start.3 = (bf16[128,2048]{1,0:T(8,128)(2,1)}, bf16[128,2048]{1,0:T(8,128)(2,1)S(1)}, u32[]{:S(2)}, u32[]{:S(2)}) collective-permute-start(bf16[128,2048]{1,0:T(8,128)(2,1)} %bitcast.35), channel_id=1, source_target_pairs={{0,28},{4,0},{8,4},{12,8},{16,12},{20,16},{24,20},{28,24},{1,29},{... | collective-permute-start | bytes 1572872 | tf_op jit(solution)/shard_map/ppermute | solution.py:17
  5.2 1.7 %shard_map.113 = (bf16[240,1024]{1,0:T(8,128)(2,1)S(1)}, bf16[240,1024]{1,0:T(8,128)(2,1)S(1)}, f32[8,128]{1,0:T(8,128)S(1)}, f32[1,2048]{1,0:T(1,128)S(1)}) custom-call(s32[1]{0:T(128)} %bitcast.1.me_ref, bf16[128,2048]{1,0:T(8,128)(2,1)} %bitcast.27, f32[1,2048]{1,0:T(1,128)} %refs_1_.1, s32[2,128]{1,0:T(2,128)} %bitcast.30, f32[2,128]{1,0:T(2,128)} %bitcast.31, ...), custom_call_target="tpu_custom_call" | custom-call | flops 1024 | bytes 1024 | tf_op jit(solution)/shard_map/pallas_call | solution.py:714
  6.9 2.0 %collective-permute-start.2 = (bf16[240,1024]{1,0:T(8,128)(2,1)S(1)}, bf16[240,1024]{1,0:T(8,128)(2,1)S(1)}, u32[]{:S(2)}, u32[]{:S(2)}) collective-permute-start(bf16[240,1024]{1,0:T(8,128)(2,1)S(1)} %get-tuple-element.40.refs_4_), channel_id=1, source_target_pairs={{0,2},{1,3},{2,0},{3,1},{4,6},{5,7},{6,4},{7,5},{8,10},{9,11},{10,... | collective-permute-start | bytes 1474568 | tf_op jit(solution)/shard_map/ppermute | solution.py:23
  8.9 1.5 %collective-permute-start.1 = (bf16[240,1024]{1,0:T(8,128)(2,1)S(1)}, bf16[240,1024]{1,0:T(8,128)(2,1)S(1)}, u32[]{:S(2)}, u32[]{:S(2)}) collective-permute-start(bf16[240,1024]{1,0:T(8,128)(2,1)S(1)} %get-tuple-element.39.refs_2_.refs_3_), channel_id=1, source_target_pairs={{0,1},{1,0},{2,3},{3,2},{4,5},{5,4},{6,7},{7,6},{8,9},{9,8},{10,11... | collective-permute-start | bytes 1474568 | tf_op jit(solution)/shard_map/ppermute | solution.py:23
  10.4 4.8 %collective-permute-done.refs_0_ = bf16[128,2048]{1,0:T(8,128)(2,1)S(1)} collective-permute-done((bf16[128,2048]{1,0:T(8,128)(2,1)}, bf16[128,2048]{1,0:T(8,128)(2,1)S(1)}, u32[]{:S(2)}, u32[]{:S(2)}) %collective-permute-start) | collective-permute-done | bytes 524320 | tf_op jit(solution)/shard_map/ppermute | solution.py:17
  15.2 0.2 shard_map.114
  15.4 2.6 %collective-permute-start.5 = (bf16[128,1024]{1,0:T(8,128)(2,1)S(1)}, bf16[128,1024]{1,0:T(8,128)(2,1)S(1)}, u32[]{:S(2)}, u32[]{:S(2)}) collective-permute-start(bf16[128,1024]{1,0:T(8,128)(2,1)S(1)} %get-tuple-element.46.refs_4_), channel_id=1, source_target_pairs={{0,2},{1,3},{2,0},{3,1},{4,6},{5,7},{6,4},{7,5},{8,10},{9,11},{10,... | collective-permute-start | bytes 786440 | tf_op jit(solution)/shard_map/ppermute | solution.py:23
  18.0 1.5 %collective-permute-start.4 = (bf16[128,1024]{1,0:T(8,128)(2,1)S(1)}, bf16[128,1024]{1,0:T(8,128)(2,1)S(1)}, u32[]{:S(2)}, u32[]{:S(2)}) collective-permute-start(bf16[128,1024]{1,0:T(8,128)(2,1)S(1)} %get-tuple-element.42.refs_1_.refs_3_), channel_id=1, source_target_pairs={{0,1},{1,0},{2,3},{3,2},{4,5},{5,4},{6,7},{7,6},{8,9},{9,8},{10,11... | collective-permute-start | bytes 786440 | tf_op jit(solution)/shard_map/ppermute | solution.py:23
  19.5 0.0 collective-permute-done.3.refs_0_
  19.5 0.6 collective-permute-start.11
  20.1 0.6 collective-permute-done.2.refs_1_.refs_3_.refs_6_
  20.7 1.9 %collective-permute-start.10 = (bf16[128,1024]{1,0:T(8,128)(2,1)S(1)}, bf16[128,1024]{1,0:T(8,128)(2,1)S(1)}, u32[]{:S(2)}, u32[]{:S(2)}) collective-permute-start(bf16[128,1024]{1,0:T(8,128)(2,1)S(1)} %get-tuple-element.43.refs_2_.refs_4_.refs_3_), channel_id=1, source_target_pairs={{0,1},{1,0},{2,3},{3,2},{4,5},{5,4},{6,7},{7,6},{8,9},{9,8},{10,11... | collective-permute-start | bytes 786440 | tf_op jit(solution)/shard_map/ppermute | solution.py:23
  22.7 0.0 collective-permute-done.1.refs_0_.refs_2_.refs_5_
  22.7 0.5 shard_map.117
  23.2 1.3 %collective-permute-start.9 = (bf16[96,1024]{1,0:T(8,128)(2,1)S(1)}, bf16[96,1024]{1,0:T(8,128)(2,1)S(1)}, u32[]{:S(2)}, u32[]{:S(2)}) collective-permute-start(bf16[96,1024]{1,0:T(8,128)(2,1)S(1)} %get-tuple-element.50), channel_id=1, source_target_pairs={{0,1},{1,0},{2,3},{3,2},{4,5},{5,4},{6,7},{7,6},{8,9},{9,8},{10,11... | collective-permute-start | bytes 589832 | tf_op jit(solution)/shard_map/ppermute | solution.py:23
  24.5 1.9 %collective-permute-done.5.refs_6_ = bf16[128,1024]{1,0:T(8,128)(2,1)S(1)} collective-permute-done((bf16[128,1024]{1,0:T(8,128)(2,1)S(1)}, bf16[128,1024]{1,0:T(8,128)(2,1)S(1)}, u32[]{:S(2)}, u32[]{:S(2)}) %collective-permute-start.5) | collective-permute-done | bytes 262176 | tf_op jit(solution)/shard_map/ppermute | solution.py:23
  26.4 2.0 %collective-permute-start.8 = (bf16[96,1024]{1,0:T(8,128)(2,1)S(1)}, bf16[96,1024]{1,0:T(8,128)(2,1)S(1)}, u32[]{:S(2)}, u32[]{:S(2)}) collective-permute-start(bf16[96,1024]{1,0:T(8,128)(2,1)S(1)} %get-tuple-element.47.refs_7_), channel_id=1, source_target_pairs={{0,2},{1,3},{2,0},{3,1},{4,6},{5,7},{6,4},{7,5},{8,10},{9,11},{10,... | collective-permute-start | bytes 589832 | tf_op jit(solution)/shard_map/ppermute | solution.py:23
  28.3 0.0 collective-permute-done.4.refs_5_
  28.3 0.9 %shard_map.118 = (bf16[192,1024]{1,0:T(8,128)(2,1)S(1)}, bf16[192,1024]{1,0:T(8,128)(2,1)S(1)}) custom-call(f32[8,128]{1,0:T(8,128)S(1)} %get-tuple-element.38.refs_0_.refs_1_, f32[8,128]{1,0:T(8,128)S(1)} %get-tuple-element.44.refs_0_.refs_1_, f32[8,128]{1,0:T(8,128)S(1)} %get-tuple-element.45.refs_1_.refs_2_.refs_0_, ...), custom_call_target="tpu_custom_call" | custom-call | flops 1024 | bytes 1024 | tf_op jit(solution)/shard_map/pallas_call | solution.py:242
  29.2 1.5 %collective-permute-start.7 = (bf16[192,1024]{1,0:T(8,128)(2,1)S(1)}, bf16[192,1024]{1,0:T(8,128)(2,1)S(1)}, u32[]{:S(2)}, u32[]{:S(2)}) collective-permute-start(bf16[192,1024]{1,0:T(8,128)(2,1)S(1)} %get-tuple-element.49), channel_id=1, source_target_pairs={{0,1},{1,0},{2,3},{3,2},{4,5},{5,4},{6,7},{7,6},{8,9},{9,8},{10,11... | collective-permute-start | bytes 1179656 | tf_op jit(solution)/shard_map/ppermute | solution.py:23
  30.7 1.2 %collective-permute-done.11.refs_6_ = bf16[128,1024]{1,0:T(8,128)(2,1)S(1)} collective-permute-done((bf16[128,1024]{1,0:T(8,128)(2,1)S(1)}, bf16[128,1024]{1,0:T(8,128)(2,1)S(1)}, u32[]{:S(2)}, u32[]{:S(2)}) %collective-permute-start.11) | collective-permute-done | bytes 262176 | tf_op jit(solution)/shard_map/ppermute | solution.py:23
  32.0 2.0 %collective-permute-start.6 = (bf16[192,1024]{1,0:T(8,128)(2,1)S(1)}, bf16[192,1024]{1,0:T(8,128)(2,1)S(1)}, u32[]{:S(2)}, u32[]{:S(2)}) collective-permute-start(bf16[192,1024]{1,0:T(8,128)(2,1)S(1)} %get-tuple-element.48.refs_7_), channel_id=1, source_target_pairs={{0,2},{1,3},{2,0},{3,1},{4,6},{5,7},{6,4},{7,5},{8,10},{9,11},{10,... | collective-permute-start | bytes 1179656 | tf_op jit(solution)/shard_map/ppermute | solution.py:23
  33.9 0.0 collective-permute-done.10.refs_5_
  33.9 1.1 %shard_map.119 = (bf16[192,1024]{1,0:T(8,128)(2,1)S(1)}, bf16[192,1024]{1,0:T(8,128)(2,1)S(1)}) custom-call(f32[8,128]{1,0:T(8,128)S(1)} %get-tuple-element.38.refs_0_.refs_1_, f32[8,128]{1,0:T(8,128)S(1)} %get-tuple-element.44.refs_0_.refs_1_, f32[8,128]{1,0:T(8,128)S(1)} %get-tuple-element.45.refs_1_.refs_2_.refs_0_, ...), custom_call_target="tpu_custom_call" | custom-call | flops 1024 | bytes 1024 | tf_op jit(solution)/shard_map/pallas_call | solution.py:242
  35.1 1.5 %collective-permute-start.15 = (bf16[192,1024]{1,0:T(8,128)(2,1)S(1)}, bf16[192,1024]{1,0:T(8,128)(2,1)S(1)}, u32[]{:S(2)}, u32[]{:S(2)}) collective-permute-start(bf16[192,1024]{1,0:T(8,128)(2,1)S(1)} %get-tuple-element.60), channel_id=1, source_target_pairs={{0,1},{1,0},{2,3},{3,2},{4,5},{5,4},{6,7},{7,6},{8,9},{9,8},{10,11... | collective-permute-start | bytes 1179656 | tf_op jit(solution)/shard_map/ppermute | solution.py:23
  36.6 1.2 %collective-permute-done.9.refs_8_ = bf16[96,1024]{1,0:T(8,128)(2,1)S(1)} collective-permute-done((bf16[96,1024]{1,0:T(8,128)(2,1)S(1)}, bf16[96,1024]{1,0:T(8,128)(2,1)S(1)}, u32[]{:S(2)}, u32[]{:S(2)}) %collective-permute-start.9) | collective-permute-done | bytes 196640 | tf_op jit(solution)/shard_map/ppermute | solution.py:23
  37.9 0.1 collective-permute-start.14
  37.9 0.0 collective-permute-done.8.refs_7_
  37.9 0.0 copy-done
  37.9 3.2 %shard_map.120 = (f32[384,768]{1,0:T(8,128)S(1)}, f32[384,768]{1,0:T(8,128)S(1)}) custom-call(f32[8,128]{1,0:T(8,128)S(1)} %get-tuple-element.38.refs_0_.refs_1_, f32[8,128]{1,0:T(8,128)S(1)} %get-tuple-element.44.refs_0_.refs_1_, f32[8,128]{1,0:T(8,128)S(1)} %get-tuple-element.45.refs_1_.refs_2_.refs_0_, ...), custom_call_target="tpu_custom_call" | custom-call | flops 2415919104 | bytes 14155776 | tf_op jit(solution)/shard_map/pallas_call | solution.py:242
  41.2 5.1 %collective-permute-done.7.refs_8_ = bf16[192,1024]{1,0:T(8,128)(2,1)S(1)} collective-permute-done((bf16[192,1024]{1,0:T(8,128)(2,1)S(1)}, bf16[192,1024]{1,0:T(8,128)(2,1)S(1)}, u32[]{:S(2)}, u32[]{:S(2)}) %collective-permute-start.7) | collective-permute-done | bytes 393248 | tf_op jit(solution)/shard_map/ppermute | solution.py:23
  46.3 0.0 collective-permute-done.6.refs_7_
  46.3 0.0 copy-done.1
  46.3 3.9 %shard_map.121 = (bf16[96,1024]{1,0:T(8,128)(2,1)S(1)}, bf16[96,1024]{1,0:T(8,128)(2,1)S(1)}, bf16[192,1024]{1,0:T(8,128)(2,1)S(1)}, bf16[384,768]{1,0:T(8,128)(2,1)S(1)}) custom-call(f32[8,128]{1,0:T(8,128)S(1)} %get-tuple-element.38.refs_0_.refs_1_, f32[8,128]{1,0:T(8,128)S(1)} %get-tuple-element.44.refs_0_.refs_1_, ...), custom_call_target="tpu_custom_call" | custom-call | flops 3019898880 | bytes 14155776 | tf_op jit(solution)/shard_map/pallas_call | solution.py:242
  50.2 0.3 collective-permute-start.12
  50.5 0.8 shard_map.122
  51.3 1.8 %collective-permute-start.13 = (bf16[192,1024]{1,0:T(8,128)(2,1)S(1)}, bf16[192,1024]{1,0:T(8,128)(2,1)S(1)}, u32[]{:S(2)}, u32[]{:S(2)}) collective-permute-start(bf16[192,1024]{1,0:T(8,128)(2,1)S(1)} %get-tuple-element.58), channel_id=1, source_target_pairs={{0,1},{1,0},{2,3},{3,2},{4,5},{5,4},{6,7},{7,6},{8,9},{9,8},{10,11... | collective-permute-start | bytes 1179656 | tf_op jit(solution)/shard_map/ppermute | solution.py:23
  53.1 1.6 %collective-permute-done.15.refs_8_ = bf16[192,1024]{1,0:T(8,128)(2,1)S(1)} collective-permute-done((bf16[192,1024]{1,0:T(8,128)(2,1)S(1)}, bf16[192,1024]{1,0:T(8,128)(2,1)S(1)}, u32[]{:S(2)}, u32[]{:S(2)}) %collective-permute-start.15) | collective-permute-done | bytes 393248 | tf_op jit(solution)/shard_map/ppermute | solution.py:23
  54.7 0.0 collective-permute-done.14.refs_7_
  54.7 4.7 %shard_map.123 = (bf16[96,1024]{1,0:T(8,128)(2,1)S(1)}, bf16[96,1024]{1,0:T(8,128)(2,1)S(1)}, bf16[192,1024]{1,0:T(8,128)(2,1)S(1)}, bf16[384,1536]{1,0:T(8,128)(2,1)S(1)}) custom-call(f32[8,128]{1,0:T(8,128)S(1)} %get-tuple-element.38.refs_0_.refs_1_, f32[8,128]{1,0:T(8,128)S(1)} %get-tuple-element.44.refs_0_.refs_1_, ...), custom_call_target="tpu_custom_call" | custom-call | flops 2415919104 | bytes 14155776 | tf_op jit(solution)/shard_map/pallas_call | solution.py:242
  59.4 0.3 collective-permute-start.19
  59.8 1.4 %shard_map.124 = (bf16[96,1024]{1,0:T(8,128)(2,1)S(1)}, bf16[96,1024]{1,0:T(8,128)(2,1)S(1)}, bf16[192,1024]{1,0:T(8,128)(2,1)S(1)}) custom-call(bf16[384,1536]{1,0:T(8,128)(2,1)S(1)} %get-tuple-element.62.both_ref, bf16[2048,1536]{1,0:T(8,128)(2,1)S(1)} %bitcast.23), custom_call_target="tpu_custom_call" | custom-call | flops 1024 | bytes 1024 | tf_op jit(solution)/shard_map/pallas_call | solution.py:242
  61.2 1.5 %collective-permute-start.18 = (bf16[192,1024]{1,0:T(8,128)(2,1)S(1)}, bf16[192,1024]{1,0:T(8,128)(2,1)S(1)}, u32[]{:S(2)}, u32[]{:S(2)}) collective-permute-start(bf16[192,1024]{1,0:T(8,128)(2,1)S(1)} %get-tuple-element.66), channel_id=1, source_target_pairs={{0,1},{1,0},{2,3},{3,2},{4,5},{5,4},{6,7},{7,6},{8,9},{9,8},{10,11... | collective-permute-start | bytes 1179656 | tf_op jit(solution)/shard_map/ppermute | solution.py:23
  62.7 0.0 collective-permute-done.12.refs_2_.refs_4_
  62.7 0.8 shard_map.125.refs_3_
  63.5 0.6 collective-permute-start.16
  64.1 0.0 collective-permute-done.13.refs_2_.refs_5_
  64.1 0.8 shard_map.126.refs_3_
  64.9 1.8 %collective-permute-start.17 = (bf16[128,1024]{1,0:T(8,128)(2,1)S(1)}, bf16[128,1024]{1,0:T(8,128)(2,1)S(1)}, u32[]{:S(2)}, u32[]{:S(2)}) collective-permute-start(bf16[128,1024]{1,0:T(8,128)(2,1)S(1)} %shard_map.126.refs_3_), channel_id=1, source_target_pairs={{0,2},{1,3},{2,0},{3,1},{4,6},{5,7},{6,4},{7,5},{8,10},{9,11},{10,... | collective-permute-start | bytes 786440 | tf_op jit(solution)/shard_map/ppermute | solution.py:23
  66.8 4.8 %collective-permute-done.19.refs_2_.refs_3_ = bf16[192,1024]{1,0:T(8,128)(2,1)S(1)} collective-permute-done((bf16[192,1024]{1,0:T(8,128)(2,1)S(1)}, bf16[192,1024]{1,0:T(8,128)(2,1)S(1)}, u32[]{:S(2)}, u32[]{:S(2)}) %collective-permute-start.19) | collective-permute-done | bytes 393248 | tf_op jit(solution)/shard_map/ppermute | solution.py:23
  71.6 0.5 shard_map.127.refs_3_
  72.0 1.3 %collective-permute-done.18.refs_2_.refs_4_ = bf16[192,1024]{1,0:T(8,128)(2,1)S(1)} collective-permute-done((bf16[192,1024]{1,0:T(8,128)(2,1)S(1)}, bf16[192,1024]{1,0:T(8,128)(2,1)S(1)}, u32[]{:S(2)}, u32[]{:S(2)}) %collective-permute-start.18) | collective-permute-done | bytes 393248 | tf_op jit(solution)/shard_map/ppermute | solution.py:23
  73.3 0.5 shard_map.128.refs_8_.refs_5_
  73.8 0.8 %collective-permute-start.21 = (bf16[128,1024]{1,0:T(8,128)(2,1)S(1)}, bf16[128,1024]{1,0:T(8,128)(2,1)S(1)}, u32[]{:S(2)}, u32[]{:S(2)}) collective-permute-start(bf16[128,1024]{1,0:T(8,128)(2,1)S(1)} %shard_map.128.refs_8_.refs_5_), channel_id=1, source_target_pairs={{0,2},{1,3},{2,0},{3,1},{4,6},{5,7},{6,4},{7,5},{8,10},{9,11},{10,... | collective-permute-start | bytes 786440 | tf_op jit(solution)/shard_map/ppermute | solution.py:23
  74.6 1.5 %collective-permute-start.20 = (bf16[128,1024]{1,0:T(8,128)(2,1)S(1)}, bf16[128,1024]{1,0:T(8,128)(2,1)S(1)}, u32[]{:S(2)}, u32[]{:S(2)}) collective-permute-start(bf16[128,1024]{1,0:T(8,128)(2,1)S(1)} %shard_map.127.refs_3_), channel_id=1, source_target_pairs={{0,1},{1,0},{2,3},{3,2},{4,5},{5,4},{6,7},{7,6},{8,9},{9,8},{10,11... | collective-permute-start | bytes 786440 | tf_op jit(solution)/shard_map/ppermute | solution.py:23
  76.1 0.6 shard_map.130
  76.7 0.8 %collective-permute-done.16.refs_6_ = bf16[128,1024]{1,0:T(8,128)(2,1)S(1)} collective-permute-done((bf16[128,1024]{1,0:T(8,128)(2,1)S(1)}, bf16[128,1024]{1,0:T(8,128)(2,1)S(1)}, u32[]{:S(2)}, u32[]{:S(2)}) %collective-permute-start.16) | collective-permute-done | bytes 262176 | tf_op jit(solution)/shard_map/ppermute | solution.py:23
  77.5 0.0 collective-permute-done.17.refs_7_
  77.5 1.7 %shard_map.129 = (bf16[128,2048]{1,0:T(8,128)(2,1)}, f32[8,128]{1,0:T(8,128)S(1)}) custom-call(bf16[128,2048]{1,0:T(8,128)(2,1)S(1)} %collective-permute-done.refs_0_, f32[8,128]{1,0:T(8,128)S(1)} %get-tuple-element.38.refs_0_.refs_1_, bf16[96,1024]{1,0:T(8,128)(2,1)S(1)} %get-tuple-element.54.refs_2_, ...), custom_call_target="tpu_custom_call" | custom-call | flops 1024 | bytes 1024 | tf_op jit(solution)/shard_map/pallas_call | solution.py:242
  79.2 1.0 %collective-permute-done.21.refs_6_ = bf16[128,1024]{1,0:T(8,128)(2,1)S(1)} collective-permute-done((bf16[128,1024]{1,0:T(8,128)(2,1)S(1)}, bf16[128,1024]{1,0:T(8,128)(2,1)S(1)}, u32[]{:S(2)}, u32[]{:S(2)}) %collective-permute-start.21) | collective-permute-done | bytes 262176 | tf_op jit(solution)/shard_map/ppermute | solution.py:23
  80.2 0.8 collective-permute-done.20.refs_5_
  81.0 0.0 copy-done.2
  81.0 1.3 %shard_map.131 = bf16[128,2048]{1,0:T(8,128)(2,1)} custom-call(bf16[128,2048]{1,0:T(8,128)(2,1)S(1)} %collective-permute-done.3.refs_0_, bf16[128,2048]{1,0:T(8,128)(2,1)S(1)} %bitcast.28, f32[1,2048]{1,0:T(1,128)S(1)} %get-tuple-element.41.refs_1_.refs_2_, f32[128,1024]{1,0:T(8,128)S(1)} %get-tuple-element.71.refs_3_, ...), custom_call_target="tpu_custom_call" | custom-call | flops 1024 | bytes 1024 | tf_op jit(solution)/shard_map/pallas_call | solution.py:242
  (5 shorter events, 0.0 us)
Async XLA Ops:
  0.6 14.6 %collective-permute-start = (bf16[128,2048]{1,0:T(8,128)(2,1)}, bf16[128,2048]{1,0:T(8,128)(2,1)S(1)}, u32[]{:S(2)}, u32[]{:S(2)}) collective-permute-start(bf16[128,2048]{1,0:T(8,128)(2,1)} %bitcast.34), channel_id=1, source_target_pairs={{0,4},{4,8},{8,12},{12,16},{16,20},{20,24},{24,28},{28,0},{1,5},{5... | collective-permute-start | bytes 1572872 | tf_op jit(solution)/shard_map/ppermute | solution.py:17
  1.1 18.4 %collective-permute-start.3 = (bf16[128,2048]{1,0:T(8,128)(2,1)}, bf16[128,2048]{1,0:T(8,128)(2,1)S(1)}, u32[]{:S(2)}, u32[]{:S(2)}) collective-permute-start(bf16[128,2048]{1,0:T(8,128)(2,1)} %bitcast.35), channel_id=1, source_target_pairs={{0,28},{4,0},{8,4},{12,8},{16,12},{20,16},{24,20},{28,24},{1,29},{... | collective-permute-start | bytes 1572872 | tf_op jit(solution)/shard_map/ppermute | solution.py:17
  6.9 13.8 %collective-permute-start.2 = (bf16[240,1024]{1,0:T(8,128)(2,1)S(1)}, bf16[240,1024]{1,0:T(8,128)(2,1)S(1)}, u32[]{:S(2)}, u32[]{:S(2)}) collective-permute-start(bf16[240,1024]{1,0:T(8,128)(2,1)S(1)} %get-tuple-element.40.refs_4_), channel_id=1, source_target_pairs={{0,2},{1,3},{2,0},{3,1},{4,6},{5,7},{6,4},{7,5},{8,10},{9,11},{10,... | collective-permute-start | bytes 1474568 | tf_op jit(solution)/shard_map/ppermute | solution.py:23
  8.9 13.7 %collective-permute-start.1 = (bf16[240,1024]{1,0:T(8,128)(2,1)S(1)}, bf16[240,1024]{1,0:T(8,128)(2,1)S(1)}, u32[]{:S(2)}, u32[]{:S(2)}) collective-permute-start(bf16[240,1024]{1,0:T(8,128)(2,1)S(1)} %get-tuple-element.39.refs_2_.refs_3_), channel_id=1, source_target_pairs={{0,1},{1,0},{2,3},{3,2},{4,5},{5,4},{6,7},{7,6},{8,9},{9,8},{10,11... | collective-permute-start | bytes 1474568 | tf_op jit(solution)/shard_map/ppermute | solution.py:23
  15.2 22.7 %copy-start = (bf16[1,1,2048,1536]{3,2,1,0:T(8,128)(2,1)S(1)}, bf16[1,1,2048,1536]{3,2,1,0:T(8,128)(2,1)}, u32[]{:S(2)}) copy-start(bf16[1,1,2048,1536]{3,2,1,0:T(8,128)(2,1)} %param.18) | copy-start | bytes 18874372
  15.4 10.9 %collective-permute-start.5 = (bf16[128,1024]{1,0:T(8,128)(2,1)S(1)}, bf16[128,1024]{1,0:T(8,128)(2,1)S(1)}, u32[]{:S(2)}, u32[]{:S(2)}) collective-permute-start(bf16[128,1024]{1,0:T(8,128)(2,1)S(1)} %get-tuple-element.46.refs_4_), channel_id=1, source_target_pairs={{0,2},{1,3},{2,0},{3,1},{4,6},{5,7},{6,4},{7,5},{8,10},{9,11},{10,... | collective-permute-start | bytes 786440 | tf_op jit(solution)/shard_map/ppermute | solution.py:23
  18.0 10.3 %collective-permute-start.4 = (bf16[128,1024]{1,0:T(8,128)(2,1)S(1)}, bf16[128,1024]{1,0:T(8,128)(2,1)S(1)}, u32[]{:S(2)}, u32[]{:S(2)}) collective-permute-start(bf16[128,1024]{1,0:T(8,128)(2,1)S(1)} %get-tuple-element.42.refs_1_.refs_3_), channel_id=1, source_target_pairs={{0,1},{1,0},{2,3},{3,2},{4,5},{5,4},{6,7},{7,6},{8,9},{9,8},{10,11... | collective-permute-start | bytes 786440 | tf_op jit(solution)/shard_map/ppermute | solution.py:23
  19.5 12.4 %collective-permute-start.11 = (bf16[128,1024]{1,0:T(8,128)(2,1)S(1)}, bf16[128,1024]{1,0:T(8,128)(2,1)S(1)}, u32[]{:S(2)}, u32[]{:S(2)}) collective-permute-start(bf16[128,1024]{1,0:T(8,128)(2,1)S(1)} %get-tuple-element.51.refs_4_), channel_id=1, source_target_pairs={{0,2},{1,3},{2,0},{3,1},{4,6},{5,7},{6,4},{7,5},{8,10},{9,11},{10,... | collective-permute-start | bytes 786440 | tf_op jit(solution)/shard_map/ppermute | solution.py:23
  20.7 13.2 %collective-permute-start.10 = (bf16[128,1024]{1,0:T(8,128)(2,1)S(1)}, bf16[128,1024]{1,0:T(8,128)(2,1)S(1)}, u32[]{:S(2)}, u32[]{:S(2)}) collective-permute-start(bf16[128,1024]{1,0:T(8,128)(2,1)S(1)} %get-tuple-element.43.refs_2_.refs_4_.refs_3_), channel_id=1, source_target_pairs={{0,1},{1,0},{2,3},{3,2},{4,5},{5,4},{6,7},{7,6},{8,9},{9,8},{10,11... | collective-permute-start | bytes 786440 | tf_op jit(solution)/shard_map/ppermute | solution.py:23
  23.2 14.7 %collective-permute-start.9 = (bf16[96,1024]{1,0:T(8,128)(2,1)S(1)}, bf16[96,1024]{1,0:T(8,128)(2,1)S(1)}, u32[]{:S(2)}, u32[]{:S(2)}) collective-permute-start(bf16[96,1024]{1,0:T(8,128)(2,1)S(1)} %get-tuple-element.50), channel_id=1, source_target_pairs={{0,1},{1,0},{2,3},{3,2},{4,5},{5,4},{6,7},{7,6},{8,9},{9,8},{10,11... | collective-permute-start | bytes 589832 | tf_op jit(solution)/shard_map/ppermute | solution.py:23
  26.4 11.6 %collective-permute-start.8 = (bf16[96,1024]{1,0:T(8,128)(2,1)S(1)}, bf16[96,1024]{1,0:T(8,128)(2,1)S(1)}, u32[]{:S(2)}, u32[]{:S(2)}) collective-permute-start(bf16[96,1024]{1,0:T(8,128)(2,1)S(1)} %get-tuple-element.47.refs_7_), channel_id=1, source_target_pairs={{0,2},{1,3},{2,0},{3,1},{4,6},{5,7},{6,4},{7,5},{8,10},{9,11},{10,... | collective-permute-start | bytes 589832 | tf_op jit(solution)/shard_map/ppermute | solution.py:23
  29.2 17.1 %collective-permute-start.7 = (bf16[192,1024]{1,0:T(8,128)(2,1)S(1)}, bf16[192,1024]{1,0:T(8,128)(2,1)S(1)}, u32[]{:S(2)}, u32[]{:S(2)}) collective-permute-start(bf16[192,1024]{1,0:T(8,128)(2,1)S(1)} %get-tuple-element.49), channel_id=1, source_target_pairs={{0,1},{1,0},{2,3},{3,2},{4,5},{5,4},{6,7},{7,6},{8,9},{9,8},{10,11... | collective-permute-start | bytes 1179656 | tf_op jit(solution)/shard_map/ppermute | solution.py:23
  32.0 14.3 %collective-permute-start.6 = (bf16[192,1024]{1,0:T(8,128)(2,1)S(1)}, bf16[192,1024]{1,0:T(8,128)(2,1)S(1)}, u32[]{:S(2)}, u32[]{:S(2)}) collective-permute-start(bf16[192,1024]{1,0:T(8,128)(2,1)S(1)} %get-tuple-element.48.refs_7_), channel_id=1, source_target_pairs={{0,2},{1,3},{2,0},{3,1},{4,6},{5,7},{6,4},{7,5},{8,10},{9,11},{10,... | collective-permute-start | bytes 1179656 | tf_op jit(solution)/shard_map/ppermute | solution.py:23
  35.1 19.6 %collective-permute-start.15 = (bf16[192,1024]{1,0:T(8,128)(2,1)S(1)}, bf16[192,1024]{1,0:T(8,128)(2,1)S(1)}, u32[]{:S(2)}, u32[]{:S(2)}) collective-permute-start(bf16[192,1024]{1,0:T(8,128)(2,1)S(1)} %get-tuple-element.60), channel_id=1, source_target_pairs={{0,1},{1,0},{2,3},{3,2},{4,5},{5,4},{6,7},{7,6},{8,9},{9,8},{10,11... | collective-permute-start | bytes 1179656 | tf_op jit(solution)/shard_map/ppermute | solution.py:23
  37.9 16.9 %collective-permute-start.14 = (bf16[192,1024]{1,0:T(8,128)(2,1)S(1)}, bf16[192,1024]{1,0:T(8,128)(2,1)S(1)}, u32[]{:S(2)}, u32[]{:S(2)}) collective-permute-start(bf16[192,1024]{1,0:T(8,128)(2,1)S(1)} %get-tuple-element.52.refs_10_), channel_id=1, source_target_pairs={{0,2},{1,3},{2,0},{3,1},{4,6},{5,7},{6,4},{7,5},{8,10},{9,11},{10,... | collective-permute-start | bytes 1179656 | tf_op jit(solution)/shard_map/ppermute | solution.py:23
  37.9 8.4 %copy-start.1 = (bf16[1,1,768,2048]{3,2,1,0:T(8,128)(2,1)S(1)}, bf16[1,1,768,2048]{3,2,1,0:T(8,128)(2,1)}, u32[]{:S(2)}) copy-start(bf16[1,1,768,2048]{3,2,1,0:T(8,128)(2,1)} %param.19) | copy-start | bytes 9437188
  50.2 12.5 %collective-permute-start.12 = (bf16[192,1024]{1,0:T(8,128)(2,1)S(1)}, bf16[192,1024]{1,0:T(8,128)(2,1)S(1)}, u32[]{:S(2)}, u32[]{:S(2)}) collective-permute-start(bf16[192,1024]{1,0:T(8,128)(2,1)S(1)} %get-tuple-element.57), channel_id=1, source_target_pairs={{0,2},{1,3},{2,0},{3,1},{4,6},{5,7},{6,4},{7,5},{8,10},{9,11},{10,... | collective-permute-start | bytes 1179656 | tf_op jit(solution)/shard_map/ppermute | solution.py:23
  51.3 12.8 %collective-permute-start.13 = (bf16[192,1024]{1,0:T(8,128)(2,1)S(1)}, bf16[192,1024]{1,0:T(8,128)(2,1)S(1)}, u32[]{:S(2)}, u32[]{:S(2)}) collective-permute-start(bf16[192,1024]{1,0:T(8,128)(2,1)S(1)} %get-tuple-element.58), channel_id=1, source_target_pairs={{0,1},{1,0},{2,3},{3,2},{4,5},{5,4},{6,7},{7,6},{8,9},{9,8},{10,11... | collective-permute-start | bytes 1179656 | tf_op jit(solution)/shard_map/ppermute | solution.py:23
  59.4 12.1 %collective-permute-start.19 = (bf16[192,1024]{1,0:T(8,128)(2,1)S(1)}, bf16[192,1024]{1,0:T(8,128)(2,1)S(1)}, u32[]{:S(2)}, u32[]{:S(2)}) collective-permute-start(bf16[192,1024]{1,0:T(8,128)(2,1)S(1)} %get-tuple-element.68), channel_id=1, source_target_pairs={{0,2},{1,3},{2,0},{3,1},{4,6},{5,7},{6,4},{7,5},{8,10},{9,11},{10,... | collective-permute-start | bytes 1179656 | tf_op jit(solution)/shard_map/ppermute | solution.py:23
  61.2 12.1 %collective-permute-start.18 = (bf16[192,1024]{1,0:T(8,128)(2,1)S(1)}, bf16[192,1024]{1,0:T(8,128)(2,1)S(1)}, u32[]{:S(2)}, u32[]{:S(2)}) collective-permute-start(bf16[192,1024]{1,0:T(8,128)(2,1)S(1)} %get-tuple-element.66), channel_id=1, source_target_pairs={{0,1},{1,0},{2,3},{3,2},{4,5},{5,4},{6,7},{7,6},{8,9},{9,8},{10,11... | collective-permute-start | bytes 1179656 | tf_op jit(solution)/shard_map/ppermute | solution.py:23
  63.5 14.0 %collective-permute-start.16 = (bf16[128,1024]{1,0:T(8,128)(2,1)S(1)}, bf16[128,1024]{1,0:T(8,128)(2,1)S(1)}, u32[]{:S(2)}, u32[]{:S(2)}) collective-permute-start(bf16[128,1024]{1,0:T(8,128)(2,1)S(1)} %shard_map.125.refs_3_), channel_id=1, source_target_pairs={{0,1},{1,0},{2,3},{3,2},{4,5},{5,4},{6,7},{7,6},{8,9},{9,8},{10,11... | collective-permute-start | bytes 786440 | tf_op jit(solution)/shard_map/ppermute | solution.py:23
  64.9 12.6 %collective-permute-start.17 = (bf16[128,1024]{1,0:T(8,128)(2,1)S(1)}, bf16[128,1024]{1,0:T(8,128)(2,1)S(1)}, u32[]{:S(2)}, u32[]{:S(2)}) collective-permute-start(bf16[128,1024]{1,0:T(8,128)(2,1)S(1)} %shard_map.126.refs_3_), channel_id=1, source_target_pairs={{0,2},{1,3},{2,0},{3,1},{4,6},{5,7},{6,4},{7,5},{8,10},{9,11},{10,... | collective-permute-start | bytes 786440 | tf_op jit(solution)/shard_map/ppermute | solution.py:23
  73.8 6.4 %collective-permute-start.21 = (bf16[128,1024]{1,0:T(8,128)(2,1)S(1)}, bf16[128,1024]{1,0:T(8,128)(2,1)S(1)}, u32[]{:S(2)}, u32[]{:S(2)}) collective-permute-start(bf16[128,1024]{1,0:T(8,128)(2,1)S(1)} %shard_map.128.refs_8_.refs_5_), channel_id=1, source_target_pairs={{0,2},{1,3},{2,0},{3,1},{4,6},{5,7},{6,4},{7,5},{8,10},{9,11},{10,... | collective-permute-start | bytes 786440 | tf_op jit(solution)/shard_map/ppermute | solution.py:23
  74.6 6.4 %collective-permute-start.20 = (bf16[128,1024]{1,0:T(8,128)(2,1)S(1)}, bf16[128,1024]{1,0:T(8,128)(2,1)S(1)}, u32[]{:S(2)}, u32[]{:S(2)}) collective-permute-start(bf16[128,1024]{1,0:T(8,128)(2,1)S(1)} %shard_map.127.refs_3_), channel_id=1, source_target_pairs={{0,1},{1,0},{2,3},{3,2},{4,5},{5,4},{6,7},{7,6},{8,9},{9,8},{10,11... | collective-permute-start | bytes 786440 | tf_op jit(solution)/shard_map/ppermute | solution.py:23
  77.5 3.5 %copy-start.2 = (bf16[1,128,2048]{2,1,0:T(8,128)(2,1)S(1)}, bf16[1,128,2048]{2,1,0:T(8,128)(2,1)}, u32[]{:S(2)}) copy-start(bf16[1,128,2048]{2,1,0:T(8,128)(2,1)} %param.12) | copy-start | bytes 1572868

commit v11 on v10

--- a/solution.py
+++ b/solution.py
@@ -9,6 +9,7 @@
 
 EPS = 1e-06
 VMEM_LIMIT = 32 * 1024 * 1024
+TABLES_COST = 6_000_000_000
 
 
 def passed_along(value, axis, steps):
@@ -637,22 +638,26 @@
     out_ref[:, half:] = (layer_ref[:, half:].astype(jnp.float32) + right).astype(jnp.bfloat16)
 
 
-def hop_bwd_near_kernel(top_count, own, keep_left, keep_right, got_y, got_x, left_ref, right_ref):
+def hop_bwd_near_kernel(
+    top_count, own, keep_left, keep_right, got_y, got_x, sum_x, left_ref, right_ref
+):
     capacity = keep_left.shape[0]
     mine = pick(own[...], 0, capacity, "b", top_count)
     near_y = pick(own[...], 2, capacity, "b", top_count)
     near_x = pick(own[...], 1, capacity, "b", top_count)
-    left_ref[...] = to_tokens(mine, keep_left[...]) + to_tokens(near_y, got_y[:capacity, :])
+    left = to_tokens(mine, keep_left[...]) + to_tokens(near_y, got_y[:capacity, :])
+    left_ref[...] = left + sum_x[...].astype(jnp.float32)
     right_ref[...] = to_tokens(mine, keep_right[...]) + to_tokens(near_x, got_x[:capacity, :])
 
 
-def hop_bwd_end_kernel(grads_ref, saved_ref, gain_ref, left_ref, right_ref, sum_x, sum_y, out_ref):
+def hop_bwd_end_kernel(grads_ref, saved_ref, gain_ref, left_ref, right_ref, sum_y, out_ref):
     features = saved_ref.shape[1]
     half = features // 2
     parts = []
-    for start, near, far in ((0, left_ref, sum_x), (half, right_ref, sum_y)):
+    right = right_ref[...] + sum_y[...].astype(jnp.float32)
+    for start, d_normed in ((0, left_ref[...]), (half, right)):
         wide = saved_ref[:, start : start + half].astype(jnp.float32)
-        scaled = (near[...] + far[...].astype(jnp.float32)) * gain_ref[:, start : start + half]
+        scaled = d_normed * gain_ref[:, start : start + half]
         parts.append((start, wide, scaled))
     square = sum(jnp.sum(wide * wide, axis=-1, keepdims=True) for _, wide, _ in parts)
     inner = sum(jnp.sum(scaled * wide, axis=-1, keepdims=True) for _, wide, scaled in parts)
@@ -763,16 +768,16 @@
         normed_kernel_halves, halves_out, (layer_in, gain_here), one_hop, moved, after=(b_left,)
     )
     f_from_x, f_from_y = crossed(f_left, f_right)
-    g_left, g_right = local_call(split_kernel, halves_out, (grad_in,), 1024, moved, after=(f_left,))
-    g_from_x, g_from_y = crossed(g_left, g_right)
     x_tab, y_tab = local_call(
         functools.partial(tables_kernel, top_count),
         [table_shape] * 2,
         (b_from_x, b_from_y),
+        TABLES_COST,
         1024,
-        1024,
-        after=(g_left,),
-    )
+        after=(f_left,),
+    )
+    g_left, g_right = local_call(split_kernel, halves_out, (grad_in,), 1024, moved, after=(x_tab,))
+    g_from_x, g_from_y = crossed(g_left, g_right)
     tabs = (own, x_tab, y_tab)
     b_to_y, b_to_x = local_call(
         functools.partial(far_kernel, "b", top_count),
@@ -863,18 +868,17 @@
     b_near = local_call(
         functools.partial(hop_bwd_near_kernel, top_count),
         [shaped(tok_rows, half, jnp.float32)] * 2,
-        (own, *b_keep, b_ret_y, b_ret_x),
+        (own, *b_keep, b_ret_y, b_ret_x, b_sum_x),
         one_hop,
         moved,
-        after=(last,),
+        after=(order,),
     )
     bwd_block = local_call(
         hop_bwd_end_kernel,
         shaped(tok_rows, features),
-        (grad_in, saved, gain_here, *b_near, b_sum_x, b_sum_y),
+        (grad_in, saved, gain_here, *b_near, b_sum_y),
         one_hop,
         moved,
-        after=(order,),
     )
     return (fwd_block[None], bwd_block[None])
 

time: 82.5 us -> 82.9 us (level)
    ppermute x20, waiting for transfers between devices: 20.4 us -> 23.1 us  [swapped(): return lax.ppermute(value, axis, pairs)]
    ppermute x2, waiting for transfers between devices: 4.77 us -> 2.47 us  [passed_along(): return lax.ppermute(value, axis, pairs)]
    ppermute x2, starting transfers between devices: 4.61 us -> 3.46 us  [passed_along(): return lax.ppermute(value, axis, pairs)]
    ppermute x20, starting transfers between devices: 27.2 us -> 28.4 us  [swapped(): return lax.ppermute(value, axis, pairs)]
where the time goes in v11:
time: 82.9 us; the launch traced here: 82.7 us
  starting transfers between devices  31.8 us (38%)
  waiting for transfers between devices  25.6 us (31%)
  Pallas kernels  24.5 us (30%)
  between operations  0.83 us (1%)
    ppermute x20, starting transfers between devices, swapped(): return lax.ppermute(value, axis, pairs)  28.4 us
    ppermute x20, waiting for transfers between devices, swapped(): return lax.ppermute(value, axis, pairs)  23.1 us
    pallas_call x18, Pallas kernels, local_call(): pl.pallas_call(body if after else kernel, out_shape=out_shapes, in_specs=...  22.8 us
    ppermute x2, starting transfers between devices, passed_along(): return lax.ppermute(value, axis, pairs)  3.46 us
    ppermute x2, waiting for transfers between devices, passed_along(): return lax.ppermute(value, axis, pairs)  2.47 us
    pallas_call x1, Pallas kernels, per_device_hops(): pl.pallas_call(functools.partial(first_kernel, top_count), out_shape=[sha...  1.68 us
  transfers between devices with their start and end apart: 22, of which 12 were waited for; matrix products, arithmetic and copies ran while one was open for 0% of the time, Pallas kernels for 28%

profile of v11, /device:TPU:0, one launch (start us, length us, event | category | flops | bytes accessed | tf_op | source)
XLA Modules:
  0.0 82.7 jit_solution(4154503210853771920)
XLA Ops:
  0.6 0.5 collective-permute-start
  1.1 1.7 %shard_map.113 = (bf16[240,1024]{1,0:T(8,128)(2,1)S(1)}, bf16[240,1024]{1,0:T(8,128)(2,1)S(1)}, f32[8,128]{1,0:T(8,128)S(1)}, f32[1,2048]{1,0:T(1,128)S(1)}) custom-call(s32[1]{0:T(128)} %bitcast.1.me_ref, bf16[128,2048]{1,0:T(8,128)(2,1)} %bitcast.29, f32[1,2048]{1,0:T(1,128)} %refs_1_.1, s32[2,128]{1,0:T(2,128)} %bitcast.32, f32[2,128]{1,0:T(2,128)} %bitcast.33, ...), custom_call_target="tpu_custom_call" | custom-call | flops 1024 | bytes 1024 | tf_op jit(solution)/shard_map/pallas_call | solution.py:719
  2.8 2.6 %collective-permute-start.2 = (bf16[240,1024]{1,0:T(8,128)(2,1)S(1)}, bf16[240,1024]{1,0:T(8,128)(2,1)S(1)}, u32[]{:S(2)}, u32[]{:S(2)}) collective-permute-start(bf16[240,1024]{1,0:T(8,128)(2,1)S(1)} %get-tuple-element.40.refs_4_), channel_id=1, source_target_pairs={{0,2},{1,3},{2,0},{3,1},{4,6},{5,7},{6,4},{7,5},{8,10},{9,11},{10,... | collective-permute-start | bytes 1474568 | tf_op jit(solution)/shard_map/ppermute | solution.py:24
  5.4 1.5 %collective-permute-start.1 = (bf16[240,1024]{1,0:T(8,128)(2,1)S(1)}, bf16[240,1024]{1,0:T(8,128)(2,1)S(1)}, u32[]{:S(2)}, u32[]{:S(2)}) collective-permute-start(bf16[240,1024]{1,0:T(8,128)(2,1)S(1)} %get-tuple-element.39.refs_2_.refs_3_), channel_id=1, source_target_pairs={{0,1},{1,0},{2,3},{3,2},{4,5},{5,4},{6,7},{7,6},{8,9},{9,8},{10,11... | collective-permute-start | bytes 1474568 | tf_op jit(solution)/shard_map/ppermute | solution.py:24
  6.9 3.0 %collective-permute-start.5 = (bf16[128,2048]{1,0:T(8,128)(2,1)}, bf16[128,2048]{1,0:T(8,128)(2,1)S(1)}, u32[]{:S(2)}, u32[]{:S(2)}) collective-permute-start(bf16[128,2048]{1,0:T(8,128)(2,1)} %bitcast.37), channel_id=1, source_target_pairs={{0,28},{4,0},{8,4},{12,8},{16,12},{20,16},{24,20},{28,24},{1,29},{... | collective-permute-start | bytes 1572872 | tf_op jit(solution)/shard_map/ppermute | solution.py:18
  9.9 2.5 %collective-permute-done.refs_0_ = bf16[128,2048]{1,0:T(8,128)(2,1)S(1)} collective-permute-done((bf16[128,2048]{1,0:T(8,128)(2,1)}, bf16[128,2048]{1,0:T(8,128)(2,1)S(1)}, u32[]{:S(2)}, u32[]{:S(2)}) %collective-permute-start) | collective-permute-done | bytes 524320 | tf_op jit(solution)/shard_map/ppermute | solution.py:18
  12.3 0.2 shard_map.114
  12.6 2.3 %collective-permute-start.4 = (bf16[128,1024]{1,0:T(8,128)(2,1)S(1)}, bf16[128,1024]{1,0:T(8,128)(2,1)S(1)}, u32[]{:S(2)}, u32[]{:S(2)}) collective-permute-start(bf16[128,1024]{1,0:T(8,128)(2,1)S(1)} %get-tuple-element.45.refs_4_), channel_id=1, source_target_pairs={{0,2},{1,3},{2,0},{3,1},{4,6},{5,7},{6,4},{7,5},{8,10},{9,11},{10,... | collective-permute-start | bytes 786440 | tf_op jit(solution)/shard_map/ppermute | solution.py:24
  14.8 2.4 %collective-permute-start.3 = (bf16[128,1024]{1,0:T(8,128)(2,1)S(1)}, bf16[128,1024]{1,0:T(8,128)(2,1)S(1)}, u32[]{:S(2)}, u32[]{:S(2)}) collective-permute-start(bf16[128,1024]{1,0:T(8,128)(2,1)S(1)} %get-tuple-element.42.refs_2_.refs_3_), channel_id=1, source_target_pairs={{0,1},{1,0},{2,3},{3,2},{4,5},{5,4},{6,7},{7,6},{8,9},{9,8},{10,11... | collective-permute-start | bytes 786440 | tf_op jit(solution)/shard_map/ppermute | solution.py:24
  17.3 0.0 collective-permute-done.2.refs_1_.refs_3_.refs_6_
  17.3 1.9 %collective-permute-done.1.refs_0_.refs_2_.refs_5_ = bf16[240,1024]{1,0:T(8,128)(2,1)S(1)} collective-permute-done((bf16[240,1024]{1,0:T(8,128)(2,1)S(1)}, bf16[240,1024]{1,0:T(8,128)(2,1)S(1)}, u32[]{:S(2)}, u32[]{:S(2)}) %collective-permute-start.1) | collective-permute-done | bytes 491552 | tf_op jit(solution)/shard_map/ppermute | solution.py:24
  19.2 0.0 collective-permute-done.5.refs_0_.grads_ref
  19.2 0.1 collective-permute-start.11
  19.3 2.0 %collective-permute-start.10 = (bf16[128,1024]{1,0:T(8,128)(2,1)S(1)}, bf16[128,1024]{1,0:T(8,128)(2,1)S(1)}, u32[]{:S(2)}, u32[]{:S(2)}) collective-permute-start(bf16[128,1024]{1,0:T(8,128)(2,1)S(1)} %get-tuple-element.46.refs_4_.refs_3_), channel_id=1, source_target_pairs={{0,1},{1,0},{2,3},{3,2},{4,5},{5,4},{6,7},{7,6},{8,9},{9,8},{10,11... | collective-permute-start | bytes 786440 | tf_op jit(solution)/shard_map/ppermute | solution.py:24
  21.3 0.5 shard_map.117
  21.8 0.2 collective-permute-start.9
  22.0 0.1 collective-permute-done.4.refs_6_
  22.1 2.4 %collective-permute-start.8 = (bf16[96,1024]{1,0:T(8,128)(2,1)S(1)}, bf16[96,1024]{1,0:T(8,128)(2,1)S(1)}, u32[]{:S(2)}, u32[]{:S(2)}) collective-permute-start(bf16[96,1024]{1,0:T(8,128)(2,1)S(1)} %get-tuple-element.47.refs_7_), channel_id=1, source_target_pairs={{0,2},{1,3},{2,0},{3,1},{4,6},{5,7},{6,4},{7,5},{8,10},{9,11},{10,... | collective-permute-start | bytes 589832 | tf_op jit(solution)/shard_map/ppermute | solution.py:24
  24.5 0.3 collective-permute-done.3.refs_5_
  24.8 0.9 %shard_map.118 = (bf16[192,1024]{1,0:T(8,128)(2,1)S(1)}, bf16[192,1024]{1,0:T(8,128)(2,1)S(1)}) custom-call(f32[8,128]{1,0:T(8,128)S(1)} %get-tuple-element.38.refs_0_.refs_1_, f32[8,128]{1,0:T(8,128)S(1)} %get-tuple-element.43.refs_1_.refs_0_, f32[8,128]{1,0:T(8,128)S(1)} %get-tuple-element.44.refs_1_.refs_2_.refs_0_, ...), custom_call_target="tpu_custom_call" | custom-call | flops 1024 | bytes 1024 | tf_op jit(solution)/shard_map/pallas_call | solution.py:243
  25.7 1.8 %collective-permute-start.7 = (bf16[192,1024]{1,0:T(8,128)(2,1)S(1)}, bf16[192,1024]{1,0:T(8,128)(2,1)S(1)}, u32[]{:S(2)}, u32[]{:S(2)}) collective-permute-start(bf16[192,1024]{1,0:T(8,128)(2,1)S(1)} %get-tuple-element.49), channel_id=1, source_target_pairs={{0,1},{1,0},{2,3},{3,2},{4,5},{5,4},{6,7},{7,6},{8,9},{9,8},{10,11... | collective-permute-start | bytes 1179656 | tf_op jit(solution)/shard_map/ppermute | solution.py:24
  27.5 1.1 %collective-permute-done.11.refs_6_ = bf16[128,1024]{1,0:T(8,128)(2,1)S(1)} collective-permute-done((bf16[128,1024]{1,0:T(8,128)(2,1)S(1)}, bf16[128,1024]{1,0:T(8,128)(2,1)S(1)}, u32[]{:S(2)}, u32[]{:S(2)}) %collective-permute-start.11) | collective-permute-done | bytes 262176 | tf_op jit(solution)/shard_map/ppermute | solution.py:24
  28.6 1.5 %collective-permute-start.6 = (bf16[192,1024]{1,0:T(8,128)(2,1)S(1)}, bf16[192,1024]{1,0:T(8,128)(2,1)S(1)}, u32[]{:S(2)}, u32[]{:S(2)}) collective-permute-start(bf16[192,1024]{1,0:T(8,128)(2,1)S(1)} %get-tuple-element.48.refs_7_), channel_id=1, source_target_pairs={{0,2},{1,3},{2,0},{3,1},{4,6},{5,7},{6,4},{7,5},{8,10},{9,11},{10,... | collective-permute-start | bytes 1179656 | tf_op jit(solution)/shard_map/ppermute | solution.py:24
  30.1 0.3 collective-permute-done.10.refs_5_
  30.4 1.1 %shard_map.119 = (bf16[192,1024]{1,0:T(8,128)(2,1)S(1)}, bf16[192,1024]{1,0:T(8,128)(2,1)S(1)}) custom-call(f32[8,128]{1,0:T(8,128)S(1)} %get-tuple-element.38.refs_0_.refs_1_, f32[8,128]{1,0:T(8,128)S(1)} %get-tuple-element.43.refs_1_.refs_0_, f32[8,128]{1,0:T(8,128)S(1)} %get-tuple-element.44.refs_1_.refs_2_.refs_0_, ...), custom_call_target="tpu_custom_call" | custom-call | flops 1024 | bytes 1024 | tf_op jit(solution)/shard_map/pallas_call | solution.py:243
  31.5 1.8 %collective-permute-start.15 = (bf16[192,1024]{1,0:T(8,128)(2,1)S(1)}, bf16[192,1024]{1,0:T(8,128)(2,1)S(1)}, u32[]{:S(2)}, u32[]{:S(2)}) collective-permute-start(bf16[192,1024]{1,0:T(8,128)(2,1)S(1)} %get-tuple-element.60), channel_id=1, source_target_pairs={{0,1},{1,0},{2,3},{3,2},{4,5},{5,4},{6,7},{7,6},{8,9},{9,8},{10,11... | collective-permute-start | bytes 1179656 | tf_op jit(solution)/shard_map/ppermute | solution.py:24
  33.3 1.3 %collective-permute-done.9.refs_8_ = bf16[96,1024]{1,0:T(8,128)(2,1)S(1)} collective-permute-done((bf16[96,1024]{1,0:T(8,128)(2,1)S(1)}, bf16[96,1024]{1,0:T(8,128)(2,1)S(1)}, u32[]{:S(2)}, u32[]{:S(2)}) %collective-permute-start.9) | collective-permute-done | bytes 196640 | tf_op jit(solution)/shard_map/ppermute | solution.py:24
  34.6 0.2 collective-permute-start.14
  34.8 0.0 collective-permute-done.8.refs_7_
  34.8 0.0 slice-done
  34.8 0.0 slice-done.1
  34.8 0.0 copy-start
  34.8 3.2 %shard_map.120 = (f32[384,768]{1,0:T(8,128)S(1)}, f32[384,768]{1,0:T(8,128)S(1)}) custom-call(f32[8,128]{1,0:T(8,128)S(1)} %get-tuple-element.38.refs_0_.refs_1_, f32[8,128]{1,0:T(8,128)S(1)} %get-tuple-element.43.refs_1_.refs_0_, f32[8,128]{1,0:T(8,128)S(1)} %get-tuple-element.44.refs_1_.refs_2_.refs_0_, ...), custom_call_target="tpu_custom_call" | custom-call | flops 2415919104 | bytes 14155776 | tf_op jit(solution)/shard_map/pallas_call | solution.py:243
  38.1 5.0 %collective-permute-done.7.refs_8_ = bf16[192,1024]{1,0:T(8,128)(2,1)S(1)} collective-permute-done((bf16[192,1024]{1,0:T(8,128)(2,1)S(1)}, bf16[192,1024]{1,0:T(8,128)(2,1)S(1)}, u32[]{:S(2)}, u32[]{:S(2)}) %collective-permute-start.7) | collective-permute-done | bytes 393248 | tf_op jit(solution)/shard_map/ppermute | solution.py:24
  43.0 0.0 collective-permute-done.6.refs_7_
  43.1 3.9 %shard_map.121 = (bf16[96,1024]{1,0:T(8,128)(2,1)S(1)}, bf16[96,1024]{1,0:T(8,128)(2,1)S(1)}, bf16[192,1024]{1,0:T(8,128)(2,1)S(1)}, bf16[384,768]{1,0:T(8,128)(2,1)S(1)}) custom-call(f32[8,128]{1,0:T(8,128)S(1)} %get-tuple-element.38.refs_0_.refs_1_, f32[8,128]{1,0:T(8,128)S(1)} %get-tuple-element.43.refs_1_.refs_0_, ...), custom_call_target="tpu_custom_call" | custom-call | flops 3019898880 | bytes 14155776 | tf_op jit(solution)/shard_map/pallas_call | solution.py:243
  46.9 0.2 collective-permute-start.12
  47.2 0.8 shard_map.122
  48.0 1.9 %collective-permute-start.13 = (bf16[192,1024]{1,0:T(8,128)(2,1)S(1)}, bf16[192,1024]{1,0:T(8,128)(2,1)S(1)}, u32[]{:S(2)}, u32[]{:S(2)}) collective-permute-start(bf16[192,1024]{1,0:T(8,128)(2,1)S(1)} %get-tuple-element.58), channel_id=1, source_target_pairs={{0,1},{1,0},{2,3},{3,2},{4,5},{5,4},{6,7},{7,6},{8,9},{9,8},{10,11... | collective-permute-start | bytes 1179656 | tf_op jit(solution)/shard_map/ppermute | solution.py:24
  49.9 1.6 %collective-permute-done.15.refs_8_ = bf16[192,1024]{1,0:T(8,128)(2,1)S(1)} collective-permute-done((bf16[192,1024]{1,0:T(8,128)(2,1)S(1)}, bf16[192,1024]{1,0:T(8,128)(2,1)S(1)}, u32[]{:S(2)}, u32[]{:S(2)}) %collective-permute-start.15) | collective-permute-done | bytes 393248 | tf_op jit(solution)/shard_map/ppermute | solution.py:24
  51.5 0.0 collective-permute-done.14.refs_7_
  51.5 4.7 %shard_map.123 = (bf16[96,1024]{1,0:T(8,128)(2,1)S(1)}, bf16[96,1024]{1,0:T(8,128)(2,1)S(1)}, bf16[192,1024]{1,0:T(8,128)(2,1)S(1)}, bf16[384,1536]{1,0:T(8,128)(2,1)S(1)}) custom-call(f32[8,128]{1,0:T(8,128)S(1)} %get-tuple-element.38.refs_0_.refs_1_, f32[8,128]{1,0:T(8,128)S(1)} %get-tuple-element.43.refs_1_.refs_0_, ...), custom_call_target="tpu_custom_call" | custom-call | flops 2415919104 | bytes 14155776 | tf_op jit(solution)/shard_map/pallas_call | solution.py:243
  56.2 0.2 collective-permute-start.19
  56.4 1.4 %shard_map.124 = (bf16[96,1024]{1,0:T(8,128)(2,1)S(1)}, bf16[96,1024]{1,0:T(8,128)(2,1)S(1)}, bf16[192,1024]{1,0:T(8,128)(2,1)S(1)}) custom-call(bf16[384,1536]{1,0:T(8,128)(2,1)S(1)} %get-tuple-element.62.both_ref, bf16[2048,1536]{1,0:T(8,128)(2,1)S(1)} %bitcast.25), custom_call_target="tpu_custom_call" | custom-call | flops 1024 | bytes 1024 | tf_op jit(solution)/shard_map/pallas_call | solution.py:243
  57.8 1.9 %collective-permute-start.18 = (bf16[192,1024]{1,0:T(8,128)(2,1)S(1)}, bf16[192,1024]{1,0:T(8,128)(2,1)S(1)}, u32[]{:S(2)}, u32[]{:S(2)}) collective-permute-start(bf16[192,1024]{1,0:T(8,128)(2,1)S(1)} %get-tuple-element.66), channel_id=1, source_target_pairs={{0,1},{1,0},{2,3},{3,2},{4,5},{5,4},{6,7},{7,6},{8,9},{9,8},{10,11... | collective-permute-start | bytes 1179656 | tf_op jit(solution)/shard_map/ppermute | solution.py:24
  59.7 0.0 collective-permute-done.12.refs_2_.refs_4_
  59.7 0.8 shard_map.125.refs_3_
  60.5 0.5 collective-permute-start.16
  61.1 0.0 collective-permute-done.13.refs_2_.refs_5_
  61.1 0.8 shard_map.126.refs_3_
  61.9 1.6 %collective-permute-start.17 = (bf16[128,1024]{1,0:T(8,128)(2,1)S(1)}, bf16[128,1024]{1,0:T(8,128)(2,1)S(1)}, u32[]{:S(2)}, u32[]{:S(2)}) collective-permute-start(bf16[128,1024]{1,0:T(8,128)(2,1)S(1)} %shard_map.126.refs_3_), channel_id=1, source_target_pairs={{0,2},{1,3},{2,0},{3,1},{4,6},{5,7},{6,4},{7,5},{8,10},{9,11},{10,... | collective-permute-start | bytes 786440 | tf_op jit(solution)/shard_map/ppermute | solution.py:24
  63.5 4.6 %collective-permute-done.19.refs_2_.refs_3_ = bf16[192,1024]{1,0:T(8,128)(2,1)S(1)} collective-permute-done((bf16[192,1024]{1,0:T(8,128)(2,1)S(1)}, bf16[192,1024]{1,0:T(8,128)(2,1)S(1)}, u32[]{:S(2)}, u32[]{:S(2)}) %collective-permute-start.19) | collective-permute-done | bytes 393248 | tf_op jit(solution)/shard_map/ppermute | solution.py:24
  68.1 0.4 shard_map.127.refs_3_
  68.6 1.9 %collective-permute-start.20 = (bf16[128,1024]{1,0:T(8,128)(2,1)S(1)}, bf16[128,1024]{1,0:T(8,128)(2,1)S(1)}, u32[]{:S(2)}, u32[]{:S(2)}) collective-permute-start(bf16[128,1024]{1,0:T(8,128)(2,1)S(1)} %shard_map.127.refs_3_), channel_id=1, source_target_pairs={{0,1},{1,0},{2,3},{3,2},{4,5},{5,4},{6,7},{7,6},{8,9},{9,8},{10,11... | collective-permute-start | bytes 786440 | tf_op jit(solution)/shard_map/ppermute | solution.py:24
  70.5 0.0 collective-permute-done.18.refs_2_.refs_4_
  70.5 0.5 shard_map.128.refs_8_
  70.9 1.3 %collective-permute-start.21 = (bf16[128,1024]{1,0:T(8,128)(2,1)S(1)}, bf16[128,1024]{1,0:T(8,128)(2,1)S(1)}, u32[]{:S(2)}, u32[]{:S(2)}) collective-permute-start(bf16[128,1024]{1,0:T(8,128)(2,1)S(1)} %shard_map.128.refs_8_), channel_id=1, source_target_pairs={{0,2},{1,3},{2,0},{3,1},{4,6},{5,7},{6,4},{7,5},{8,10},{9,11},{10,... | collective-permute-start | bytes 786440 | tf_op jit(solution)/shard_map/ppermute | solution.py:24
  72.2 3.3 %collective-permute-done.16.refs_6_ = bf16[128,1024]{1,0:T(8,128)(2,1)S(1)} collective-permute-done((bf16[128,1024]{1,0:T(8,128)(2,1)S(1)}, bf16[128,1024]{1,0:T(8,128)(2,1)S(1)}, u32[]{:S(2)}, u32[]{:S(2)}) %collective-permute-start.16) | collective-permute-done | bytes 262176 | tf_op jit(solution)/shard_map/ppermute | solution.py:24
  75.5 0.0 collective-permute-done.17.refs_7_
  75.5 1.7 %shard_map.129 = (bf16[128,2048]{1,0:T(8,128)(2,1)}, f32[8,128]{1,0:T(8,128)S(1)}) custom-call(bf16[128,2048]{1,0:T(8,128)(2,1)S(1)} %collective-permute-done.refs_0_, f32[8,128]{1,0:T(8,128)S(1)} %get-tuple-element.38.refs_0_.refs_1_, bf16[96,1024]{1,0:T(8,128)(2,1)S(1)} %get-tuple-element.54.refs_2_, ...), custom_call_target="tpu_custom_call" | custom-call | flops 1024 | bytes 1024 | tf_op jit(solution)/shard_map/pallas_call | solution.py:243
  77.2 3.6 %collective-permute-done.20.refs_5_ = bf16[128,1024]{1,0:T(8,128)(2,1)S(1)} collective-permute-done((bf16[128,1024]{1,0:T(8,128)(2,1)S(1)}, bf16[128,1024]{1,0:T(8,128)(2,1)S(1)}, u32[]{:S(2)}, u32[]{:S(2)}) %collective-permute-start.20) | collective-permute-done | bytes 262176 | tf_op jit(solution)/shard_map/ppermute | solution.py:24
  80.8 0.6 shard_map.130
  81.4 0.0 collective-permute-done.21.sum_y
  81.4 1.3 %shard_map.131 = bf16[128,2048]{1,0:T(8,128)(2,1)} custom-call(bf16[128,2048]{1,0:T(8,128)(2,1)S(1)} %collective-permute-done.5.refs_0_.grads_ref, bf16[128,2048]{1,0:T(8,128)(2,1)S(1)} %bitcast.30, f32[1,2048]{1,0:T(1,128)S(1)} %get-tuple-element.41.refs_1_.gain_ref, f32[128,1024]{1,0:T(8,128)S(1)} %get-tuple-element.72.left_ref, ...), custom_call_target="tpu_custom_call" | custom-call | flops 1024 | bytes 1024 | tf_op jit(solution)/shard_map/pallas_call | solution.py:243
  (8 shorter events, 0.1 us)
Async XLA Ops:
  0.6 11.7 %collective-permute-start = (bf16[128,2048]{1,0:T(8,128)(2,1)}, bf16[128,2048]{1,0:T(8,128)(2,1)S(1)}, u32[]{:S(2)}, u32[]{:S(2)}) collective-permute-start(bf16[128,2048]{1,0:T(8,128)(2,1)} %bitcast.36), channel_id=1, source_target_pairs={{0,4},{4,8},{8,12},{12,16},{16,20},{20,24},{24,28},{28,0},{1,5},{5... | collective-permute-start | bytes 1572872 | tf_op jit(solution)/shard_map/ppermute | solution.py:18
  2.8 14.5 %collective-permute-start.2 = (bf16[240,1024]{1,0:T(8,128)(2,1)S(1)}, bf16[240,1024]{1,0:T(8,128)(2,1)S(1)}, u32[]{:S(2)}, u32[]{:S(2)}) collective-permute-start(bf16[240,1024]{1,0:T(8,128)(2,1)S(1)} %get-tuple-element.40.refs_4_), channel_id=1, source_target_pairs={{0,2},{1,3},{2,0},{3,1},{4,6},{5,7},{6,4},{7,5},{8,10},{9,11},{10,... | collective-permute-start | bytes 1474568 | tf_op jit(solution)/shard_map/ppermute | solution.py:24
  5.4 13.8 %collective-permute-start.1 = (bf16[240,1024]{1,0:T(8,128)(2,1)S(1)}, bf16[240,1024]{1,0:T(8,128)(2,1)S(1)}, u32[]{:S(2)}, u32[]{:S(2)}) collective-permute-start(bf16[240,1024]{1,0:T(8,128)(2,1)S(1)} %get-tuple-element.39.refs_2_.refs_3_), channel_id=1, source_target_pairs={{0,1},{1,0},{2,3},{3,2},{4,5},{5,4},{6,7},{7,6},{8,9},{9,8},{10,11... | collective-permute-start | bytes 1474568 | tf_op jit(solution)/shard_map/ppermute | solution.py:24
  6.9 12.3 %collective-permute-start.5 = (bf16[128,2048]{1,0:T(8,128)(2,1)}, bf16[128,2048]{1,0:T(8,128)(2,1)S(1)}, u32[]{:S(2)}, u32[]{:S(2)}) collective-permute-start(bf16[128,2048]{1,0:T(8,128)(2,1)} %bitcast.37), channel_id=1, source_target_pairs={{0,28},{4,0},{8,4},{12,8},{16,12},{20,16},{24,20},{28,24},{1,29},{... | collective-permute-start | bytes 1572872 | tf_op jit(solution)/shard_map/ppermute | solution.py:18
  12.3 22.5 %slice-start = ((s8[6291456]{0:T(1024)(128)(4,1)}), s8[4194304]{0:T(1024)(128)(4,1)S(1)}, s32[]{:S(2)}) async-start(s8[6291456]{0:T(1024)(128)(4,1)} %bitcast.20), calls=%async_computation | async-start | bytes 8388608
  12.6 9.5 %collective-permute-start.4 = (bf16[128,1024]{1,0:T(8,128)(2,1)S(1)}, bf16[128,1024]{1,0:T(8,128)(2,1)S(1)}, u32[]{:S(2)}, u32[]{:S(2)}) collective-permute-start(bf16[128,1024]{1,0:T(8,128)(2,1)S(1)} %get-tuple-element.45.refs_4_), channel_id=1, source_target_pairs={{0,2},{1,3},{2,0},{3,1},{4,6},{5,7},{6,4},{7,5},{8,10},{9,11},{10,... | collective-permute-start | bytes 786440 | tf_op jit(solution)/shard_map/ppermute | solution.py:24
  14.8 20.0 %slice-start.1 = ((s8[6291456]{0:T(1024)(128)(4,1)}), s8[2097152]{0:T(1024)(128)(4,1)S(1)}, s32[]{:S(2)}) async-start(s8[6291456]{0:T(1024)(128)(4,1)} %bitcast.20), calls=%async_computation.1 | async-start | bytes 4194304
  14.8 10.0 %collective-permute-start.3 = (bf16[128,1024]{1,0:T(8,128)(2,1)S(1)}, bf16[128,1024]{1,0:T(8,128)(2,1)S(1)}, u32[]{:S(2)}, u32[]{:S(2)}) collective-permute-start(bf16[128,1024]{1,0:T(8,128)(2,1)S(1)} %get-tuple-element.42.refs_2_.refs_3_), channel_id=1, source_target_pairs={{0,1},{1,0},{2,3},{3,2},{4,5},{5,4},{6,7},{7,6},{8,9},{9,8},{10,11... | collective-permute-start | bytes 786440 | tf_op jit(solution)/shard_map/ppermute | solution.py:24
  19.2 9.3 %collective-permute-start.11 = (bf16[128,1024]{1,0:T(8,128)(2,1)S(1)}, bf16[128,1024]{1,0:T(8,128)(2,1)S(1)}, u32[]{:S(2)}, u32[]{:S(2)}) collective-permute-start(bf16[128,1024]{1,0:T(8,128)(2,1)S(1)} %get-tuple-element.51.refs_4_), channel_id=1, source_target_pairs={{0,2},{1,3},{2,0},{3,1},{4,6},{5,7},{6,4},{7,5},{8,10},{9,11},{10,... | collective-permute-start | bytes 786440 | tf_op jit(solution)/shard_map/ppermute | solution.py:24
  19.3 11.1 %collective-permute-start.10 = (bf16[128,1024]{1,0:T(8,128)(2,1)S(1)}, bf16[128,1024]{1,0:T(8,128)(2,1)S(1)}, u32[]{:S(2)}, u32[]{:S(2)}) collective-permute-start(bf16[128,1024]{1,0:T(8,128)(2,1)S(1)} %get-tuple-element.46.refs_4_.refs_3_), channel_id=1, source_target_pairs={{0,1},{1,0},{2,3},{3,2},{4,5},{5,4},{6,7},{7,6},{8,9},{9,8},{10,11... | collective-permute-start | bytes 786440 | tf_op jit(solution)/shard_map/ppermute | solution.py:24
  21.8 12.8 %collective-permute-start.9 = (bf16[96,1024]{1,0:T(8,128)(2,1)S(1)}, bf16[96,1024]{1,0:T(8,128)(2,1)S(1)}, u32[]{:S(2)}, u32[]{:S(2)}) collective-permute-start(bf16[96,1024]{1,0:T(8,128)(2,1)S(1)} %get-tuple-element.50), channel_id=1, source_target_pairs={{0,1},{1,0},{2,3},{3,2},{4,5},{5,4},{6,7},{7,6},{8,9},{9,8},{10,11... | collective-permute-start | bytes 589832 | tf_op jit(solution)/shard_map/ppermute | solution.py:24
  22.1 12.7 %collective-permute-start.8 = (bf16[96,1024]{1,0:T(8,128)(2,1)S(1)}, bf16[96,1024]{1,0:T(8,128)(2,1)S(1)}, u32[]{:S(2)}, u32[]{:S(2)}) collective-permute-start(bf16[96,1024]{1,0:T(8,128)(2,1)S(1)} %get-tuple-element.47.refs_7_), channel_id=1, source_target_pairs={{0,2},{1,3},{2,0},{3,1},{4,6},{5,7},{6,4},{7,5},{8,10},{9,11},{10,... | collective-permute-start | bytes 589832 | tf_op jit(solution)/shard_map/ppermute | solution.py:24
  25.7 17.4 %collective-permute-start.7 = (bf16[192,1024]{1,0:T(8,128)(2,1)S(1)}, bf16[192,1024]{1,0:T(8,128)(2,1)S(1)}, u32[]{:S(2)}, u32[]{:S(2)}) collective-permute-start(bf16[192,1024]{1,0:T(8,128)(2,1)S(1)} %get-tuple-element.49), channel_id=1, source_target_pairs={{0,1},{1,0},{2,3},{3,2},{4,5},{5,4},{6,7},{7,6},{8,9},{9,8},{10,11... | collective-permute-start | bytes 1179656 | tf_op jit(solution)/shard_map/ppermute | solution.py:24
  28.6 14.5 %collective-permute-start.6 = (bf16[192,1024]{1,0:T(8,128)(2,1)S(1)}, bf16[192,1024]{1,0:T(8,128)(2,1)S(1)}, u32[]{:S(2)}, u32[]{:S(2)}) collective-permute-start(bf16[192,1024]{1,0:T(8,128)(2,1)S(1)} %get-tuple-element.48.refs_7_), channel_id=1, source_target_pairs={{0,2},{1,3},{2,0},{3,1},{4,6},{5,7},{6,4},{7,5},{8,10},{9,11},{10,... | collective-permute-start | bytes 1179656 | tf_op jit(solution)/shard_map/ppermute | solution.py:24
  31.5 19.9 %collective-permute-start.15 = (bf16[192,1024]{1,0:T(8,128)(2,1)S(1)}, bf16[192,1024]{1,0:T(8,128)(2,1)S(1)}, u32[]{:S(2)}, u32[]{:S(2)}) collective-permute-start(bf16[192,1024]{1,0:T(8,128)(2,1)S(1)} %get-tuple-element.60), channel_id=1, source_target_pairs={{0,1},{1,0},{2,3},{3,2},{4,5},{5,4},{6,7},{7,6},{8,9},{9,8},{10,11... | collective-permute-start | bytes 1179656 | tf_op jit(solution)/shard_map/ppermute | solution.py:24
  34.6 16.9 %collective-permute-start.14 = (bf16[192,1024]{1,0:T(8,128)(2,1)S(1)}, bf16[192,1024]{1,0:T(8,128)(2,1)S(1)}, u32[]{:S(2)}, u32[]{:S(2)}) collective-permute-start(bf16[192,1024]{1,0:T(8,128)(2,1)S(1)} %get-tuple-element.52.refs_10_), channel_id=1, source_target_pairs={{0,2},{1,3},{2,0},{3,1},{4,6},{5,7},{6,4},{7,5},{8,10},{9,11},{10,... | collective-permute-start | bytes 1179656 | tf_op jit(solution)/shard_map/ppermute | solution.py:24
  34.8 8.2 %copy-start = (bf16[1,1,768,2048]{3,2,1,0:T(8,128)(2,1)S(1)}, bf16[1,1,768,2048]{3,2,1,0:T(8,128)(2,1)}, u32[]{:S(2)}) copy-start(bf16[1,1,768,2048]{3,2,1,0:T(8,128)(2,1)} %param.19) | copy-start | bytes 9437188
  46.9 12.8 %collective-permute-start.12 = (bf16[192,1024]{1,0:T(8,128)(2,1)S(1)}, bf16[192,1024]{1,0:T(8,128)(2,1)S(1)}, u32[]{:S(2)}, u32[]{:S(2)}) collective-permute-start(bf16[192,1024]{1,0:T(8,128)(2,1)S(1)} %get-tuple-element.57), channel_id=1, source_target_pairs={{0,2},{1,3},{2,0},{3,1},{4,6},{5,7},{6,4},{7,5},{8,10},{9,11},{10,... | collective-permute-start | bytes 1179656 | tf_op jit(solution)/shard_map/ppermute | solution.py:24
  48.0 13.1 %collective-permute-start.13 = (bf16[192,1024]{1,0:T(8,128)(2,1)S(1)}, bf16[192,1024]{1,0:T(8,128)(2,1)S(1)}, u32[]{:S(2)}, u32[]{:S(2)}) collective-permute-start(bf16[192,1024]{1,0:T(8,128)(2,1)S(1)} %get-tuple-element.58), channel_id=1, source_target_pairs={{0,1},{1,0},{2,3},{3,2},{4,5},{5,4},{6,7},{7,6},{8,9},{9,8},{10,11... | collective-permute-start | bytes 1179656 | tf_op jit(solution)/shard_map/ppermute | solution.py:24
  56.2 12.0 %collective-permute-start.19 = (bf16[192,1024]{1,0:T(8,128)(2,1)S(1)}, bf16[192,1024]{1,0:T(8,128)(2,1)S(1)}, u32[]{:S(2)}, u32[]{:S(2)}) collective-permute-start(bf16[192,1024]{1,0:T(8,128)(2,1)S(1)} %get-tuple-element.68), channel_id=1, source_target_pairs={{0,2},{1,3},{2,0},{3,1},{4,6},{5,7},{6,4},{7,5},{8,10},{9,11},{10,... | collective-permute-start | bytes 1179656 | tf_op jit(solution)/shard_map/ppermute | solution.py:24
  57.8 12.6 %collective-permute-start.18 = (bf16[192,1024]{1,0:T(8,128)(2,1)S(1)}, bf16[192,1024]{1,0:T(8,128)(2,1)S(1)}, u32[]{:S(2)}, u32[]{:S(2)}) collective-permute-start(bf16[192,1024]{1,0:T(8,128)(2,1)S(1)} %get-tuple-element.66), channel_id=1, source_target_pairs={{0,1},{1,0},{2,3},{3,2},{4,5},{5,4},{6,7},{7,6},{8,9},{9,8},{10,11... | collective-permute-start | bytes 1179656 | tf_op jit(solution)/shard_map/ppermute | solution.py:24
  60.5 15.0 %collective-permute-start.16 = (bf16[128,1024]{1,0:T(8,128)(2,1)S(1)}, bf16[128,1024]{1,0:T(8,128)(2,1)S(1)}, u32[]{:S(2)}, u32[]{:S(2)}) collective-permute-start(bf16[128,1024]{1,0:T(8,128)(2,1)S(1)} %shard_map.125.refs_3_), channel_id=1, source_target_pairs={{0,1},{1,0},{2,3},{3,2},{4,5},{5,4},{6,7},{7,6},{8,9},{9,8},{10,11... | collective-permute-start | bytes 786440 | tf_op jit(solution)/shard_map/ppermute | solution.py:24
  61.9 13.7 %collective-permute-start.17 = (bf16[128,1024]{1,0:T(8,128)(2,1)S(1)}, bf16[128,1024]{1,0:T(8,128)(2,1)S(1)}, u32[]{:S(2)}, u32[]{:S(2)}) collective-permute-start(bf16[128,1024]{1,0:T(8,128)(2,1)S(1)} %shard_map.126.refs_3_), channel_id=1, source_target_pairs={{0,2},{1,3},{2,0},{3,1},{4,6},{5,7},{6,4},{7,5},{8,10},{9,11},{10,... | collective-permute-start | bytes 786440 | tf_op jit(solution)/shard_map/ppermute | solution.py:24
  68.6 12.2 %collective-permute-start.20 = (bf16[128,1024]{1,0:T(8,128)(2,1)S(1)}, bf16[128,1024]{1,0:T(8,128)(2,1)S(1)}, u32[]{:S(2)}, u32[]{:S(2)}) collective-permute-start(bf16[128,1024]{1,0:T(8,128)(2,1)S(1)} %shard_map.127.refs_3_), channel_id=1, source_target_pairs={{0,1},{1,0},{2,3},{3,2},{4,5},{5,4},{6,7},{7,6},{8,9},{9,8},{10,11... | collective-permute-start | bytes 786440 | tf_op jit(solution)/shard_map/ppermute | solution.py:24
  70.9 10.5 %collective-permute-start.21 = (bf16[128,1024]{1,0:T(8,128)(2,1)S(1)}, bf16[128,1024]{1,0:T(8,128)(2,1)S(1)}, u32[]{:S(2)}, u32[]{:S(2)}) collective-permute-start(bf16[128,1024]{1,0:T(8,128)(2,1)S(1)} %shard_map.128.refs_8_), channel_id=1, source_target_pairs={{0,2},{1,3},{2,0},{3,1},{4,6},{5,7},{6,4},{7,5},{8,10},{9,11},{10,... | collective-permute-start | bytes 786440 | tf_op jit(solution)/shard_map/ppermute | solution.py:24
  77.2 4.2 %copy-start.1 = (bf16[1,128,2048]{2,1,0:T(8,128)(2,1)S(1)}, bf16[1,128,2048]{2,1,0:T(8,128)(2,1)}, u32[]{:S(2)}) copy-start(bf16[1,128,2048]{2,1,0:T(8,128)(2,1)} %param.12) | copy-start | bytes 1572868

commit v12 on v11

--- a/solution.py
+++ b/solution.py
@@ -506,6 +506,29 @@
     rows[3 * capacity :, half:] = got_x[-capacity:, :]
 
 
+def near_kernel(
+    kind, top_count, own, x_tab, y_tab, left, right, from_x, from_y, mine_ref, x_left, y_right
+):
+    capacity, half = x_left.shape
+    tok_rows = own.shape[1]
+    mine = pick(own[...], 0, capacity, kind, top_count)
+    mine_ref[:, :half] = to_slots(mine, left[:tok_rows, :])
+    mine_ref[:, half:] = to_slots(mine, right[:tok_rows, :])
+    x_left[...] = to_slots(pick(x_tab[...], 1, capacity, kind, top_count), from_x[:tok_rows, :])
+    y_right[...] = to_slots(pick(y_tab[...], 2, capacity, kind, top_count), from_y[:tok_rows, :])
+
+
+def gathered_rows(mine, x_left, y_right, got_y, got_x, rows):
+    capacity, half = x_left.shape
+    rows[:capacity, :] = mine[...]
+    rows[capacity : 2 * capacity, :half] = x_left[...]
+    rows[capacity : 2 * capacity, half:] = got_x[:capacity, :]
+    rows[2 * capacity : 3 * capacity, :half] = got_y[:capacity, :]
+    rows[2 * capacity : 3 * capacity, half:] = y_right[...]
+    rows[3 * capacity :, :half] = got_y[capacity:, :]
+    rows[3 * capacity :, half:] = got_x[capacity:, :]
+
+
 def hand_out(out, at, capacity, to_left, keep, near, onward):
     size = out.shape[1]
     rows = out.astype(jnp.bfloat16)
@@ -564,12 +587,12 @@
         )
 
 
-def hop_fwd_kernel(top_count, *refs):
-    dispatch, refs = refs[:9], refs[9:]
+def hop_fwd_kernel(*refs):
+    dispatch, refs = refs[:5], refs[5:]
     weight_in, weight_out = refs[:2]
     outs, hidden_ref, rows_ref = refs[2:5], refs[5], refs[6]
     hidden_units = weight_out.shape[0]
-    assemble("f", top_count, *dispatch, rows_ref)
+    gathered_rows(*dispatch, rows_ref)
     for start, size in tiles(hidden_units, 256):
         gate = jnp.dot(
             rows_ref[...], weight_in[:, start : start + size], preferred_element_type=jnp.float32
@@ -585,12 +608,12 @@
     fwd_half(hidden_ref, weight_out, True, *outs)
 
 
-def hop_bwd_kernel(top_count, *refs):
-    dispatch, refs = refs[:9], refs[9:]
+def hop_bwd_kernel(*refs):
+    dispatch, refs = refs[:5], refs[5:]
     gate_ref, up_ref, weight_in, weight_out = refs[:4]
     outs, both_ref, grads_ref = refs[4:7], refs[7], refs[8]
     hidden_units = weight_out.shape[0]
-    assemble("bg", top_count, *dispatch, grads_ref)
+    gathered_rows(*dispatch, grads_ref)
     for start, size in tiles(hidden_units, 256):
         gate = gate_ref[:, start : start + size]
         up = up_ref[:, start : start + size]
@@ -789,7 +812,6 @@
     )
     b_got_y, b_got_x = swapped(b_to_y, "expert", 2), swapped(b_to_x, "expert", 1)
     f_got_y, f_got_x, f_to_y = onward("f", (f_left, f_right), (f_from_x, f_from_y), (b_to_y,))
-    g_got_y, g_got_x, g_to_y = onward("bg", (g_left, g_right), (g_from_x, g_from_y), (f_to_y,))
     gate_pre, up_pre = local_call(
         functools.partial(hop_again_kernel, top_count),
         [shaped(slot_total, hidden_units, jnp.float32)] * 2,
@@ -797,16 +819,34 @@
         2 * expert_flops,
         expert_moved,
         scratch=(rows_scratch,),
+        after=(f_to_y,),
+    )
+    g_got_y, g_got_x, g_to_y = onward("bg", (g_left, g_right), (g_from_x, g_from_y), (gate_pre,))
+    near_out = [shaped(capacity, features), shaped(capacity, half), shaped(capacity, half)]
+    g_near = local_call(
+        functools.partial(near_kernel, "bg", top_count),
+        near_out,
+        (*tabs, g_left, g_right, g_from_x, g_from_y),
+        one_hop,
+        moved,
         after=(g_to_y,),
     )
+    f_near = local_call(
+        functools.partial(near_kernel, "f", top_count),
+        near_out,
+        (*tabs, f_left, f_right, f_from_x, f_from_y),
+        one_hop,
+        moved,
+        after=(g_near[1],),
+    )
     f_keep_l, f_near_l, f_on_l, hidden = local_call(
-        functools.partial(hop_fwd_kernel, top_count),
+        hop_fwd_kernel,
         half_out + [hidden_shape],
-        (*tabs, f_left, f_right, f_from_x, f_from_y, f_got_y, f_got_x, weight_in, weight_out),
+        (*f_near, f_got_y, f_got_x, weight_in, weight_out),
         5 * expert_flops // 2,
         expert_moved,
         scratch=(rows_scratch,),
-        after=(gate_pre,),
+        after=(f_near[1],),
     )
     f_ret_y = swapped(f_on_l, "expert", 2)
     f_keep_r, f_near_r, f_on_r = local_call(
@@ -814,21 +854,9 @@
     )
     f_ret_x = swapped(f_on_r, "expert", 1)
     b_keep_l, b_near_l, b_on_l, both = local_call(
-        functools.partial(hop_bwd_kernel, top_count),
+        hop_bwd_kernel,
         half_out + [both_shape],
-        (
-            *tabs,
-            g_left,
-            g_right,
-            g_from_x,
-            g_from_y,
-            g_got_y,
-            g_got_x,
-            gate_pre,
-            up_pre,
-            weight_in,
-            weight_out,
-        ),
+        (*g_near, g_got_y, g_got_x, gate_pre, up_pre, weight_in, weight_out),
         2 * expert_flops,
         expert_moved,
         scratch=(rows_scratch,),

time: 82.9 us -> 86.8 us (1.047)
  waiting for transfers between devices: 25.6 us -> 30.9 us
  starting transfers between devices: 31.8 us -> 30.3 us
    ppermute x20, waiting for transfers between devices: 23.1 us -> 28.4 us  [swapped(): return lax.ppermute(value, axis, pairs)]
    ppermute x20, starting transfers between devices: 28.4 us -> 26.8 us  [swapped(): return lax.ppermute(value, axis, pairs)]
    pallas_call x18 -> x20, Pallas kernels: 22.8 us -> 22.9 us  [local_call(): pl.pallas_call(body if after else kernel, out_shape=out_shapes, in_specs=...]
  transfers between devices with their start and end apart: 22 -> 22, of which waited for: 12 -> 13; matrix products, arithmetic and copies ran while one was open for 0% -> 0% of each run, Pallas kernels for 28% -> 27%
where the time goes in v12:
time: 86.8 us; the launch traced here: 86.7 us
  waiting for transfers between devices  30.9 us (36%)
  starting transfers between devices  30.3 us (35%)
  Pallas kernels  24.6 us (28%)
    ppermute x20, waiting for transfers between devices, swapped(): return lax.ppermute(value, axis, pairs)  28.4 us
    ppermute x20, starting transfers between devices, swapped(): return lax.ppermute(value, axis, pairs)  26.8 us
    pallas_call x20, Pallas kernels, local_call(): pl.pallas_call(body if after else kernel, out_shape=out_shapes, in_specs=...  22.9 us
    ppermute x2, starting transfers between devices, passed_along(): return lax.ppermute(value, axis, pairs)  3.46 us
    ppermute x2, waiting for transfers between devices, passed_along(): return lax.ppermute(value, axis, pairs)  2.47 us
  transfers between devices with their start and end apart: 22, of which 13 were waited for; matrix products, arithmetic and copies ran while one was open for 0% of the time, Pallas kernels for 27%

profile of v12, /device:TPU:0, one launch (start us, length us, event | category | flops | bytes accessed | tf_op | source)
XLA Modules:
  0.0 86.7 jit_solution(11894885315386082145)
XLA Ops:
  0.6 0.5 collective-permute-start
  1.1 1.7 %shard_map.113 = (bf16[240,1024]{1,0:T(8,128)(2,1)S(1)}, bf16[240,1024]{1,0:T(8,128)(2,1)S(1)}, f32[8,128]{1,0:T(8,128)S(1)}, f32[1,2048]{1,0:T(1,128)S(1)}) custom-call(s32[1]{0:T(128)} %bitcast.1.me_ref, bf16[128,2048]{1,0:T(8,128)(2,1)} %bitcast.29, f32[1,2048]{1,0:T(1,128)} %refs_1_.1, s32[2,128]{1,0:T(2,128)} %bitcast.32, f32[2,128]{1,0:T(2,128)} %bitcast.33, ...), custom_call_target="tpu_custom_call" | custom-call | flops 1024 | bytes 1024 | tf_op jit(solution)/shard_map/pallas_call | solution.py:742
  2.8 2.6 %collective-permute-start.1 = (bf16[240,1024]{1,0:T(8,128)(2,1)S(1)}, bf16[240,1024]{1,0:T(8,128)(2,1)S(1)}, u32[]{:S(2)}, u32[]{:S(2)}) collective-permute-start(bf16[240,1024]{1,0:T(8,128)(2,1)S(1)} %get-tuple-element.45.refs_2_.refs_3_), channel_id=1, source_target_pairs={{0,1},{1,0},{2,3},{3,2},{4,5},{5,4},{6,7},{7,6},{8,9},{9,8},{10,11... | collective-permute-start | bytes 1474568 | tf_op jit(solution)/shard_map/ppermute | solution.py:24
  5.4 1.5 %collective-permute-start.2 = (bf16[240,1024]{1,0:T(8,128)(2,1)S(1)}, bf16[240,1024]{1,0:T(8,128)(2,1)S(1)}, u32[]{:S(2)}, u32[]{:S(2)}) collective-permute-start(bf16[240,1024]{1,0:T(8,128)(2,1)S(1)} %get-tuple-element.46.refs_4_), channel_id=1, source_target_pairs={{0,2},{1,3},{2,0},{3,1},{4,6},{5,7},{6,4},{7,5},{8,10},{9,11},{10,... | collective-permute-start | bytes 1474568 | tf_op jit(solution)/shard_map/ppermute | solution.py:24
  6.9 3.0 %collective-permute-start.5 = (bf16[128,2048]{1,0:T(8,128)(2,1)}, bf16[128,2048]{1,0:T(8,128)(2,1)S(1)}, u32[]{:S(2)}, u32[]{:S(2)}) collective-permute-start(bf16[128,2048]{1,0:T(8,128)(2,1)} %bitcast.37), channel_id=1, source_target_pairs={{0,28},{4,0},{8,4},{12,8},{16,12},{20,16},{24,20},{28,24},{1,29},{... | collective-permute-start | bytes 1572872 | tf_op jit(solution)/shard_map/ppermute | solution.py:18
  9.9 2.5 %collective-permute-done.refs_0_ = bf16[128,2048]{1,0:T(8,128)(2,1)S(1)} collective-permute-done((bf16[128,2048]{1,0:T(8,128)(2,1)}, bf16[128,2048]{1,0:T(8,128)(2,1)S(1)}, u32[]{:S(2)}, u32[]{:S(2)}) %collective-permute-start) | collective-permute-done | bytes 524320 | tf_op jit(solution)/shard_map/ppermute | solution.py:18
  12.3 0.2 shard_map.114
  12.6 2.2 %collective-permute-start.3 = (bf16[128,1024]{1,0:T(8,128)(2,1)S(1)}, bf16[128,1024]{1,0:T(8,128)(2,1)S(1)}, u32[]{:S(2)}, u32[]{:S(2)}) collective-permute-start(bf16[128,1024]{1,0:T(8,128)(2,1)S(1)} %get-tuple-element.48.refs_2_.refs_3_), channel_id=1, source_target_pairs={{0,1},{1,0},{2,3},{3,2},{4,5},{5,4},{6,7},{7,6},{8,9},{9,8},{10,11... | collective-permute-start | bytes 786440 | tf_op jit(solution)/shard_map/ppermute | solution.py:24
  14.7 2.5 %collective-permute-start.4 = (bf16[128,1024]{1,0:T(8,128)(2,1)S(1)}, bf16[128,1024]{1,0:T(8,128)(2,1)S(1)}, u32[]{:S(2)}, u32[]{:S(2)}) collective-permute-start(bf16[128,1024]{1,0:T(8,128)(2,1)S(1)} %get-tuple-element.51.refs_4_), channel_id=1, source_target_pairs={{0,2},{1,3},{2,0},{3,1},{4,6},{5,7},{6,4},{7,5},{8,10},{9,11},{10,... | collective-permute-start | bytes 786440 | tf_op jit(solution)/shard_map/ppermute | solution.py:24
  17.3 0.0 collective-permute-done.1.refs_0_.refs_2_.refs_5_
  17.3 1.9 %collective-permute-done.2.refs_1_.refs_3_.refs_6_ = bf16[240,1024]{1,0:T(8,128)(2,1)S(1)} collective-permute-done((bf16[240,1024]{1,0:T(8,128)(2,1)S(1)}, bf16[240,1024]{1,0:T(8,128)(2,1)S(1)}, u32[]{:S(2)}, u32[]{:S(2)}) %collective-permute-start.2) | collective-permute-done | bytes 491552 | tf_op jit(solution)/shard_map/ppermute | solution.py:24
  19.2 0.0 collective-permute-done.5.refs_0_.grads_ref
  19.2 0.5 shard_map.117
  19.7 1.6 %collective-permute-start.8 = (bf16[96,1024]{1,0:T(8,128)(2,1)S(1)}, bf16[96,1024]{1,0:T(8,128)(2,1)S(1)}, u32[]{:S(2)}, u32[]{:S(2)}) collective-permute-start(bf16[96,1024]{1,0:T(8,128)(2,1)S(1)} %get-tuple-element.54.refs_7_), channel_id=1, source_target_pairs={{0,2},{1,3},{2,0},{3,1},{4,6},{5,7},{6,4},{7,5},{8,10},{9,11},{10,... | collective-permute-start | bytes 589832 | tf_op jit(solution)/shard_map/ppermute | solution.py:24
  21.3 0.5 collective-permute-start.9
  21.8 0.1 collective-permute-done.3.refs_5_
  22.0 2.8 %collective-permute-done.4.refs_6_ = bf16[128,1024]{1,0:T(8,128)(2,1)S(1)} collective-permute-done((bf16[128,1024]{1,0:T(8,128)(2,1)S(1)}, bf16[128,1024]{1,0:T(8,128)(2,1)S(1)}, u32[]{:S(2)}, u32[]{:S(2)}) %collective-permute-start.4) | collective-permute-done | bytes 262176 | tf_op jit(solution)/shard_map/ppermute | solution.py:24
  24.8 0.9 shard_map.118
  25.6 1.8 %collective-permute-start.10 = (bf16[192,1024]{1,0:T(8,128)(2,1)S(1)}, bf16[192,1024]{1,0:T(8,128)(2,1)S(1)}, u32[]{:S(2)}, u32[]{:S(2)}) collective-permute-start(bf16[192,1024]{1,0:T(8,128)(2,1)S(1)} %get-tuple-element.56.refs_10_), channel_id=1, source_target_pairs={{0,2},{1,3},{2,0},{3,1},{4,6},{5,7},{6,4},{7,5},{8,10},{9,11},{10,... | collective-permute-start | bytes 1179656 | tf_op jit(solution)/shard_map/ppermute | solution.py:24
  27.5 0.3 collective-permute-start.11
  27.8 1.7 %collective-permute-start.6 = (bf16[128,1024]{1,0:T(8,128)(2,1)S(1)}, bf16[128,1024]{1,0:T(8,128)(2,1)S(1)}, u32[]{:S(2)}, u32[]{:S(2)}) collective-permute-start(bf16[128,1024]{1,0:T(8,128)(2,1)S(1)} %get-tuple-element.52.refs_4_.refs_3_), channel_id=1, source_target_pairs={{0,1},{1,0},{2,3},{3,2},{4,5},{5,4},{6,7},{7,6},{8,9},{9,8},{10,11... | collective-permute-start | bytes 786440 | tf_op jit(solution)/shard_map/ppermute | solution.py:24
  29.5 0.0 collective-permute-done.8.refs_7_
  29.5 1.2 %collective-permute-start.7 = (bf16[128,1024]{1,0:T(8,128)(2,1)S(1)}, bf16[128,1024]{1,0:T(8,128)(2,1)S(1)}, u32[]{:S(2)}, u32[]{:S(2)}) collective-permute-start(bf16[128,1024]{1,0:T(8,128)(2,1)S(1)} %get-tuple-element.53.refs_4_), channel_id=1, source_target_pairs={{0,2},{1,3},{2,0},{3,1},{4,6},{5,7},{6,4},{7,5},{8,10},{9,11},{10,... | collective-permute-start | bytes 786440 | tf_op jit(solution)/shard_map/ppermute | solution.py:24
  30.7 0.0 collective-permute-done.9.refs_8_
  30.7 0.0 slice-done
  30.8 3.2 %shard_map.119 = (f32[384,768]{1,0:T(8,128)S(1)}, f32[384,768]{1,0:T(8,128)S(1)}) custom-call(f32[8,128]{1,0:T(8,128)S(1)} %get-tuple-element.44.refs_0_.refs_1_, f32[8,128]{1,0:T(8,128)S(1)} %get-tuple-element.49.refs_1_.refs_0_, f32[8,128]{1,0:T(8,128)S(1)} %get-tuple-element.50.refs_1_.refs_2_.refs_0_, ...), custom_call_target="tpu_custom_call" | custom-call | flops 2415919104 | bytes 14155776 | tf_op jit(solution)/shard_map/pallas_call | solution.py:243
  34.0 10.2 %collective-permute-done.6.refs_5_ = bf16[128,1024]{1,0:T(8,128)(2,1)S(1)} collective-permute-done((bf16[128,1024]{1,0:T(8,128)(2,1)S(1)}, bf16[128,1024]{1,0:T(8,128)(2,1)S(1)}, u32[]{:S(2)}, u32[]{:S(2)}) %collective-permute-start.6) | collective-permute-done | bytes 262176 | tf_op jit(solution)/shard_map/ppermute | solution.py:24
  44.1 0.0 collective-permute-done.7.refs_6_
  44.1 1.1 %shard_map.120 = (bf16[192,1024]{1,0:T(8,128)(2,1)S(1)}, bf16[192,1024]{1,0:T(8,128)(2,1)S(1)}) custom-call(f32[8,128]{1,0:T(8,128)S(1)} %get-tuple-element.44.refs_0_.refs_1_, f32[8,128]{1,0:T(8,128)S(1)} %get-tuple-element.49.refs_1_.refs_0_, f32[8,128]{1,0:T(8,128)S(1)} %get-tuple-element.50.refs_1_.refs_2_.refs_0_, ...), custom_call_target="tpu_custom_call" | custom-call | flops 1024 | bytes 1024 | tf_op jit(solution)/shard_map/pallas_call | solution.py:243
  45.3 0.8 collective-permute-start.14
  46.1 0.5 collective-permute-start.15
  46.6 1.0 %shard_map.121 = (bf16[96,2048]{1,0:T(8,128)(2,1)S(1)}, bf16[96,1024]{1,0:T(8,128)(2,1)S(1)}, bf16[96,1024]{1,0:T(8,128)(2,1)S(1)}) custom-call(f32[8,128]{1,0:T(8,128)S(1)} %get-tuple-element.44.refs_0_.refs_1_, f32[8,128]{1,0:T(8,128)S(1)} %get-tuple-element.49.refs_1_.refs_0_, f32[8,128]{1,0:T(8,128)S(1)} %get-tuple-element.50.refs_1_.refs_2_.refs_0_, ...), custom_call_target="tpu_custom_call" | custom-call | flops 1024 | bytes 1024 | tf_op jit(solution)/shard_map/pallas_call | solution.py:243
  47.6 0.8 shard_map.122
  48.4 0.0 collective-permute-done.10.refs_3_
  48.4 0.0 collective-permute-done.11.refs_4_
  48.4 3.2 %shard_map.123 = (bf16[96,1024]{1,0:T(8,128)(2,1)S(1)}, bf16[96,1024]{1,0:T(8,128)(2,1)S(1)}, bf16[192,1024]{1,0:T(8,128)(2,1)S(1)}, bf16[384,768]{1,0:T(8,128)(2,1)S(1)}) custom-call(bf16[96,2048]{1,0:T(8,128)(2,1)S(1)} %get-tuple-element.60.refs_0_, bf16[96,1024]{1,0:T(8,128)(2,1)S(1)} %get-tuple-element.61.refs_1_.refs_7_, ...), custom_call_target="tpu_custom_call" | custom-call | flops 3019898880 | bytes 14155776 | tf_op jit(solution)/shard_map/pallas_call | solution.py:243
  51.7 0.8 shard_map.124
  52.4 1.6 %collective-permute-start.12 = (bf16[192,1024]{1,0:T(8,128)(2,1)S(1)}, bf16[192,1024]{1,0:T(8,128)(2,1)S(1)}, u32[]{:S(2)}, u32[]{:S(2)}) collective-permute-start(bf16[192,1024]{1,0:T(8,128)(2,1)S(1)} %get-tuple-element.67), channel_id=1, source_target_pairs={{0,2},{1,3},{2,0},{3,1},{4,6},{5,7},{6,4},{7,5},{8,10},{9,11},{10,... | collective-permute-start | bytes 1179656 | tf_op jit(solution)/shard_map/ppermute | solution.py:24
  54.0 1.3 %collective-permute-start.13 = (bf16[192,1024]{1,0:T(8,128)(2,1)S(1)}, bf16[192,1024]{1,0:T(8,128)(2,1)S(1)}, u32[]{:S(2)}, u32[]{:S(2)}) collective-permute-start(bf16[192,1024]{1,0:T(8,128)(2,1)S(1)} %get-tuple-element.68), channel_id=1, source_target_pairs={{0,1},{1,0},{2,3},{3,2},{4,5},{5,4},{6,7},{7,6},{8,9},{9,8},{10,11... | collective-permute-start | bytes 1179656 | tf_op jit(solution)/shard_map/ppermute | solution.py:24
  55.3 1.4 %collective-permute-done.14.refs_3_ = bf16[192,1024]{1,0:T(8,128)(2,1)S(1)} collective-permute-done((bf16[192,1024]{1,0:T(8,128)(2,1)S(1)}, bf16[192,1024]{1,0:T(8,128)(2,1)S(1)}, u32[]{:S(2)}, u32[]{:S(2)}) %collective-permute-start.14) | collective-permute-done | bytes 393248 | tf_op jit(solution)/shard_map/ppermute | solution.py:24
  56.6 1.2 %collective-permute-done.15.refs_4_ = bf16[192,1024]{1,0:T(8,128)(2,1)S(1)} collective-permute-done((bf16[192,1024]{1,0:T(8,128)(2,1)S(1)}, bf16[192,1024]{1,0:T(8,128)(2,1)S(1)}, u32[]{:S(2)}, u32[]{:S(2)}) %collective-permute-start.15) | collective-permute-done | bytes 393248 | tf_op jit(solution)/shard_map/ppermute | solution.py:24
  57.8 3.7 %shard_map.125 = (bf16[96,1024]{1,0:T(8,128)(2,1)S(1)}, bf16[96,1024]{1,0:T(8,128)(2,1)S(1)}, bf16[192,1024]{1,0:T(8,128)(2,1)S(1)}, bf16[384,1536]{1,0:T(8,128)(2,1)S(1)}) custom-call(bf16[96,2048]{1,0:T(8,128)(2,1)S(1)} %get-tuple-element.70.refs_0_, bf16[96,1024]{1,0:T(8,128)(2,1)S(1)} %get-tuple-element.59.refs_7_.refs_1_, ...), custom_call_target="tpu_custom_call" | custom-call | flops 2415919104 | bytes 14155776 | tf_op jit(solution)/shard_map/pallas_call | solution.py:243
  61.6 0.7 collective-permute-start.19
  62.2 1.4 %shard_map.126 = (bf16[96,1024]{1,0:T(8,128)(2,1)S(1)}, bf16[96,1024]{1,0:T(8,128)(2,1)S(1)}, bf16[192,1024]{1,0:T(8,128)(2,1)S(1)}) custom-call(bf16[384,1536]{1,0:T(8,128)(2,1)S(1)} %get-tuple-element.74.both_ref, bf16[2048,1536]{1,0:T(8,128)(2,1)S(1)} %bitcast.25), custom_call_target="tpu_custom_call" | custom-call | flops 1024 | bytes 1024 | tf_op jit(solution)/shard_map/pallas_call | solution.py:243
  63.6 1.1 %collective-permute-start.18 = (bf16[192,1024]{1,0:T(8,128)(2,1)S(1)}, bf16[192,1024]{1,0:T(8,128)(2,1)S(1)}, u32[]{:S(2)}, u32[]{:S(2)}) collective-permute-start(bf16[192,1024]{1,0:T(8,128)(2,1)S(1)} %get-tuple-element.78), channel_id=1, source_target_pairs={{0,1},{1,0},{2,3},{3,2},{4,5},{5,4},{6,7},{7,6},{8,9},{9,8},{10,11... | collective-permute-start | bytes 1179656 | tf_op jit(solution)/shard_map/ppermute | solution.py:24
  64.8 0.3 collective-permute-done.12.refs_2_.refs_4_
  65.1 0.8 shard_map.127.refs_3_
  65.9 1.1 %collective-permute-start.16 = (bf16[128,1024]{1,0:T(8,128)(2,1)S(1)}, bf16[128,1024]{1,0:T(8,128)(2,1)S(1)}, u32[]{:S(2)}, u32[]{:S(2)}) collective-permute-start(bf16[128,1024]{1,0:T(8,128)(2,1)S(1)} %shard_map.127.refs_3_), channel_id=1, source_target_pairs={{0,1},{1,0},{2,3},{3,2},{4,5},{5,4},{6,7},{7,6},{8,9},{9,8},{10,11... | collective-permute-start | bytes 786440 | tf_op jit(solution)/shard_map/ppermute | solution.py:24
  67.0 0.0 collective-permute-done.13.refs_2_.refs_5_
  67.0 0.8 shard_map.128.refs_3_
  67.8 1.3 %collective-permute-start.17 = (bf16[128,1024]{1,0:T(8,128)(2,1)S(1)}, bf16[128,1024]{1,0:T(8,128)(2,1)S(1)}, u32[]{:S(2)}, u32[]{:S(2)}) collective-permute-start(bf16[128,1024]{1,0:T(8,128)(2,1)S(1)} %shard_map.128.refs_3_), channel_id=1, source_target_pairs={{0,2},{1,3},{2,0},{3,1},{4,6},{5,7},{6,4},{7,5},{8,10},{9,11},{10,... | collective-permute-start | bytes 786440 | tf_op jit(solution)/shard_map/ppermute | solution.py:24
  69.1 4.6 %collective-permute-done.19.refs_2_.refs_3_ = bf16[192,1024]{1,0:T(8,128)(2,1)S(1)} collective-permute-done((bf16[192,1024]{1,0:T(8,128)(2,1)S(1)}, bf16[192,1024]{1,0:T(8,128)(2,1)S(1)}, u32[]{:S(2)}, u32[]{:S(2)}) %collective-permute-start.19) | collective-permute-done | bytes 393248 | tf_op jit(solution)/shard_map/ppermute | solution.py:24
  73.7 0.5 shard_map.129.refs_3_
  74.1 1.0 %collective-permute-start.20 = (bf16[128,1024]{1,0:T(8,128)(2,1)S(1)}, bf16[128,1024]{1,0:T(8,128)(2,1)S(1)}, u32[]{:S(2)}, u32[]{:S(2)}) collective-permute-start(bf16[128,1024]{1,0:T(8,128)(2,1)S(1)} %shard_map.129.refs_3_), channel_id=1, source_target_pairs={{0,1},{1,0},{2,3},{3,2},{4,5},{5,4},{6,7},{7,6},{8,9},{9,8},{10,11... | collective-permute-start | bytes 786440 | tf_op jit(solution)/shard_map/ppermute | solution.py:24
  75.1 0.6 collective-permute-done.18.refs_2_.refs_4_
  75.7 0.5 shard_map.130.refs_8_
  76.2 1.5 %collective-permute-start.21 = (bf16[128,1024]{1,0:T(8,128)(2,1)S(1)}, bf16[128,1024]{1,0:T(8,128)(2,1)S(1)}, u32[]{:S(2)}, u32[]{:S(2)}) collective-permute-start(bf16[128,1024]{1,0:T(8,128)(2,1)S(1)} %shard_map.130.refs_8_), channel_id=1, source_target_pairs={{0,2},{1,3},{2,0},{3,1},{4,6},{5,7},{6,4},{7,5},{8,10},{9,11},{10,... | collective-permute-start | bytes 786440 | tf_op jit(solution)/shard_map/ppermute | solution.py:24
  77.7 1.6 %collective-permute-done.17.refs_7_ = bf16[128,1024]{1,0:T(8,128)(2,1)S(1)} collective-permute-done((bf16[128,1024]{1,0:T(8,128)(2,1)S(1)}, bf16[128,1024]{1,0:T(8,128)(2,1)S(1)}, u32[]{:S(2)}, u32[]{:S(2)}) %collective-permute-start.17) | collective-permute-done | bytes 262176 | tf_op jit(solution)/shard_map/ppermute | solution.py:24
  79.3 2.1 %collective-permute-done.16.refs_6_ = bf16[128,1024]{1,0:T(8,128)(2,1)S(1)} collective-permute-done((bf16[128,1024]{1,0:T(8,128)(2,1)S(1)}, bf16[128,1024]{1,0:T(8,128)(2,1)S(1)}, u32[]{:S(2)}, u32[]{:S(2)}) %collective-permute-start.16) | collective-permute-done | bytes 262176 | tf_op jit(solution)/shard_map/ppermute | solution.py:24
  81.4 1.7 %shard_map.131 = (bf16[128,2048]{1,0:T(8,128)(2,1)}, f32[8,128]{1,0:T(8,128)S(1)}) custom-call(bf16[128,2048]{1,0:T(8,128)(2,1)S(1)} %collective-permute-done.refs_0_, f32[8,128]{1,0:T(8,128)S(1)} %get-tuple-element.44.refs_0_.refs_1_, bf16[96,1024]{1,0:T(8,128)(2,1)S(1)} %get-tuple-element.64.refs_2_, ...), custom_call_target="tpu_custom_call" | custom-call | flops 1024 | bytes 1024 | tf_op jit(solution)/shard_map/pallas_call | solution.py:243
  83.1 1.7 %collective-permute-done.20.refs_5_ = bf16[128,1024]{1,0:T(8,128)(2,1)S(1)} collective-permute-done((bf16[128,1024]{1,0:T(8,128)(2,1)S(1)}, bf16[128,1024]{1,0:T(8,128)(2,1)S(1)}, u32[]{:S(2)}, u32[]{:S(2)}) %collective-permute-start.20) | collective-permute-done | bytes 262176 | tf_op jit(solution)/shard_map/ppermute | solution.py:24
  84.8 0.6 shard_map.132
  85.4 0.0 collective-permute-done.21.sum_y
  85.4 1.3 %shard_map.133 = bf16[128,2048]{1,0:T(8,128)(2,1)} custom-call(bf16[128,2048]{1,0:T(8,128)(2,1)S(1)} %collective-permute-done.5.refs_0_.grads_ref, bf16[128,2048]{1,0:T(8,128)(2,1)S(1)} %bitcast.30, f32[1,2048]{1,0:T(1,128)S(1)} %get-tuple-element.47.refs_1_.gain_ref, f32[128,1024]{1,0:T(8,128)S(1)} %get-tuple-element.84.left_ref, ...), custom_call_target="tpu_custom_call" | custom-call | flops 1024 | bytes 1024 | tf_op jit(solution)/shard_map/pallas_call | solution.py:243
  (10 shorter events, 0.1 us)
Async XLA Ops:
  0.6 11.7 %collective-permute-start = (bf16[128,2048]{1,0:T(8,128)(2,1)}, bf16[128,2048]{1,0:T(8,128)(2,1)S(1)}, u32[]{:S(2)}, u32[]{:S(2)}) collective-permute-start(bf16[128,2048]{1,0:T(8,128)(2,1)} %bitcast.36), channel_id=1, source_target_pairs={{0,4},{4,8},{8,12},{12,16},{16,20},{20,24},{24,28},{28,0},{1,5},{5... | collective-permute-start | bytes 1572872 | tf_op jit(solution)/shard_map/ppermute | solution.py:18
  2.8 14.5 %collective-permute-start.1 = (bf16[240,1024]{1,0:T(8,128)(2,1)S(1)}, bf16[240,1024]{1,0:T(8,128)(2,1)S(1)}, u32[]{:S(2)}, u32[]{:S(2)}) collective-permute-start(bf16[240,1024]{1,0:T(8,128)(2,1)S(1)} %get-tuple-element.45.refs_2_.refs_3_), channel_id=1, source_target_pairs={{0,1},{1,0},{2,3},{3,2},{4,5},{5,4},{6,7},{7,6},{8,9},{9,8},{10,11... | collective-permute-start | bytes 1474568 | tf_op jit(solution)/shard_map/ppermute | solution.py:24
  5.4 13.8 %collective-permute-start.2 = (bf16[240,1024]{1,0:T(8,128)(2,1)S(1)}, bf16[240,1024]{1,0:T(8,128)(2,1)S(1)}, u32[]{:S(2)}, u32[]{:S(2)}) collective-permute-start(bf16[240,1024]{1,0:T(8,128)(2,1)S(1)} %get-tuple-element.46.refs_4_), channel_id=1, source_target_pairs={{0,2},{1,3},{2,0},{3,1},{4,6},{5,7},{6,4},{7,5},{8,10},{9,11},{10,... | collective-permute-start | bytes 1474568 | tf_op jit(solution)/shard_map/ppermute | solution.py:24
  6.9 12.3 %collective-permute-start.5 = (bf16[128,2048]{1,0:T(8,128)(2,1)}, bf16[128,2048]{1,0:T(8,128)(2,1)S(1)}, u32[]{:S(2)}, u32[]{:S(2)}) collective-permute-start(bf16[128,2048]{1,0:T(8,128)(2,1)} %bitcast.37), channel_id=1, source_target_pairs={{0,28},{4,0},{8,4},{12,8},{16,12},{20,16},{24,20},{28,24},{1,29},{... | collective-permute-start | bytes 1572872 | tf_op jit(solution)/shard_map/ppermute | solution.py:18
  12.3 18.4 %slice-start = ((s8[6291456]{0:T(1024)(128)(4,1)}), s8[4194304]{0:T(1024)(128)(4,1)S(1)}, s32[]{:S(2)}) async-start(s8[6291456]{0:T(1024)(128)(4,1)} %bitcast.20), calls=%async_computation | async-start | bytes 8388608
  12.6 9.4 %collective-permute-start.3 = (bf16[128,1024]{1,0:T(8,128)(2,1)S(1)}, bf16[128,1024]{1,0:T(8,128)(2,1)S(1)}, u32[]{:S(2)}, u32[]{:S(2)}) collective-permute-start(bf16[128,1024]{1,0:T(8,128)(2,1)S(1)} %get-tuple-element.48.refs_2_.refs_3_), channel_id=1, source_target_pairs={{0,1},{1,0},{2,3},{3,2},{4,5},{5,4},{6,7},{7,6},{8,9},{9,8},{10,11... | collective-permute-start | bytes 786440 | tf_op jit(solution)/shard_map/ppermute | solution.py:24
  14.7 16.0 %slice-start.1 = ((s8[6291456]{0:T(1024)(128)(4,1)}), s8[2097152]{0:T(1024)(128)(4,1)S(1)}, s32[]{:S(2)}) async-start(s8[6291456]{0:T(1024)(128)(4,1)} %bitcast.20), calls=%async_computation.1 | async-start | bytes 4194304
  14.7 10.0 %collective-permute-start.4 = (bf16[128,1024]{1,0:T(8,128)(2,1)S(1)}, bf16[128,1024]{1,0:T(8,128)(2,1)S(1)}, u32[]{:S(2)}, u32[]{:S(2)}) collective-permute-start(bf16[128,1024]{1,0:T(8,128)(2,1)S(1)} %get-tuple-element.51.refs_4_), channel_id=1, source_target_pairs={{0,2},{1,3},{2,0},{3,1},{4,6},{5,7},{6,4},{7,5},{8,10},{9,11},{10,... | collective-permute-start | bytes 786440 | tf_op jit(solution)/shard_map/ppermute | solution.py:24
  19.7 9.8 %collective-permute-start.8 = (bf16[96,1024]{1,0:T(8,128)(2,1)S(1)}, bf16[96,1024]{1,0:T(8,128)(2,1)S(1)}, u32[]{:S(2)}, u32[]{:S(2)}) collective-permute-start(bf16[96,1024]{1,0:T(8,128)(2,1)S(1)} %get-tuple-element.54.refs_7_), channel_id=1, source_target_pairs={{0,2},{1,3},{2,0},{3,1},{4,6},{5,7},{6,4},{7,5},{8,10},{9,11},{10,... | collective-permute-start | bytes 589832 | tf_op jit(solution)/shard_map/ppermute | solution.py:24
  21.3 9.4 %collective-permute-start.9 = (bf16[96,1024]{1,0:T(8,128)(2,1)S(1)}, bf16[96,1024]{1,0:T(8,128)(2,1)S(1)}, u32[]{:S(2)}, u32[]{:S(2)}) collective-permute-start(bf16[96,1024]{1,0:T(8,128)(2,1)S(1)} %get-tuple-element.55), channel_id=1, source_target_pairs={{0,1},{1,0},{2,3},{3,2},{4,5},{5,4},{6,7},{7,6},{8,9},{9,8},{10,11... | collective-permute-start | bytes 589832 | tf_op jit(solution)/shard_map/ppermute | solution.py:24
  25.6 22.7 %collective-permute-start.10 = (bf16[192,1024]{1,0:T(8,128)(2,1)S(1)}, bf16[192,1024]{1,0:T(8,128)(2,1)S(1)}, u32[]{:S(2)}, u32[]{:S(2)}) collective-permute-start(bf16[192,1024]{1,0:T(8,128)(2,1)S(1)} %get-tuple-element.56.refs_10_), channel_id=1, source_target_pairs={{0,2},{1,3},{2,0},{3,1},{4,6},{5,7},{6,4},{7,5},{8,10},{9,11},{10,... | collective-permute-start | bytes 1179656 | tf_op jit(solution)/shard_map/ppermute | solution.py:24
  27.5 20.9 %collective-permute-start.11 = (bf16[192,1024]{1,0:T(8,128)(2,1)S(1)}, bf16[192,1024]{1,0:T(8,128)(2,1)S(1)}, u32[]{:S(2)}, u32[]{:S(2)}) collective-permute-start(bf16[192,1024]{1,0:T(8,128)(2,1)S(1)} %get-tuple-element.63), channel_id=1, source_target_pairs={{0,1},{1,0},{2,3},{3,2},{4,5},{5,4},{6,7},{7,6},{8,9},{9,8},{10,11... | collective-permute-start | bytes 1179656 | tf_op jit(solution)/shard_map/ppermute | solution.py:24
  27.8 16.4 %collective-permute-start.6 = (bf16[128,1024]{1,0:T(8,128)(2,1)S(1)}, bf16[128,1024]{1,0:T(8,128)(2,1)S(1)}, u32[]{:S(2)}, u32[]{:S(2)}) collective-permute-start(bf16[128,1024]{1,0:T(8,128)(2,1)S(1)} %get-tuple-element.52.refs_4_.refs_3_), channel_id=1, source_target_pairs={{0,1},{1,0},{2,3},{3,2},{4,5},{5,4},{6,7},{7,6},{8,9},{9,8},{10,11... | collective-permute-start | bytes 786440 | tf_op jit(solution)/shard_map/ppermute | solution.py:24
  29.5 14.6 %collective-permute-start.7 = (bf16[128,1024]{1,0:T(8,128)(2,1)S(1)}, bf16[128,1024]{1,0:T(8,128)(2,1)S(1)}, u32[]{:S(2)}, u32[]{:S(2)}) collective-permute-start(bf16[128,1024]{1,0:T(8,128)(2,1)S(1)} %get-tuple-element.53.refs_4_), channel_id=1, source_target_pairs={{0,2},{1,3},{2,0},{3,1},{4,6},{5,7},{6,4},{7,5},{8,10},{9,11},{10,... | collective-permute-start | bytes 786440 | tf_op jit(solution)/shard_map/ppermute | solution.py:24
  44.1 4.3 %copy-start = (bf16[1,1,768,2048]{3,2,1,0:T(8,128)(2,1)S(1)}, bf16[1,1,768,2048]{3,2,1,0:T(8,128)(2,1)}, u32[]{:S(2)}) copy-start(bf16[1,1,768,2048]{3,2,1,0:T(8,128)(2,1)} %param.19) | copy-start | bytes 9437188
  45.3 11.4 %collective-permute-start.14 = (bf16[192,1024]{1,0:T(8,128)(2,1)S(1)}, bf16[192,1024]{1,0:T(8,128)(2,1)S(1)}, u32[]{:S(2)}, u32[]{:S(2)}) collective-permute-start(bf16[192,1024]{1,0:T(8,128)(2,1)S(1)} %get-tuple-element.58.refs_7_), channel_id=1, source_target_pairs={{0,2},{1,3},{2,0},{3,1},{4,6},{5,7},{6,4},{7,5},{8,10},{9,11},{10,... | collective-permute-start | bytes 1179656 | tf_op jit(solution)/shard_map/ppermute | solution.py:24
  46.1 11.7 %collective-permute-start.15 = (bf16[192,1024]{1,0:T(8,128)(2,1)S(1)}, bf16[192,1024]{1,0:T(8,128)(2,1)S(1)}, u32[]{:S(2)}, u32[]{:S(2)}) collective-permute-start(bf16[192,1024]{1,0:T(8,128)(2,1)S(1)} %get-tuple-element.72), channel_id=1, source_target_pairs={{0,1},{1,0},{2,3},{3,2},{4,5},{5,4},{6,7},{7,6},{8,9},{9,8},{10,11... | collective-permute-start | bytes 1179656 | tf_op jit(solution)/shard_map/ppermute | solution.py:24
  52.4 12.6 %collective-permute-start.12 = (bf16[192,1024]{1,0:T(8,128)(2,1)S(1)}, bf16[192,1024]{1,0:T(8,128)(2,1)S(1)}, u32[]{:S(2)}, u32[]{:S(2)}) collective-permute-start(bf16[192,1024]{1,0:T(8,128)(2,1)S(1)} %get-tuple-element.67), channel_id=1, source_target_pairs={{0,2},{1,3},{2,0},{3,1},{4,6},{5,7},{6,4},{7,5},{8,10},{9,11},{10,... | collective-permute-start | bytes 1179656 | tf_op jit(solution)/shard_map/ppermute | solution.py:24
  54.0 13.0 %collective-permute-start.13 = (bf16[192,1024]{1,0:T(8,128)(2,1)S(1)}, bf16[192,1024]{1,0:T(8,128)(2,1)S(1)}, u32[]{:S(2)}, u32[]{:S(2)}) collective-permute-start(bf16[192,1024]{1,0:T(8,128)(2,1)S(1)} %get-tuple-element.68), channel_id=1, source_target_pairs={{0,1},{1,0},{2,3},{3,2},{4,5},{5,4},{6,7},{7,6},{8,9},{9,8},{10,11... | collective-permute-start | bytes 1179656 | tf_op jit(solution)/shard_map/ppermute | solution.py:24
  61.6 12.1 %collective-permute-start.19 = (bf16[192,1024]{1,0:T(8,128)(2,1)S(1)}, bf16[192,1024]{1,0:T(8,128)(2,1)S(1)}, u32[]{:S(2)}, u32[]{:S(2)}) collective-permute-start(bf16[192,1024]{1,0:T(8,128)(2,1)S(1)} %get-tuple-element.80), channel_id=1, source_target_pairs={{0,2},{1,3},{2,0},{3,1},{4,6},{5,7},{6,4},{7,5},{8,10},{9,11},{10,... | collective-permute-start | bytes 1179656 | tf_op jit(solution)/shard_map/ppermute | solution.py:24
  63.6 12.1 %collective-permute-start.18 = (bf16[192,1024]{1,0:T(8,128)(2,1)S(1)}, bf16[192,1024]{1,0:T(8,128)(2,1)S(1)}, u32[]{:S(2)}, u32[]{:S(2)}) collective-permute-start(bf16[192,1024]{1,0:T(8,128)(2,1)S(1)} %get-tuple-element.78), channel_id=1, source_target_pairs={{0,1},{1,0},{2,3},{3,2},{4,5},{5,4},{6,7},{7,6},{8,9},{9,8},{10,11... | collective-permute-start | bytes 1179656 | tf_op jit(solution)/shard_map/ppermute | solution.py:24
  65.9 15.5 %collective-permute-start.16 = (bf16[128,1024]{1,0:T(8,128)(2,1)S(1)}, bf16[128,1024]{1,0:T(8,128)(2,1)S(1)}, u32[]{:S(2)}, u32[]{:S(2)}) collective-permute-start(bf16[128,1024]{1,0:T(8,128)(2,1)S(1)} %shard_map.127.refs_3_), channel_id=1, source_target_pairs={{0,1},{1,0},{2,3},{3,2},{4,5},{5,4},{6,7},{7,6},{8,9},{9,8},{10,11... | collective-permute-start | bytes 786440 | tf_op jit(solution)/shard_map/ppermute | solution.py:24
  67.8 11.5 %collective-permute-start.17 = (bf16[128,1024]{1,0:T(8,128)(2,1)S(1)}, bf16[128,1024]{1,0:T(8,128)(2,1)S(1)}, u32[]{:S(2)}, u32[]{:S(2)}) collective-permute-start(bf16[128,1024]{1,0:T(8,128)(2,1)S(1)} %shard_map.128.refs_3_), channel_id=1, source_target_pairs={{0,2},{1,3},{2,0},{3,1},{4,6},{5,7},{6,4},{7,5},{8,10},{9,11},{10,... | collective-permute-start | bytes 786440 | tf_op jit(solution)/shard_map/ppermute | solution.py:24
  74.1 10.6 %collective-permute-start.20 = (bf16[128,1024]{1,0:T(8,128)(2,1)S(1)}, bf16[128,1024]{1,0:T(8,128)(2,1)S(1)}, u32[]{:S(2)}, u32[]{:S(2)}) collective-permute-start(bf16[128,1024]{1,0:T(8,128)(2,1)S(1)} %shard_map.129.refs_3_), channel_id=1, source_target_pairs={{0,1},{1,0},{2,3},{3,2},{4,5},{5,4},{6,7},{7,6},{8,9},{9,8},{10,11... | collective-permute-start | bytes 786440 | tf_op jit(solution)/shard_map/ppermute | solution.py:24
  76.2 9.2 %collective-permute-start.21 = (bf16[128,1024]{1,0:T(8,128)(2,1)S(1)}, bf16[128,1024]{1,0:T(8,128)(2,1)S(1)}, u32[]{:S(2)}, u32[]{:S(2)}) collective-permute-start(bf16[128,1024]{1,0:T(8,128)(2,1)S(1)} %shard_map.130.refs_8_), channel_id=1, source_target_pairs={{0,2},{1,3},{2,0},{3,1},{4,6},{5,7},{6,4},{7,5},{8,10},{9,11},{10,... | collective-permute-start | bytes 786440 | tf_op jit(solution)/shard_map/ppermute | solution.py:24
  83.1 2.3 %copy-start.1 = (bf16[1,128,2048]{2,1,0:T(8,128)(2,1)S(1)}, bf16[1,128,2048]{2,1,0:T(8,128)(2,1)}, u32[]{:S(2)}) copy-start(bf16[1,128,2048]{2,1,0:T(8,128)(2,1)} %param.12) | copy-start | bytes 1572868

commit v13 on v12

--- a/solution.py
+++ b/solution.py
@@ -812,6 +812,7 @@
     )
     b_got_y, b_got_x = swapped(b_to_y, "expert", 2), swapped(b_to_x, "expert", 1)
     f_got_y, f_got_x, f_to_y = onward("f", (f_left, f_right), (f_from_x, f_from_y), (b_to_y,))
+    g_got_y, g_got_x, g_to_y = onward("bg", (g_left, g_right), (g_from_x, g_from_y), (f_to_y,))
     gate_pre, up_pre = local_call(
         functools.partial(hop_again_kernel, top_count),
         [shaped(slot_total, hidden_units, jnp.float32)] * 2,
@@ -819,9 +820,8 @@
         2 * expert_flops,
         expert_moved,
         scratch=(rows_scratch,),
-        after=(f_to_y,),
-    )
-    g_got_y, g_got_x, g_to_y = onward("bg", (g_left, g_right), (g_from_x, g_from_y), (gate_pre,))
+        after=(g_to_y,),
+    )
     near_out = [shaped(capacity, features), shaped(capacity, half), shaped(capacity, half)]
     g_near = local_call(
         functools.partial(near_kernel, "bg", top_count),
@@ -829,7 +829,7 @@
         (*tabs, g_left, g_right, g_from_x, g_from_y),
         one_hop,
         moved,
-        after=(g_to_y,),
+        after=(gate_pre,),
     )
     f_near = local_call(
         functools.partial(near_kernel, "f", top_count),

time: 86.8 us -> 82 us (0.945)
  waiting for transfers between devices: 30.9 us -> 23.8 us
  starting transfers between devices: 30.3 us -> 32.5 us
    ppermute x20, waiting for transfers between devices: 28.4 us -> 21.3 us  [swapped(): return lax.ppermute(value, axis, pairs)]
    ppermute x20, starting transfers between devices: 26.8 us -> 29.1 us  [swapped(): return lax.ppermute(value, axis, pairs)]
  transfers between devices with their start and end apart: 22 -> 22, of which waited for: 13 -> 12; matrix products, arithmetic and copies ran while one was open for 0% -> 0% of each run, Pallas kernels for 27% -> 29%
where the time goes in v13:
time: 82 us; the launch traced here: 81.8 us
  starting transfers between devices  32.5 us (40%)
  Pallas kernels  24.6 us (30%)
  waiting for transfers between devices  23.8 us (29%)
  between operations  0.85 us (1%)
    ppermute x20, starting transfers between devices, swapped(): return lax.ppermute(value, axis, pairs)  29.1 us
    pallas_call x20, Pallas kernels, local_call(): pl.pallas_call(body if after else kernel, out_shape=out_shapes, in_specs=...  22.9 us
    ppermute x20, waiting for transfers between devices, swapped(): return lax.ppermute(value, axis, pairs)  21.3 us
    ppermute x2, starting transfers between devices, passed_along(): return lax.ppermute(value, axis, pairs)  3.46 us
    ppermute x2, waiting for transfers between devices, passed_along(): return lax.ppermute(value, axis, pairs)  2.47 us
    pallas_call x1, Pallas kernels, per_device_hops(): pl.pallas_call(functools.partial(first_kernel, top_count), out_shape=[sha...  1.68 us
  transfers between devices with their start and end apart: 22, of which 12 were waited for; matrix products, arithmetic and copies ran while one was open for 0% of the time, Pallas kernels for 29%

profile of v13, /device:TPU:0, one launch (start us, length us, event | category | flops | bytes accessed | tf_op | source)
XLA Modules:
  0.0 81.8 jit_solution(10961669247212891257)
XLA Ops:
  0.6 0.5 collective-permute-start
  1.1 1.7 %shard_map.113 = (bf16[240,1024]{1,0:T(8,128)(2,1)S(1)}, bf16[240,1024]{1,0:T(8,128)(2,1)S(1)}, f32[8,128]{1,0:T(8,128)S(1)}, f32[1,2048]{1,0:T(1,128)S(1)}) custom-call(s32[1]{0:T(128)} %bitcast.1.me_ref, bf16[128,2048]{1,0:T(8,128)(2,1)} %bitcast.29, f32[1,2048]{1,0:T(1,128)} %refs_1_.1, s32[2,128]{1,0:T(2,128)} %bitcast.32, f32[2,128]{1,0:T(2,128)} %bitcast.33, ...), custom_call_target="tpu_custom_call" | custom-call | flops 1024 | bytes 1024 | tf_op jit(solution)/shard_map/pallas_call | solution.py:742
  2.8 2.6 %collective-permute-start.2 = (bf16[240,1024]{1,0:T(8,128)(2,1)S(1)}, bf16[240,1024]{1,0:T(8,128)(2,1)S(1)}, u32[]{:S(2)}, u32[]{:S(2)}) collective-permute-start(bf16[240,1024]{1,0:T(8,128)(2,1)S(1)} %get-tuple-element.46.refs_4_), channel_id=1, source_target_pairs={{0,2},{1,3},{2,0},{3,1},{4,6},{5,7},{6,4},{7,5},{8,10},{9,11},{10,... | collective-permute-start | bytes 1474568 | tf_op jit(solution)/shard_map/ppermute | solution.py:24
  5.4 1.5 %collective-permute-start.1 = (bf16[240,1024]{1,0:T(8,128)(2,1)S(1)}, bf16[240,1024]{1,0:T(8,128)(2,1)S(1)}, u32[]{:S(2)}, u32[]{:S(2)}) collective-permute-start(bf16[240,1024]{1,0:T(8,128)(2,1)S(1)} %get-tuple-element.45.refs_2_.refs_3_), channel_id=1, source_target_pairs={{0,1},{1,0},{2,3},{3,2},{4,5},{5,4},{6,7},{7,6},{8,9},{9,8},{10,11... | collective-permute-start | bytes 1474568 | tf_op jit(solution)/shard_map/ppermute | solution.py:24
  6.9 3.0 %collective-permute-start.5 = (bf16[128,2048]{1,0:T(8,128)(2,1)}, bf16[128,2048]{1,0:T(8,128)(2,1)S(1)}, u32[]{:S(2)}, u32[]{:S(2)}) collective-permute-start(bf16[128,2048]{1,0:T(8,128)(2,1)} %bitcast.37), channel_id=1, source_target_pairs={{0,28},{4,0},{8,4},{12,8},{16,12},{20,16},{24,20},{28,24},{1,29},{... | collective-permute-start | bytes 1572872 | tf_op jit(solution)/shard_map/ppermute | solution.py:18
  9.9 2.5 %collective-permute-done.refs_0_ = bf16[128,2048]{1,0:T(8,128)(2,1)S(1)} collective-permute-done((bf16[128,2048]{1,0:T(8,128)(2,1)}, bf16[128,2048]{1,0:T(8,128)(2,1)S(1)}, u32[]{:S(2)}, u32[]{:S(2)}) %collective-permute-start) | collective-permute-done | bytes 524320 | tf_op jit(solution)/shard_map/ppermute | solution.py:18
  12.3 0.2 shard_map.114
  12.6 2.3 %collective-permute-start.4 = (bf16[128,1024]{1,0:T(8,128)(2,1)S(1)}, bf16[128,1024]{1,0:T(8,128)(2,1)S(1)}, u32[]{:S(2)}, u32[]{:S(2)}) collective-permute-start(bf16[128,1024]{1,0:T(8,128)(2,1)S(1)} %get-tuple-element.51.refs_4_), channel_id=1, source_target_pairs={{0,2},{1,3},{2,0},{3,1},{4,6},{5,7},{6,4},{7,5},{8,10},{9,11},{10,... | collective-permute-start | bytes 786440 | tf_op jit(solution)/shard_map/ppermute | solution.py:24
  14.8 2.4 %collective-permute-start.3 = (bf16[128,1024]{1,0:T(8,128)(2,1)S(1)}, bf16[128,1024]{1,0:T(8,128)(2,1)S(1)}, u32[]{:S(2)}, u32[]{:S(2)}) collective-permute-start(bf16[128,1024]{1,0:T(8,128)(2,1)S(1)} %get-tuple-element.48.refs_2_.refs_3_), channel_id=1, source_target_pairs={{0,1},{1,0},{2,3},{3,2},{4,5},{5,4},{6,7},{7,6},{8,9},{9,8},{10,11... | collective-permute-start | bytes 786440 | tf_op jit(solution)/shard_map/ppermute | solution.py:24
  17.3 0.0 collective-permute-done.2.refs_1_.refs_3_.refs_6_
  17.3 1.9 %collective-permute-done.1.refs_0_.refs_2_.refs_5_ = bf16[240,1024]{1,0:T(8,128)(2,1)S(1)} collective-permute-done((bf16[240,1024]{1,0:T(8,128)(2,1)S(1)}, bf16[240,1024]{1,0:T(8,128)(2,1)S(1)}, u32[]{:S(2)}, u32[]{:S(2)}) %collective-permute-start.1) | collective-permute-done | bytes 491552 | tf_op jit(solution)/shard_map/ppermute | solution.py:24
  19.2 0.0 collective-permute-done.5.refs_0_.grads_ref
  19.2 0.1 collective-permute-start.7
  19.3 2.0 %collective-permute-start.6 = (bf16[128,1024]{1,0:T(8,128)(2,1)S(1)}, bf16[128,1024]{1,0:T(8,128)(2,1)S(1)}, u32[]{:S(2)}, u32[]{:S(2)}) collective-permute-start(bf16[128,1024]{1,0:T(8,128)(2,1)S(1)} %get-tuple-element.52.refs_4_.refs_3_), channel_id=1, source_target_pairs={{0,1},{1,0},{2,3},{3,2},{4,5},{5,4},{6,7},{7,6},{8,9},{9,8},{10,11... | collective-permute-start | bytes 786440 | tf_op jit(solution)/shard_map/ppermute | solution.py:24
  21.3 0.5 shard_map.117
  21.8 0.2 collective-permute-start.9
  22.0 0.1 collective-permute-done.4.refs_6_
  22.1 2.4 %collective-permute-start.8 = (bf16[96,1024]{1,0:T(8,128)(2,1)S(1)}, bf16[96,1024]{1,0:T(8,128)(2,1)S(1)}, u32[]{:S(2)}, u32[]{:S(2)}) collective-permute-start(bf16[96,1024]{1,0:T(8,128)(2,1)S(1)} %get-tuple-element.54.refs_7_), channel_id=1, source_target_pairs={{0,2},{1,3},{2,0},{3,1},{4,6},{5,7},{6,4},{7,5},{8,10},{9,11},{10,... | collective-permute-start | bytes 589832 | tf_op jit(solution)/shard_map/ppermute | solution.py:24
  24.5 0.3 collective-permute-done.3.refs_5_
  24.8 0.9 %shard_map.118 = (bf16[192,1024]{1,0:T(8,128)(2,1)S(1)}, bf16[192,1024]{1,0:T(8,128)(2,1)S(1)}) custom-call(f32[8,128]{1,0:T(8,128)S(1)} %get-tuple-element.44.refs_0_.refs_1_, f32[8,128]{1,0:T(8,128)S(1)} %get-tuple-element.49.refs_1_.refs_0_, f32[8,128]{1,0:T(8,128)S(1)} %get-tuple-element.50.refs_1_.refs_2_.refs_0_, ...), custom_call_target="tpu_custom_call" | custom-call | flops 1024 | bytes 1024 | tf_op jit(solution)/shard_map/pallas_call | solution.py:243
  25.7 1.8 %collective-permute-start.11 = (bf16[192,1024]{1,0:T(8,128)(2,1)S(1)}, bf16[192,1024]{1,0:T(8,128)(2,1)S(1)}, u32[]{:S(2)}, u32[]{:S(2)}) collective-permute-start(bf16[192,1024]{1,0:T(8,128)(2,1)S(1)} %get-tuple-element.63), channel_id=1, source_target_pairs={{0,1},{1,0},{2,3},{3,2},{4,5},{5,4},{6,7},{7,6},{8,9},{9,8},{10,11... | collective-permute-start | bytes 1179656 | tf_op jit(solution)/shard_map/ppermute | solution.py:24
  27.5 1.1 %collective-permute-done.7.refs_6_ = bf16[128,1024]{1,0:T(8,128)(2,1)S(1)} collective-permute-done((bf16[128,1024]{1,0:T(8,128)(2,1)S(1)}, bf16[128,1024]{1,0:T(8,128)(2,1)S(1)}, u32[]{:S(2)}, u32[]{:S(2)}) %collective-permute-start.7) | collective-permute-done | bytes 262176 | tf_op jit(solution)/shard_map/ppermute | solution.py:24
  28.6 1.5 %collective-permute-start.10 = (bf16[192,1024]{1,0:T(8,128)(2,1)S(1)}, bf16[192,1024]{1,0:T(8,128)(2,1)S(1)}, u32[]{:S(2)}, u32[]{:S(2)}) collective-permute-start(bf16[192,1024]{1,0:T(8,128)(2,1)S(1)} %get-tuple-element.56.refs_7_), channel_id=1, source_target_pairs={{0,2},{1,3},{2,0},{3,1},{4,6},{5,7},{6,4},{7,5},{8,10},{9,11},{10,... | collective-permute-start | bytes 1179656 | tf_op jit(solution)/shard_map/ppermute | solution.py:24
  30.1 0.3 collective-permute-done.6.refs_5_
  30.4 1.1 %shard_map.119 = (bf16[192,1024]{1,0:T(8,128)(2,1)S(1)}, bf16[192,1024]{1,0:T(8,128)(2,1)S(1)}) custom-call(f32[8,128]{1,0:T(8,128)S(1)} %get-tuple-element.44.refs_0_.refs_1_, f32[8,128]{1,0:T(8,128)S(1)} %get-tuple-element.49.refs_1_.refs_0_, f32[8,128]{1,0:T(8,128)S(1)} %get-tuple-element.50.refs_1_.refs_2_.refs_0_, ...), custom_call_target="tpu_custom_call" | custom-call | flops 1024 | bytes 1024 | tf_op jit(solution)/shard_map/pallas_call | solution.py:243
  31.5 1.8 %collective-permute-start.15 = (bf16[192,1024]{1,0:T(8,128)(2,1)S(1)}, bf16[192,1024]{1,0:T(8,128)(2,1)S(1)}, u32[]{:S(2)}, u32[]{:S(2)}) collective-permute-start(bf16[192,1024]{1,0:T(8,128)(2,1)S(1)} %get-tuple-element.72), channel_id=1, source_target_pairs={{0,1},{1,0},{2,3},{3,2},{4,5},{5,4},{6,7},{7,6},{8,9},{9,8},{10,11... | collective-permute-start | bytes 1179656 | tf_op jit(solution)/shard_map/ppermute | solution.py:24
  33.3 1.3 %collective-permute-done.9.refs_8_ = bf16[96,1024]{1,0:T(8,128)(2,1)S(1)} collective-permute-done((bf16[96,1024]{1,0:T(8,128)(2,1)S(1)}, bf16[96,1024]{1,0:T(8,128)(2,1)S(1)}, u32[]{:S(2)}, u32[]{:S(2)}) %collective-permute-start.9) | collective-permute-done | bytes 196640 | tf_op jit(solution)/shard_map/ppermute | solution.py:24
  34.6 0.2 collective-permute-start.14
  34.8 0.0 collective-permute-done.8.refs_7_
  34.8 3.2 %shard_map.120 = (f32[384,768]{1,0:T(8,128)S(1)}, f32[384,768]{1,0:T(8,128)S(1)}) custom-call(f32[8,128]{1,0:T(8,128)S(1)} %get-tuple-element.44.refs_0_.refs_1_, f32[8,128]{1,0:T(8,128)S(1)} %get-tuple-element.49.refs_1_.refs_0_, f32[8,128]{1,0:T(8,128)S(1)} %get-tuple-element.50.refs_1_.refs_2_.refs_0_, ...), custom_call_target="tpu_custom_call" | custom-call | flops 2415919104 | bytes 14155776 | tf_op jit(solution)/shard_map/pallas_call | solution.py:243
  38.0 0.0 copy-start
  38.0 1.0 %shard_map.121 = (bf16[96,2048]{1,0:T(8,128)(2,1)S(1)}, bf16[96,1024]{1,0:T(8,128)(2,1)S(1)}, bf16[96,1024]{1,0:T(8,128)(2,1)S(1)}) custom-call(f32[8,128]{1,0:T(8,128)S(1)} %get-tuple-element.44.refs_0_.refs_1_, f32[8,128]{1,0:T(8,128)S(1)} %get-tuple-element.49.refs_1_.refs_0_, f32[8,128]{1,0:T(8,128)S(1)} %get-tuple-element.50.refs_1_.refs_2_.refs_0_, ...), custom_call_target="tpu_custom_call" | custom-call | flops 1024 | bytes 1024 | tf_op jit(solution)/shard_map/pallas_call | solution.py:243
  39.0 0.8 shard_map.122
  39.8 3.2 %collective-permute-done.11.refs_4_ = bf16[192,1024]{1,0:T(8,128)(2,1)S(1)} collective-permute-done((bf16[192,1024]{1,0:T(8,128)(2,1)S(1)}, bf16[192,1024]{1,0:T(8,128)(2,1)S(1)}, u32[]{:S(2)}, u32[]{:S(2)}) %collective-permute-start.11) | collective-permute-done | bytes 393248 | tf_op jit(solution)/shard_map/ppermute | solution.py:24
  43.0 0.0 collective-permute-done.10.refs_3_
  43.1 3.2 %shard_map.123 = (bf16[96,1024]{1,0:T(8,128)(2,1)S(1)}, bf16[96,1024]{1,0:T(8,128)(2,1)S(1)}, bf16[192,1024]{1,0:T(8,128)(2,1)S(1)}, bf16[384,768]{1,0:T(8,128)(2,1)S(1)}) custom-call(bf16[96,2048]{1,0:T(8,128)(2,1)S(1)} %get-tuple-element.60.refs_0_, bf16[96,1024]{1,0:T(8,128)(2,1)S(1)} %get-tuple-element.61.refs_1_.refs_7_, ...), custom_call_target="tpu_custom_call" | custom-call | flops 3019898880 | bytes 14155776 | tf_op jit(solution)/shard_map/pallas_call | solution.py:243
  46.3 0.2 collective-permute-start.12
  46.5 0.8 shard_map.124
  47.3 1.9 %collective-permute-start.13 = (bf16[192,1024]{1,0:T(8,128)(2,1)S(1)}, bf16[192,1024]{1,0:T(8,128)(2,1)S(1)}, u32[]{:S(2)}, u32[]{:S(2)}) collective-permute-start(bf16[192,1024]{1,0:T(8,128)(2,1)S(1)} %get-tuple-element.68), channel_id=1, source_target_pairs={{0,1},{1,0},{2,3},{3,2},{4,5},{5,4},{6,7},{7,6},{8,9},{9,8},{10,11... | collective-permute-start | bytes 1179656 | tf_op jit(solution)/shard_map/ppermute | solution.py:24
  49.2 2.2 %collective-permute-done.15.refs_4_ = bf16[192,1024]{1,0:T(8,128)(2,1)S(1)} collective-permute-done((bf16[192,1024]{1,0:T(8,128)(2,1)S(1)}, bf16[192,1024]{1,0:T(8,128)(2,1)S(1)}, u32[]{:S(2)}, u32[]{:S(2)}) %collective-permute-start.15) | collective-permute-done | bytes 393248 | tf_op jit(solution)/shard_map/ppermute | solution.py:24
  51.5 0.0 collective-permute-done.14.refs_3_
  51.5 3.7 %shard_map.125 = (bf16[96,1024]{1,0:T(8,128)(2,1)S(1)}, bf16[96,1024]{1,0:T(8,128)(2,1)S(1)}, bf16[192,1024]{1,0:T(8,128)(2,1)S(1)}, bf16[384,1536]{1,0:T(8,128)(2,1)S(1)}) custom-call(bf16[96,2048]{1,0:T(8,128)(2,1)S(1)} %get-tuple-element.70.refs_0_, bf16[96,1024]{1,0:T(8,128)(2,1)S(1)} %get-tuple-element.59.refs_7_.refs_1_, ...), custom_call_target="tpu_custom_call" | custom-call | flops 2415919104 | bytes 14155776 | tf_op jit(solution)/shard_map/pallas_call | solution.py:243
  55.2 0.2 collective-permute-start.19
  55.5 1.4 %shard_map.126 = (bf16[96,1024]{1,0:T(8,128)(2,1)S(1)}, bf16[96,1024]{1,0:T(8,128)(2,1)S(1)}, bf16[192,1024]{1,0:T(8,128)(2,1)S(1)}) custom-call(bf16[384,1536]{1,0:T(8,128)(2,1)S(1)} %get-tuple-element.74.both_ref, bf16[2048,1536]{1,0:T(8,128)(2,1)S(1)} %bitcast.25), custom_call_target="tpu_custom_call" | custom-call | flops 1024 | bytes 1024 | tf_op jit(solution)/shard_map/pallas_call | solution.py:243
  56.9 1.9 %collective-permute-start.18 = (bf16[192,1024]{1,0:T(8,128)(2,1)S(1)}, bf16[192,1024]{1,0:T(8,128)(2,1)S(1)}, u32[]{:S(2)}, u32[]{:S(2)}) collective-permute-start(bf16[192,1024]{1,0:T(8,128)(2,1)S(1)} %get-tuple-element.78), channel_id=1, source_target_pairs={{0,1},{1,0},{2,3},{3,2},{4,5},{5,4},{6,7},{7,6},{8,9},{9,8},{10,11... | collective-permute-start | bytes 1179656 | tf_op jit(solution)/shard_map/ppermute | solution.py:24
  58.8 0.0 collective-permute-done.12.refs_2_.refs_4_
  58.8 0.8 shard_map.127.refs_3_
  59.6 1.4 %collective-permute-start.16 = (bf16[128,1024]{1,0:T(8,128)(2,1)S(1)}, bf16[128,1024]{1,0:T(8,128)(2,1)S(1)}, u32[]{:S(2)}, u32[]{:S(2)}) collective-permute-start(bf16[128,1024]{1,0:T(8,128)(2,1)S(1)} %shard_map.127.refs_3_), channel_id=1, source_target_pairs={{0,1},{1,0},{2,3},{3,2},{4,5},{5,4},{6,7},{7,6},{8,9},{9,8},{10,11... | collective-permute-start | bytes 786440 | tf_op jit(solution)/shard_map/ppermute | solution.py:24
  61.0 0.0 collective-permute-done.13.refs_2_.refs_5_
  61.0 0.8 shard_map.128.refs_3_
  61.8 1.6 %collective-permute-start.17 = (bf16[128,1024]{1,0:T(8,128)(2,1)S(1)}, bf16[128,1024]{1,0:T(8,128)(2,1)S(1)}, u32[]{:S(2)}, u32[]{:S(2)}) collective-permute-start(bf16[128,1024]{1,0:T(8,128)(2,1)S(1)} %shard_map.128.refs_3_), channel_id=1, source_target_pairs={{0,2},{1,3},{2,0},{3,1},{4,6},{5,7},{6,4},{7,5},{8,10},{9,11},{10,... | collective-permute-start | bytes 786440 | tf_op jit(solution)/shard_map/ppermute | solution.py:24
  63.4 3.9 %collective-permute-done.19.refs_2_.refs_3_ = bf16[192,1024]{1,0:T(8,128)(2,1)S(1)} collective-permute-done((bf16[192,1024]{1,0:T(8,128)(2,1)S(1)}, bf16[192,1024]{1,0:T(8,128)(2,1)S(1)}, u32[]{:S(2)}, u32[]{:S(2)}) %collective-permute-start.19) | collective-permute-done | bytes 393248 | tf_op jit(solution)/shard_map/ppermute | solution.py:24
  67.3 0.5 shard_map.129.refs_3_
  67.7 1.9 %collective-permute-start.20 = (bf16[128,1024]{1,0:T(8,128)(2,1)S(1)}, bf16[128,1024]{1,0:T(8,128)(2,1)S(1)}, u32[]{:S(2)}, u32[]{:S(2)}) collective-permute-start(bf16[128,1024]{1,0:T(8,128)(2,1)S(1)} %shard_map.129.refs_3_), channel_id=1, source_target_pairs={{0,1},{1,0},{2,3},{3,2},{4,5},{5,4},{6,7},{7,6},{8,9},{9,8},{10,11... | collective-permute-start | bytes 786440 | tf_op jit(solution)/shard_map/ppermute | solution.py:24
  69.6 0.0 collective-permute-done.18.refs_2_.refs_4_
  69.6 0.5 shard_map.130.refs_8_
  70.1 1.2 %collective-permute-start.21 = (bf16[128,1024]{1,0:T(8,128)(2,1)S(1)}, bf16[128,1024]{1,0:T(8,128)(2,1)S(1)}, u32[]{:S(2)}, u32[]{:S(2)}) collective-permute-start(bf16[128,1024]{1,0:T(8,128)(2,1)S(1)} %shard_map.130.refs_8_), channel_id=1, source_target_pairs={{0,2},{1,3},{2,0},{3,1},{4,6},{5,7},{6,4},{7,5},{8,10},{9,11},{10,... | collective-permute-start | bytes 786440 | tf_op jit(solution)/shard_map/ppermute | solution.py:24
  71.2 3.4 %collective-permute-done.16.refs_6_ = bf16[128,1024]{1,0:T(8,128)(2,1)S(1)} collective-permute-done((bf16[128,1024]{1,0:T(8,128)(2,1)S(1)}, bf16[128,1024]{1,0:T(8,128)(2,1)S(1)}, u32[]{:S(2)}, u32[]{:S(2)}) %collective-permute-start.16) | collective-permute-done | bytes 262176 | tf_op jit(solution)/shard_map/ppermute | solution.py:24
  74.6 0.0 collective-permute-done.17.refs_7_
  74.6 1.7 %shard_map.131 = (bf16[128,2048]{1,0:T(8,128)(2,1)}, f32[8,128]{1,0:T(8,128)S(1)}) custom-call(bf16[128,2048]{1,0:T(8,128)(2,1)S(1)} %collective-permute-done.refs_0_, f32[8,128]{1,0:T(8,128)S(1)} %get-tuple-element.44.refs_0_.refs_1_, bf16[96,1024]{1,0:T(8,128)(2,1)S(1)} %get-tuple-element.64.refs_2_, ...), custom_call_target="tpu_custom_call" | custom-call | flops 1024 | bytes 1024 | tf_op jit(solution)/shard_map/pallas_call | solution.py:243
  76.3 3.6 %collective-permute-done.20.refs_5_ = bf16[128,1024]{1,0:T(8,128)(2,1)S(1)} collective-permute-done((bf16[128,1024]{1,0:T(8,128)(2,1)S(1)}, bf16[128,1024]{1,0:T(8,128)(2,1)S(1)}, u32[]{:S(2)}, u32[]{:S(2)}) %collective-permute-start.20) | collective-permute-done | bytes 262176 | tf_op jit(solution)/shard_map/ppermute | solution.py:24
  79.9 0.6 shard_map.132
  80.5 0.0 collective-permute-done.21.sum_y
  80.5 1.3 %shard_map.133 = bf16[128,2048]{1,0:T(8,128)(2,1)} custom-call(bf16[128,2048]{1,0:T(8,128)(2,1)S(1)} %collective-permute-done.5.refs_0_.grads_ref, bf16[128,2048]{1,0:T(8,128)(2,1)S(1)} %bitcast.30, f32[1,2048]{1,0:T(1,128)S(1)} %get-tuple-element.47.refs_1_.gain_ref, f32[128,1024]{1,0:T(8,128)S(1)} %get-tuple-element.84.left_ref, ...), custom_call_target="tpu_custom_call" | custom-call | flops 1024 | bytes 1024 | tf_op jit(solution)/shard_map/pallas_call | solution.py:243
  (10 shorter events, 0.1 us)
Async XLA Ops:
  0.6 11.7 %collective-permute-start = (bf16[128,2048]{1,0:T(8,128)(2,1)}, bf16[128,2048]{1,0:T(8,128)(2,1)S(1)}, u32[]{:S(2)}, u32[]{:S(2)}) collective-permute-start(bf16[128,2048]{1,0:T(8,128)(2,1)} %bitcast.36), channel_id=1, source_target_pairs={{0,4},{4,8},{8,12},{12,16},{16,20},{20,24},{24,28},{28,0},{1,5},{5... | collective-permute-start | bytes 1572872 | tf_op jit(solution)/shard_map/ppermute | solution.py:18
  2.8 14.5 %collective-permute-start.2 = (bf16[240,1024]{1,0:T(8,128)(2,1)S(1)}, bf16[240,1024]{1,0:T(8,128)(2,1)S(1)}, u32[]{:S(2)}, u32[]{:S(2)}) collective-permute-start(bf16[240,1024]{1,0:T(8,128)(2,1)S(1)} %get-tuple-element.46.refs_4_), channel_id=1, source_target_pairs={{0,2},{1,3},{2,0},{3,1},{4,6},{5,7},{6,4},{7,5},{8,10},{9,11},{10,... | collective-permute-start | bytes 1474568 | tf_op jit(solution)/shard_map/ppermute | solution.py:24
  5.4 13.8 %collective-permute-start.1 = (bf16[240,1024]{1,0:T(8,128)(2,1)S(1)}, bf16[240,1024]{1,0:T(8,128)(2,1)S(1)}, u32[]{:S(2)}, u32[]{:S(2)}) collective-permute-start(bf16[240,1024]{1,0:T(8,128)(2,1)S(1)} %get-tuple-element.45.refs_2_.refs_3_), channel_id=1, source_target_pairs={{0,1},{1,0},{2,3},{3,2},{4,5},{5,4},{6,7},{7,6},{8,9},{9,8},{10,11... | collective-permute-start | bytes 1474568 | tf_op jit(solution)/shard_map/ppermute | solution.py:24
  6.9 12.3 %collective-permute-start.5 = (bf16[128,2048]{1,0:T(8,128)(2,1)}, bf16[128,2048]{1,0:T(8,128)(2,1)S(1)}, u32[]{:S(2)}, u32[]{:S(2)}) collective-permute-start(bf16[128,2048]{1,0:T(8,128)(2,1)} %bitcast.37), channel_id=1, source_target_pairs={{0,28},{4,0},{8,4},{12,8},{16,12},{20,16},{24,20},{28,24},{1,29},{... | collective-permute-start | bytes 1572872 | tf_op jit(solution)/shard_map/ppermute | solution.py:18
  12.3 22.5 %slice-start = ((s8[6291456]{0:T(1024)(128)(4,1)}), s8[4194304]{0:T(1024)(128)(4,1)S(1)}, s32[]{:S(2)}) async-start(s8[6291456]{0:T(1024)(128)(4,1)} %bitcast.20), calls=%async_computation | async-start | bytes 8388608
  12.6 9.5 %collective-permute-start.4 = (bf16[128,1024]{1,0:T(8,128)(2,1)S(1)}, bf16[128,1024]{1,0:T(8,128)(2,1)S(1)}, u32[]{:S(2)}, u32[]{:S(2)}) collective-permute-start(bf16[128,1024]{1,0:T(8,128)(2,1)S(1)} %get-tuple-element.51.refs_4_), channel_id=1, source_target_pairs={{0,2},{1,3},{2,0},{3,1},{4,6},{5,7},{6,4},{7,5},{8,10},{9,11},{10,... | collective-permute-start | bytes 786440 | tf_op jit(solution)/shard_map/ppermute | solution.py:24
  14.8 20.0 %slice-start.1 = ((s8[6291456]{0:T(1024)(128)(4,1)}), s8[2097152]{0:T(1024)(128)(4,1)S(1)}, s32[]{:S(2)}) async-start(s8[6291456]{0:T(1024)(128)(4,1)} %bitcast.20), calls=%async_computation.1 | async-start | bytes 4194304
  14.8 10.0 %collective-permute-start.3 = (bf16[128,1024]{1,0:T(8,128)(2,1)S(1)}, bf16[128,1024]{1,0:T(8,128)(2,1)S(1)}, u32[]{:S(2)}, u32[]{:S(2)}) collective-permute-start(bf16[128,1024]{1,0:T(8,128)(2,1)S(1)} %get-tuple-element.48.refs_2_.refs_3_), channel_id=1, source_target_pairs={{0,1},{1,0},{2,3},{3,2},{4,5},{5,4},{6,7},{7,6},{8,9},{9,8},{10,11... | collective-permute-start | bytes 786440 | tf_op jit(solution)/shard_map/ppermute | solution.py:24
  19.2 9.3 %collective-permute-start.7 = (bf16[128,1024]{1,0:T(8,128)(2,1)S(1)}, bf16[128,1024]{1,0:T(8,128)(2,1)S(1)}, u32[]{:S(2)}, u32[]{:S(2)}) collective-permute-start(bf16[128,1024]{1,0:T(8,128)(2,1)S(1)} %get-tuple-element.53.refs_4_), channel_id=1, source_target_pairs={{0,2},{1,3},{2,0},{3,1},{4,6},{5,7},{6,4},{7,5},{8,10},{9,11},{10,... | collective-permute-start | bytes 786440 | tf_op jit(solution)/shard_map/ppermute | solution.py:24
  19.3 11.1 %collective-permute-start.6 = (bf16[128,1024]{1,0:T(8,128)(2,1)S(1)}, bf16[128,1024]{1,0:T(8,128)(2,1)S(1)}, u32[]{:S(2)}, u32[]{:S(2)}) collective-permute-start(bf16[128,1024]{1,0:T(8,128)(2,1)S(1)} %get-tuple-element.52.refs_4_.refs_3_), channel_id=1, source_target_pairs={{0,1},{1,0},{2,3},{3,2},{4,5},{5,4},{6,7},{7,6},{8,9},{9,8},{10,11... | collective-permute-start | bytes 786440 | tf_op jit(solution)/shard_map/ppermute | solution.py:24
  21.8 12.8 %collective-permute-start.9 = (bf16[96,1024]{1,0:T(8,128)(2,1)S(1)}, bf16[96,1024]{1,0:T(8,128)(2,1)S(1)}, u32[]{:S(2)}, u32[]{:S(2)}) collective-permute-start(bf16[96,1024]{1,0:T(8,128)(2,1)S(1)} %get-tuple-element.55), channel_id=1, source_target_pairs={{0,1},{1,0},{2,3},{3,2},{4,5},{5,4},{6,7},{7,6},{8,9},{9,8},{10,11... | collective-permute-start | bytes 589832 | tf_op jit(solution)/shard_map/ppermute | solution.py:24
  22.1 12.7 %collective-permute-start.8 = (bf16[96,1024]{1,0:T(8,128)(2,1)S(1)}, bf16[96,1024]{1,0:T(8,128)(2,1)S(1)}, u32[]{:S(2)}, u32[]{:S(2)}) collective-permute-start(bf16[96,1024]{1,0:T(8,128)(2,1)S(1)} %get-tuple-element.54.refs_7_), channel_id=1, source_target_pairs={{0,2},{1,3},{2,0},{3,1},{4,6},{5,7},{6,4},{7,5},{8,10},{9,11},{10,... | collective-permute-start | bytes 589832 | tf_op jit(solution)/shard_map/ppermute | solution.py:24
  25.7 17.4 %collective-permute-start.11 = (bf16[192,1024]{1,0:T(8,128)(2,1)S(1)}, bf16[192,1024]{1,0:T(8,128)(2,1)S(1)}, u32[]{:S(2)}, u32[]{:S(2)}) collective-permute-start(bf16[192,1024]{1,0:T(8,128)(2,1)S(1)} %get-tuple-element.63), channel_id=1, source_target_pairs={{0,1},{1,0},{2,3},{3,2},{4,5},{5,4},{6,7},{7,6},{8,9},{9,8},{10,11... | collective-permute-start | bytes 1179656 | tf_op jit(solution)/shard_map/ppermute | solution.py:24
  28.6 14.5 %collective-permute-start.10 = (bf16[192,1024]{1,0:T(8,128)(2,1)S(1)}, bf16[192,1024]{1,0:T(8,128)(2,1)S(1)}, u32[]{:S(2)}, u32[]{:S(2)}) collective-permute-start(bf16[192,1024]{1,0:T(8,128)(2,1)S(1)} %get-tuple-element.56.refs_7_), channel_id=1, source_target_pairs={{0,2},{1,3},{2,0},{3,1},{4,6},{5,7},{6,4},{7,5},{8,10},{9,11},{10,... | collective-permute-start | bytes 1179656 | tf_op jit(solution)/shard_map/ppermute | solution.py:24
  31.5 19.9 %collective-permute-start.15 = (bf16[192,1024]{1,0:T(8,128)(2,1)S(1)}, bf16[192,1024]{1,0:T(8,128)(2,1)S(1)}, u32[]{:S(2)}, u32[]{:S(2)}) collective-permute-start(bf16[192,1024]{1,0:T(8,128)(2,1)S(1)} %get-tuple-element.72), channel_id=1, source_target_pairs={{0,1},{1,0},{2,3},{3,2},{4,5},{5,4},{6,7},{7,6},{8,9},{9,8},{10,11... | collective-permute-start | bytes 1179656 | tf_op jit(solution)/shard_map/ppermute | solution.py:24
  34.6 16.9 %collective-permute-start.14 = (bf16[192,1024]{1,0:T(8,128)(2,1)S(1)}, bf16[192,1024]{1,0:T(8,128)(2,1)S(1)}, u32[]{:S(2)}, u32[]{:S(2)}) collective-permute-start(bf16[192,1024]{1,0:T(8,128)(2,1)S(1)} %get-tuple-element.57.refs_10_), channel_id=1, source_target_pairs={{0,2},{1,3},{2,0},{3,1},{4,6},{5,7},{6,4},{7,5},{8,10},{9,11},{10,... | collective-permute-start | bytes 1179656 | tf_op jit(solution)/shard_map/ppermute | solution.py:24
  38.0 5.0 %copy-start = (bf16[1,1,768,2048]{3,2,1,0:T(8,128)(2,1)S(1)}, bf16[1,1,768,2048]{3,2,1,0:T(8,128)(2,1)}, u32[]{:S(2)}) copy-start(bf16[1,1,768,2048]{3,2,1,0:T(8,128)(2,1)} %param.19) | copy-start | bytes 9437188
  46.3 12.5 %collective-permute-start.12 = (bf16[192,1024]{1,0:T(8,128)(2,1)S(1)}, bf16[192,1024]{1,0:T(8,128)(2,1)S(1)}, u32[]{:S(2)}, u32[]{:S(2)}) collective-permute-start(bf16[192,1024]{1,0:T(8,128)(2,1)S(1)} %get-tuple-element.67), channel_id=1, source_target_pairs={{0,2},{1,3},{2,0},{3,1},{4,6},{5,7},{6,4},{7,5},{8,10},{9,11},{10,... | collective-permute-start | bytes 1179656 | tf_op jit(solution)/shard_map/ppermute | solution.py:24
  47.3 13.7 %collective-permute-start.13 = (bf16[192,1024]{1,0:T(8,128)(2,1)S(1)}, bf16[192,1024]{1,0:T(8,128)(2,1)S(1)}, u32[]{:S(2)}, u32[]{:S(2)}) collective-permute-start(bf16[192,1024]{1,0:T(8,128)(2,1)S(1)} %get-tuple-element.68), channel_id=1, source_target_pairs={{0,1},{1,0},{2,3},{3,2},{4,5},{5,4},{6,7},{7,6},{8,9},{9,8},{10,11... | collective-permute-start | bytes 1179656 | tf_op jit(solution)/shard_map/ppermute | solution.py:24
  55.2 12.1 %collective-permute-start.19 = (bf16[192,1024]{1,0:T(8,128)(2,1)S(1)}, bf16[192,1024]{1,0:T(8,128)(2,1)S(1)}, u32[]{:S(2)}, u32[]{:S(2)}) collective-permute-start(bf16[192,1024]{1,0:T(8,128)(2,1)S(1)} %get-tuple-element.80), channel_id=1, source_target_pairs={{0,2},{1,3},{2,0},{3,1},{4,6},{5,7},{6,4},{7,5},{8,10},{9,11},{10,... | collective-permute-start | bytes 1179656 | tf_op jit(solution)/shard_map/ppermute | solution.py:24
  56.9 12.7 %collective-permute-start.18 = (bf16[192,1024]{1,0:T(8,128)(2,1)S(1)}, bf16[192,1024]{1,0:T(8,128)(2,1)S(1)}, u32[]{:S(2)}, u32[]{:S(2)}) collective-permute-start(bf16[192,1024]{1,0:T(8,128)(2,1)S(1)} %get-tuple-element.78), channel_id=1, source_target_pairs={{0,1},{1,0},{2,3},{3,2},{4,5},{5,4},{6,7},{7,6},{8,9},{9,8},{10,11... | collective-permute-start | bytes 1179656 | tf_op jit(solution)/shard_map/ppermute | solution.py:24
  59.6 15.0 %collective-permute-start.16 = (bf16[128,1024]{1,0:T(8,128)(2,1)S(1)}, bf16[128,1024]{1,0:T(8,128)(2,1)S(1)}, u32[]{:S(2)}, u32[]{:S(2)}) collective-permute-start(bf16[128,1024]{1,0:T(8,128)(2,1)S(1)} %shard_map.127.refs_3_), channel_id=1, source_target_pairs={{0,1},{1,0},{2,3},{3,2},{4,5},{5,4},{6,7},{7,6},{8,9},{9,8},{10,11... | collective-permute-start | bytes 786440 | tf_op jit(solution)/shard_map/ppermute | solution.py:24
  61.8 12.8 %collective-permute-start.17 = (bf16[128,1024]{1,0:T(8,128)(2,1)S(1)}, bf16[128,1024]{1,0:T(8,128)(2,1)S(1)}, u32[]{:S(2)}, u32[]{:S(2)}) collective-permute-start(bf16[128,1024]{1,0:T(8,128)(2,1)S(1)} %shard_map.128.refs_3_), channel_id=1, source_target_pairs={{0,2},{1,3},{2,0},{3,1},{4,6},{5,7},{6,4},{7,5},{8,10},{9,11},{10,... | collective-permute-start | bytes 786440 | tf_op jit(solution)/shard_map/ppermute | solution.py:24
  67.7 12.2 %collective-permute-start.20 = (bf16[128,1024]{1,0:T(8,128)(2,1)S(1)}, bf16[128,1024]{1,0:T(8,128)(2,1)S(1)}, u32[]{:S(2)}, u32[]{:S(2)}) collective-permute-start(bf16[128,1024]{1,0:T(8,128)(2,1)S(1)} %shard_map.129.refs_3_), channel_id=1, source_target_pairs={{0,1},{1,0},{2,3},{3,2},{4,5},{5,4},{6,7},{7,6},{8,9},{9,8},{10,11... | collective-permute-start | bytes 786440 | tf_op jit(solution)/shard_map/ppermute | solution.py:24
  70.1 10.4 %collective-permute-start.21 = (bf16[128,1024]{1,0:T(8,128)(2,1)S(1)}, bf16[128,1024]{1,0:T(8,128)(2,1)S(1)}, u32[]{:S(2)}, u32[]{:S(2)}) collective-permute-start(bf16[128,1024]{1,0:T(8,128)(2,1)S(1)} %shard_map.130.refs_8_), channel_id=1, source_target_pairs={{0,2},{1,3},{2,0},{3,1},{4,6},{5,7},{6,4},{7,5},{8,10},{9,11},{10,... | collective-permute-start | bytes 786440 | tf_op jit(solution)/shard_map/ppermute | solution.py:24
  76.3 4.2 %copy-start.1 = (bf16[1,128,2048]{2,1,0:T(8,128)(2,1)S(1)}, bf16[1,128,2048]{2,1,0:T(8,128)(2,1)}, u32[]{:S(2)}) copy-start(bf16[1,128,2048]{2,1,0:T(8,128)(2,1)} %param.12) | copy-start | bytes 1572868

commit v14 on v13

--- a/solution.py
+++ b/solution.py
@@ -662,23 +662,27 @@
 
 
 def hop_bwd_near_kernel(
-    top_count, own, keep_left, keep_right, got_y, got_x, sum_x, left_ref, right_ref
+    top_count, own, keep_left, keep_right, got_y, got_x, left_ref, right_ref
 ):
     capacity = keep_left.shape[0]
     mine = pick(own[...], 0, capacity, "b", top_count)
     near_y = pick(own[...], 2, capacity, "b", top_count)
     near_x = pick(own[...], 1, capacity, "b", top_count)
-    left = to_tokens(mine, keep_left[...]) + to_tokens(near_y, got_y[:capacity, :])
-    left_ref[...] = left + sum_x[...].astype(jnp.float32)
+    left_ref[...] = to_tokens(mine, keep_left[...]) + to_tokens(near_y, got_y[:capacity, :])
     right_ref[...] = to_tokens(mine, keep_right[...]) + to_tokens(near_x, got_x[:capacity, :])
 
 
-def hop_bwd_end_kernel(grads_ref, saved_ref, gain_ref, left_ref, right_ref, sum_y, out_ref):
+def order_kernel(order_ref):
+    order_ref[...] = jnp.zeros_like(order_ref)
+
+
+def hop_bwd_end_kernel(grads_ref, saved_ref, gain_ref, left_ref, right_ref, sum_x, sum_y, out_ref):
     features = saved_ref.shape[1]
     half = features // 2
     parts = []
+    left = left_ref[...] + sum_x[...].astype(jnp.float32)
     right = right_ref[...] + sum_y[...].astype(jnp.float32)
-    for start, d_normed in ((0, left_ref[...]), (half, right)):
+    for start, d_normed in ((0, left), (half, right)):
         wide = saved_ref[:, start : start + half].astype(jnp.float32)
         scaled = d_normed * gain_ref[:, start : start + half]
         parts.append((start, wide, scaled))
@@ -896,17 +900,26 @@
     b_near = local_call(
         functools.partial(hop_bwd_near_kernel, top_count),
         [shaped(tok_rows, half, jnp.float32)] * 2,
-        (own, *b_keep, b_ret_y, b_ret_x, b_sum_x),
+        (own, *b_keep, b_ret_y, b_ret_x),
         one_hop,
         moved,
-        after=(order,),
+        after=(last,),
+    )
+    x_there = local_call(
+        order_kernel,
+        shaped(8, 128, jnp.float32),
+        (),
+        one_hop,
+        moved,
+        after=(order, b_near[0], b_sum_x),
     )
     bwd_block = local_call(
         hop_bwd_end_kernel,
         shaped(tok_rows, features),
-        (grad_in, saved, gain_here, *b_near, b_sum_y),
+        (grad_in, saved, gain_here, *b_near, b_sum_x, b_sum_y),
         one_hop,
         moved,
+        after=(x_there,),
     )
     return (fwd_block[None], bwd_block[None])
 

time: 82 us -> 81.4 us (level)
    pallas_call x20 -> x21, Pallas kernels: 22.9 us -> 23 us  [local_call(): pl.pallas_call(body if after else kernel, out_shape=out_shapes, in_specs=...]
where the time goes in v14:
time: 81.4 us; the launch traced here: 81.2 us
  starting transfers between devices  32.5 us (40%)
  Pallas kernels  24.6 us (30%)
  waiting for transfers between devices  23.2 us (29%)
  between operations  0.84 us (1%)
    ppermute x20, starting transfers between devices, swapped(): return lax.ppermute(value, axis, pairs)  29 us
    pallas_call x21, Pallas kernels, local_call(): pl.pallas_call(body if after else kernel, out_shape=out_shapes, in_specs=...  23 us
    ppermute x20, waiting for transfers between devices, swapped(): return lax.ppermute(value, axis, pairs)  20.8 us
    ppermute x2, starting transfers between devices, passed_along(): return lax.ppermute(value, axis, pairs)  3.46 us
    ppermute x2, waiting for transfers between devices, passed_along(): return lax.ppermute(value, axis, pairs)  2.47 us
    pallas_call x1, Pallas kernels, per_device_hops(): pl.pallas_call(functools.partial(first_kernel, top_count), out_shape=[sha...  1.68 us
  transfers between devices with their start and end apart: 22, of which 12 were waited for; matrix products, arithmetic and copies ran while one was open for 0% of the time, Pallas kernels for 29%

profile of v14, /device:TPU:0, one launch (start us, length us, event | category | flops | bytes accessed | tf_op | source)
XLA Modules:
  0.0 81.2 jit_solution(7634408675231999313)
XLA Ops:
  0.6 0.5 collective-permute-start
  1.1 1.7 %shard_map.113 = (bf16[240,1024]{1,0:T(8,128)(2,1)S(1)}, bf16[240,1024]{1,0:T(8,128)(2,1)S(1)}, f32[8,128]{1,0:T(8,128)S(1)}, f32[1,2048]{1,0:T(1,128)S(1)}) custom-call(s32[1]{0:T(128)} %bitcast.1.me_ref, bf16[128,2048]{1,0:T(8,128)(2,1)} %bitcast.29, f32[1,2048]{1,0:T(1,128)} %refs_1_.1, s32[2,128]{1,0:T(2,128)} %bitcast.32, f32[2,128]{1,0:T(2,128)} %bitcast.33, ...), custom_call_target="tpu_custom_call" | custom-call | flops 1024 | bytes 1024 | tf_op jit(solution)/shard_map/pallas_call | solution.py:746
  2.8 2.6 %collective-permute-start.2 = (bf16[240,1024]{1,0:T(8,128)(2,1)S(1)}, bf16[240,1024]{1,0:T(8,128)(2,1)S(1)}, u32[]{:S(2)}, u32[]{:S(2)}) collective-permute-start(bf16[240,1024]{1,0:T(8,128)(2,1)S(1)} %get-tuple-element.46.refs_4_), channel_id=1, source_target_pairs={{0,2},{1,3},{2,0},{3,1},{4,6},{5,7},{6,4},{7,5},{8,10},{9,11},{10,... | collective-permute-start | bytes 1474568 | tf_op jit(solution)/shard_map/ppermute | solution.py:24
  5.4 1.5 %collective-permute-start.1 = (bf16[240,1024]{1,0:T(8,128)(2,1)S(1)}, bf16[240,1024]{1,0:T(8,128)(2,1)S(1)}, u32[]{:S(2)}, u32[]{:S(2)}) collective-permute-start(bf16[240,1024]{1,0:T(8,128)(2,1)S(1)} %get-tuple-element.45.refs_2_.refs_3_), channel_id=1, source_target_pairs={{0,1},{1,0},{2,3},{3,2},{4,5},{5,4},{6,7},{7,6},{8,9},{9,8},{10,11... | collective-permute-start | bytes 1474568 | tf_op jit(solution)/shard_map/ppermute | solution.py:24
  6.9 3.0 %collective-permute-start.5 = (bf16[128,2048]{1,0:T(8,128)(2,1)}, bf16[128,2048]{1,0:T(8,128)(2,1)S(1)}, u32[]{:S(2)}, u32[]{:S(2)}) collective-permute-start(bf16[128,2048]{1,0:T(8,128)(2,1)} %bitcast.37), channel_id=1, source_target_pairs={{0,28},{4,0},{8,4},{12,8},{16,12},{20,16},{24,20},{28,24},{1,29},{... | collective-permute-start | bytes 1572872 | tf_op jit(solution)/shard_map/ppermute | solution.py:18
  9.9 2.5 %collective-permute-done.refs_0_ = bf16[128,2048]{1,0:T(8,128)(2,1)S(1)} collective-permute-done((bf16[128,2048]{1,0:T(8,128)(2,1)}, bf16[128,2048]{1,0:T(8,128)(2,1)S(1)}, u32[]{:S(2)}, u32[]{:S(2)}) %collective-permute-start) | collective-permute-done | bytes 524320 | tf_op jit(solution)/shard_map/ppermute | solution.py:18
  12.3 0.2 shard_map.114
  12.6 2.3 %collective-permute-start.4 = (bf16[128,1024]{1,0:T(8,128)(2,1)S(1)}, bf16[128,1024]{1,0:T(8,128)(2,1)S(1)}, u32[]{:S(2)}, u32[]{:S(2)}) collective-permute-start(bf16[128,1024]{1,0:T(8,128)(2,1)S(1)} %get-tuple-element.51.refs_4_), channel_id=1, source_target_pairs={{0,2},{1,3},{2,0},{3,1},{4,6},{5,7},{6,4},{7,5},{8,10},{9,11},{10,... | collective-permute-start | bytes 786440 | tf_op jit(solution)/shard_map/ppermute | solution.py:24
  14.8 2.4 %collective-permute-start.3 = (bf16[128,1024]{1,0:T(8,128)(2,1)S(1)}, bf16[128,1024]{1,0:T(8,128)(2,1)S(1)}, u32[]{:S(2)}, u32[]{:S(2)}) collective-permute-start(bf16[128,1024]{1,0:T(8,128)(2,1)S(1)} %get-tuple-element.48.refs_2_.refs_3_), channel_id=1, source_target_pairs={{0,1},{1,0},{2,3},{3,2},{4,5},{5,4},{6,7},{7,6},{8,9},{9,8},{10,11... | collective-permute-start | bytes 786440 | tf_op jit(solution)/shard_map/ppermute | solution.py:24
  17.3 0.0 collective-permute-done.2.refs_1_.refs_3_.refs_6_
  17.3 1.9 %collective-permute-done.1.refs_0_.refs_2_.refs_5_ = bf16[240,1024]{1,0:T(8,128)(2,1)S(1)} collective-permute-done((bf16[240,1024]{1,0:T(8,128)(2,1)S(1)}, bf16[240,1024]{1,0:T(8,128)(2,1)S(1)}, u32[]{:S(2)}, u32[]{:S(2)}) %collective-permute-start.1) | collective-permute-done | bytes 491552 | tf_op jit(solution)/shard_map/ppermute | solution.py:24
  19.2 0.0 collective-permute-done.5.refs_0_
  19.2 0.1 collective-permute-start.7
  19.3 2.0 %collective-permute-start.6 = (bf16[128,1024]{1,0:T(8,128)(2,1)S(1)}, bf16[128,1024]{1,0:T(8,128)(2,1)S(1)}, u32[]{:S(2)}, u32[]{:S(2)}) collective-permute-start(bf16[128,1024]{1,0:T(8,128)(2,1)S(1)} %get-tuple-element.52.refs_4_.refs_3_), channel_id=1, source_target_pairs={{0,1},{1,0},{2,3},{3,2},{4,5},{5,4},{6,7},{7,6},{8,9},{9,8},{10,11... | collective-permute-start | bytes 786440 | tf_op jit(solution)/shard_map/ppermute | solution.py:24
  21.3 0.5 shard_map.117
  21.8 0.2 collective-permute-start.9
  22.0 0.1 collective-permute-done.4.refs_6_
  22.1 2.4 %collective-permute-start.8 = (bf16[96,1024]{1,0:T(8,128)(2,1)S(1)}, bf16[96,1024]{1,0:T(8,128)(2,1)S(1)}, u32[]{:S(2)}, u32[]{:S(2)}) collective-permute-start(bf16[96,1024]{1,0:T(8,128)(2,1)S(1)} %get-tuple-element.54.refs_7_), channel_id=1, source_target_pairs={{0,2},{1,3},{2,0},{3,1},{4,6},{5,7},{6,4},{7,5},{8,10},{9,11},{10,... | collective-permute-start | bytes 589832 | tf_op jit(solution)/shard_map/ppermute | solution.py:24
  24.5 0.3 collective-permute-done.3.refs_5_
  24.8 0.9 %shard_map.118 = (bf16[192,1024]{1,0:T(8,128)(2,1)S(1)}, bf16[192,1024]{1,0:T(8,128)(2,1)S(1)}) custom-call(f32[8,128]{1,0:T(8,128)S(1)} %get-tuple-element.44.refs_0_.refs_1_, f32[8,128]{1,0:T(8,128)S(1)} %get-tuple-element.49.refs_1_.refs_0_, f32[8,128]{1,0:T(8,128)S(1)} %get-tuple-element.50.refs_1_.refs_2_.refs_0_, ...), custom_call_target="tpu_custom_call" | custom-call | flops 1024 | bytes 1024 | tf_op jit(solution)/shard_map/pallas_call | solution.py:243
  25.7 1.8 %collective-permute-start.11 = (bf16[192,1024]{1,0:T(8,128)(2,1)S(1)}, bf16[192,1024]{1,0:T(8,128)(2,1)S(1)}, u32[]{:S(2)}, u32[]{:S(2)}) collective-permute-start(bf16[192,1024]{1,0:T(8,128)(2,1)S(1)} %get-tuple-element.63), channel_id=1, source_target_pairs={{0,1},{1,0},{2,3},{3,2},{4,5},{5,4},{6,7},{7,6},{8,9},{9,8},{10,11... | collective-permute-start | bytes 1179656 | tf_op jit(solution)/shard_map/ppermute | solution.py:24
  27.5 1.1 %collective-permute-done.7.refs_6_ = bf16[128,1024]{1,0:T(8,128)(2,1)S(1)} collective-permute-done((bf16[128,1024]{1,0:T(8,128)(2,1)S(1)}, bf16[128,1024]{1,0:T(8,128)(2,1)S(1)}, u32[]{:S(2)}, u32[]{:S(2)}) %collective-permute-start.7) | collective-permute-done | bytes 262176 | tf_op jit(solution)/shard_map/ppermute | solution.py:24
  28.6 1.5 %collective-permute-start.10 = (bf16[192,1024]{1,0:T(8,128)(2,1)S(1)}, bf16[192,1024]{1,0:T(8,128)(2,1)S(1)}, u32[]{:S(2)}, u32[]{:S(2)}) collective-permute-start(bf16[192,1024]{1,0:T(8,128)(2,1)S(1)} %get-tuple-element.56.refs_7_), channel_id=1, source_target_pairs={{0,2},{1,3},{2,0},{3,1},{4,6},{5,7},{6,4},{7,5},{8,10},{9,11},{10,... | collective-permute-start | bytes 1179656 | tf_op jit(solution)/shard_map/ppermute | solution.py:24
  30.1 0.3 collective-permute-done.6.refs_5_
  30.4 1.1 %shard_map.119 = (bf16[192,1024]{1,0:T(8,128)(2,1)S(1)}, bf16[192,1024]{1,0:T(8,128)(2,1)S(1)}) custom-call(f32[8,128]{1,0:T(8,128)S(1)} %get-tuple-element.44.refs_0_.refs_1_, f32[8,128]{1,0:T(8,128)S(1)} %get-tuple-element.49.refs_1_.refs_0_, f32[8,128]{1,0:T(8,128)S(1)} %get-tuple-element.50.refs_1_.refs_2_.refs_0_, ...), custom_call_target="tpu_custom_call" | custom-call | flops 1024 | bytes 1024 | tf_op jit(solution)/shard_map/pallas_call | solution.py:243
  31.5 1.8 %collective-permute-start.15 = (bf16[192,1024]{1,0:T(8,128)(2,1)S(1)}, bf16[192,1024]{1,0:T(8,128)(2,1)S(1)}, u32[]{:S(2)}, u32[]{:S(2)}) collective-permute-start(bf16[192,1024]{1,0:T(8,128)(2,1)S(1)} %get-tuple-element.72), channel_id=1, source_target_pairs={{0,1},{1,0},{2,3},{3,2},{4,5},{5,4},{6,7},{7,6},{8,9},{9,8},{10,11... | collective-permute-start | bytes 1179656 | tf_op jit(solution)/shard_map/ppermute | solution.py:24
  33.3 1.3 %collective-permute-done.9.refs_8_ = bf16[96,1024]{1,0:T(8,128)(2,1)S(1)} collective-permute-done((bf16[96,1024]{1,0:T(8,128)(2,1)S(1)}, bf16[96,1024]{1,0:T(8,128)(2,1)S(1)}, u32[]{:S(2)}, u32[]{:S(2)}) %collective-permute-start.9) | collective-permute-done | bytes 196640 | tf_op jit(solution)/shard_map/ppermute | solution.py:24
  34.6 0.2 collective-permute-start.14
  34.8 0.0 collective-permute-done.8.refs_7_
  34.8 3.2 %shard_map.120 = (f32[384,768]{1,0:T(8,128)S(1)}, f32[384,768]{1,0:T(8,128)S(1)}) custom-call(f32[8,128]{1,0:T(8,128)S(1)} %get-tuple-element.44.refs_0_.refs_1_, f32[8,128]{1,0:T(8,128)S(1)} %get-tuple-element.49.refs_1_.refs_0_, f32[8,128]{1,0:T(8,128)S(1)} %get-tuple-element.50.refs_1_.refs_2_.refs_0_, ...), custom_call_target="tpu_custom_call" | custom-call | flops 2415919104 | bytes 14155776 | tf_op jit(solution)/shard_map/pallas_call | solution.py:243
  38.0 0.0 copy-start
  38.0 1.0 %shard_map.121 = (bf16[96,2048]{1,0:T(8,128)(2,1)S(1)}, bf16[96,1024]{1,0:T(8,128)(2,1)S(1)}, bf16[96,1024]{1,0:T(8,128)(2,1)S(1)}) custom-call(f32[8,128]{1,0:T(8,128)S(1)} %get-tuple-element.44.refs_0_.refs_1_, f32[8,128]{1,0:T(8,128)S(1)} %get-tuple-element.49.refs_1_.refs_0_, f32[8,128]{1,0:T(8,128)S(1)} %get-tuple-element.50.refs_1_.refs_2_.refs_0_, ...), custom_call_target="tpu_custom_call" | custom-call | flops 1024 | bytes 1024 | tf_op jit(solution)/shard_map/pallas_call | solution.py:243
  39.0 0.8 shard_map.122
  39.8 3.2 %collective-permute-done.11.refs_4_ = bf16[192,1024]{1,0:T(8,128)(2,1)S(1)} collective-permute-done((bf16[192,1024]{1,0:T(8,128)(2,1)S(1)}, bf16[192,1024]{1,0:T(8,128)(2,1)S(1)}, u32[]{:S(2)}, u32[]{:S(2)}) %collective-permute-start.11) | collective-permute-done | bytes 393248 | tf_op jit(solution)/shard_map/ppermute | solution.py:24
  43.0 0.0 collective-permute-done.10.refs_3_
  43.1 3.2 %shard_map.123 = (bf16[96,1024]{1,0:T(8,128)(2,1)S(1)}, bf16[96,1024]{1,0:T(8,128)(2,1)S(1)}, bf16[192,1024]{1,0:T(8,128)(2,1)S(1)}, bf16[384,768]{1,0:T(8,128)(2,1)S(1)}) custom-call(bf16[96,2048]{1,0:T(8,128)(2,1)S(1)} %get-tuple-element.60.refs_0_, bf16[96,1024]{1,0:T(8,128)(2,1)S(1)} %get-tuple-element.61.refs_1_.refs_7_, ...), custom_call_target="tpu_custom_call" | custom-call | flops 3019898880 | bytes 14155776 | tf_op jit(solution)/shard_map/pallas_call | solution.py:243
  46.3 0.2 collective-permute-start.12
  46.5 0.8 shard_map.124
  47.3 1.9 %collective-permute-start.13 = (bf16[192,1024]{1,0:T(8,128)(2,1)S(1)}, bf16[192,1024]{1,0:T(8,128)(2,1)S(1)}, u32[]{:S(2)}, u32[]{:S(2)}) collective-permute-start(bf16[192,1024]{1,0:T(8,128)(2,1)S(1)} %get-tuple-element.68), channel_id=1, source_target_pairs={{0,1},{1,0},{2,3},{3,2},{4,5},{5,4},{6,7},{7,6},{8,9},{9,8},{10,11... | collective-permute-start | bytes 1179656 | tf_op jit(solution)/shard_map/ppermute | solution.py:24
  49.2 2.3 %collective-permute-done.15.refs_4_ = bf16[192,1024]{1,0:T(8,128)(2,1)S(1)} collective-permute-done((bf16[192,1024]{1,0:T(8,128)(2,1)S(1)}, bf16[192,1024]{1,0:T(8,128)(2,1)S(1)}, u32[]{:S(2)}, u32[]{:S(2)}) %collective-permute-start.15) | collective-permute-done | bytes 393248 | tf_op jit(solution)/shard_map/ppermute | solution.py:24
  51.5 0.0 collective-permute-done.14.refs_3_
  51.5 3.7 %shard_map.125 = (bf16[96,1024]{1,0:T(8,128)(2,1)S(1)}, bf16[96,1024]{1,0:T(8,128)(2,1)S(1)}, bf16[192,1024]{1,0:T(8,128)(2,1)S(1)}, bf16[384,1536]{1,0:T(8,128)(2,1)S(1)}) custom-call(bf16[96,2048]{1,0:T(8,128)(2,1)S(1)} %get-tuple-element.70.refs_0_, bf16[96,1024]{1,0:T(8,128)(2,1)S(1)} %get-tuple-element.59.refs_7_.refs_1_, ...), custom_call_target="tpu_custom_call" | custom-call | flops 2415919104 | bytes 14155776 | tf_op jit(solution)/shard_map/pallas_call | solution.py:243
  55.2 0.2 collective-permute-start.19
  55.5 1.4 %shard_map.126 = (bf16[96,1024]{1,0:T(8,128)(2,1)S(1)}, bf16[96,1024]{1,0:T(8,128)(2,1)S(1)}, bf16[192,1024]{1,0:T(8,128)(2,1)S(1)}) custom-call(bf16[384,1536]{1,0:T(8,128)(2,1)S(1)} %get-tuple-element.74.both_ref, bf16[2048,1536]{1,0:T(8,128)(2,1)S(1)} %bitcast.25), custom_call_target="tpu_custom_call" | custom-call | flops 1024 | bytes 1024 | tf_op jit(solution)/shard_map/pallas_call | solution.py:243
  56.9 1.9 %collective-permute-start.18 = (bf16[192,1024]{1,0:T(8,128)(2,1)S(1)}, bf16[192,1024]{1,0:T(8,128)(2,1)S(1)}, u32[]{:S(2)}, u32[]{:S(2)}) collective-permute-start(bf16[192,1024]{1,0:T(8,128)(2,1)S(1)} %get-tuple-element.78), channel_id=1, source_target_pairs={{0,1},{1,0},{2,3},{3,2},{4,5},{5,4},{6,7},{7,6},{8,9},{9,8},{10,11... | collective-permute-start | bytes 1179656 | tf_op jit(solution)/shard_map/ppermute | solution.py:24
  58.8 0.0 collective-permute-done.12.refs_2_.refs_4_
  58.8 0.8 shard_map.127.refs_3_
  59.6 1.4 %collective-permute-start.16 = (bf16[128,1024]{1,0:T(8,128)(2,1)S(1)}, bf16[128,1024]{1,0:T(8,128)(2,1)S(1)}, u32[]{:S(2)}, u32[]{:S(2)}) collective-permute-start(bf16[128,1024]{1,0:T(8,128)(2,1)S(1)} %shard_map.127.refs_3_), channel_id=1, source_target_pairs={{0,1},{1,0},{2,3},{3,2},{4,5},{5,4},{6,7},{7,6},{8,9},{9,8},{10,11... | collective-permute-start | bytes 786440 | tf_op jit(solution)/shard_map/ppermute | solution.py:24
  61.0 0.0 collective-permute-done.13.refs_2_.refs_5_
  61.0 0.8 shard_map.128.refs_3_
  61.8 1.6 %collective-permute-start.17 = (bf16[128,1024]{1,0:T(8,128)(2,1)S(1)}, bf16[128,1024]{1,0:T(8,128)(2,1)S(1)}, u32[]{:S(2)}, u32[]{:S(2)}) collective-permute-start(bf16[128,1024]{1,0:T(8,128)(2,1)S(1)} %shard_map.128.refs_3_), channel_id=1, source_target_pairs={{0,2},{1,3},{2,0},{3,1},{4,6},{5,7},{6,4},{7,5},{8,10},{9,11},{10,... | collective-permute-start | bytes 786440 | tf_op jit(solution)/shard_map/ppermute | solution.py:24
  63.4 3.9 %collective-permute-done.19.refs_2_.refs_3_ = bf16[192,1024]{1,0:T(8,128)(2,1)S(1)} collective-permute-done((bf16[192,1024]{1,0:T(8,128)(2,1)S(1)}, bf16[192,1024]{1,0:T(8,128)(2,1)S(1)}, u32[]{:S(2)}, u32[]{:S(2)}) %collective-permute-start.19) | collective-permute-done | bytes 393248 | tf_op jit(solution)/shard_map/ppermute | solution.py:24
  67.3 0.5 shard_map.129.refs_3_
  67.7 1.9 %collective-permute-start.20 = (bf16[128,1024]{1,0:T(8,128)(2,1)S(1)}, bf16[128,1024]{1,0:T(8,128)(2,1)S(1)}, u32[]{:S(2)}, u32[]{:S(2)}) collective-permute-start(bf16[128,1024]{1,0:T(8,128)(2,1)S(1)} %shard_map.129.refs_3_), channel_id=1, source_target_pairs={{0,1},{1,0},{2,3},{3,2},{4,5},{5,4},{6,7},{7,6},{8,9},{9,8},{10,11... | collective-permute-start | bytes 786440 | tf_op jit(solution)/shard_map/ppermute | solution.py:24
  69.6 0.0 collective-permute-done.18.refs_2_.refs_4_
  69.6 0.5 shard_map.130.refs_8_.refs_5_
  70.1 1.2 %collective-permute-start.21 = (bf16[128,1024]{1,0:T(8,128)(2,1)S(1)}, bf16[128,1024]{1,0:T(8,128)(2,1)S(1)}, u32[]{:S(2)}, u32[]{:S(2)}) collective-permute-start(bf16[128,1024]{1,0:T(8,128)(2,1)S(1)} %shard_map.130.refs_8_.refs_5_), channel_id=1, source_target_pairs={{0,2},{1,3},{2,0},{3,1},{4,6},{5,7},{6,4},{7,5},{8,10},{9,11},{10,... | collective-permute-start | bytes 786440 | tf_op jit(solution)/shard_map/ppermute | solution.py:24
  71.2 0.6 shard_map.132
  71.9 2.8 %collective-permute-done.16.refs_6_ = bf16[128,1024]{1,0:T(8,128)(2,1)S(1)} collective-permute-done((bf16[128,1024]{1,0:T(8,128)(2,1)S(1)}, bf16[128,1024]{1,0:T(8,128)(2,1)S(1)}, u32[]{:S(2)}, u32[]{:S(2)}) %collective-permute-start.16) | collective-permute-done | bytes 262176 | tf_op jit(solution)/shard_map/ppermute | solution.py:24
  74.6 0.0 collective-permute-done.17.refs_7_
  74.6 1.7 %shard_map.131 = (bf16[128,2048]{1,0:T(8,128)(2,1)}, f32[8,128]{1,0:T(8,128)S(1)}) custom-call(bf16[128,2048]{1,0:T(8,128)(2,1)S(1)} %collective-permute-done.refs_0_, f32[8,128]{1,0:T(8,128)S(1)} %get-tuple-element.44.refs_0_.refs_1_, bf16[96,1024]{1,0:T(8,128)(2,1)S(1)} %get-tuple-element.64.refs_2_, ...), custom_call_target="tpu_custom_call" | custom-call | flops 1024 | bytes 1024 | tf_op jit(solution)/shard_map/pallas_call | solution.py:243
  76.3 3.6 %collective-permute-done.20.refs_2_.refs_5_ = bf16[128,1024]{1,0:T(8,128)(2,1)S(1)} collective-permute-done((bf16[128,1024]{1,0:T(8,128)(2,1)S(1)}, bf16[128,1024]{1,0:T(8,128)(2,1)S(1)}, u32[]{:S(2)}, u32[]{:S(2)}) %collective-permute-start.20) | collective-permute-done | bytes 262176 | tf_op jit(solution)/shard_map/ppermute | solution.py:24
  79.9 0.0 collective-permute-done.21.refs_6_
  79.9 1.3 %shard_map.134 = bf16[128,2048]{1,0:T(8,128)(2,1)} custom-call(bf16[128,2048]{1,0:T(8,128)(2,1)S(1)} %collective-permute-done.5.refs_0_, bf16[128,2048]{1,0:T(8,128)(2,1)S(1)} %bitcast.30, f32[1,2048]{1,0:T(1,128)S(1)} %get-tuple-element.47.refs_1_.refs_2_, f32[128,1024]{1,0:T(8,128)S(1)} %get-tuple-element.83.refs_1_.refs_3_, ...), custom_call_target="tpu_custom_call" | custom-call | flops 1024 | bytes 1024 | tf_op jit(solution)/shard_map/pallas_call | solution.py:243
  (11 shorter events, 0.1 us)
Async XLA Ops:
  0.6 11.7 %collective-permute-start = (bf16[128,2048]{1,0:T(8,128)(2,1)}, bf16[128,2048]{1,0:T(8,128)(2,1)S(1)}, u32[]{:S(2)}, u32[]{:S(2)}) collective-permute-start(bf16[128,2048]{1,0:T(8,128)(2,1)} %bitcast.36), channel_id=1, source_target_pairs={{0,4},{4,8},{8,12},{12,16},{16,20},{20,24},{24,28},{28,0},{1,5},{5... | collective-permute-start | bytes 1572872 | tf_op jit(solution)/shard_map/ppermute | solution.py:18
  2.8 14.5 %collective-permute-start.2 = (bf16[240,1024]{1,0:T(8,128)(2,1)S(1)}, bf16[240,1024]{1,0:T(8,128)(2,1)S(1)}, u32[]{:S(2)}, u32[]{:S(2)}) collective-permute-start(bf16[240,1024]{1,0:T(8,128)(2,1)S(1)} %get-tuple-element.46.refs_4_), channel_id=1, source_target_pairs={{0,2},{1,3},{2,0},{3,1},{4,6},{5,7},{6,4},{7,5},{8,10},{9,11},{10,... | collective-permute-start | bytes 1474568 | tf_op jit(solution)/shard_map/ppermute | solution.py:24
  5.4 13.8 %collective-permute-start.1 = (bf16[240,1024]{1,0:T(8,128)(2,1)S(1)}, bf16[240,1024]{1,0:T(8,128)(2,1)S(1)}, u32[]{:S(2)}, u32[]{:S(2)}) collective-permute-start(bf16[240,1024]{1,0:T(8,128)(2,1)S(1)} %get-tuple-element.45.refs_2_.refs_3_), channel_id=1, source_target_pairs={{0,1},{1,0},{2,3},{3,2},{4,5},{5,4},{6,7},{7,6},{8,9},{9,8},{10,11... | collective-permute-start | bytes 1474568 | tf_op jit(solution)/shard_map/ppermute | solution.py:24
  6.9 12.3 %collective-permute-start.5 = (bf16[128,2048]{1,0:T(8,128)(2,1)}, bf16[128,2048]{1,0:T(8,128)(2,1)S(1)}, u32[]{:S(2)}, u32[]{:S(2)}) collective-permute-start(bf16[128,2048]{1,0:T(8,128)(2,1)} %bitcast.37), channel_id=1, source_target_pairs={{0,28},{4,0},{8,4},{12,8},{16,12},{20,16},{24,20},{28,24},{1,29},{... | collective-permute-start | bytes 1572872 | tf_op jit(solution)/shard_map/ppermute | solution.py:18
  12.3 22.5 %slice-start = ((s8[6291456]{0:T(1024)(128)(4,1)}), s8[4194304]{0:T(1024)(128)(4,1)S(1)}, s32[]{:S(2)}) async-start(s8[6291456]{0:T(1024)(128)(4,1)} %bitcast.20), calls=%async_computation | async-start | bytes 8388608
  12.6 9.5 %collective-permute-start.4 = (bf16[128,1024]{1,0:T(8,128)(2,1)S(1)}, bf16[128,1024]{1,0:T(8,128)(2,1)S(1)}, u32[]{:S(2)}, u32[]{:S(2)}) collective-permute-start(bf16[128,1024]{1,0:T(8,128)(2,1)S(1)} %get-tuple-element.51.refs_4_), channel_id=1, source_target_pairs={{0,2},{1,3},{2,0},{3,1},{4,6},{5,7},{6,4},{7,5},{8,10},{9,11},{10,... | collective-permute-start | bytes 786440 | tf_op jit(solution)/shard_map/ppermute | solution.py:24
  14.8 20.0 %slice-start.1 = ((s8[6291456]{0:T(1024)(128)(4,1)}), s8[2097152]{0:T(1024)(128)(4,1)S(1)}, s32[]{:S(2)}) async-start(s8[6291456]{0:T(1024)(128)(4,1)} %bitcast.20), calls=%async_computation.1 | async-start | bytes 4194304
  14.8 10.0 %collective-permute-start.3 = (bf16[128,1024]{1,0:T(8,128)(2,1)S(1)}, bf16[128,1024]{1,0:T(8,128)(2,1)S(1)}, u32[]{:S(2)}, u32[]{:S(2)}) collective-permute-start(bf16[128,1024]{1,0:T(8,128)(2,1)S(1)} %get-tuple-element.48.refs_2_.refs_3_), channel_id=1, source_target_pairs={{0,1},{1,0},{2,3},{3,2},{4,5},{5,4},{6,7},{7,6},{8,9},{9,8},{10,11... | collective-permute-start | bytes 786440 | tf_op jit(solution)/shard_map/ppermute | solution.py:24
  19.2 9.3 %collective-permute-start.7 = (bf16[128,1024]{1,0:T(8,128)(2,1)S(1)}, bf16[128,1024]{1,0:T(8,128)(2,1)S(1)}, u32[]{:S(2)}, u32[]{:S(2)}) collective-permute-start(bf16[128,1024]{1,0:T(8,128)(2,1)S(1)} %get-tuple-element.53.refs_4_), channel_id=1, source_target_pairs={{0,2},{1,3},{2,0},{3,1},{4,6},{5,7},{6,4},{7,5},{8,10},{9,11},{10,... | collective-permute-start | bytes 786440 | tf_op jit(solution)/shard_map/ppermute | solution.py:24
  19.3 11.1 %collective-permute-start.6 = (bf16[128,1024]{1,0:T(8,128)(2,1)S(1)}, bf16[128,1024]{1,0:T(8,128)(2,1)S(1)}, u32[]{:S(2)}, u32[]{:S(2)}) collective-permute-start(bf16[128,1024]{1,0:T(8,128)(2,1)S(1)} %get-tuple-element.52.refs_4_.refs_3_), channel_id=1, source_target_pairs={{0,1},{1,0},{2,3},{3,2},{4,5},{5,4},{6,7},{7,6},{8,9},{9,8},{10,11... | collective-permute-start | bytes 786440 | tf_op jit(solution)/shard_map/ppermute | solution.py:24
  21.8 12.8 %collective-permute-start.9 = (bf16[96,1024]{1,0:T(8,128)(2,1)S(1)}, bf16[96,1024]{1,0:T(8,128)(2,1)S(1)}, u32[]{:S(2)}, u32[]{:S(2)}) collective-permute-start(bf16[96,1024]{1,0:T(8,128)(2,1)S(1)} %get-tuple-element.55), channel_id=1, source_target_pairs={{0,1},{1,0},{2,3},{3,2},{4,5},{5,4},{6,7},{7,6},{8,9},{9,8},{10,11... | collective-permute-start | bytes 589832 | tf_op jit(solution)/shard_map/ppermute | solution.py:24
  22.1 12.7 %collective-permute-start.8 = (bf16[96,1024]{1,0:T(8,128)(2,1)S(1)}, bf16[96,1024]{1,0:T(8,128)(2,1)S(1)}, u32[]{:S(2)}, u32[]{:S(2)}) collective-permute-start(bf16[96,1024]{1,0:T(8,128)(2,1)S(1)} %get-tuple-element.54.refs_7_), channel_id=1, source_target_pairs={{0,2},{1,3},{2,0},{3,1},{4,6},{5,7},{6,4},{7,5},{8,10},{9,11},{10,... | collective-permute-start | bytes 589832 | tf_op jit(solution)/shard_map/ppermute | solution.py:24
  25.7 17.4 %collective-permute-start.11 = (bf16[192,1024]{1,0:T(8,128)(2,1)S(1)}, bf16[192,1024]{1,0:T(8,128)(2,1)S(1)}, u32[]{:S(2)}, u32[]{:S(2)}) collective-permute-start(bf16[192,1024]{1,0:T(8,128)(2,1)S(1)} %get-tuple-element.63), channel_id=1, source_target_pairs={{0,1},{1,0},{2,3},{3,2},{4,5},{5,4},{6,7},{7,6},{8,9},{9,8},{10,11... | collective-permute-start | bytes 1179656 | tf_op jit(solution)/shard_map/ppermute | solution.py:24
  28.6 14.5 %collective-permute-start.10 = (bf16[192,1024]{1,0:T(8,128)(2,1)S(1)}, bf16[192,1024]{1,0:T(8,128)(2,1)S(1)}, u32[]{:S(2)}, u32[]{:S(2)}) collective-permute-start(bf16[192,1024]{1,0:T(8,128)(2,1)S(1)} %get-tuple-element.56.refs_7_), channel_id=1, source_target_pairs={{0,2},{1,3},{2,0},{3,1},{4,6},{5,7},{6,4},{7,5},{8,10},{9,11},{10,... | collective-permute-start | bytes 1179656 | tf_op jit(solution)/shard_map/ppermute | solution.py:24
  31.5 19.9 %collective-permute-start.15 = (bf16[192,1024]{1,0:T(8,128)(2,1)S(1)}, bf16[192,1024]{1,0:T(8,128)(2,1)S(1)}, u32[]{:S(2)}, u32[]{:S(2)}) collective-permute-start(bf16[192,1024]{1,0:T(8,128)(2,1)S(1)} %get-tuple-element.72), channel_id=1, source_target_pairs={{0,1},{1,0},{2,3},{3,2},{4,5},{5,4},{6,7},{7,6},{8,9},{9,8},{10,11... | collective-permute-start | bytes 1179656 | tf_op jit(solution)/shard_map/ppermute | solution.py:24
  34.6 16.9 %collective-permute-start.14 = (bf16[192,1024]{1,0:T(8,128)(2,1)S(1)}, bf16[192,1024]{1,0:T(8,128)(2,1)S(1)}, u32[]{:S(2)}, u32[]{:S(2)}) collective-permute-start(bf16[192,1024]{1,0:T(8,128)(2,1)S(1)} %get-tuple-element.57.refs_10_), channel_id=1, source_target_pairs={{0,2},{1,3},{2,0},{3,1},{4,6},{5,7},{6,4},{7,5},{8,10},{9,11},{10,... | collective-permute-start | bytes 1179656 | tf_op jit(solution)/shard_map/ppermute | solution.py:24
  38.0 5.0 %copy-start = (bf16[1,1,768,2048]{3,2,1,0:T(8,128)(2,1)S(1)}, bf16[1,1,768,2048]{3,2,1,0:T(8,128)(2,1)}, u32[]{:S(2)}) copy-start(bf16[1,1,768,2048]{3,2,1,0:T(8,128)(2,1)} %param.19) | copy-start | bytes 9437188
  46.3 12.5 %collective-permute-start.12 = (bf16[192,1024]{1,0:T(8,128)(2,1)S(1)}, bf16[192,1024]{1,0:T(8,128)(2,1)S(1)}, u32[]{:S(2)}, u32[]{:S(2)}) collective-permute-start(bf16[192,1024]{1,0:T(8,128)(2,1)S(1)} %get-tuple-element.67), channel_id=1, source_target_pairs={{0,2},{1,3},{2,0},{3,1},{4,6},{5,7},{6,4},{7,5},{8,10},{9,11},{10,... | collective-permute-start | bytes 1179656 | tf_op jit(solution)/shard_map/ppermute | solution.py:24
  47.3 13.7 %collective-permute-start.13 = (bf16[192,1024]{1,0:T(8,128)(2,1)S(1)}, bf16[192,1024]{1,0:T(8,128)(2,1)S(1)}, u32[]{:S(2)}, u32[]{:S(2)}) collective-permute-start(bf16[192,1024]{1,0:T(8,128)(2,1)S(1)} %get-tuple-element.68), channel_id=1, source_target_pairs={{0,1},{1,0},{2,3},{3,2},{4,5},{5,4},{6,7},{7,6},{8,9},{9,8},{10,11... | collective-permute-start | bytes 1179656 | tf_op jit(solution)/shard_map/ppermute | solution.py:24
  55.2 12.1 %collective-permute-start.19 = (bf16[192,1024]{1,0:T(8,128)(2,1)S(1)}, bf16[192,1024]{1,0:T(8,128)(2,1)S(1)}, u32[]{:S(2)}, u32[]{:S(2)}) collective-permute-start(bf16[192,1024]{1,0:T(8,128)(2,1)S(1)} %get-tuple-element.80), channel_id=1, source_target_pairs={{0,2},{1,3},{2,0},{3,1},{4,6},{5,7},{6,4},{7,5},{8,10},{9,11},{10,... | collective-permute-start | bytes 1179656 | tf_op jit(solution)/shard_map/ppermute | solution.py:24
  56.9 12.7 %collective-permute-start.18 = (bf16[192,1024]{1,0:T(8,128)(2,1)S(1)}, bf16[192,1024]{1,0:T(8,128)(2,1)S(1)}, u32[]{:S(2)}, u32[]{:S(2)}) collective-permute-start(bf16[192,1024]{1,0:T(8,128)(2,1)S(1)} %get-tuple-element.78), channel_id=1, source_target_pairs={{0,1},{1,0},{2,3},{3,2},{4,5},{5,4},{6,7},{7,6},{8,9},{9,8},{10,11... | collective-permute-start | bytes 1179656 | tf_op jit(solution)/shard_map/ppermute | solution.py:24
  59.6 15.0 %collective-permute-start.16 = (bf16[128,1024]{1,0:T(8,128)(2,1)S(1)}, bf16[128,1024]{1,0:T(8,128)(2,1)S(1)}, u32[]{:S(2)}, u32[]{:S(2)}) collective-permute-start(bf16[128,1024]{1,0:T(8,128)(2,1)S(1)} %shard_map.127.refs_3_), channel_id=1, source_target_pairs={{0,1},{1,0},{2,3},{3,2},{4,5},{5,4},{6,7},{7,6},{8,9},{9,8},{10,11... | collective-permute-start | bytes 786440 | tf_op jit(solution)/shard_map/ppermute | solution.py:24
  61.8 12.8 %collective-permute-start.17 = (bf16[128,1024]{1,0:T(8,128)(2,1)S(1)}, bf16[128,1024]{1,0:T(8,128)(2,1)S(1)}, u32[]{:S(2)}, u32[]{:S(2)}) collective-permute-start(bf16[128,1024]{1,0:T(8,128)(2,1)S(1)} %shard_map.128.refs_3_), channel_id=1, source_target_pairs={{0,2},{1,3},{2,0},{3,1},{4,6},{5,7},{6,4},{7,5},{8,10},{9,11},{10,... | collective-permute-start | bytes 786440 | tf_op jit(solution)/shard_map/ppermute | solution.py:24
  67.7 12.2 %collective-permute-start.20 = (bf16[128,1024]{1,0:T(8,128)(2,1)S(1)}, bf16[128,1024]{1,0:T(8,128)(2,1)S(1)}, u32[]{:S(2)}, u32[]{:S(2)}) collective-permute-start(bf16[128,1024]{1,0:T(8,128)(2,1)S(1)} %shard_map.129.refs_3_), channel_id=1, source_target_pairs={{0,1},{1,0},{2,3},{3,2},{4,5},{5,4},{6,7},{7,6},{8,9},{9,8},{10,11... | collective-permute-start | bytes 786440 | tf_op jit(solution)/shard_map/ppermute | solution.py:24
  70.1 9.8 %collective-permute-start.21 = (bf16[128,1024]{1,0:T(8,128)(2,1)S(1)}, bf16[128,1024]{1,0:T(8,128)(2,1)S(1)}, u32[]{:S(2)}, u32[]{:S(2)}) collective-permute-start(bf16[128,1024]{1,0:T(8,128)(2,1)S(1)} %shard_map.130.refs_8_.refs_5_), channel_id=1, source_target_pairs={{0,2},{1,3},{2,0},{3,1},{4,6},{5,7},{6,4},{7,5},{8,10},{9,11},{10,... | collective-permute-start | bytes 786440 | tf_op jit(solution)/shard_map/ppermute | solution.py:24
  74.6 5.3 %copy-start.1 = (bf16[1,128,2048]{2,1,0:T(8,128)(2,1)S(1)}, bf16[1,128,2048]{2,1,0:T(8,128)(2,1)}, u32[]{:S(2)}) copy-start(bf16[1,128,2048]{2,1,0:T(8,128)(2,1)} %param.12) | copy-start | bytes 1572868

commit v15 on v14

--- a/solution.py
+++ b/solution.py
@@ -642,23 +642,24 @@
     ).astype(jnp.bfloat16)
 
 
-def summed(kind, top_count, own, keep_left, keep_right, got_y, got_x, sum_x, sum_y):
-    capacity = keep_left.shape[0]
-    mine = pick(own[...], 0, capacity, kind, top_count)
-    near_y = pick(own[...], 2, capacity, kind, top_count)
-    near_x = pick(own[...], 1, capacity, kind, top_count)
+def hop_fwd_near_kernel(
+    top_count, layer_ref, own, keep_left, keep_right, got_y, got_x, sum_y, left_ref, right_ref
+):
+    capacity, half = keep_left.shape
+    mine = pick(own[...], 0, capacity, "fg", top_count)
+    near_y = pick(own[...], 2, capacity, "fg", top_count)
+    near_x = pick(own[...], 1, capacity, "fg", top_count)
     left = to_tokens(mine, keep_left[...]) + to_tokens(near_y, got_y[:capacity, :])
     right = to_tokens(mine, keep_right[...]) + to_tokens(near_x, got_x[:capacity, :])
-    return left + sum_x[...].astype(jnp.float32), right + sum_y[...].astype(jnp.float32)
-
-
-def hop_fwd_end_kernel(top_count, layer_ref, *refs):
-    out_ref, order_ref = refs[-2:]
-    order_ref[...] = jnp.zeros_like(order_ref)
-    half = layer_ref.shape[1] // 2
-    left, right = summed("fg", top_count, *refs[:-2])
-    out_ref[:, :half] = (layer_ref[:, :half].astype(jnp.float32) + left).astype(jnp.bfloat16)
-    out_ref[:, half:] = (layer_ref[:, half:].astype(jnp.float32) + right).astype(jnp.bfloat16)
+    left_ref[...] = layer_ref[:, :half].astype(jnp.float32) + left
+    right = right + sum_y[...].astype(jnp.float32)
+    right_ref[...] = layer_ref[:, half:].astype(jnp.float32) + right
+
+
+def hop_fwd_end_kernel(left_ref, right_ref, sum_x, out_ref):
+    half = left_ref.shape[1]
+    out_ref[:, :half] = (left_ref[...] + sum_x[...].astype(jnp.float32)).astype(jnp.bfloat16)
+    out_ref[:, half:] = right_ref[...].astype(jnp.bfloat16)
 
 
 def hop_bwd_near_kernel(
@@ -676,7 +677,10 @@
     order_ref[...] = jnp.zeros_like(order_ref)
 
 
-def hop_bwd_end_kernel(grads_ref, saved_ref, gain_ref, left_ref, right_ref, sum_x, sum_y, out_ref):
+def hop_bwd_end_kernel(
+    grads_ref, saved_ref, gain_ref, left_ref, right_ref, sum_x, sum_y, out_ref, order_ref
+):
+    order_ref[...] = jnp.zeros_like(order_ref)
     features = saved_ref.shape[1]
     half = features // 2
     parts = []
@@ -868,7 +872,7 @@
     )
     b_ret_y = swapped(b_on_l, "expert", 2)
     b_keep_r, b_near_r, b_on_r = local_call(
-        bwd_right_kernel, half_out, (both, weight_in), 1024, 1024
+        bwd_right_kernel, half_out, (both, weight_in), 1024, 1024, after=(f_ret_y,)
     )
     b_ret_x = swapped(b_on_r, "expert", 1)
 
@@ -883,43 +887,46 @@
         )
         return swapped(part, "expert", here), part
 
-    f_sum_x, last = summed_call("fg", 1, x_tab, f_near_l, f_ret_y, (b_keep_r,))
-    f_sum_y, last = summed_call("fg", 2, y_tab, f_near_r, f_ret_x, (last,))
+    f_sum_y, last = summed_call("fg", 2, y_tab, f_near_r, f_ret_x, (b_keep_r,))
     b_sum_x, last = summed_call("b", 1, x_tab, b_near_l, b_ret_y, (last,))
     b_sum_y, last = summed_call("b", 2, y_tab, b_near_r, b_ret_x, (last,))
-    f_keep = (f_keep_l, f_keep_r)
-    b_keep = (b_keep_l, b_keep_r)
-    fwd_block, order = local_call(
-        functools.partial(hop_fwd_end_kernel, top_count),
-        [shaped(tok_rows, features), shaped(8, 128, jnp.float32)],
-        (layer_in, own, *f_keep, f_ret_y, f_ret_x, f_sum_x, f_sum_y),
+    f_sum_x, last = summed_call("fg", 1, x_tab, f_near_l, f_ret_y, (last,))
+    order_shape = shaped(8, 128, jnp.float32)
+    wide_halves = [shaped(tok_rows, half, jnp.float32)] * 2
+    b_part = local_call(
+        functools.partial(hop_bwd_near_kernel, top_count),
+        wide_halves,
+        (own, b_keep_l, b_keep_r, b_ret_y, b_ret_x),
         one_hop,
         moved,
         after=(last,),
     )
-    b_near = local_call(
-        functools.partial(hop_bwd_near_kernel, top_count),
-        [shaped(tok_rows, half, jnp.float32)] * 2,
-        (own, *b_keep, b_ret_y, b_ret_x),
+    f_part = local_call(
+        functools.partial(hop_fwd_near_kernel, top_count),
+        wide_halves,
+        (layer_in, own, f_keep_l, f_keep_r, f_ret_y, f_ret_x, f_sum_y),
         one_hop,
         moved,
-        after=(last,),
+        after=(b_part[0],),
     )
     x_there = local_call(
-        order_kernel,
-        shaped(8, 128, jnp.float32),
-        (),
-        one_hop,
-        moved,
-        after=(order, b_near[0], b_sum_x),
-    )
-    bwd_block = local_call(
+        order_kernel, order_shape, (), one_hop, moved, after=(f_part[0], b_sum_x)
+    )
+    bwd_block, order = local_call(
         hop_bwd_end_kernel,
-        shaped(tok_rows, features),
-        (grad_in, saved, gain_here, *b_near, b_sum_x, b_sum_y),
+        [shaped(tok_rows, features), order_shape],
+        (grad_in, saved, gain_here, *b_part, b_sum_x, b_sum_y),
         one_hop,
         moved,
         after=(x_there,),
+    )
+    fwd_block = local_call(
+        hop_fwd_end_kernel,
+        shaped(tok_rows, features),
+        (*f_part, f_sum_x),
+        one_hop,
+        moved,
+        after=(order,),
     )
     return (fwd_block[None], bwd_block[None])
 

time: 81.4 us -> 83.9 us (1.031)
  waiting for transfers between devices: 23.2 us -> 24.7 us
  starting transfers between devices: 32.5 us -> 33.5 us
    ppermute x20, waiting for transfers between devices: 20.8 us -> 22.2 us  [swapped(): return lax.ppermute(value, axis, pairs)]
    ppermute x20, starting transfers between devices: 29 us -> 30.1 us  [swapped(): return lax.ppermute(value, axis, pairs)]
    pallas_call x21 -> x22, Pallas kernels: 23 us -> 23 us  [local_call(): pl.pallas_call(body if after else kernel, out_shape=out_shapes, in_specs=...]
  transfers between devices with their start and end apart: 22 -> 22, of which waited for: 12 -> 14; matrix products, arithmetic and copies ran while one was open for 0% -> 0% of each run, Pallas kernels for 29% -> 28%
where the time goes in v15:
time: 83.9 us; the launch traced here: 83.7 us
  starting transfers between devices  33.5 us (40%)
  waiting for transfers between devices  24.7 us (29%)
  Pallas kernels  24.6 us (29%)
  between operations  0.87 us (1%)
    ppermute x20, starting transfers between devices, swapped(): return lax.ppermute(value, axis, pairs)  30.1 us
    pallas_call x22, Pallas kernels, local_call(): pl.pallas_call(body if after else kernel, out_shape=out_shapes, in_specs=...  23 us
    ppermute x20, waiting for transfers between devices, swapped(): return lax.ppermute(value, axis, pairs)  22.2 us
    ppermute x2, starting transfers between devices, passed_along(): return lax.ppermute(value, axis, pairs)  3.46 us
    ppermute x2, waiting for transfers between devices, passed_along(): return lax.ppermute(value, axis, pairs)  2.47 us
  transfers between devices with their start and end apart: 22, of which 14 were waited for; matrix products, arithmetic and copies ran while one was open for 0% of the time, Pallas kernels for 28%

profile of v15, /device:TPU:0, one launch (start us, length us, event | category | flops | bytes accessed | tf_op | source)
XLA Modules:
  0.0 83.7 jit_solution(18394464928152685919)
XLA Ops:
  0.6 0.5 collective-permute-start
  1.1 1.7 %shard_map.113 = (bf16[240,1024]{1,0:T(8,128)(2,1)S(1)}, bf16[240,1024]{1,0:T(8,128)(2,1)S(1)}, f32[8,128]{1,0:T(8,128)S(1)}, f32[1,2048]{1,0:T(1,128)S(1)}) custom-call(s32[1]{0:T(128)} %bitcast.1.me_ref, bf16[128,2048]{1,0:T(8,128)(2,1)} %bitcast.29, f32[1,2048]{1,0:T(1,128)} %refs_1_.1, s32[2,128]{1,0:T(2,128)} %bitcast.32, f32[2,128]{1,0:T(2,128)} %bitcast.33, ...), custom_call_target="tpu_custom_call" | custom-call | flops 1024 | bytes 1024 | tf_op jit(solution)/shard_map/pallas_call | solution.py:750
  2.8 2.6 %collective-permute-start.2 = (bf16[240,1024]{1,0:T(8,128)(2,1)S(1)}, bf16[240,1024]{1,0:T(8,128)(2,1)S(1)}, u32[]{:S(2)}, u32[]{:S(2)}) collective-permute-start(bf16[240,1024]{1,0:T(8,128)(2,1)S(1)} %get-tuple-element.48.refs_4_), channel_id=1, source_target_pairs={{0,2},{1,3},{2,0},{3,1},{4,6},{5,7},{6,4},{7,5},{8,10},{9,11},{10,... | collective-permute-start | bytes 1474568 | tf_op jit(solution)/shard_map/ppermute | solution.py:24
  5.4 1.5 %collective-permute-start.1 = (bf16[240,1024]{1,0:T(8,128)(2,1)S(1)}, bf16[240,1024]{1,0:T(8,128)(2,1)S(1)}, u32[]{:S(2)}, u32[]{:S(2)}) collective-permute-start(bf16[240,1024]{1,0:T(8,128)(2,1)S(1)} %get-tuple-element.47.refs_2_.refs_3_), channel_id=1, source_target_pairs={{0,1},{1,0},{2,3},{3,2},{4,5},{5,4},{6,7},{7,6},{8,9},{9,8},{10,11... | collective-permute-start | bytes 1474568 | tf_op jit(solution)/shard_map/ppermute | solution.py:24
  6.9 3.0 %collective-permute-start.5 = (bf16[128,2048]{1,0:T(8,128)(2,1)}, bf16[128,2048]{1,0:T(8,128)(2,1)S(1)}, u32[]{:S(2)}, u32[]{:S(2)}) collective-permute-start(bf16[128,2048]{1,0:T(8,128)(2,1)} %bitcast.37), channel_id=1, source_target_pairs={{0,28},{4,0},{8,4},{12,8},{16,12},{20,16},{24,20},{28,24},{1,29},{... | collective-permute-start | bytes 1572872 | tf_op jit(solution)/shard_map/ppermute | solution.py:18
  9.9 2.5 %collective-permute-done.refs_0_ = bf16[128,2048]{1,0:T(8,128)(2,1)S(1)} collective-permute-done((bf16[128,2048]{1,0:T(8,128)(2,1)}, bf16[128,2048]{1,0:T(8,128)(2,1)S(1)}, u32[]{:S(2)}, u32[]{:S(2)}) %collective-permute-start) | collective-permute-done | bytes 524320 | tf_op jit(solution)/shard_map/ppermute | solution.py:18
  12.3 0.2 shard_map.114
  12.6 2.3 %collective-permute-start.4 = (bf16[128,1024]{1,0:T(8,128)(2,1)S(1)}, bf16[128,1024]{1,0:T(8,128)(2,1)S(1)}, u32[]{:S(2)}, u32[]{:S(2)}) collective-permute-start(bf16[128,1024]{1,0:T(8,128)(2,1)S(1)} %get-tuple-element.53.refs_4_), channel_id=1, source_target_pairs={{0,2},{1,3},{2,0},{3,1},{4,6},{5,7},{6,4},{7,5},{8,10},{9,11},{10,... | collective-permute-start | bytes 786440 | tf_op jit(solution)/shard_map/ppermute | solution.py:24
  14.8 2.4 %collective-permute-start.3 = (bf16[128,1024]{1,0:T(8,128)(2,1)S(1)}, bf16[128,1024]{1,0:T(8,128)(2,1)S(1)}, u32[]{:S(2)}, u32[]{:S(2)}) collective-permute-start(bf16[128,1024]{1,0:T(8,128)(2,1)S(1)} %get-tuple-element.50.refs_2_.refs_3_), channel_id=1, source_target_pairs={{0,1},{1,0},{2,3},{3,2},{4,5},{5,4},{6,7},{7,6},{8,9},{9,8},{10,11... | collective-permute-start | bytes 786440 | tf_op jit(solution)/shard_map/ppermute | solution.py:24
  17.3 0.0 collective-permute-done.2.refs_1_.refs_3_.refs_6_
  17.3 1.9 %collective-permute-done.1.refs_0_.refs_2_.refs_5_ = bf16[240,1024]{1,0:T(8,128)(2,1)S(1)} collective-permute-done((bf16[240,1024]{1,0:T(8,128)(2,1)S(1)}, bf16[240,1024]{1,0:T(8,128)(2,1)S(1)}, u32[]{:S(2)}, u32[]{:S(2)}) %collective-permute-start.1) | collective-permute-done | bytes 491552 | tf_op jit(solution)/shard_map/ppermute | solution.py:24
  19.2 0.0 collective-permute-done.5.refs_0_
  19.2 0.1 collective-permute-start.7
  19.3 2.0 %collective-permute-start.6 = (bf16[128,1024]{1,0:T(8,128)(2,1)S(1)}, bf16[128,1024]{1,0:T(8,128)(2,1)S(1)}, u32[]{:S(2)}, u32[]{:S(2)}) collective-permute-start(bf16[128,1024]{1,0:T(8,128)(2,1)S(1)} %get-tuple-element.54.refs_4_.refs_3_), channel_id=1, source_target_pairs={{0,1},{1,0},{2,3},{3,2},{4,5},{5,4},{6,7},{7,6},{8,9},{9,8},{10,11... | collective-permute-start | bytes 786440 | tf_op jit(solution)/shard_map/ppermute | solution.py:24
  21.3 0.5 shard_map.117
  21.8 0.2 collective-permute-start.9
  22.0 0.1 collective-permute-done.4.refs_6_
  22.1 2.4 %collective-permute-start.8 = (bf16[96,1024]{1,0:T(8,128)(2,1)S(1)}, bf16[96,1024]{1,0:T(8,128)(2,1)S(1)}, u32[]{:S(2)}, u32[]{:S(2)}) collective-permute-start(bf16[96,1024]{1,0:T(8,128)(2,1)S(1)} %get-tuple-element.56.refs_7_), channel_id=1, source_target_pairs={{0,2},{1,3},{2,0},{3,1},{4,6},{5,7},{6,4},{7,5},{8,10},{9,11},{10,... | collective-permute-start | bytes 589832 | tf_op jit(solution)/shard_map/ppermute | solution.py:24
  24.5 0.3 collective-permute-done.3.refs_5_
  24.8 0.9 %shard_map.118 = (bf16[192,1024]{1,0:T(8,128)(2,1)S(1)}, bf16[192,1024]{1,0:T(8,128)(2,1)S(1)}) custom-call(f32[8,128]{1,0:T(8,128)S(1)} %get-tuple-element.46.refs_0_.refs_1_, f32[8,128]{1,0:T(8,128)S(1)} %get-tuple-element.51.refs_1_.refs_0_, f32[8,128]{1,0:T(8,128)S(1)} %get-tuple-element.52.refs_1_.refs_2_.refs_0_, ...), custom_call_target="tpu_custom_call" | custom-call | flops 1024 | bytes 1024 | tf_op jit(solution)/shard_map/pallas_call | solution.py:243
  25.7 1.8 %collective-permute-start.11 = (bf16[192,1024]{1,0:T(8,128)(2,1)S(1)}, bf16[192,1024]{1,0:T(8,128)(2,1)S(1)}, u32[]{:S(2)}, u32[]{:S(2)}) collective-permute-start(bf16[192,1024]{1,0:T(8,128)(2,1)S(1)} %get-tuple-element.65), channel_id=1, source_target_pairs={{0,1},{1,0},{2,3},{3,2},{4,5},{5,4},{6,7},{7,6},{8,9},{9,8},{10,11... | collective-permute-start | bytes 1179656 | tf_op jit(solution)/shard_map/ppermute | solution.py:24
  27.5 1.1 %collective-permute-done.7.refs_6_ = bf16[128,1024]{1,0:T(8,128)(2,1)S(1)} collective-permute-done((bf16[128,1024]{1,0:T(8,128)(2,1)S(1)}, bf16[128,1024]{1,0:T(8,128)(2,1)S(1)}, u32[]{:S(2)}, u32[]{:S(2)}) %collective-permute-start.7) | collective-permute-done | bytes 262176 | tf_op jit(solution)/shard_map/ppermute | solution.py:24
  28.6 1.5 %collective-permute-start.10 = (bf16[192,1024]{1,0:T(8,128)(2,1)S(1)}, bf16[192,1024]{1,0:T(8,128)(2,1)S(1)}, u32[]{:S(2)}, u32[]{:S(2)}) collective-permute-start(bf16[192,1024]{1,0:T(8,128)(2,1)S(1)} %get-tuple-element.58.refs_7_), channel_id=1, source_target_pairs={{0,2},{1,3},{2,0},{3,1},{4,6},{5,7},{6,4},{7,5},{8,10},{9,11},{10,... | collective-permute-start | bytes 1179656 | tf_op jit(solution)/shard_map/ppermute | solution.py:24
  30.1 0.3 collective-permute-done.6.refs_5_
  30.4 1.1 %shard_map.119 = (bf16[192,1024]{1,0:T(8,128)(2,1)S(1)}, bf16[192,1024]{1,0:T(8,128)(2,1)S(1)}) custom-call(f32[8,128]{1,0:T(8,128)S(1)} %get-tuple-element.46.refs_0_.refs_1_, f32[8,128]{1,0:T(8,128)S(1)} %get-tuple-element.51.refs_1_.refs_0_, f32[8,128]{1,0:T(8,128)S(1)} %get-tuple-element.52.refs_1_.refs_2_.refs_0_, ...), custom_call_target="tpu_custom_call" | custom-call | flops 1024 | bytes 1024 | tf_op jit(solution)/shard_map/pallas_call | solution.py:243
  31.5 1.8 %collective-permute-start.15 = (bf16[192,1024]{1,0:T(8,128)(2,1)S(1)}, bf16[192,1024]{1,0:T(8,128)(2,1)S(1)}, u32[]{:S(2)}, u32[]{:S(2)}) collective-permute-start(bf16[192,1024]{1,0:T(8,128)(2,1)S(1)} %get-tuple-element.74), channel_id=1, source_target_pairs={{0,1},{1,0},{2,3},{3,2},{4,5},{5,4},{6,7},{7,6},{8,9},{9,8},{10,11... | collective-permute-start | bytes 1179656 | tf_op jit(solution)/shard_map/ppermute | solution.py:24
  33.3 1.3 %collective-permute-done.9.refs_8_ = bf16[96,1024]{1,0:T(8,128)(2,1)S(1)} collective-permute-done((bf16[96,1024]{1,0:T(8,128)(2,1)S(1)}, bf16[96,1024]{1,0:T(8,128)(2,1)S(1)}, u32[]{:S(2)}, u32[]{:S(2)}) %collective-permute-start.9) | collective-permute-done | bytes 196640 | tf_op jit(solution)/shard_map/ppermute | solution.py:24
  34.6 0.2 collective-permute-start.14
  34.8 0.0 collective-permute-done.8.refs_7_
  34.8 3.2 %shard_map.120 = (f32[384,768]{1,0:T(8,128)S(1)}, f32[384,768]{1,0:T(8,128)S(1)}) custom-call(f32[8,128]{1,0:T(8,128)S(1)} %get-tuple-element.46.refs_0_.refs_1_, f32[8,128]{1,0:T(8,128)S(1)} %get-tuple-element.51.refs_1_.refs_0_, f32[8,128]{1,0:T(8,128)S(1)} %get-tuple-element.52.refs_1_.refs_2_.refs_0_, ...), custom_call_target="tpu_custom_call" | custom-call | flops 2415919104 | bytes 14155776 | tf_op jit(solution)/shard_map/pallas_call | solution.py:243
  38.0 0.0 copy-start
  38.0 1.0 %shard_map.121 = (bf16[96,2048]{1,0:T(8,128)(2,1)S(1)}, bf16[96,1024]{1,0:T(8,128)(2,1)S(1)}, bf16[96,1024]{1,0:T(8,128)(2,1)S(1)}) custom-call(f32[8,128]{1,0:T(8,128)S(1)} %get-tuple-element.46.refs_0_.refs_1_, f32[8,128]{1,0:T(8,128)S(1)} %get-tuple-element.51.refs_1_.refs_0_, f32[8,128]{1,0:T(8,128)S(1)} %get-tuple-element.52.refs_1_.refs_2_.refs_0_, ...), custom_call_target="tpu_custom_call" | custom-call | flops 1024 | bytes 1024 | tf_op jit(solution)/shard_map/pallas_call | solution.py:243
  39.0 0.8 shard_map.122
  39.8 3.2 %collective-permute-done.11.refs_4_ = bf16[192,1024]{1,0:T(8,128)(2,1)S(1)} collective-permute-done((bf16[192,1024]{1,0:T(8,128)(2,1)S(1)}, bf16[192,1024]{1,0:T(8,128)(2,1)S(1)}, u32[]{:S(2)}, u32[]{:S(2)}) %collective-permute-start.11) | collective-permute-done | bytes 393248 | tf_op jit(solution)/shard_map/ppermute | solution.py:24
  43.0 0.0 collective-permute-done.10.refs_3_
  43.1 3.2 %shard_map.123 = (bf16[96,1024]{1,0:T(8,128)(2,1)S(1)}, bf16[96,1024]{1,0:T(8,128)(2,1)S(1)}, bf16[192,1024]{1,0:T(8,128)(2,1)S(1)}, bf16[384,768]{1,0:T(8,128)(2,1)S(1)}) custom-call(bf16[96,2048]{1,0:T(8,128)(2,1)S(1)} %get-tuple-element.62.refs_0_, bf16[96,1024]{1,0:T(8,128)(2,1)S(1)} %get-tuple-element.63.refs_1_.refs_7_, ...), custom_call_target="tpu_custom_call" | custom-call | flops 3019898880 | bytes 14155776 | tf_op jit(solution)/shard_map/pallas_call | solution.py:243
  46.3 0.2 collective-permute-start.12
  46.5 0.8 shard_map.124
  47.3 1.9 %collective-permute-start.13 = (bf16[192,1024]{1,0:T(8,128)(2,1)S(1)}, bf16[192,1024]{1,0:T(8,128)(2,1)S(1)}, u32[]{:S(2)}, u32[]{:S(2)}) collective-permute-start(bf16[192,1024]{1,0:T(8,128)(2,1)S(1)} %get-tuple-element.70), channel_id=1, source_target_pairs={{0,1},{1,0},{2,3},{3,2},{4,5},{5,4},{6,7},{7,6},{8,9},{9,8},{10,11... | collective-permute-start | bytes 1179656 | tf_op jit(solution)/shard_map/ppermute | solution.py:24
  49.2 2.3 %collective-permute-done.15.refs_4_ = bf16[192,1024]{1,0:T(8,128)(2,1)S(1)} collective-permute-done((bf16[192,1024]{1,0:T(8,128)(2,1)S(1)}, bf16[192,1024]{1,0:T(8,128)(2,1)S(1)}, u32[]{:S(2)}, u32[]{:S(2)}) %collective-permute-start.15) | collective-permute-done | bytes 393248 | tf_op jit(solution)/shard_map/ppermute | solution.py:24
  51.5 3.7 %shard_map.125 = (bf16[96,1024]{1,0:T(8,128)(2,1)S(1)}, bf16[96,1024]{1,0:T(8,128)(2,1)S(1)}, bf16[192,1024]{1,0:T(8,128)(2,1)S(1)}, bf16[384,1536]{1,0:T(8,128)(2,1)S(1)}) custom-call(bf16[96,2048]{1,0:T(8,128)(2,1)S(1)} %get-tuple-element.72.refs_0_, bf16[96,1024]{1,0:T(8,128)(2,1)S(1)} %get-tuple-element.61.refs_7_.refs_1_, ...), custom_call_target="tpu_custom_call" | custom-call | flops 2415919104 | bytes 14155776 | tf_op jit(solution)/shard_map/pallas_call | solution.py:243
  55.2 0.2 collective-permute-start.17
  55.5 2.8 %collective-permute-done.12.refs_2_.refs_4_ = bf16[192,1024]{1,0:T(8,128)(2,1)S(1)} collective-permute-done((bf16[192,1024]{1,0:T(8,128)(2,1)S(1)}, bf16[192,1024]{1,0:T(8,128)(2,1)S(1)}, u32[]{:S(2)}, u32[]{:S(2)}) %collective-permute-start.12) | collective-permute-done | bytes 393248 | tf_op jit(solution)/shard_map/ppermute | solution.py:24
  58.2 1.4 %shard_map.126 = (bf16[96,1024]{1,0:T(8,128)(2,1)S(1)}, bf16[96,1024]{1,0:T(8,128)(2,1)S(1)}, bf16[192,1024]{1,0:T(8,128)(2,1)S(1)}) custom-call(bf16[384,1536]{1,0:T(8,128)(2,1)S(1)} %get-tuple-element.76.refs_0_, bf16[2048,1536]{1,0:T(8,128)(2,1)S(1)} %bitcast.25, bf16[192,1024]{1,0:T(8,128)(2,1)S(1)} %collective-permute-done.12.refs_2_.refs_4_), custom_call_target="tpu_custom_call" | custom-call | flops 1024 | bytes 1024 | tf_op jit(solution)/shard_map/pallas_call | solution.py:243
  59.6 2.0 %collective-permute-start.18 = (bf16[192,1024]{1,0:T(8,128)(2,1)S(1)}, bf16[192,1024]{1,0:T(8,128)(2,1)S(1)}, u32[]{:S(2)}, u32[]{:S(2)}) collective-permute-start(bf16[192,1024]{1,0:T(8,128)(2,1)S(1)} %get-tuple-element.80), channel_id=1, source_target_pairs={{0,1},{1,0},{2,3},{3,2},{4,5},{5,4},{6,7},{7,6},{8,9},{9,8},{10,11... | collective-permute-start | bytes 1179656 | tf_op jit(solution)/shard_map/ppermute | solution.py:24
  61.6 0.8 shard_map.127.refs_3_
  62.4 1.6 %collective-permute-start.16 = (bf16[128,1024]{1,0:T(8,128)(2,1)S(1)}, bf16[128,1024]{1,0:T(8,128)(2,1)S(1)}, u32[]{:S(2)}, u32[]{:S(2)}) collective-permute-start(bf16[128,1024]{1,0:T(8,128)(2,1)S(1)} %shard_map.127.refs_3_), channel_id=1, source_target_pairs={{0,2},{1,3},{2,0},{3,1},{4,6},{5,7},{6,4},{7,5},{8,10},{9,11},{10,... | collective-permute-start | bytes 786440 | tf_op jit(solution)/shard_map/ppermute | solution.py:24
  64.0 3.3 %collective-permute-done.17.refs_2_.refs_3_ = bf16[192,1024]{1,0:T(8,128)(2,1)S(1)} collective-permute-done((bf16[192,1024]{1,0:T(8,128)(2,1)S(1)}, bf16[192,1024]{1,0:T(8,128)(2,1)S(1)}, u32[]{:S(2)}, u32[]{:S(2)}) %collective-permute-start.17) | collective-permute-done | bytes 393248 | tf_op jit(solution)/shard_map/ppermute | solution.py:24
  67.3 0.4 shard_map.128.refs_3_
  67.7 1.9 %collective-permute-start.20 = (bf16[128,1024]{1,0:T(8,128)(2,1)S(1)}, bf16[128,1024]{1,0:T(8,128)(2,1)S(1)}, u32[]{:S(2)}, u32[]{:S(2)}) collective-permute-start(bf16[128,1024]{1,0:T(8,128)(2,1)S(1)} %shard_map.128.refs_3_), channel_id=1, source_target_pairs={{0,1},{1,0},{2,3},{3,2},{4,5},{5,4},{6,7},{7,6},{8,9},{9,8},{10,11... | collective-permute-start | bytes 786440 | tf_op jit(solution)/shard_map/ppermute | solution.py:24
  69.6 2.0 %collective-permute-done.18.refs_2_.refs_4_ = bf16[192,1024]{1,0:T(8,128)(2,1)S(1)} collective-permute-done((bf16[192,1024]{1,0:T(8,128)(2,1)S(1)}, bf16[192,1024]{1,0:T(8,128)(2,1)S(1)}, u32[]{:S(2)}, u32[]{:S(2)}) %collective-permute-start.18) | collective-permute-done | bytes 393248 | tf_op jit(solution)/shard_map/ppermute | solution.py:24
  71.6 0.5 shard_map.129.refs_3_
  72.1 1.2 %collective-permute-start.21 = (bf16[128,1024]{1,0:T(8,128)(2,1)S(1)}, bf16[128,1024]{1,0:T(8,128)(2,1)S(1)}, u32[]{:S(2)}, u32[]{:S(2)}) collective-permute-start(bf16[128,1024]{1,0:T(8,128)(2,1)S(1)} %shard_map.129.refs_3_), channel_id=1, source_target_pairs={{0,2},{1,3},{2,0},{3,1},{4,6},{5,7},{6,4},{7,5},{8,10},{9,11},{10,... | collective-permute-start | bytes 786440 | tf_op jit(solution)/shard_map/ppermute | solution.py:24
  73.3 0.8 shard_map.130.refs_5_
  74.1 2.4 %collective-permute-start.19 = (bf16[128,1024]{1,0:T(8,128)(2,1)S(1)}, bf16[128,1024]{1,0:T(8,128)(2,1)S(1)}, u32[]{:S(2)}, u32[]{:S(2)}) collective-permute-start(bf16[128,1024]{1,0:T(8,128)(2,1)S(1)} %shard_map.130.refs_5_), channel_id=1, source_target_pairs={{0,1},{1,0},{2,3},{3,2},{4,5},{5,4},{6,7},{7,6},{8,9},{9,8},{10,11... | collective-permute-start | bytes 786440 | tf_op jit(solution)/shard_map/ppermute | solution.py:24
  76.4 0.6 shard_map.131
  77.0 0.0 collective-permute-done.16.refs_6_
  77.0 0.0 copy-start.1
  77.1 0.9 %shard_map.132 = (f32[128,1024]{1,0:T(8,128)S(1)}, f32[128,1024]{1,0:T(8,128)S(1)}) custom-call(bf16[128,2048]{1,0:T(8,128)(2,1)S(1)} %collective-permute-done.refs_0_, f32[8,128]{1,0:T(8,128)S(1)} %get-tuple-element.46.refs_0_.refs_1_, bf16[96,1024]{1,0:T(8,128)(2,1)S(1)} %get-tuple-element.66.refs_2_, ...), custom_call_target="tpu_custom_call" | custom-call | flops 1024 | bytes 1024 | tf_op jit(solution)/shard_map/pallas_call | solution.py:243
  77.9 0.0 collective-permute-done.20.refs_1_.refs_5_
  78.0 2.6 %collective-permute-done.21.refs_6_ = bf16[128,1024]{1,0:T(8,128)(2,1)S(1)} collective-permute-done((bf16[128,1024]{1,0:T(8,128)(2,1)S(1)}, bf16[128,1024]{1,0:T(8,128)(2,1)S(1)}, u32[]{:S(2)}, u32[]{:S(2)}) %collective-permute-start.21) | collective-permute-done | bytes 262176 | tf_op jit(solution)/shard_map/ppermute | solution.py:24
  80.5 1.3 %shard_map.134 = (bf16[128,2048]{1,0:T(8,128)(2,1)}, f32[8,128]{1,0:T(8,128)S(1)}) custom-call(bf16[128,2048]{1,0:T(8,128)(2,1)S(1)} %collective-permute-done.5.refs_0_, bf16[128,2048]{1,0:T(8,128)(2,1)S(1)} %bitcast.30, f32[1,2048]{1,0:T(1,128)S(1)} %get-tuple-element.49.refs_1_.refs_2_, f32[128,1024]{1,0:T(8,128)S(1)} %get-tuple-element.84.refs_7_.refs_3_, ...), custom_call_target="tpu_custom_call" | custom-call | flops 1024 | bytes 1024 | tf_op jit(solution)/shard_map/pallas_call | solution.py:243
  81.8 1.0 %collective-permute-done.19.refs_2_ = bf16[128,1024]{1,0:T(8,128)(2,1)S(1)} collective-permute-done((bf16[128,1024]{1,0:T(8,128)(2,1)S(1)}, bf16[128,1024]{1,0:T(8,128)(2,1)S(1)}, u32[]{:S(2)}, u32[]{:S(2)}) %collective-permute-start.19) | collective-permute-done | bytes 262176 | tf_op jit(solution)/shard_map/ppermute | solution.py:24
  82.9 0.9 %shard_map.135 = bf16[128,2048]{1,0:T(8,128)(2,1)} custom-call(f32[128,1024]{1,0:T(8,128)S(1)} %get-tuple-element.85.refs_0_, f32[128,1024]{1,0:T(8,128)S(1)} %get-tuple-element.86.refs_1_, bf16[128,1024]{1,0:T(8,128)(2,1)S(1)} %collective-permute-done.19.refs_2_, f32[8,128]{1,0:T(8,128)S(1)} %get-tuple-element.88.refs_3_), custom_call_target="tpu_custom_call" | custom-call | flops 1024 | bytes 1024 | tf_op jit(solution)/shard_map/pallas_call | solution.py:243
  (12 shorter events, 0.1 us)
Async XLA Ops:
  0.6 11.7 %collective-permute-start = (bf16[128,2048]{1,0:T(8,128)(2,1)}, bf16[128,2048]{1,0:T(8,128)(2,1)S(1)}, u32[]{:S(2)}, u32[]{:S(2)}) collective-permute-start(bf16[128,2048]{1,0:T(8,128)(2,1)} %bitcast.36), channel_id=1, source_target_pairs={{0,4},{4,8},{8,12},{12,16},{16,20},{20,24},{24,28},{28,0},{1,5},{5... | collective-permute-start | bytes 1572872 | tf_op jit(solution)/shard_map/ppermute | solution.py:18
  2.8 14.5 %collective-permute-start.2 = (bf16[240,1024]{1,0:T(8,128)(2,1)S(1)}, bf16[240,1024]{1,0:T(8,128)(2,1)S(1)}, u32[]{:S(2)}, u32[]{:S(2)}) collective-permute-start(bf16[240,1024]{1,0:T(8,128)(2,1)S(1)} %get-tuple-element.48.refs_4_), channel_id=1, source_target_pairs={{0,2},{1,3},{2,0},{3,1},{4,6},{5,7},{6,4},{7,5},{8,10},{9,11},{10,... | collective-permute-start | bytes 1474568 | tf_op jit(solution)/shard_map/ppermute | solution.py:24
  5.4 13.8 %collective-permute-start.1 = (bf16[240,1024]{1,0:T(8,128)(2,1)S(1)}, bf16[240,1024]{1,0:T(8,128)(2,1)S(1)}, u32[]{:S(2)}, u32[]{:S(2)}) collective-permute-start(bf16[240,1024]{1,0:T(8,128)(2,1)S(1)} %get-tuple-element.47.refs_2_.refs_3_), channel_id=1, source_target_pairs={{0,1},{1,0},{2,3},{3,2},{4,5},{5,4},{6,7},{7,6},{8,9},{9,8},{10,11... | collective-permute-start | bytes 1474568 | tf_op jit(solution)/shard_map/ppermute | solution.py:24
  6.9 12.3 %collective-permute-start.5 = (bf16[128,2048]{1,0:T(8,128)(2,1)}, bf16[128,2048]{1,0:T(8,128)(2,1)S(1)}, u32[]{:S(2)}, u32[]{:S(2)}) collective-permute-start(bf16[128,2048]{1,0:T(8,128)(2,1)} %bitcast.37), channel_id=1, source_target_pairs={{0,28},{4,0},{8,4},{12,8},{16,12},{20,16},{24,20},{28,24},{1,29},{... | collective-permute-start | bytes 1572872 | tf_op jit(solution)/shard_map/ppermute | solution.py:18
  12.3 22.5 %slice-start = ((s8[6291456]{0:T(1024)(128)(4,1)}), s8[4194304]{0:T(1024)(128)(4,1)S(1)}, s32[]{:S(2)}) async-start(s8[6291456]{0:T(1024)(128)(4,1)} %bitcast.20), calls=%async_computation | async-start | bytes 8388608
  12.6 9.5 %collective-permute-start.4 = (bf16[128,1024]{1,0:T(8,128)(2,1)S(1)}, bf16[128,1024]{1,0:T(8,128)(2,1)S(1)}, u32[]{:S(2)}, u32[]{:S(2)}) collective-permute-start(bf16[128,1024]{1,0:T(8,128)(2,1)S(1)} %get-tuple-element.53.refs_4_), channel_id=1, source_target_pairs={{0,2},{1,3},{2,0},{3,1},{4,6},{5,7},{6,4},{7,5},{8,10},{9,11},{10,... | collective-permute-start | bytes 786440 | tf_op jit(solution)/shard_map/ppermute | solution.py:24
  14.8 20.0 %slice-start.1 = ((s8[6291456]{0:T(1024)(128)(4,1)}), s8[2097152]{0:T(1024)(128)(4,1)S(1)}, s32[]{:S(2)}) async-start(s8[6291456]{0:T(1024)(128)(4,1)} %bitcast.20), calls=%async_computation.1 | async-start | bytes 4194304
  14.8 10.0 %collective-permute-start.3 = (bf16[128,1024]{1,0:T(8,128)(2,1)S(1)}, bf16[128,1024]{1,0:T(8,128)(2,1)S(1)}, u32[]{:S(2)}, u32[]{:S(2)}) collective-permute-start(bf16[128,1024]{1,0:T(8,128)(2,1)S(1)} %get-tuple-element.50.refs_2_.refs_3_), channel_id=1, source_target_pairs={{0,1},{1,0},{2,3},{3,2},{4,5},{5,4},{6,7},{7,6},{8,9},{9,8},{10,11... | collective-permute-start | bytes 786440 | tf_op jit(solution)/shard_map/ppermute | solution.py:24
  19.2 9.3 %collective-permute-start.7 = (bf16[128,1024]{1,0:T(8,128)(2,1)S(1)}, bf16[128,1024]{1,0:T(8,128)(2,1)S(1)}, u32[]{:S(2)}, u32[]{:S(2)}) collective-permute-start(bf16[128,1024]{1,0:T(8,128)(2,1)S(1)} %get-tuple-element.55.refs_4_), channel_id=1, source_target_pairs={{0,2},{1,3},{2,0},{3,1},{4,6},{5,7},{6,4},{7,5},{8,10},{9,11},{10,... | collective-permute-start | bytes 786440 | tf_op jit(solution)/shard_map/ppermute | solution.py:24
  19.3 11.1 %collective-permute-start.6 = (bf16[128,1024]{1,0:T(8,128)(2,1)S(1)}, bf16[128,1024]{1,0:T(8,128)(2,1)S(1)}, u32[]{:S(2)}, u32[]{:S(2)}) collective-permute-start(bf16[128,1024]{1,0:T(8,128)(2,1)S(1)} %get-tuple-element.54.refs_4_.refs_3_), channel_id=1, source_target_pairs={{0,1},{1,0},{2,3},{3,2},{4,5},{5,4},{6,7},{7,6},{8,9},{9,8},{10,11... | collective-permute-start | bytes 786440 | tf_op jit(solution)/shard_map/ppermute | solution.py:24
  21.8 12.8 %collective-permute-start.9 = (bf16[96,1024]{1,0:T(8,128)(2,1)S(1)}, bf16[96,1024]{1,0:T(8,128)(2,1)S(1)}, u32[]{:S(2)}, u32[]{:S(2)}) collective-permute-start(bf16[96,1024]{1,0:T(8,128)(2,1)S(1)} %get-tuple-element.57), channel_id=1, source_target_pairs={{0,1},{1,0},{2,3},{3,2},{4,5},{5,4},{6,7},{7,6},{8,9},{9,8},{10,11... | collective-permute-start | bytes 589832 | tf_op jit(solution)/shard_map/ppermute | solution.py:24
  22.1 12.7 %collective-permute-start.8 = (bf16[96,1024]{1,0:T(8,128)(2,1)S(1)}, bf16[96,1024]{1,0:T(8,128)(2,1)S(1)}, u32[]{:S(2)}, u32[]{:S(2)}) collective-permute-start(bf16[96,1024]{1,0:T(8,128)(2,1)S(1)} %get-tuple-element.56.refs_7_), channel_id=1, source_target_pairs={{0,2},{1,3},{2,0},{3,1},{4,6},{5,7},{6,4},{7,5},{8,10},{9,11},{10,... | collective-permute-start | bytes 589832 | tf_op jit(solution)/shard_map/ppermute | solution.py:24
  25.7 17.4 %collective-permute-start.11 = (bf16[192,1024]{1,0:T(8,128)(2,1)S(1)}, bf16[192,1024]{1,0:T(8,128)(2,1)S(1)}, u32[]{:S(2)}, u32[]{:S(2)}) collective-permute-start(bf16[192,1024]{1,0:T(8,128)(2,1)S(1)} %get-tuple-element.65), channel_id=1, source_target_pairs={{0,1},{1,0},{2,3},{3,2},{4,5},{5,4},{6,7},{7,6},{8,9},{9,8},{10,11... | collective-permute-start | bytes 1179656 | tf_op jit(solution)/shard_map/ppermute | solution.py:24
  28.6 14.5 %collective-permute-start.10 = (bf16[192,1024]{1,0:T(8,128)(2,1)S(1)}, bf16[192,1024]{1,0:T(8,128)(2,1)S(1)}, u32[]{:S(2)}, u32[]{:S(2)}) collective-permute-start(bf16[192,1024]{1,0:T(8,128)(2,1)S(1)} %get-tuple-element.58.refs_7_), channel_id=1, source_target_pairs={{0,2},{1,3},{2,0},{3,1},{4,6},{5,7},{6,4},{7,5},{8,10},{9,11},{10,... | collective-permute-start | bytes 1179656 | tf_op jit(solution)/shard_map/ppermute | solution.py:24
  31.5 19.9 %collective-permute-start.15 = (bf16[192,1024]{1,0:T(8,128)(2,1)S(1)}, bf16[192,1024]{1,0:T(8,128)(2,1)S(1)}, u32[]{:S(2)}, u32[]{:S(2)}) collective-permute-start(bf16[192,1024]{1,0:T(8,128)(2,1)S(1)} %get-tuple-element.74), channel_id=1, source_target_pairs={{0,1},{1,0},{2,3},{3,2},{4,5},{5,4},{6,7},{7,6},{8,9},{9,8},{10,11... | collective-permute-start | bytes 1179656 | tf_op jit(solution)/shard_map/ppermute | solution.py:24
  34.6 16.9 %collective-permute-start.14 = (bf16[192,1024]{1,0:T(8,128)(2,1)S(1)}, bf16[192,1024]{1,0:T(8,128)(2,1)S(1)}, u32[]{:S(2)}, u32[]{:S(2)}) collective-permute-start(bf16[192,1024]{1,0:T(8,128)(2,1)S(1)} %get-tuple-element.59.refs_10_), channel_id=1, source_target_pairs={{0,2},{1,3},{2,0},{3,1},{4,6},{5,7},{6,4},{7,5},{8,10},{9,11},{10,... | collective-permute-start | bytes 1179656 | tf_op jit(solution)/shard_map/ppermute | solution.py:24
  38.0 5.0 %copy-start = (bf16[1,1,768,2048]{3,2,1,0:T(8,128)(2,1)S(1)}, bf16[1,1,768,2048]{3,2,1,0:T(8,128)(2,1)}, u32[]{:S(2)}) copy-start(bf16[1,1,768,2048]{3,2,1,0:T(8,128)(2,1)} %param.19) | copy-start | bytes 9437188
  46.3 11.9 %collective-permute-start.12 = (bf16[192,1024]{1,0:T(8,128)(2,1)S(1)}, bf16[192,1024]{1,0:T(8,128)(2,1)S(1)}, u32[]{:S(2)}, u32[]{:S(2)}) collective-permute-start(bf16[192,1024]{1,0:T(8,128)(2,1)S(1)} %get-tuple-element.69), channel_id=1, source_target_pairs={{0,2},{1,3},{2,0},{3,1},{4,6},{5,7},{6,4},{7,5},{8,10},{9,11},{10,... | collective-permute-start | bytes 1179656 | tf_op jit(solution)/shard_map/ppermute | solution.py:24
  47.3 14.3 %collective-permute-start.13 = (bf16[192,1024]{1,0:T(8,128)(2,1)S(1)}, bf16[192,1024]{1,0:T(8,128)(2,1)S(1)}, u32[]{:S(2)}, u32[]{:S(2)}) collective-permute-start(bf16[192,1024]{1,0:T(8,128)(2,1)S(1)} %get-tuple-element.70), channel_id=1, source_target_pairs={{0,1},{1,0},{2,3},{3,2},{4,5},{5,4},{6,7},{7,6},{8,9},{9,8},{10,11... | collective-permute-start | bytes 1179656 | tf_op jit(solution)/shard_map/ppermute | solution.py:24
  55.2 12.1 %collective-permute-start.17 = (bf16[192,1024]{1,0:T(8,128)(2,1)S(1)}, bf16[192,1024]{1,0:T(8,128)(2,1)S(1)}, u32[]{:S(2)}, u32[]{:S(2)}) collective-permute-start(bf16[192,1024]{1,0:T(8,128)(2,1)S(1)} %get-tuple-element.79), channel_id=1, source_target_pairs={{0,2},{1,3},{2,0},{3,1},{4,6},{5,7},{6,4},{7,5},{8,10},{9,11},{10,... | collective-permute-start | bytes 1179656 | tf_op jit(solution)/shard_map/ppermute | solution.py:24
  59.6 12.0 %collective-permute-start.18 = (bf16[192,1024]{1,0:T(8,128)(2,1)S(1)}, bf16[192,1024]{1,0:T(8,128)(2,1)S(1)}, u32[]{:S(2)}, u32[]{:S(2)}) collective-permute-start(bf16[192,1024]{1,0:T(8,128)(2,1)S(1)} %get-tuple-element.80), channel_id=1, source_target_pairs={{0,1},{1,0},{2,3},{3,2},{4,5},{5,4},{6,7},{7,6},{8,9},{9,8},{10,11... | collective-permute-start | bytes 1179656 | tf_op jit(solution)/shard_map/ppermute | solution.py:24
  62.4 14.6 %collective-permute-start.16 = (bf16[128,1024]{1,0:T(8,128)(2,1)S(1)}, bf16[128,1024]{1,0:T(8,128)(2,1)S(1)}, u32[]{:S(2)}, u32[]{:S(2)}) collective-permute-start(bf16[128,1024]{1,0:T(8,128)(2,1)S(1)} %shard_map.127.refs_3_), channel_id=1, source_target_pairs={{0,2},{1,3},{2,0},{3,1},{4,6},{5,7},{6,4},{7,5},{8,10},{9,11},{10,... | collective-permute-start | bytes 786440 | tf_op jit(solution)/shard_map/ppermute | solution.py:24
  67.7 10.2 %collective-permute-start.20 = (bf16[128,1024]{1,0:T(8,128)(2,1)S(1)}, bf16[128,1024]{1,0:T(8,128)(2,1)S(1)}, u32[]{:S(2)}, u32[]{:S(2)}) collective-permute-start(bf16[128,1024]{1,0:T(8,128)(2,1)S(1)} %shard_map.128.refs_3_), channel_id=1, source_target_pairs={{0,1},{1,0},{2,3},{3,2},{4,5},{5,4},{6,7},{7,6},{8,9},{9,8},{10,11... | collective-permute-start | bytes 786440 | tf_op jit(solution)/shard_map/ppermute | solution.py:24
  72.1 8.4 %collective-permute-start.21 = (bf16[128,1024]{1,0:T(8,128)(2,1)S(1)}, bf16[128,1024]{1,0:T(8,128)(2,1)S(1)}, u32[]{:S(2)}, u32[]{:S(2)}) collective-permute-start(bf16[128,1024]{1,0:T(8,128)(2,1)S(1)} %shard_map.129.refs_3_), channel_id=1, source_target_pairs={{0,2},{1,3},{2,0},{3,1},{4,6},{5,7},{6,4},{7,5},{8,10},{9,11},{10,... | collective-permute-start | bytes 786440 | tf_op jit(solution)/shard_map/ppermute | solution.py:24
  74.1 8.8 %collective-permute-start.19 = (bf16[128,1024]{1,0:T(8,128)(2,1)S(1)}, bf16[128,1024]{1,0:T(8,128)(2,1)S(1)}, u32[]{:S(2)}, u32[]{:S(2)}) collective-permute-start(bf16[128,1024]{1,0:T(8,128)(2,1)S(1)} %shard_map.130.refs_5_), channel_id=1, source_target_pairs={{0,1},{1,0},{2,3},{3,2},{4,5},{5,4},{6,7},{7,6},{8,9},{9,8},{10,11... | collective-permute-start | bytes 786440 | tf_op jit(solution)/shard_map/ppermute | solution.py:24
  77.0 3.5 %copy-start.1 = (bf16[1,128,2048]{2,1,0:T(8,128)(2,1)S(1)}, bf16[1,128,2048]{2,1,0:T(8,128)(2,1)}, u32[]{:S(2)}) copy-start(bf16[1,128,2048]{2,1,0:T(8,128)(2,1)} %param.12) | copy-start | bytes 1572868

commit v16 on v14

--- a/solution.py
+++ b/solution.py
@@ -662,8 +662,11 @@
 
 
 def hop_bwd_near_kernel(
-    top_count, own, keep_left, keep_right, got_y, got_x, left_ref, right_ref
+    top_count, own, keep_left, keep_right, got_y, got_x, saved_ref, left_ref, right_ref, inv_ref
 ):
+    wide = saved_ref[...].astype(jnp.float32)
+    inv_rms = lax.rsqrt(jnp.mean(wide * wide, axis=-1, keepdims=True) + EPS)
+    inv_ref[...] = jnp.broadcast_to(inv_rms, inv_ref.shape)
     capacity = keep_left.shape[0]
     mine = pick(own[...], 0, capacity, "b", top_count)
     near_y = pick(own[...], 2, capacity, "b", top_count)
@@ -676,7 +679,7 @@
     order_ref[...] = jnp.zeros_like(order_ref)
 
 
-def hop_bwd_end_kernel(grads_ref, saved_ref, gain_ref, left_ref, right_ref, sum_x, sum_y, out_ref):
+def hop_bwd_end_kernel(grads_ref, saved_ref, gain_ref, left_ref, right_ref, inv_ref, sum_x, sum_y, out_ref):
     features = saved_ref.shape[1]
     half = features // 2
     parts = []
@@ -686,9 +689,8 @@
         wide = saved_ref[:, start : start + half].astype(jnp.float32)
         scaled = d_normed * gain_ref[:, start : start + half]
         parts.append((start, wide, scaled))
-    square = sum(jnp.sum(wide * wide, axis=-1, keepdims=True) for _, wide, _ in parts)
     inner = sum(jnp.sum(scaled * wide, axis=-1, keepdims=True) for _, wide, scaled in parts)
-    inv_rms = lax.rsqrt(square / features + EPS)
+    inv_rms = inv_ref[:, :1]
     factor = inv_rms * inv_rms * inv_rms / features * inner
     for start, wide, scaled in parts:
         out_ref[:, start : start + half] = (
@@ -899,8 +901,8 @@
     )
     b_near = local_call(
         functools.partial(hop_bwd_near_kernel, top_count),
-        [shaped(tok_rows, half, jnp.float32)] * 2,
-        (own, *b_keep, b_ret_y, b_ret_x),
+        [shaped(tok_rows, half, jnp.float32)] * 2 + [shaped(tok_rows, 128, jnp.float32)],
+        (own, *b_keep, b_ret_y, b_ret_x, saved),
         one_hop,
         moved,
         after=(last,),

time: 81.4 us -> 81.4 us (level)
  no operation moved by 1% of the time
where the time goes in v16:
time: 81.4 us; the launch traced here: 81.2 us
  starting transfers between devices  32.5 us (40%)
  Pallas kernels  24.6 us (30%)
  waiting for transfers between devices  23.2 us (29%)
  between operations  0.84 us (1%)
    ppermute x20, starting transfers between devices, swapped(): return lax.ppermute(value, axis, pairs)  29 us
    pallas_call x21, Pallas kernels, local_call(): pl.pallas_call(body if after else kernel, out_shape=out_shapes, in_specs=...  23 us
    ppermute x20, waiting for transfers between devices, swapped(): return lax.ppermute(value, axis, pairs)  20.8 us
    ppermute x2, starting transfers between devices, passed_along(): return lax.ppermute(value, axis, pairs)  3.46 us
    ppermute x2, waiting for transfers between devices, passed_along(): return lax.ppermute(value, axis, pairs)  2.47 us
    pallas_call x1, Pallas kernels, per_device_hops(): pl.pallas_call(functools.partial(first_kernel, top_count), out_shape=[sha...  1.68 us
  transfers between devices with their start and end apart: 22, of which 12 were waited for; matrix products, arithmetic and copies ran while one was open for 0% of the time, Pallas kernels for 29%

profile of v16, /device:TPU:0, one launch (start us, length us, event | category | flops | bytes accessed | tf_op | source)
XLA Modules:
  0.0 81.2 jit_solution(6188826903154244307)
XLA Ops:
  0.6 0.5 collective-permute-start
  1.1 1.7 %shard_map.113 = (bf16[240,1024]{1,0:T(8,128)(2,1)S(1)}, bf16[240,1024]{1,0:T(8,128)(2,1)S(1)}, f32[8,128]{1,0:T(8,128)S(1)}, f32[1,2048]{1,0:T(1,128)S(1)}) custom-call(s32[1]{0:T(128)} %bitcast.1.me_ref, bf16[128,2048]{1,0:T(8,128)(2,1)} %bitcast.29, f32[1,2048]{1,0:T(1,128)} %refs_1_.1, s32[2,128]{1,0:T(2,128)} %bitcast.33, f32[2,128]{1,0:T(2,128)} %bitcast.34, ...), custom_call_target="tpu_custom_call" | custom-call | flops 1024 | bytes 1024 | tf_op jit(solution)/shard_map/pallas_call | solution.py:748
  2.8 2.6 %collective-permute-start.2 = (bf16[240,1024]{1,0:T(8,128)(2,1)S(1)}, bf16[240,1024]{1,0:T(8,128)(2,1)S(1)}, u32[]{:S(2)}, u32[]{:S(2)}) collective-permute-start(bf16[240,1024]{1,0:T(8,128)(2,1)S(1)} %get-tuple-element.47.refs_4_), channel_id=1, source_target_pairs={{0,2},{1,3},{2,0},{3,1},{4,6},{5,7},{6,4},{7,5},{8,10},{9,11},{10,... | collective-permute-start | bytes 1474568 | tf_op jit(solution)/shard_map/ppermute | solution.py:24
  5.4 1.5 %collective-permute-start.1 = (bf16[240,1024]{1,0:T(8,128)(2,1)S(1)}, bf16[240,1024]{1,0:T(8,128)(2,1)S(1)}, u32[]{:S(2)}, u32[]{:S(2)}) collective-permute-start(bf16[240,1024]{1,0:T(8,128)(2,1)S(1)} %get-tuple-element.46.refs_2_.refs_3_), channel_id=1, source_target_pairs={{0,1},{1,0},{2,3},{3,2},{4,5},{5,4},{6,7},{7,6},{8,9},{9,8},{10,11... | collective-permute-start | bytes 1474568 | tf_op jit(solution)/shard_map/ppermute | solution.py:24
  6.9 3.0 %collective-permute-start.5 = (bf16[128,2048]{1,0:T(8,128)(2,1)}, bf16[128,2048]{1,0:T(8,128)(2,1)S(1)}, u32[]{:S(2)}, u32[]{:S(2)}) collective-permute-start(bf16[128,2048]{1,0:T(8,128)(2,1)} %bitcast.38), channel_id=1, source_target_pairs={{0,28},{4,0},{8,4},{12,8},{16,12},{20,16},{24,20},{28,24},{1,29},{... | collective-permute-start | bytes 1572872 | tf_op jit(solution)/shard_map/ppermute | solution.py:18
  9.9 2.5 %collective-permute-done.refs_0_ = bf16[128,2048]{1,0:T(8,128)(2,1)S(1)} collective-permute-done((bf16[128,2048]{1,0:T(8,128)(2,1)}, bf16[128,2048]{1,0:T(8,128)(2,1)S(1)}, u32[]{:S(2)}, u32[]{:S(2)}) %collective-permute-start) | collective-permute-done | bytes 524320 | tf_op jit(solution)/shard_map/ppermute | solution.py:18
  12.3 0.2 shard_map.114
  12.6 2.3 %collective-permute-start.4 = (bf16[128,1024]{1,0:T(8,128)(2,1)S(1)}, bf16[128,1024]{1,0:T(8,128)(2,1)S(1)}, u32[]{:S(2)}, u32[]{:S(2)}) collective-permute-start(bf16[128,1024]{1,0:T(8,128)(2,1)S(1)} %get-tuple-element.52.refs_4_), channel_id=1, source_target_pairs={{0,2},{1,3},{2,0},{3,1},{4,6},{5,7},{6,4},{7,5},{8,10},{9,11},{10,... | collective-permute-start | bytes 786440 | tf_op jit(solution)/shard_map/ppermute | solution.py:24
  14.8 2.4 %collective-permute-start.3 = (bf16[128,1024]{1,0:T(8,128)(2,1)S(1)}, bf16[128,1024]{1,0:T(8,128)(2,1)S(1)}, u32[]{:S(2)}, u32[]{:S(2)}) collective-permute-start(bf16[128,1024]{1,0:T(8,128)(2,1)S(1)} %get-tuple-element.49.refs_2_.refs_3_), channel_id=1, source_target_pairs={{0,1},{1,0},{2,3},{3,2},{4,5},{5,4},{6,7},{7,6},{8,9},{9,8},{10,11... | collective-permute-start | bytes 786440 | tf_op jit(solution)/shard_map/ppermute | solution.py:24
  17.3 0.0 collective-permute-done.2.refs_1_.refs_3_.refs_6_
  17.3 1.9 %collective-permute-done.1.refs_0_.refs_2_.refs_5_ = bf16[240,1024]{1,0:T(8,128)(2,1)S(1)} collective-permute-done((bf16[240,1024]{1,0:T(8,128)(2,1)S(1)}, bf16[240,1024]{1,0:T(8,128)(2,1)S(1)}, u32[]{:S(2)}, u32[]{:S(2)}) %collective-permute-start.1) | collective-permute-done | bytes 491552 | tf_op jit(solution)/shard_map/ppermute | solution.py:24
  19.2 0.0 collective-permute-done.5.refs_0_
  19.2 0.1 collective-permute-start.7
  19.3 2.0 %collective-permute-start.6 = (bf16[128,1024]{1,0:T(8,128)(2,1)S(1)}, bf16[128,1024]{1,0:T(8,128)(2,1)S(1)}, u32[]{:S(2)}, u32[]{:S(2)}) collective-permute-start(bf16[128,1024]{1,0:T(8,128)(2,1)S(1)} %get-tuple-element.53.refs_4_.refs_3_), channel_id=1, source_target_pairs={{0,1},{1,0},{2,3},{3,2},{4,5},{5,4},{6,7},{7,6},{8,9},{9,8},{10,11... | collective-permute-start | bytes 786440 | tf_op jit(solution)/shard_map/ppermute | solution.py:24
  21.3 0.5 shard_map.117
  21.8 0.2 collective-permute-start.9
  22.0 0.1 collective-permute-done.4.refs_6_
  22.1 2.4 %collective-permute-start.8 = (bf16[96,1024]{1,0:T(8,128)(2,1)S(1)}, bf16[96,1024]{1,0:T(8,128)(2,1)S(1)}, u32[]{:S(2)}, u32[]{:S(2)}) collective-permute-start(bf16[96,1024]{1,0:T(8,128)(2,1)S(1)} %get-tuple-element.55.refs_7_), channel_id=1, source_target_pairs={{0,2},{1,3},{2,0},{3,1},{4,6},{5,7},{6,4},{7,5},{8,10},{9,11},{10,... | collective-permute-start | bytes 589832 | tf_op jit(solution)/shard_map/ppermute | solution.py:24
  24.5 0.3 collective-permute-done.3.refs_5_
  24.8 0.9 %shard_map.118 = (bf16[192,1024]{1,0:T(8,128)(2,1)S(1)}, bf16[192,1024]{1,0:T(8,128)(2,1)S(1)}) custom-call(f32[8,128]{1,0:T(8,128)S(1)} %get-tuple-element.45.refs_0_.refs_1_, f32[8,128]{1,0:T(8,128)S(1)} %get-tuple-element.50.refs_1_.refs_0_, f32[8,128]{1,0:T(8,128)S(1)} %get-tuple-element.51.refs_1_.refs_2_.refs_0_, ...), custom_call_target="tpu_custom_call" | custom-call | flops 1024 | bytes 1024 | tf_op jit(solution)/shard_map/pallas_call | solution.py:243
  25.7 1.8 %collective-permute-start.11 = (bf16[192,1024]{1,0:T(8,128)(2,1)S(1)}, bf16[192,1024]{1,0:T(8,128)(2,1)S(1)}, u32[]{:S(2)}, u32[]{:S(2)}) collective-permute-start(bf16[192,1024]{1,0:T(8,128)(2,1)S(1)} %get-tuple-element.64), channel_id=1, source_target_pairs={{0,1},{1,0},{2,3},{3,2},{4,5},{5,4},{6,7},{7,6},{8,9},{9,8},{10,11... | collective-permute-start | bytes 1179656 | tf_op jit(solution)/shard_map/ppermute | solution.py:24
  27.5 1.1 %collective-permute-done.7.refs_6_ = bf16[128,1024]{1,0:T(8,128)(2,1)S(1)} collective-permute-done((bf16[128,1024]{1,0:T(8,128)(2,1)S(1)}, bf16[128,1024]{1,0:T(8,128)(2,1)S(1)}, u32[]{:S(2)}, u32[]{:S(2)}) %collective-permute-start.7) | collective-permute-done | bytes 262176 | tf_op jit(solution)/shard_map/ppermute | solution.py:24
  28.6 1.5 %collective-permute-start.10 = (bf16[192,1024]{1,0:T(8,128)(2,1)S(1)}, bf16[192,1024]{1,0:T(8,128)(2,1)S(1)}, u32[]{:S(2)}, u32[]{:S(2)}) collective-permute-start(bf16[192,1024]{1,0:T(8,128)(2,1)S(1)} %get-tuple-element.57.refs_7_), channel_id=1, source_target_pairs={{0,2},{1,3},{2,0},{3,1},{4,6},{5,7},{6,4},{7,5},{8,10},{9,11},{10,... | collective-permute-start | bytes 1179656 | tf_op jit(solution)/shard_map/ppermute | solution.py:24
  30.1 0.3 collective-permute-done.6.refs_5_
  30.4 1.1 %shard_map.119 = (bf16[192,1024]{1,0:T(8,128)(2,1)S(1)}, bf16[192,1024]{1,0:T(8,128)(2,1)S(1)}) custom-call(f32[8,128]{1,0:T(8,128)S(1)} %get-tuple-element.45.refs_0_.refs_1_, f32[8,128]{1,0:T(8,128)S(1)} %get-tuple-element.50.refs_1_.refs_0_, f32[8,128]{1,0:T(8,128)S(1)} %get-tuple-element.51.refs_1_.refs_2_.refs_0_, ...), custom_call_target="tpu_custom_call" | custom-call | flops 1024 | bytes 1024 | tf_op jit(solution)/shard_map/pallas_call | solution.py:243
  31.5 1.8 %collective-permute-start.15 = (bf16[192,1024]{1,0:T(8,128)(2,1)S(1)}, bf16[192,1024]{1,0:T(8,128)(2,1)S(1)}, u32[]{:S(2)}, u32[]{:S(2)}) collective-permute-start(bf16[192,1024]{1,0:T(8,128)(2,1)S(1)} %get-tuple-element.73), channel_id=1, source_target_pairs={{0,1},{1,0},{2,3},{3,2},{4,5},{5,4},{6,7},{7,6},{8,9},{9,8},{10,11... | collective-permute-start | bytes 1179656 | tf_op jit(solution)/shard_map/ppermute | solution.py:24
  33.3 1.3 %collective-permute-done.9.refs_8_ = bf16[96,1024]{1,0:T(8,128)(2,1)S(1)} collective-permute-done((bf16[96,1024]{1,0:T(8,128)(2,1)S(1)}, bf16[96,1024]{1,0:T(8,128)(2,1)S(1)}, u32[]{:S(2)}, u32[]{:S(2)}) %collective-permute-start.9) | collective-permute-done | bytes 196640 | tf_op jit(solution)/shard_map/ppermute | solution.py:24
  34.6 0.2 collective-permute-start.14
  34.8 0.0 collective-permute-done.8.refs_7_
  34.8 3.2 %shard_map.120 = (f32[384,768]{1,0:T(8,128)S(1)}, f32[384,768]{1,0:T(8,128)S(1)}) custom-call(f32[8,128]{1,0:T(8,128)S(1)} %get-tuple-element.45.refs_0_.refs_1_, f32[8,128]{1,0:T(8,128)S(1)} %get-tuple-element.50.refs_1_.refs_0_, f32[8,128]{1,0:T(8,128)S(1)} %get-tuple-element.51.refs_1_.refs_2_.refs_0_, ...), custom_call_target="tpu_custom_call" | custom-call | flops 2415919104 | bytes 14155776 | tf_op jit(solution)/shard_map/pallas_call | solution.py:243
  38.0 0.0 copy-start
  38.0 1.0 %shard_map.121 = (bf16[96,2048]{1,0:T(8,128)(2,1)S(1)}, bf16[96,1024]{1,0:T(8,128)(2,1)S(1)}, bf16[96,1024]{1,0:T(8,128)(2,1)S(1)}) custom-call(f32[8,128]{1,0:T(8,128)S(1)} %get-tuple-element.45.refs_0_.refs_1_, f32[8,128]{1,0:T(8,128)S(1)} %get-tuple-element.50.refs_1_.refs_0_, f32[8,128]{1,0:T(8,128)S(1)} %get-tuple-element.51.refs_1_.refs_2_.refs_0_, ...), custom_call_target="tpu_custom_call" | custom-call | flops 1024 | bytes 1024 | tf_op jit(solution)/shard_map/pallas_call | solution.py:243
  39.0 0.8 shard_map.122
  39.8 3.2 %collective-permute-done.11.refs_4_ = bf16[192,1024]{1,0:T(8,128)(2,1)S(1)} collective-permute-done((bf16[192,1024]{1,0:T(8,128)(2,1)S(1)}, bf16[192,1024]{1,0:T(8,128)(2,1)S(1)}, u32[]{:S(2)}, u32[]{:S(2)}) %collective-permute-start.11) | collective-permute-done | bytes 393248 | tf_op jit(solution)/shard_map/ppermute | solution.py:24
  43.0 0.0 collective-permute-done.10.refs_3_
  43.1 3.2 %shard_map.123 = (bf16[96,1024]{1,0:T(8,128)(2,1)S(1)}, bf16[96,1024]{1,0:T(8,128)(2,1)S(1)}, bf16[192,1024]{1,0:T(8,128)(2,1)S(1)}, bf16[384,768]{1,0:T(8,128)(2,1)S(1)}) custom-call(bf16[96,2048]{1,0:T(8,128)(2,1)S(1)} %get-tuple-element.61.refs_0_, bf16[96,1024]{1,0:T(8,128)(2,1)S(1)} %get-tuple-element.62.refs_1_.refs_7_, ...), custom_call_target="tpu_custom_call" | custom-call | flops 3019898880 | bytes 14155776 | tf_op jit(solution)/shard_map/pallas_call | solution.py:243
  46.3 0.2 collective-permute-start.12
  46.5 0.8 shard_map.124
  47.3 1.9 %collective-permute-start.13 = (bf16[192,1024]{1,0:T(8,128)(2,1)S(1)}, bf16[192,1024]{1,0:T(8,128)(2,1)S(1)}, u32[]{:S(2)}, u32[]{:S(2)}) collective-permute-start(bf16[192,1024]{1,0:T(8,128)(2,1)S(1)} %get-tuple-element.69), channel_id=1, source_target_pairs={{0,1},{1,0},{2,3},{3,2},{4,5},{5,4},{6,7},{7,6},{8,9},{9,8},{10,11... | collective-permute-start | bytes 1179656 | tf_op jit(solution)/shard_map/ppermute | solution.py:24
  49.2 2.3 %collective-permute-done.15.refs_4_ = bf16[192,1024]{1,0:T(8,128)(2,1)S(1)} collective-permute-done((bf16[192,1024]{1,0:T(8,128)(2,1)S(1)}, bf16[192,1024]{1,0:T(8,128)(2,1)S(1)}, u32[]{:S(2)}, u32[]{:S(2)}) %collective-permute-start.15) | collective-permute-done | bytes 393248 | tf_op jit(solution)/shard_map/ppermute | solution.py:24
  51.5 0.0 collective-permute-done.14.refs_3_
  51.5 3.7 %shard_map.125 = (bf16[96,1024]{1,0:T(8,128)(2,1)S(1)}, bf16[96,1024]{1,0:T(8,128)(2,1)S(1)}, bf16[192,1024]{1,0:T(8,128)(2,1)S(1)}, bf16[384,1536]{1,0:T(8,128)(2,1)S(1)}) custom-call(bf16[96,2048]{1,0:T(8,128)(2,1)S(1)} %get-tuple-element.71.refs_0_, bf16[96,1024]{1,0:T(8,128)(2,1)S(1)} %get-tuple-element.60.refs_7_.refs_1_, ...), custom_call_target="tpu_custom_call" | custom-call | flops 2415919104 | bytes 14155776 | tf_op jit(solution)/shard_map/pallas_call | solution.py:243
  55.2 0.2 collective-permute-start.19
  55.5 1.4 %shard_map.126 = (bf16[96,1024]{1,0:T(8,128)(2,1)S(1)}, bf16[96,1024]{1,0:T(8,128)(2,1)S(1)}, bf16[192,1024]{1,0:T(8,128)(2,1)S(1)}) custom-call(bf16[384,1536]{1,0:T(8,128)(2,1)S(1)} %get-tuple-element.75.both_ref, bf16[2048,1536]{1,0:T(8,128)(2,1)S(1)} %bitcast.25), custom_call_target="tpu_custom_call" | custom-call | flops 1024 | bytes 1024 | tf_op jit(solution)/shard_map/pallas_call | solution.py:243
  56.9 1.9 %collective-permute-start.18 = (bf16[192,1024]{1,0:T(8,128)(2,1)S(1)}, bf16[192,1024]{1,0:T(8,128)(2,1)S(1)}, u32[]{:S(2)}, u32[]{:S(2)}) collective-permute-start(bf16[192,1024]{1,0:T(8,128)(2,1)S(1)} %get-tuple-element.79), channel_id=1, source_target_pairs={{0,1},{1,0},{2,3},{3,2},{4,5},{5,4},{6,7},{7,6},{8,9},{9,8},{10,11... | collective-permute-start | bytes 1179656 | tf_op jit(solution)/shard_map/ppermute | solution.py:24
  58.8 0.0 collective-permute-done.12.refs_2_.refs_4_
  58.8 0.8 shard_map.127.refs_3_
  59.6 1.4 %collective-permute-start.16 = (bf16[128,1024]{1,0:T(8,128)(2,1)S(1)}, bf16[128,1024]{1,0:T(8,128)(2,1)S(1)}, u32[]{:S(2)}, u32[]{:S(2)}) collective-permute-start(bf16[128,1024]{1,0:T(8,128)(2,1)S(1)} %shard_map.127.refs_3_), channel_id=1, source_target_pairs={{0,1},{1,0},{2,3},{3,2},{4,5},{5,4},{6,7},{7,6},{8,9},{9,8},{10,11... | collective-permute-start | bytes 786440 | tf_op jit(solution)/shard_map/ppermute | solution.py:24
  61.0 0.0 collective-permute-done.13.refs_2_.refs_5_
  61.0 0.8 shard_map.128.refs_3_
  61.8 0.0 copy-start.1
  61.8 1.6 %collective-permute-start.17 = (bf16[128,1024]{1,0:T(8,128)(2,1)S(1)}, bf16[128,1024]{1,0:T(8,128)(2,1)S(1)}, u32[]{:S(2)}, u32[]{:S(2)}) collective-permute-start(bf16[128,1024]{1,0:T(8,128)(2,1)S(1)} %shard_map.128.refs_3_), channel_id=1, source_target_pairs={{0,2},{1,3},{2,0},{3,1},{4,6},{5,7},{6,4},{7,5},{8,10},{9,11},{10,... | collective-permute-start | bytes 786440 | tf_op jit(solution)/shard_map/ppermute | solution.py:24
  63.4 3.9 %collective-permute-done.19.refs_2_.refs_3_ = bf16[192,1024]{1,0:T(8,128)(2,1)S(1)} collective-permute-done((bf16[192,1024]{1,0:T(8,128)(2,1)S(1)}, bf16[192,1024]{1,0:T(8,128)(2,1)S(1)}, u32[]{:S(2)}, u32[]{:S(2)}) %collective-permute-start.19) | collective-permute-done | bytes 393248 | tf_op jit(solution)/shard_map/ppermute | solution.py:24
  67.3 0.4 shard_map.129.refs_3_
  67.7 1.9 %collective-permute-start.20 = (bf16[128,1024]{1,0:T(8,128)(2,1)S(1)}, bf16[128,1024]{1,0:T(8,128)(2,1)S(1)}, u32[]{:S(2)}, u32[]{:S(2)}) collective-permute-start(bf16[128,1024]{1,0:T(8,128)(2,1)S(1)} %shard_map.129.refs_3_), channel_id=1, source_target_pairs={{0,1},{1,0},{2,3},{3,2},{4,5},{5,4},{6,7},{7,6},{8,9},{9,8},{10,11... | collective-permute-start | bytes 786440 | tf_op jit(solution)/shard_map/ppermute | solution.py:24
  69.6 0.0 collective-permute-done.18.refs_2_.refs_4_
  69.6 0.5 shard_map.130.refs_8_.refs_6_
  70.1 1.2 %collective-permute-start.21 = (bf16[128,1024]{1,0:T(8,128)(2,1)S(1)}, bf16[128,1024]{1,0:T(8,128)(2,1)S(1)}, u32[]{:S(2)}, u32[]{:S(2)}) collective-permute-start(bf16[128,1024]{1,0:T(8,128)(2,1)S(1)} %shard_map.130.refs_8_.refs_6_), channel_id=1, source_target_pairs={{0,2},{1,3},{2,0},{3,1},{4,6},{5,7},{6,4},{7,5},{8,10},{9,11},{10,... | collective-permute-start | bytes 786440 | tf_op jit(solution)/shard_map/ppermute | solution.py:24
  71.2 0.6 shard_map.132
  71.9 2.8 %collective-permute-done.16.refs_6_ = bf16[128,1024]{1,0:T(8,128)(2,1)S(1)} collective-permute-done((bf16[128,1024]{1,0:T(8,128)(2,1)S(1)}, bf16[128,1024]{1,0:T(8,128)(2,1)S(1)}, u32[]{:S(2)}, u32[]{:S(2)}) %collective-permute-start.16) | collective-permute-done | bytes 262176 | tf_op jit(solution)/shard_map/ppermute | solution.py:24
  74.6 0.0 collective-permute-done.17.refs_7_
  74.6 1.7 %shard_map.131 = (bf16[128,2048]{1,0:T(8,128)(2,1)}, f32[8,128]{1,0:T(8,128)S(1)}) custom-call(bf16[128,2048]{1,0:T(8,128)(2,1)S(1)} %collective-permute-done.refs_0_, f32[8,128]{1,0:T(8,128)S(1)} %get-tuple-element.45.refs_0_.refs_1_, bf16[96,1024]{1,0:T(8,128)(2,1)S(1)} %get-tuple-element.65.refs_2_, ...), custom_call_target="tpu_custom_call" | custom-call | flops 1024 | bytes 1024 | tf_op jit(solution)/shard_map/pallas_call | solution.py:243
  76.3 3.6 %collective-permute-done.20.refs_2_.refs_6_ = bf16[128,1024]{1,0:T(8,128)(2,1)S(1)} collective-permute-done((bf16[128,1024]{1,0:T(8,128)(2,1)S(1)}, bf16[128,1024]{1,0:T(8,128)(2,1)S(1)}, u32[]{:S(2)}, u32[]{:S(2)}) %collective-permute-start.20) | collective-permute-done | bytes 262176 | tf_op jit(solution)/shard_map/ppermute | solution.py:24
  79.9 1.3 %shard_map.134 = bf16[128,2048]{1,0:T(8,128)(2,1)} custom-call(bf16[128,2048]{1,0:T(8,128)(2,1)S(1)} %collective-permute-done.5.refs_0_, bf16[128,2048]{1,0:T(8,128)(2,1)S(1)} %bitcast.31, f32[1,2048]{1,0:T(1,128)S(1)} %get-tuple-element.48.refs_1_.refs_2_, f32[128,1024]{1,0:T(8,128)S(1)} %get-tuple-element.84.refs_1_.refs_3_, ...), custom_call_target="tpu_custom_call" | custom-call | flops 1024 | bytes 1024 | tf_op jit(solution)/shard_map/pallas_call | solution.py:243
  (11 shorter events, 0.1 us)
Async XLA Ops:
  0.6 11.7 %collective-permute-start = (bf16[128,2048]{1,0:T(8,128)(2,1)}, bf16[128,2048]{1,0:T(8,128)(2,1)S(1)}, u32[]{:S(2)}, u32[]{:S(2)}) collective-permute-start(bf16[128,2048]{1,0:T(8,128)(2,1)} %bitcast.37), channel_id=1, source_target_pairs={{0,4},{4,8},{8,12},{12,16},{16,20},{20,24},{24,28},{28,0},{1,5},{5... | collective-permute-start | bytes 1572872 | tf_op jit(solution)/shard_map/ppermute | solution.py:18
  2.8 14.5 %collective-permute-start.2 = (bf16[240,1024]{1,0:T(8,128)(2,1)S(1)}, bf16[240,1024]{1,0:T(8,128)(2,1)S(1)}, u32[]{:S(2)}, u32[]{:S(2)}) collective-permute-start(bf16[240,1024]{1,0:T(8,128)(2,1)S(1)} %get-tuple-element.47.refs_4_), channel_id=1, source_target_pairs={{0,2},{1,3},{2,0},{3,1},{4,6},{5,7},{6,4},{7,5},{8,10},{9,11},{10,... | collective-permute-start | bytes 1474568 | tf_op jit(solution)/shard_map/ppermute | solution.py:24
  5.4 13.8 %collective-permute-start.1 = (bf16[240,1024]{1,0:T(8,128)(2,1)S(1)}, bf16[240,1024]{1,0:T(8,128)(2,1)S(1)}, u32[]{:S(2)}, u32[]{:S(2)}) collective-permute-start(bf16[240,1024]{1,0:T(8,128)(2,1)S(1)} %get-tuple-element.46.refs_2_.refs_3_), channel_id=1, source_target_pairs={{0,1},{1,0},{2,3},{3,2},{4,5},{5,4},{6,7},{7,6},{8,9},{9,8},{10,11... | collective-permute-start | bytes 1474568 | tf_op jit(solution)/shard_map/ppermute | solution.py:24
  6.9 12.3 %collective-permute-start.5 = (bf16[128,2048]{1,0:T(8,128)(2,1)}, bf16[128,2048]{1,0:T(8,128)(2,1)S(1)}, u32[]{:S(2)}, u32[]{:S(2)}) collective-permute-start(bf16[128,2048]{1,0:T(8,128)(2,1)} %bitcast.38), channel_id=1, source_target_pairs={{0,28},{4,0},{8,4},{12,8},{16,12},{20,16},{24,20},{28,24},{1,29},{... | collective-permute-start | bytes 1572872 | tf_op jit(solution)/shard_map/ppermute | solution.py:18
  12.3 22.5 %slice-start = ((s8[6291456]{0:T(1024)(128)(4,1)}), s8[4194304]{0:T(1024)(128)(4,1)S(1)}, s32[]{:S(2)}) async-start(s8[6291456]{0:T(1024)(128)(4,1)} %bitcast.20), calls=%async_computation | async-start | bytes 8388608
  12.6 9.5 %collective-permute-start.4 = (bf16[128,1024]{1,0:T(8,128)(2,1)S(1)}, bf16[128,1024]{1,0:T(8,128)(2,1)S(1)}, u32[]{:S(2)}, u32[]{:S(2)}) collective-permute-start(bf16[128,1024]{1,0:T(8,128)(2,1)S(1)} %get-tuple-element.52.refs_4_), channel_id=1, source_target_pairs={{0,2},{1,3},{2,0},{3,1},{4,6},{5,7},{6,4},{7,5},{8,10},{9,11},{10,... | collective-permute-start | bytes 786440 | tf_op jit(solution)/shard_map/ppermute | solution.py:24
  14.8 20.0 %slice-start.1 = ((s8[6291456]{0:T(1024)(128)(4,1)}), s8[2097152]{0:T(1024)(128)(4,1)S(1)}, s32[]{:S(2)}) async-start(s8[6291456]{0:T(1024)(128)(4,1)} %bitcast.20), calls=%async_computation.1 | async-start | bytes 4194304
  14.8 10.0 %collective-permute-start.3 = (bf16[128,1024]{1,0:T(8,128)(2,1)S(1)}, bf16[128,1024]{1,0:T(8,128)(2,1)S(1)}, u32[]{:S(2)}, u32[]{:S(2)}) collective-permute-start(bf16[128,1024]{1,0:T(8,128)(2,1)S(1)} %get-tuple-element.49.refs_2_.refs_3_), channel_id=1, source_target_pairs={{0,1},{1,0},{2,3},{3,2},{4,5},{5,4},{6,7},{7,6},{8,9},{9,8},{10,11... | collective-permute-start | bytes 786440 | tf_op jit(solution)/shard_map/ppermute | solution.py:24
  19.2 9.3 %collective-permute-start.7 = (bf16[128,1024]{1,0:T(8,128)(2,1)S(1)}, bf16[128,1024]{1,0:T(8,128)(2,1)S(1)}, u32[]{:S(2)}, u32[]{:S(2)}) collective-permute-start(bf16[128,1024]{1,0:T(8,128)(2,1)S(1)} %get-tuple-element.54.refs_4_), channel_id=1, source_target_pairs={{0,2},{1,3},{2,0},{3,1},{4,6},{5,7},{6,4},{7,5},{8,10},{9,11},{10,... | collective-permute-start | bytes 786440 | tf_op jit(solution)/shard_map/ppermute | solution.py:24
  19.3 11.1 %collective-permute-start.6 = (bf16[128,1024]{1,0:T(8,128)(2,1)S(1)}, bf16[128,1024]{1,0:T(8,128)(2,1)S(1)}, u32[]{:S(2)}, u32[]{:S(2)}) collective-permute-start(bf16[128,1024]{1,0:T(8,128)(2,1)S(1)} %get-tuple-element.53.refs_4_.refs_3_), channel_id=1, source_target_pairs={{0,1},{1,0},{2,3},{3,2},{4,5},{5,4},{6,7},{7,6},{8,9},{9,8},{10,11... | collective-permute-start | bytes 786440 | tf_op jit(solution)/shard_map/ppermute | solution.py:24
  21.8 12.8 %collective-permute-start.9 = (bf16[96,1024]{1,0:T(8,128)(2,1)S(1)}, bf16[96,1024]{1,0:T(8,128)(2,1)S(1)}, u32[]{:S(2)}, u32[]{:S(2)}) collective-permute-start(bf16[96,1024]{1,0:T(8,128)(2,1)S(1)} %get-tuple-element.56), channel_id=1, source_target_pairs={{0,1},{1,0},{2,3},{3,2},{4,5},{5,4},{6,7},{7,6},{8,9},{9,8},{10,11... | collective-permute-start | bytes 589832 | tf_op jit(solution)/shard_map/ppermute | solution.py:24
  22.1 12.7 %collective-permute-start.8 = (bf16[96,1024]{1,0:T(8,128)(2,1)S(1)}, bf16[96,1024]{1,0:T(8,128)(2,1)S(1)}, u32[]{:S(2)}, u32[]{:S(2)}) collective-permute-start(bf16[96,1024]{1,0:T(8,128)(2,1)S(1)} %get-tuple-element.55.refs_7_), channel_id=1, source_target_pairs={{0,2},{1,3},{2,0},{3,1},{4,6},{5,7},{6,4},{7,5},{8,10},{9,11},{10,... | collective-permute-start | bytes 589832 | tf_op jit(solution)/shard_map/ppermute | solution.py:24
  25.7 17.4 %collective-permute-start.11 = (bf16[192,1024]{1,0:T(8,128)(2,1)S(1)}, bf16[192,1024]{1,0:T(8,128)(2,1)S(1)}, u32[]{:S(2)}, u32[]{:S(2)}) collective-permute-start(bf16[192,1024]{1,0:T(8,128)(2,1)S(1)} %get-tuple-element.64), channel_id=1, source_target_pairs={{0,1},{1,0},{2,3},{3,2},{4,5},{5,4},{6,7},{7,6},{8,9},{9,8},{10,11... | collective-permute-start | bytes 1179656 | tf_op jit(solution)/shard_map/ppermute | solution.py:24
  28.6 14.5 %collective-permute-start.10 = (bf16[192,1024]{1,0:T(8,128)(2,1)S(1)}, bf16[192,1024]{1,0:T(8,128)(2,1)S(1)}, u32[]{:S(2)}, u32[]{:S(2)}) collective-permute-start(bf16[192,1024]{1,0:T(8,128)(2,1)S(1)} %get-tuple-element.57.refs_7_), channel_id=1, source_target_pairs={{0,2},{1,3},{2,0},{3,1},{4,6},{5,7},{6,4},{7,5},{8,10},{9,11},{10,... | collective-permute-start | bytes 1179656 | tf_op jit(solution)/shard_map/ppermute | solution.py:24
  31.5 19.9 %collective-permute-start.15 = (bf16[192,1024]{1,0:T(8,128)(2,1)S(1)}, bf16[192,1024]{1,0:T(8,128)(2,1)S(1)}, u32[]{:S(2)}, u32[]{:S(2)}) collective-permute-start(bf16[192,1024]{1,0:T(8,128)(2,1)S(1)} %get-tuple-element.73), channel_id=1, source_target_pairs={{0,1},{1,0},{2,3},{3,2},{4,5},{5,4},{6,7},{7,6},{8,9},{9,8},{10,11... | collective-permute-start | bytes 1179656 | tf_op jit(solution)/shard_map/ppermute | solution.py:24
  34.6 16.9 %collective-permute-start.14 = (bf16[192,1024]{1,0:T(8,128)(2,1)S(1)}, bf16[192,1024]{1,0:T(8,128)(2,1)S(1)}, u32[]{:S(2)}, u32[]{:S(2)}) collective-permute-start(bf16[192,1024]{1,0:T(8,128)(2,1)S(1)} %get-tuple-element.58.refs_10_), channel_id=1, source_target_pairs={{0,2},{1,3},{2,0},{3,1},{4,6},{5,7},{6,4},{7,5},{8,10},{9,11},{10,... | collective-permute-start | bytes 1179656 | tf_op jit(solution)/shard_map/ppermute | solution.py:24
  38.0 5.0 %copy-start = (bf16[1,1,768,2048]{3,2,1,0:T(8,128)(2,1)S(1)}, bf16[1,1,768,2048]{3,2,1,0:T(8,128)(2,1)}, u32[]{:S(2)}) copy-start(bf16[1,1,768,2048]{3,2,1,0:T(8,128)(2,1)} %param.19) | copy-start | bytes 9437188
  46.3 12.5 %collective-permute-start.12 = (bf16[192,1024]{1,0:T(8,128)(2,1)S(1)}, bf16[192,1024]{1,0:T(8,128)(2,1)S(1)}, u32[]{:S(2)}, u32[]{:S(2)}) collective-permute-start(bf16[192,1024]{1,0:T(8,128)(2,1)S(1)} %get-tuple-element.68), channel_id=1, source_target_pairs={{0,2},{1,3},{2,0},{3,1},{4,6},{5,7},{6,4},{7,5},{8,10},{9,11},{10,... | collective-permute-start | bytes 1179656 | tf_op jit(solution)/shard_map/ppermute | solution.py:24
  47.3 13.7 %collective-permute-start.13 = (bf16[192,1024]{1,0:T(8,128)(2,1)S(1)}, bf16[192,1024]{1,0:T(8,128)(2,1)S(1)}, u32[]{:S(2)}, u32[]{:S(2)}) collective-permute-start(bf16[192,1024]{1,0:T(8,128)(2,1)S(1)} %get-tuple-element.69), channel_id=1, source_target_pairs={{0,1},{1,0},{2,3},{3,2},{4,5},{5,4},{6,7},{7,6},{8,9},{9,8},{10,11... | collective-permute-start | bytes 1179656 | tf_op jit(solution)/shard_map/ppermute | solution.py:24
  55.2 12.1 %collective-permute-start.19 = (bf16[192,1024]{1,0:T(8,128)(2,1)S(1)}, bf16[192,1024]{1,0:T(8,128)(2,1)S(1)}, u32[]{:S(2)}, u32[]{:S(2)}) collective-permute-start(bf16[192,1024]{1,0:T(8,128)(2,1)S(1)} %get-tuple-element.81), channel_id=1, source_target_pairs={{0,2},{1,3},{2,0},{3,1},{4,6},{5,7},{6,4},{7,5},{8,10},{9,11},{10,... | collective-permute-start | bytes 1179656 | tf_op jit(solution)/shard_map/ppermute | solution.py:24
  56.9 12.7 %collective-permute-start.18 = (bf16[192,1024]{1,0:T(8,128)(2,1)S(1)}, bf16[192,1024]{1,0:T(8,128)(2,1)S(1)}, u32[]{:S(2)}, u32[]{:S(2)}) collective-permute-start(bf16[192,1024]{1,0:T(8,128)(2,1)S(1)} %get-tuple-element.79), channel_id=1, source_target_pairs={{0,1},{1,0},{2,3},{3,2},{4,5},{5,4},{6,7},{7,6},{8,9},{9,8},{10,11... | collective-permute-start | bytes 1179656 | tf_op jit(solution)/shard_map/ppermute | solution.py:24
  59.6 15.0 %collective-permute-start.16 = (bf16[128,1024]{1,0:T(8,128)(2,1)S(1)}, bf16[128,1024]{1,0:T(8,128)(2,1)S(1)}, u32[]{:S(2)}, u32[]{:S(2)}) collective-permute-start(bf16[128,1024]{1,0:T(8,128)(2,1)S(1)} %shard_map.127.refs_3_), channel_id=1, source_target_pairs={{0,1},{1,0},{2,3},{3,2},{4,5},{5,4},{6,7},{7,6},{8,9},{9,8},{10,11... | collective-permute-start | bytes 786440 | tf_op jit(solution)/shard_map/ppermute | solution.py:24
  61.8 9.5 %copy-start.1 = (bf16[1,128,2048]{2,1,0:T(8,128)(2,1)S(1)}, bf16[1,128,2048]{2,1,0:T(8,128)(2,1)}, u32[]{:S(2)}) copy-start(bf16[1,128,2048]{2,1,0:T(8,128)(2,1)} %param.12) | copy-start | bytes 1572868
  61.8 12.8 %collective-permute-start.17 = (bf16[128,1024]{1,0:T(8,128)(2,1)S(1)}, bf16[128,1024]{1,0:T(8,128)(2,1)S(1)}, u32[]{:S(2)}, u32[]{:S(2)}) collective-permute-start(bf16[128,1024]{1,0:T(8,128)(2,1)S(1)} %shard_map.128.refs_3_), channel_id=1, source_target_pairs={{0,2},{1,3},{2,0},{3,1},{4,6},{5,7},{6,4},{7,5},{8,10},{9,11},{10,... | collective-permute-start | bytes 786440 | tf_op jit(solution)/shard_map/ppermute | solution.py:24
  67.7 12.2 %collective-permute-start.20 = (bf16[128,1024]{1,0:T(8,128)(2,1)S(1)}, bf16[128,1024]{1,0:T(8,128)(2,1)S(1)}, u32[]{:S(2)}, u32[]{:S(2)}) collective-permute-start(bf16[128,1024]{1,0:T(8,128)(2,1)S(1)} %shard_map.129.refs_3_), channel_id=1, source_target_pairs={{0,1},{1,0},{2,3},{3,2},{4,5},{5,4},{6,7},{7,6},{8,9},{9,8},{10,11... | collective-permute-start | bytes 786440 | tf_op jit(solution)/shard_map/ppermute | solution.py:24
  70.1 9.8 %collective-permute-start.21 = (bf16[128,1024]{1,0:T(8,128)(2,1)S(1)}, bf16[128,1024]{1,0:T(8,128)(2,1)S(1)}, u32[]{:S(2)}, u32[]{:S(2)}) collective-permute-start(bf16[128,1024]{1,0:T(8,128)(2,1)S(1)} %shard_map.130.refs_8_.refs_6_), channel_id=1, source_target_pairs={{0,2},{1,3},{2,0},{3,1},{4,6},{5,7},{6,4},{7,5},{8,10},{9,11},{10,... | collective-permute-start | bytes 786440 | tf_op jit(solution)/shard_map/ppermute | solution.py:24
